TPU v7x, 32 devices: a whole 2x2x4 slice. The times are simulated.
32 devices in a mesh: set: 1, kb: 32 (over z, y, x, core).
Axes of the slice: x: 2, y: 2, z: 4, core: 2. Of those that a mesh axis runs over, the one named last changes fastest.
Arguments:
- green_momentum_grid: float32 [2, 4, 4096, 512], P('set', None, 'kb'), may hold values from -6 to 6
- pair_table: int32 [8, 2], replicated, may hold values from 0 to 3, as said below
- mirror_map: int32 [3, 16], P('set'), may hold values from 0 to 15, as said below
Outputs:
- chi_out: float32 [2, 8, 4096, 512], P('set', None, 'kb')
Inputs may be any that keep to these rules, and one draw needn't show every extreme that they name: `pair_table`: each of the two columns names every entry number 0 to 3 at least once. Each row d is a reflection: mirror_map[d,x] = (c_d - x) mod 16 for a centre c_d of that row.
All inputs are finite; a program needn't handle non-finite values.
Results may differ from a plain program's by a relative error of at most 0.0003.
Values sent between devices are 32-bit elements; how exact they have to be, the bound alone decides.
No kernel may reach another device: no remote copies, remote signals or barrier semaphores. Data moves between devices by JAX's collectives and lax.ppermute only.
A program may use at most 128 MiB of HBM per device.

v0:
```python
import functools
import math

import jax
import jax.numpy as jnp
import ml_dtypes
import numpy as np
from jax import lax
from jax.experimental import pallas as pl
from jax.experimental.pallas import tpu as pltpu
from jax.sharding import PartitionSpec as P

LANES = 128
ROWS = 8
GROUPS = 2


def split_constant(matrix):
    high = matrix.astype(np.float32).astype(ml_dtypes.bfloat16)
    low = (matrix - high.astype(np.float64)).astype(np.float32).astype(ml_dtypes.bfloat16)
    return high, low


def split_value(value):
    high = value.astype(jnp.bfloat16)
    low = (value - high.astype(jnp.float32)).astype(jnp.bfloat16)
    return high, low


def dot3(left, right, dims):
    (k_left,), (k_right,) = dims
    a = jnp.concatenate([left[0], left[0], left[1]], axis=k_left)
    b = jnp.concatenate([right[0], right[1], right[0]], axis=k_right)
    return lax.dot_general(a, b, (dims, ((), ())), preferred_element_type=jnp.float32)


def fermion_matrix(rows, count):
    n = np.arange(count, dtype=np.int64)
    angle = ((2 * n[None, :] - count + 1) * (2 * rows[:, None] + 1)) % (4 * count)
    angle = np.pi * angle / (2 * count)
    return np.concatenate([np.cos(angle), np.sin(angle)], axis=0) * count**-0.5


def boson_matrix(rows, count):
    v = np.arange(count, dtype=np.int64)
    angle = ((v[None, :] - count // 2) * (2 * rows[:, None] + 1)) % (2 * count)
    angle = np.pi * angle / count
    return np.concatenate([np.cos(angle), np.sin(angle)], axis=0) * count**-0.5


def plane_parts(side):
    p = np.arange(side * side, dtype=np.int64)
    angle = ((p[:, None] // side) * (p[None, :] // side) + (p[:, None] % side) * (p[None, :] % side)) % side
    angle = 2 * np.pi * angle / side
    scale = side**-1.5
    return np.cos(angle) * scale, np.sin(angle) * scale


def times_w4(re, im, power, sign):
    power = (power * sign) % 4
    if power == 0:
        return re, im
    if power == 1:
        return -im, re
    if power == 2:
        return -re, -im
    return im, -re


def dft4(values, sign):
    (r0, i0), (r1, i1), (r2, i2), (r3, i3) = values
    sr, si, dr, di = r0 + r2, i0 + i2, r0 - r2, i0 - i2
    tr, ti, er, ei = r1 + r3, i1 + i3, r1 - r3, i1 - i3
    if sign > 0:
        return [(sr + tr, si + ti), (dr - ei, di + er), (sr - tr, si - ti), (dr + ei, di - er)]
    return [(sr + tr, si + ti), (dr + ei, di - er), (sr - tr, si - ti), (dr - ei, di + er)]


def twiddle(value, power, sign, side):
    re, im = value
    if power % (side // 4) == 0:
        return times_w4(re, im, power // (side // 4), sign)
    angle = 2.0 * np.pi * power / side
    c, s = float(np.cos(angle)), float(sign * np.sin(angle))
    return re * c - im * s, re * s + im * c


def dft_line(values, sign):
    side = len(values)
    if side == 1:
        return values
    if side == 2:
        (r0, i0), (r1, i1) = values
        return [(r0 + r1, i0 + i1), (r0 - r1, i0 - i1)]
    if side == 4:
        return dft4(values, sign)
    inner = side // 4
    parts = [dft_line(values[b::4], sign) for b in range(4)]
    out = [None] * side
    for k1 in range(inner):
        column = [twiddle(parts[b][k1], b * k1, sign, side) for b in range(4)]
        for k2, value in enumerate(dft4(column, sign)):
            out[k1 + inner * k2] = value
    return out


def relative_rows(matrix_ref, me):
    parts, devices = matrix_ref.shape[:2]
    rows = [matrix_ref[part, slot ^ me] for part in range(parts) for slot in range(devices)]
    return jnp.concatenate(rows, axis=0)


def times_kernel(order, me_ref, g_ref, m_ref, *outs):
    _, entries, lanes, _ = g_ref.shape
    _, devices, rows, _ = m_ref.shape
    half = devices * rows
    matrix = split_value(relative_rows(m_ref, me_ref[0]))
    for e in range(entries):
        g = jnp.concatenate([g_ref[0, e], g_ref[1, e]], axis=0)
        d = dot3(matrix, split_value(g), ((1,), (1,)))
        c_re, c_im = d[:half, :lanes], d[:half, lanes:]
        s_re, s_im = d[half:, :lanes], d[half:, lanes:]
        for where, value in (
            ((0, 0), c_re + s_im),
            ((0, 1), c_im - s_re),
            ((1, 0), s_im - c_re),
            ((1, 1), -(c_im + s_re)),
        ):
            for out_ref, slot in zip(outs, order):
                out_ref[where[0], where[1], e] = value[slot * rows : (slot + 1) * rows]


def call_kernel(kernel, order, me, args, arg_specs, shape, scratch, limit, name):
    pieces = pl.pallas_call(
        kernel,
        in_specs=[pl.BlockSpec(memory_space=pltpu.SMEM)] + arg_specs,
        out_specs=[pl.BlockSpec(memory_space=pltpu.VMEM)] * len(order),
        out_shape=[jax.ShapeDtypeStruct(shape, jnp.float32)] * len(order),
        scratch_shapes=scratch,
        compiler_params=pltpu.CompilerParams(vmem_limit_bytes=limit << 20),
        name=name,
    )(me, *args)
    return dict(zip(order, pieces))


def to_times(green, matrix, me, order):
    _, entries, lanes, _ = green.shape
    shape = (2, 2, entries, matrix.shape[2], lanes)
    vmem = pl.BlockSpec(memory_space=pltpu.VMEM)
    kernel = functools.partial(times_kernel, order)
    return call_kernel(kernel, order, me, (green, matrix), [vmem] * 2, shape, [], 40, "to_times")


def fill_block(ref, cosine, sine):
    plane = cosine.shape[0]
    lanes = plane // 2
    for block in range(2):
        cut = slice(block * lanes, (block + 1) * lanes)
        re = slice(2 * block * lanes, (2 * block + 1) * lanes)
        im = slice((2 * block + 1) * lanes, (2 * block + 2) * lanes)
        ref[:plane, re] = cosine[:, cut].astype(jnp.bfloat16)
        ref[plane:, im] = cosine[:, cut].astype(jnp.bfloat16)
        ref[:plane, im] = sine[:, cut].astype(jnp.bfloat16)
        ref[plane:, re] = (-sine[:, cut]).astype(jnp.bfloat16)


def middle_kernel(order, me_ref, table_ref, mirror_ref, index_ref, ch_ref, cl_ref, sh_ref, sl_ref, *refs):
    count = len(order)
    pieces = dict(zip(order, refs[:count]))
    outs = dict(zip(order, refs[count : 2 * count]))
    forward, backward, mid, space, chi = refs[2 * count :]
    halves, _, side, _, entries, rows, lanes = space.shape
    plane = 2 * lanes
    units, _, _, members, _, _ = chi.shape
    line, core = me_ref[0] // 2, me_ref[0] % 2
    row = lax.broadcasted_iota(jnp.int32, (plane, plane), 0)
    pick = (row == index_ref[...]).astype(jnp.float32).astype(jnp.bfloat16)

    def dot(a, b):
        return jnp.dot(a, b, preferred_element_type=jnp.float32)

    def turned(value, axis):
        first = lax.slice_in_dim(value, 0, lanes, axis=axis)
        second = lax.slice_in_dim(value, lanes, plane, axis=axis)
        return jnp.where(core == 0, value, jnp.concatenate([second, first], axis=axis))

    for part, (c_ref, s_ref) in enumerate(((ch_ref, sh_ref), (cl_ref, sl_ref))):
        cosine, sine = c_ref[...].astype(jnp.float32), s_ref[...].astype(jnp.float32)
        fill_block(forward.at[0, part], turned(cosine, 0), turned(sine, 0))
        fill_block(backward.at[0, part], turned(cosine, 1), turned(-sine, 1))
        fill_block(
            forward.at[1, part], turned(dot(c_ref[...], pick), 0), turned(dot(s_ref[...], pick), 0)
        )
        fill_block(
            backward.at[1, part], turned(dot(pick, c_ref[...]), 1), turned(-dot(pick, s_ref[...]), 1)
        )

    def plane_dot(value, matrix, half, block):
        cut = slice(2 * block * lanes, 2 * (block + 1) * lanes)
        return dot3(value, (matrix[half, 0, :, cut], matrix[half, 1, :, cut]), ((1,), (0,)))

    def arrive(half):
        columns = []
        for ri in range(2):
            for h in range(2):
                rows_of = [pieces[2 * x + h][half, ri].reshape(entries * rows, lanes) for x in range(side)]
                columns.append(jnp.concatenate(rows_of, axis=0))
        return split_value(jnp.concatenate(columns, axis=1))

    def to_plane(value, half, block):
        d = plane_dot(value, forward, half, block)
        for ri in range(2):
            piece = d[:, ri * lanes : (ri + 1) * lanes]
            mid[half, block, ri] = piece.reshape(side, entries, rows, lanes)

    def along_line(half, block, e):
        values = [(mid[half, block, 0, x ^ line, e], mid[half, block, 1, x ^ line, e]) for x in range(side)]
        for x, (re, im) in enumerate(dft_line(values, 1)):
            space[half, block, x, 0, e] = re
            space[half, block, x, 1, e] = im

    def product(unit, block, c):
        half, first = unit % halves, unit // halves * members
        left, right = table_ref[first + c, 0], table_ref[first + c, 1]
        values = []
        for x in range(side):
            other = mirror_ref[0, x]
            a_re, a_im = space[half, block, x, 0, left], space[half, block, x, 1, left]
            b_re, b_im = space[1 - half, block, other, 0, right], space[1 - half, block, other, 1, right]
            values.append((a_re * b_re - a_im * b_im, a_re * b_im + a_im * b_re))
        cut = slice(block * lanes, (block + 1) * lanes)
        for x, (re, im) in enumerate(dft_line(values, -1)):
            chi[unit, 0, x ^ line, c, :, cut] = re
            chi[unit, 1, x ^ line, c, :, cut] = im

    def from_plane(unit, value, h):
        half, first = unit % halves, unit // halves * members
        d = plane_dot(value, backward, half, h)
        for ri in range(2):
            piece = d[:, ri * lanes : (ri + 1) * lanes].reshape(side, members, rows, lanes)
            for x in range(side):
                outs[2 * x + h][half, ri, first : first + members] = piece[x]

    def collect(unit):
        whole = (side * members * rows, plane)
        return split_value(jnp.concatenate([chi[unit, ri].reshape(whole) for ri in range(2)], axis=1))

    places = [(half, block) for half in range(halves) for block in range(2)]
    for step in range(len(places) + 1):
        if step < len(places):
            half, block = places[step]
            if block == 0:
                value = arrive(half)
            to_plane(value, half, block)
        if step > 0:
            for e in range(entries):
                along_line(*places[step - 1], e)

    for unit in range(units + 1):
        tasks = [(block, c) for block in range(2) for c in range(members)] if unit < units else []
        if unit > 0:
            value = collect(unit - 1)
        for h in range(2):
            if unit > 0:
                from_plane(unit - 1, value, h)
            for block, c in tasks[h * members : (h + 1) * members]:
                product(unit, block, c)


def middle(pieces, table, mirror_map, me, order):
    halves, _, entries, rows, lanes = pieces[0].shape
    plane = 2 * lanes
    side = len(order) // 2
    components = table.shape[0]
    members = components // GROUPS
    units = halves * GROUPS
    index = (mirror_map[1][:, None] * side + mirror_map[2][None, :]).reshape(1, plane)
    cosine, sine = plane_parts(side)
    parts = [jnp.asarray(part) for part in split_constant(cosine) + split_constant(sine)]
    smem = pl.BlockSpec(memory_space=pltpu.SMEM)
    vmem = pl.BlockSpec(memory_space=pltpu.VMEM)
    matrices = pltpu.VMEM((halves, 2, 2 * plane, 2 * plane), jnp.bfloat16)
    scratch = [
        matrices,
        matrices,
        pltpu.VMEM((halves, 2, 2, side, entries, rows, lanes), jnp.float32),
        pltpu.VMEM((halves, 2, side, 2, entries, rows, lanes), jnp.float32),
        pltpu.VMEM((units, 2, side, members, rows, plane), jnp.float32),
    ]
    args = (table, mirror_map, index, *parts) + tuple(pieces[slot] for slot in order)
    specs = [smem, smem, vmem] + [vmem] * (4 + len(order))
    shape = (halves, 2, components, rows, lanes)
    kernel = functools.partial(middle_kernel, order)
    return call_kernel(kernel, order, me, args, specs, shape, scratch, 40, "middle")


def frequency_kernel(order, me_ref, m_ref, *refs):
    pieces = dict(zip(order, refs[: len(order)]))
    out_ref, stage, sems = refs[len(order) :]
    components, lanes = stage.shape[1:3]
    groups = sems.shape[0]
    members = components // groups
    matrix = split_value(relative_rows(m_ref, me_ref[0]))
    copies = []
    for group in range(groups):
        values = []
        for c in range(group * members, (group + 1) * members):
            part = [
                [jnp.concatenate([pieces[slot][half, ri, c] for slot in range(len(order))], axis=0) for ri in range(2)]
                for half in range(2)
            ]
            sums = [part[0][ri] + part[1][ri] for ri in range(2)]
            differences = [part[0][ri] - part[1][ri] for ri in range(2)]
            values.append(jnp.concatenate([sums[0], -differences[1]], axis=0).T)
            values.append(jnp.concatenate([sums[1], differences[0]], axis=0).T)
        d = dot3(split_value(jnp.concatenate(values, axis=0)), matrix, ((1,), (0,)))
        d = d.reshape(members, 2, lanes, d.shape[1])
        for ri in range(2):
            stage[ri, group * members : (group + 1) * members] = d[:, ri]
        cut = pl.ds(group * members, members)
        copies.append(pltpu.make_async_copy(stage.at[:, cut], out_ref.at[:, cut], sems.at[group]))
        copies[-1].start()
    for copy in copies:
        copy.wait()


def to_frequencies(pieces, matrix, me, order):
    _, _, components, rows, lanes = pieces[0].shape
    shape = (2, components, lanes, matrix.shape[3])
    vmem = pl.BlockSpec(memory_space=pltpu.VMEM)
    return pl.pallas_call(
        functools.partial(frequency_kernel, order),
        in_specs=[pl.BlockSpec(memory_space=pltpu.SMEM)] + [vmem] * (1 + len(order)),
        out_specs=pl.BlockSpec(memory_space=pltpu.HBM),
        out_shape=jax.ShapeDtypeStruct(shape, jnp.float32),
        scratch_shapes=[pltpu.VMEM(shape, jnp.float32), pltpu.SemaphoreType.DMA((components // 2,))],
        compiler_params=pltpu.CompilerParams(vmem_limit_bytes=40 << 20),
        name="to_frequencies",
    )(me, matrix, *[pieces[slot] for slot in order])


def swap(pieces, order):
    moved = {}
    for slot in order:
        pairs = [(device, device ^ slot) for device in range(len(order))]
        moved[slot] = lax.ppermute(pieces[slot], "kb", pairs) if slot else pieces[slot]
    return moved


def slot_order(devices):
    half = devices // 2
    return [slot for near in range(half) for slot in (near + half, near)]


def trig_pair(angle_int, period, scale):
    angle = 2.0 * math.pi / period * angle_int.astype(jnp.float32)
    return (scale * jnp.cos(angle), scale * jnp.sin(angle))


def complex_combine(formula, cosine, sine, real_part, imag_part):
    first_term = jnp.einsum(formula, cosine, real_part + imag_part, precision=lax.Precision.HIGHEST)
    second_term = jnp.einsum(formula, cosine + sine, imag_part, precision=lax.Precision.HIGHEST)
    third_term = jnp.einsum(formula, sine - cosine, real_part, precision=lax.Precision.HIGHEST)
    return (first_term - second_term, first_term + third_term)


def forward_imaginary_time(tau_rows, frequency_count):
    freq_index = jnp.arange(frequency_count, dtype=jnp.int32)
    angle_int = (
        (2 * freq_index[None, :] - frequency_count + 1)
        * (2 * tau_rows[:, None] + 1)
        % (4 * frequency_count)
    )
    cosine, sine = trig_pair(angle_int, 4 * frequency_count, frequency_count ** (-0.5))
    return (cosine, -sine)


def tau_backward(tau_rows, frequency_count):
    freq_index = jnp.arange(frequency_count, dtype=jnp.int32)
    angle_int = (
        (freq_index[:, None] - frequency_count // 2)
        * (2 * tau_rows[None, :] + 1)
        % (2 * frequency_count)
    )
    return trig_pair(angle_int, 2 * frequency_count, frequency_count ** (-0.5))


def grid_transform(real_part, imag_part, grid_side, direction):
    shape = real_part.shape
    plane = jnp.arange(grid_side * grid_side, dtype=jnp.int32)
    upper = plane // grid_side
    lower = plane % grid_side
    plane_int = (upper[:, None] * upper[None, :] + lower[:, None] * lower[None, :]) % grid_side
    plane_cos, plane_sin = trig_pair(plane_int, grid_side, 1.0 / grid_side)
    line = jnp.arange(grid_side, dtype=jnp.int32)
    line_cos, line_sin = trig_pair(
        line[:, None] * line[None, :] % grid_side, grid_side, grid_side ** (-0.5)
    )
    real_part = real_part.reshape(shape[:-1] + (grid_side, grid_side * grid_side))
    imag_part = imag_part.reshape(shape[:-1] + (grid_side, grid_side * grid_side))
    real_part, imag_part = complex_combine(
        "pq,...xq->...xp", plane_cos, direction * plane_sin, real_part, imag_part
    )
    real_part, imag_part = complex_combine(
        "ax,...xp->...ap", line_cos, direction * line_sin, real_part, imag_part
    )
    return (real_part.reshape(shape), imag_part.reshape(shape))


def mirror_index(mirror_map, grid_side):
    index_x = mirror_map[0][:, None, None]
    index_y = mirror_map[1][None, :, None]
    index_z = mirror_map[2][None, None, :]
    return (index_x * grid_side * grid_side + index_y * grid_side + index_z).reshape(-1)


def bubble(gr_re, gr_im, mirror_re, mirror_im, pair_table, entries):
    entry_ids = jnp.arange(entries, dtype=jnp.int32)
    pick_left = (pair_table[:, 0][:, None] == entry_ids[None, :]).astype(jnp.float32)
    pick_right = (pair_table[:, 1][:, None] == entry_ids[None, :]).astype(jnp.float32)
    left_re = jnp.einsum("me,e...->m...", pick_left, gr_re, precision=lax.Precision.HIGHEST)
    left_im = jnp.einsum("me,e...->m...", pick_left, gr_im, precision=lax.Precision.HIGHEST)
    right_re = jnp.einsum("me,e...->m...", pick_right, mirror_re, precision=lax.Precision.HIGHEST)
    right_im = jnp.einsum("me,e...->m...", pick_right, mirror_im, precision=lax.Precision.HIGHEST)
    return (left_re * right_re - left_im * right_im, left_re * right_im + left_im * right_re)


def general(green_momentum_grid, pair_table, mirror_map):
    grid_side = mirror_map.shape[1]
    entries = green_momentum_grid.shape[1]
    frequency_count = green_momentum_grid.shape[3]
    position = jnp.arange(frequency_count, dtype=jnp.int32)
    fwd_cos, fwd_sin = forward_imaginary_time(position, frequency_count)
    tau_re, tau_im = complex_combine(
        "qa,fsa->fqs", fwd_cos, fwd_sin, green_momentum_grid[0], green_momentum_grid[1]
    )
    stacked = jnp.stack([tau_re, tau_im])

    def to_real_space(pieces):
        space_re, space_im = grid_transform(pieces[0], pieces[1], grid_side, 1.0)
        return jnp.stack([space_re, space_im])

    mirror_flat = mirror_index(mirror_map, grid_side)
    partner_rows = frequency_count - 1 - position
    reflected_cosine, reflected_sine = forward_imaginary_time(partner_rows, frequency_count)
    partner_real, partner_imaginary = complex_combine(
        "qa,fsa->fqs",
        reflected_cosine,
        reflected_sine,
        green_momentum_grid[0],
        green_momentum_grid[1],
    )
    other_stacked = jnp.stack([partner_real, partner_imaginary])
    pieces = (
        lax.all_to_all(stacked, "kb", split_axis=2, concat_axis=3, tiled=True),
        lax.all_to_all(other_stacked, "kb", split_axis=2, concat_axis=3, tiled=True),
    )
    in_cells = to_real_space(pieces[0])
    partner = to_real_space(pieces[1])
    mirrored = jnp.take(partner, mirror_flat, axis=3)
    chi_re, chi_im = bubble(in_cells[0], in_cells[1], mirrored[0], mirrored[1], pair_table, entries)
    chi_re, chi_im = grid_transform(chi_re, chi_im, grid_side, -1.0)
    momenta = jnp.stack([chi_re, chi_im])
    back_cos, back_sin = tau_backward(position, frequency_count)
    pieces = lax.all_to_all(momenta, "kb", split_axis=3, concat_axis=2, tiled=True)
    out_re, out_im = complex_combine("vj,ejk->ekv", back_cos, back_sin, pieces[0], pieces[1])
    return jnp.stack([out_re, out_im])


def local(green, pair_table, mirror_map):
    side = mirror_map.shape[1]
    plane = side * side
    lanes, count = green.shape[2], green.shape[3]
    devices = side * plane // lanes
    pairs = count // (2 * devices)
    if lanes != LANES or pairs != ROWS or 2 * lanes != plane:
        return general(green, pair_table, mirror_map)
    rows = np.arange(devices * pairs)
    shape = (2, devices, pairs, count)
    forward = jnp.asarray(fermion_matrix(rows, count).reshape(shape).astype(np.float32))
    backward = jnp.asarray(boson_matrix(rows, count).reshape(shape).astype(np.float32))
    order = slot_order(devices)
    me = lax.axis_index("kb").astype(jnp.int32).reshape(1)
    pieces = swap(to_times(green, forward, me, order), order)
    pieces = swap(middle(pieces, pair_table, mirror_map, me, order), order)
    return to_frequencies(pieces, backward, me, order)


def solution(mesh):
    placed = (P("set", None, "kb", None), P(), P("set", None))
    return jax.shard_map(
        local, mesh=mesh, in_specs=placed, out_specs=P("set", None, "kb", None), check_vma=False
    )
```

profile of v0, /device:TPU:0, one launch (start us, length us, event | category | flops | bytes accessed | tf_op | source)
XLA Modules:
  0.0 180.4 jit_solution(6776105558577965027)
XLA Ops:
  4.7 4.1 %collective-permute-start = (f32[2,2,4,8,128]{4,3,2,1,0:T(8,128)S(1)}, f32[2,2,4,8,128]{4,3,2,1,0:T(8,128)S(1)}, u32[]{:S(2)}, u32[]{:S(2)}) collective-permute-start(f32[2,2,4,8,128]{4,3,2,1,0:T(8,128)S(1)} %get-tuple-element.69), channel_id=1, source_target_pairs={{0,16},{1,17},{2,18},{3,19},{4,20},{5,21},{6,22},{7,23},{8,24},{9,... | collective-permute-start | bytes 196616 | tf_op jit(solution)/shard_map/ppermute | solution.py:346
  9.0 3.8 %collective-permute-start.3 = (f32[2,2,4,8,128]{4,3,2,1,0:T(8,128)S(1)}, f32[2,2,4,8,128]{4,3,2,1,0:T(8,128)S(1)}, u32[]{:S(2)}, u32[]{:S(2)}) collective-permute-start(f32[2,2,4,8,128]{4,3,2,1,0:T(8,128)S(1)} %get-tuple-element.73), channel_id=1, source_target_pairs={{0,18},{1,19},{2,16},{3,17},{4,22},{5,23},{6,20},{7,21},{8,26},{9,... | collective-permute-start | bytes 196616 | tf_op jit(solution)/shard_map/ppermute | solution.py:346
  13.7 3.3 %collective-permute-done.1.refs_2_ = f32[2,2,4,8,128]{4,3,2,1,0:T(8,128)S(1)} collective-permute-done((f32[2,2,4,8,128]{4,3,2,1,0:T(8,128)S(1)}, f32[2,2,4,8,128]{4,3,2,1,0:T(8,128)S(1)}, u32[]{:S(2)}, u32[]{:S(2)}) %collective-permute-start.1) | collective-permute-done | bytes 65568 | tf_op jit(solution)/shard_map/ppermute | solution.py:346
  20.7 2.3 %collective-permute-start.9 = (f32[2,2,4,8,128]{4,3,2,1,0:T(8,128)S(1)}, f32[2,2,4,8,128]{4,3,2,1,0:T(8,128)S(1)}, u32[]{:S(2)}, u32[]{:S(2)}) collective-permute-start(f32[2,2,4,8,128]{4,3,2,1,0:T(8,128)S(1)} %get-tuple-element.79), channel_id=1, source_target_pairs={{0,21},{1,20},{2,23},{3,22},{4,17},{5,16},{6,19},{7,18},{8,29},{9,... | collective-permute-start | bytes 196616 | tf_op jit(solution)/shard_map/ppermute | solution.py:346
  24.9 2.2 %collective-permute-start.12 = (f32[2,2,4,8,128]{4,3,2,1,0:T(8,128)S(1)}, f32[2,2,4,8,128]{4,3,2,1,0:T(8,128)S(1)}, u32[]{:S(2)}, u32[]{:S(2)}) collective-permute-start(f32[2,2,4,8,128]{4,3,2,1,0:T(8,128)S(1)} %get-tuple-element.82), channel_id=1, source_target_pairs={{0,6},{1,7},{2,4},{3,5},{4,2},{5,3},{6,0},{7,1},{8,14},{9,15},{10,... | collective-permute-start | bytes 196616 | tf_op jit(solution)/shard_map/ppermute | solution.py:346
  28.9 2.1 %collective-permute-start.14 = (f32[2,2,4,8,128]{4,3,2,1,0:T(8,128)S(1)}, f32[2,2,4,8,128]{4,3,2,1,0:T(8,128)S(1)}, u32[]{:S(2)}, u32[]{:S(2)}) collective-permute-start(f32[2,2,4,8,128]{4,3,2,1,0:T(8,128)S(1)} %get-tuple-element.84), channel_id=1, source_target_pairs={{0,7},{1,6},{2,5},{3,4},{4,3},{5,2},{6,1},{7,0},{8,15},{9,14},{10,... | collective-permute-start | bytes 196616 | tf_op jit(solution)/shard_map/ppermute | solution.py:346
  31.0 4.9 %collective-permute-start.15 = (f32[2,2,4,8,128]{4,3,2,1,0:T(8,128)S(1)}, f32[2,2,4,8,128]{4,3,2,1,0:T(8,128)S(1)}, u32[]{:S(2)}, u32[]{:S(2)}) collective-permute-start(f32[2,2,4,8,128]{4,3,2,1,0:T(8,128)S(1)} %get-tuple-element.85), channel_id=1, source_target_pairs={{0,24},{1,25},{2,26},{3,27},{4,28},{5,29},{6,30},{7,31},{8,16},{9,... | collective-permute-start | bytes 196616 | tf_op jit(solution)/shard_map/ppermute | solution.py:346
  38.0 3.5 %collective-permute-start.19 = (f32[2,2,4,8,128]{4,3,2,1,0:T(8,128)S(1)}, f32[2,2,4,8,128]{4,3,2,1,0:T(8,128)S(1)}, u32[]{:S(2)}, u32[]{:S(2)}) collective-permute-start(f32[2,2,4,8,128]{4,3,2,1,0:T(8,128)S(1)} %get-tuple-element.89), channel_id=1, source_target_pairs={{0,26},{1,27},{2,24},{3,25},{4,30},{5,31},{6,28},{7,29},{8,18},{9,... | collective-permute-start | bytes 196616 | tf_op jit(solution)/shard_map/ppermute | solution.py:346
  44.8 3.2 %collective-permute-start.23 = (f32[2,2,4,8,128]{4,3,2,1,0:T(8,128)S(1)}, f32[2,2,4,8,128]{4,3,2,1,0:T(8,128)S(1)}, u32[]{:S(2)}, u32[]{:S(2)}) collective-permute-start(f32[2,2,4,8,128]{4,3,2,1,0:T(8,128)S(1)} %get-tuple-element.93), channel_id=1, source_target_pairs={{0,28},{1,29},{2,30},{3,31},{4,24},{5,25},{6,26},{7,27},{8,20},{9,... | collective-permute-start | bytes 196616 | tf_op jit(solution)/shard_map/ppermute | solution.py:346
  52.1 2.8 %collective-permute-start.27 = (f32[2,2,4,8,128]{4,3,2,1,0:T(8,128)S(1)}, f32[2,2,4,8,128]{4,3,2,1,0:T(8,128)S(1)}, u32[]{:S(2)}, u32[]{:S(2)}) collective-permute-start(f32[2,2,4,8,128]{4,3,2,1,0:T(8,128)S(1)} %get-tuple-element.97), channel_id=1, source_target_pairs={{0,30},{1,31},{2,28},{3,29},{4,26},{5,27},{6,24},{7,25},{8,22},{9,... | collective-permute-start | bytes 196616 | tf_op jit(solution)/shard_map/ppermute | solution.py:346
  62.1 2.1 %collective-permute-done.29.refs_30_ = f32[2,2,4,8,128]{4,3,2,1,0:T(8,128)S(1)} collective-permute-done((f32[2,2,4,8,128]{4,3,2,1,0:T(8,128)S(1)}, f32[2,2,4,8,128]{4,3,2,1,0:T(8,128)S(1)}, u32[]{:S(2)}, u32[]{:S(2)}) %collective-permute-start.29) | collective-permute-done | bytes 65568 | tf_op jit(solution)/shard_map/ppermute | solution.py:346
  69.0 8.4 %middle.1 = (f32[2,2,8,8,128]{4,3,2,1,0:T(8,128)S(1)}, f32[2,2,8,8,128]{4,3,2,1,0:T(8,128)S(1)}, f32[2,2,8,8,128]{4,3,2,1,0:T(8,128)S(1)}, f32[2,2,8,8,128]{4,3,...) custom-call(s32[1]{0:T(128)} %bitcast.me_ref, ...), custom_call_target="tpu_custom_call" | custom-call | tf_op jit(solution)/shard_map/middle/pallas_call | solution.py:134
  83.1 10.0 %collective-permute-done.31.refs_0_ = f32[2,2,8,8,128]{4,3,2,1,0:T(8,128)S(1)} collective-permute-done((f32[2,2,8,8,128]{4,3,2,1,0:T(8,128)S(1)}, f32[2,2,8,8,128]{4,3,2,1,0:T(8,128)S(1)}, u32[]{:S(2)}, u32[]{:S(2)}) %collective-permute-start.31) | collective-permute-done | bytes 131104 | tf_op jit(solution)/shard_map/ppermute | solution.py:346
  93.1 2.8 %collective-permute-done.32.refs_2_ = f32[2,2,8,8,128]{4,3,2,1,0:T(8,128)S(1)} collective-permute-done((f32[2,2,8,8,128]{4,3,2,1,0:T(8,128)S(1)}, f32[2,2,8,8,128]{4,3,2,1,0:T(8,128)S(1)}, u32[]{:S(2)}, u32[]{:S(2)}) %collective-permute-start.32) | collective-permute-done | bytes 131104 | tf_op jit(solution)/shard_map/ppermute | solution.py:346
  98.2 3.4 %collective-permute-done.34.refs_4_ = f32[2,2,8,8,128]{4,3,2,1,0:T(8,128)S(1)} collective-permute-done((f32[2,2,8,8,128]{4,3,2,1,0:T(8,128)S(1)}, f32[2,2,8,8,128]{4,3,2,1,0:T(8,128)S(1)}, u32[]{:S(2)}, u32[]{:S(2)}) %collective-permute-start.34) | collective-permute-done | bytes 131104 | tf_op jit(solution)/shard_map/ppermute | solution.py:346
  101.6 4.2 %collective-permute-start.39 = (f32[2,2,8,8,128]{4,3,2,1,0:T(8,128)S(1)}, f32[2,2,8,8,128]{4,3,2,1,0:T(8,128)S(1)}, u32[]{:S(2)}, u32[]{:S(2)}) collective-permute-start(f32[2,2,8,8,128]{4,3,2,1,0:T(8,128)S(1)} %get-tuple-element.110), channel_id=1, source_target_pairs={{0,4},{1,5},{2,6},{3,7},{4,0},{5,1},{6,2},{7,3},{8,12},{9,13},{10,... | collective-permute-start | bytes 393224 | tf_op jit(solution)/shard_map/ppermute | solution.py:346
  108.2 2.2 %collective-permute-start.42 = (f32[2,2,8,8,128]{4,3,2,1,0:T(8,128)S(1)}, f32[2,2,8,8,128]{4,3,2,1,0:T(8,128)S(1)}, u32[]{:S(2)}, u32[]{:S(2)}) collective-permute-start(f32[2,2,8,8,128]{4,3,2,1,0:T(8,128)S(1)} %get-tuple-element.113), channel_id=1, source_target_pairs={{0,22},{1,23},{2,20},{3,21},{4,18},{5,19},{6,16},{7,17},{8,30},{9,... | collective-permute-start | bytes 393224 | tf_op jit(solution)/shard_map/ppermute | solution.py:346
  110.4 6.1 %collective-permute-done.38.refs_8_ = f32[2,2,8,8,128]{4,3,2,1,0:T(8,128)S(1)} collective-permute-done((f32[2,2,8,8,128]{4,3,2,1,0:T(8,128)S(1)}, f32[2,2,8,8,128]{4,3,2,1,0:T(8,128)S(1)}, u32[]{:S(2)}, u32[]{:S(2)}) %collective-permute-start.38) | collective-permute-done | bytes 131104 | tf_op jit(solution)/shard_map/ppermute | solution.py:346
  116.5 6.4 %collective-permute-done.40.refs_10_ = f32[2,2,8,8,128]{4,3,2,1,0:T(8,128)S(1)} collective-permute-done((f32[2,2,8,8,128]{4,3,2,1,0:T(8,128)S(1)}, f32[2,2,8,8,128]{4,3,2,1,0:T(8,128)S(1)}, u32[]{:S(2)}, u32[]{:S(2)}) %collective-permute-start.40) | collective-permute-done | bytes 131104 | tf_op jit(solution)/shard_map/ppermute | solution.py:346
  123.0 2.7 %collective-permute-done.42.refs_12_ = f32[2,2,8,8,128]{4,3,2,1,0:T(8,128)S(1)} collective-permute-done((f32[2,2,8,8,128]{4,3,2,1,0:T(8,128)S(1)}, f32[2,2,8,8,128]{4,3,2,1,0:T(8,128)S(1)}, u32[]{:S(2)}, u32[]{:S(2)}) %collective-permute-start.42) | collective-permute-done | bytes 131104 | tf_op jit(solution)/shard_map/ppermute | solution.py:346
  125.7 3.9 %collective-permute-done.43.refs_13_ = f32[2,2,8,8,128]{4,3,2,1,0:T(8,128)S(1)} collective-permute-done((f32[2,2,8,8,128]{4,3,2,1,0:T(8,128)S(1)}, f32[2,2,8,8,128]{4,3,2,1,0:T(8,128)S(1)}, u32[]{:S(2)}, u32[]{:S(2)}) %collective-permute-start.43) | collective-permute-done | bytes 131104 | tf_op jit(solution)/shard_map/ppermute | solution.py:346
  133.3 2.8 %collective-permute-start.51 = (f32[2,2,8,8,128]{4,3,2,1,0:T(8,128)S(1)}, f32[2,2,8,8,128]{4,3,2,1,0:T(8,128)S(1)}, u32[]{:S(2)}, u32[]{:S(2)}) collective-permute-start(f32[2,2,8,8,128]{4,3,2,1,0:T(8,128)S(1)} %get-tuple-element.122), channel_id=1, source_target_pairs={{0,10},{1,11},{2,8},{3,9},{4,14},{5,15},{6,12},{7,13},{8,2},{9,3},... | collective-permute-start | bytes 393224 | tf_op jit(solution)/shard_map/ppermute | solution.py:346
  137.9 2.2 %collective-permute-start.53 = (f32[2,2,8,8,128]{4,3,2,1,0:T(8,128)S(1)}, f32[2,2,8,8,128]{4,3,2,1,0:T(8,128)S(1)}, u32[]{:S(2)}, u32[]{:S(2)}) collective-permute-start(f32[2,2,8,8,128]{4,3,2,1,0:T(8,128)S(1)} %get-tuple-element.124), channel_id=1, source_target_pairs={{0,11},{1,10},{2,9},{3,8},{4,15},{5,14},{6,13},{7,12},{8,3},{9,2},... | collective-permute-start | bytes 393224 | tf_op jit(solution)/shard_map/ppermute | solution.py:346
  141.0 3.0 %collective-permute-start.54 = (f32[2,2,8,8,128]{4,3,2,1,0:T(8,128)S(1)}, f32[2,2,8,8,128]{4,3,2,1,0:T(8,128)S(1)}, u32[]{:S(2)}, u32[]{:S(2)}) collective-permute-start(f32[2,2,8,8,128]{4,3,2,1,0:T(8,128)S(1)} %get-tuple-element.125), channel_id=1, source_target_pairs={{0,28},{1,29},{2,30},{3,31},{4,24},{5,25},{6,26},{7,27},{8,20},{9,... | collective-permute-start | bytes 393224 | tf_op jit(solution)/shard_map/ppermute | solution.py:346
  144.0 4.3 %collective-permute-start.55 = (f32[2,2,8,8,128]{4,3,2,1,0:T(8,128)S(1)}, f32[2,2,8,8,128]{4,3,2,1,0:T(8,128)S(1)}, u32[]{:S(2)}, u32[]{:S(2)}) collective-permute-start(f32[2,2,8,8,128]{4,3,2,1,0:T(8,128)S(1)} %get-tuple-element.126), channel_id=1, source_target_pairs={{0,12},{1,13},{2,14},{3,15},{4,8},{5,9},{6,10},{7,11},{8,4},{9,5},... | collective-permute-start | bytes 393224 | tf_op jit(solution)/shard_map/ppermute | solution.py:346
  150.2 3.1 %collective-permute-start.57 = (f32[2,2,8,8,128]{4,3,2,1,0:T(8,128)S(1)}, f32[2,2,8,8,128]{4,3,2,1,0:T(8,128)S(1)}, u32[]{:S(2)}, u32[]{:S(2)}) collective-permute-start(f32[2,2,8,8,128]{4,3,2,1,0:T(8,128)S(1)} %get-tuple-element.128), channel_id=1, source_target_pairs={{0,13},{1,12},{2,15},{3,14},{4,9},{5,8},{6,11},{7,10},{8,5},{9,4},... | collective-permute-start | bytes 393224 | tf_op jit(solution)/shard_map/ppermute | solution.py:346
  153.2 3.3 %collective-permute-start.58 = (f32[2,2,8,8,128]{4,3,2,1,0:T(8,128)S(1)}, f32[2,2,8,8,128]{4,3,2,1,0:T(8,128)S(1)}, u32[]{:S(2)}, u32[]{:S(2)}) collective-permute-start(f32[2,2,8,8,128]{4,3,2,1,0:T(8,128)S(1)} %get-tuple-element.129), channel_id=1, source_target_pairs={{0,30},{1,31},{2,28},{3,29},{4,26},{5,27},{6,24},{7,25},{8,22},{9,... | collective-permute-start | bytes 393224 | tf_op jit(solution)/shard_map/ppermute | solution.py:346
  156.6 2.7 %collective-permute-start.59 = (f32[2,2,8,8,128]{4,3,2,1,0:T(8,128)S(1)}, f32[2,2,8,8,128]{4,3,2,1,0:T(8,128)S(1)}, u32[]{:S(2)}, u32[]{:S(2)}) collective-permute-start(f32[2,2,8,8,128]{4,3,2,1,0:T(8,128)S(1)} %get-tuple-element.130), channel_id=1, source_target_pairs={{0,14},{1,15},{2,12},{3,13},{4,10},{5,11},{6,8},{7,9},{8,6},{9,7},... | collective-permute-start | bytes 393224 | tf_op jit(solution)/shard_map/ppermute | solution.py:346
  159.3 3.9 %collective-permute-start.60 = (f32[2,2,8,8,128]{4,3,2,1,0:T(8,128)S(1)}, f32[2,2,8,8,128]{4,3,2,1,0:T(8,128)S(1)}, u32[]{:S(2)}, u32[]{:S(2)}) collective-permute-start(f32[2,2,8,8,128]{4,3,2,1,0:T(8,128)S(1)} %get-tuple-element.131), channel_id=1, source_target_pairs={{0,31},{1,30},{2,29},{3,28},{4,27},{5,26},{6,25},{7,24},{8,23},{9,... | collective-permute-start | bytes 393224 | tf_op jit(solution)/shard_map/ppermute | solution.py:346
  164.6 4.6 %collective-permute-done.58.refs_28_ = f32[2,2,8,8,128]{4,3,2,1,0:T(8,128)S(1)} collective-permute-done((f32[2,2,8,8,128]{4,3,2,1,0:T(8,128)S(1)}, f32[2,2,8,8,128]{4,3,2,1,0:T(8,128)S(1)}, u32[]{:S(2)}, u32[]{:S(2)}) %collective-permute-start.58) | collective-permute-done | bytes 131104 | tf_op jit(solution)/shard_map/ppermute | solution.py:346
  169.2 6.4 %collective-permute-done.60.refs_30_ = f32[2,2,8,8,128]{4,3,2,1,0:T(8,128)S(1)} collective-permute-done((f32[2,2,8,8,128]{4,3,2,1,0:T(8,128)S(1)}, f32[2,2,8,8,128]{4,3,2,1,0:T(8,128)S(1)}, u32[]{:S(2)}, u32[]{:S(2)}) %collective-permute-start.60) | collective-permute-done | bytes 131104 | tf_op jit(solution)/shard_map/ppermute | solution.py:346
  175.6 4.6 %to_frequencies.1 = f32[2,8,128,512]{3,2,1,0:T(8,128)} custom-call(s32[1]{0:T(128)} %bitcast.me_ref, f32[2,32,8,512]{3,2,1,0:T(8,128)S(1)} %copy-done.1, f32[2,2,8,8,128]{4,3,2,1,0:T(8,128)S(1)} %collective-permute-done.31.refs_0_, f32[2,2,8,8,128]{4,3,2,1,0:T(8,128)S(1)} %get-tuple-element.102.refs_1_, ...), custom_call_target="tpu_custom_call" | custom-call | tf_op jit(solution)/shard_map/to_frequencies/pallas_call | solution.py:331
  (115 shorter events, 54.8 us)
Async XLA Ops:
  23.6 12.3 %collective-permute-start.11 = (f32[2,2,4,8,128]{4,3,2,1,0:T(8,128)S(1)}, f32[2,2,4,8,128]{4,3,2,1,0:T(8,128)S(1)}, u32[]{:S(2)}, u32[]{:S(2)}) collective-permute-start(f32[2,2,4,8,128]{4,3,2,1,0:T(8,128)S(1)} %get-tuple-element.81), channel_id=1, source_target_pairs={{0,22},{1,23},{2,20},{3,21},{4,18},{5,19},{6,16},{7,17},{8,30},{9,... | collective-permute-start | bytes 196616 | tf_op jit(solution)/shard_map/ppermute | solution.py:346
  24.9 11.3 %collective-permute-start.12 = (f32[2,2,4,8,128]{4,3,2,1,0:T(8,128)S(1)}, f32[2,2,4,8,128]{4,3,2,1,0:T(8,128)S(1)}, u32[]{:S(2)}, u32[]{:S(2)}) collective-permute-start(f32[2,2,4,8,128]{4,3,2,1,0:T(8,128)S(1)} %get-tuple-element.82), channel_id=1, source_target_pairs={{0,6},{1,7},{2,4},{3,5},{4,2},{5,3},{6,0},{7,1},{8,14},{9,15},{10,... | collective-permute-start | bytes 196616 | tf_op jit(solution)/shard_map/ppermute | solution.py:346
  31.0 10.5 %collective-permute-start.15 = (f32[2,2,4,8,128]{4,3,2,1,0:T(8,128)S(1)}, f32[2,2,4,8,128]{4,3,2,1,0:T(8,128)S(1)}, u32[]{:S(2)}, u32[]{:S(2)}) collective-permute-start(f32[2,2,4,8,128]{4,3,2,1,0:T(8,128)S(1)} %get-tuple-element.85), channel_id=1, source_target_pairs={{0,24},{1,25},{2,26},{3,27},{4,28},{5,29},{6,30},{7,31},{8,16},{9,... | collective-permute-start | bytes 196616 | tf_op jit(solution)/shard_map/ppermute | solution.py:346
  77.4 15.7 %collective-permute-start.31 = (f32[2,2,8,8,128]{4,3,2,1,0:T(8,128)S(1)}, f32[2,2,8,8,128]{4,3,2,1,0:T(8,128)S(1)}, u32[]{:S(2)}, u32[]{:S(2)}) collective-permute-start(f32[2,2,8,8,128]{4,3,2,1,0:T(8,128)S(1)} %get-tuple-element.101), channel_id=1, source_target_pairs={{0,16},{1,17},{2,18},{3,19},{4,20},{5,21},{6,22},{7,23},{8,24},{9,... | collective-permute-start | bytes 393224 | tf_op jit(solution)/shard_map/ppermute | solution.py:346
  78.6 17.3 %collective-permute-start.32 = (f32[2,2,8,8,128]{4,3,2,1,0:T(8,128)S(1)}, f32[2,2,8,8,128]{4,3,2,1,0:T(8,128)S(1)}, u32[]{:S(2)}, u32[]{:S(2)}) collective-permute-start(f32[2,2,8,8,128]{4,3,2,1,0:T(8,128)S(1)} %get-tuple-element.103), channel_id=1, source_target_pairs={{0,17},{1,16},{2,19},{3,18},{4,21},{5,20},{6,23},{7,22},{8,25},{9,... | collective-permute-start | bytes 393224 | tf_op jit(solution)/shard_map/ppermute | solution.py:346
  80.7 15.5 %collective-permute-start.33 = (f32[2,2,8,8,128]{4,3,2,1,0:T(8,128)S(1)}, f32[2,2,8,8,128]{4,3,2,1,0:T(8,128)S(1)}, u32[]{:S(2)}, u32[]{:S(2)}) collective-permute-start(f32[2,2,8,8,128]{4,3,2,1,0:T(8,128)S(1)} %get-tuple-element.104), channel_id=1, source_target_pairs={{0,1},{1,0},{2,3},{3,2},{4,5},{5,4},{6,7},{7,6},{8,9},{9,8},{10,11... | collective-permute-start | bytes 393224 | tf_op jit(solution)/shard_map/ppermute | solution.py:346
  80.7 20.9 %collective-permute-start.34 = (f32[2,2,8,8,128]{4,3,2,1,0:T(8,128)S(1)}, f32[2,2,8,8,128]{4,3,2,1,0:T(8,128)S(1)}, u32[]{:S(2)}, u32[]{:S(2)}) collective-permute-start(f32[2,2,8,8,128]{4,3,2,1,0:T(8,128)S(1)} %get-tuple-element.105), channel_id=1, source_target_pairs={{0,18},{1,19},{2,16},{3,17},{4,22},{5,23},{6,20},{7,21},{8,26},{9,... | collective-permute-start | bytes 393224 | tf_op jit(solution)/shard_map/ppermute | solution.py:346
  82.5 23.3 %collective-permute-start.35 = (f32[2,2,8,8,128]{4,3,2,1,0:T(8,128)S(1)}, f32[2,2,8,8,128]{4,3,2,1,0:T(8,128)S(1)}, u32[]{:S(2)}, u32[]{:S(2)}) collective-permute-start(f32[2,2,8,8,128]{4,3,2,1,0:T(8,128)S(1)} %get-tuple-element.106), channel_id=1, source_target_pairs={{0,2},{1,3},{2,0},{3,1},{4,6},{5,7},{6,4},{7,5},{8,10},{9,11},{10,... | collective-permute-start | bytes 393224 | tf_op jit(solution)/shard_map/ppermute | solution.py:346
  93.1 14.1 %collective-permute-start.36 = (f32[2,2,8,8,128]{4,3,2,1,0:T(8,128)S(1)}, f32[2,2,8,8,128]{4,3,2,1,0:T(8,128)S(1)}, u32[]{:S(2)}, u32[]{:S(2)}) collective-permute-start(f32[2,2,8,8,128]{4,3,2,1,0:T(8,128)S(1)} %get-tuple-element.107), channel_id=1, source_target_pairs={{0,19},{1,18},{2,17},{3,16},{4,23},{5,22},{6,21},{7,20},{8,27},{9,... | collective-permute-start | bytes 393224 | tf_op jit(solution)/shard_map/ppermute | solution.py:346
  96.0 12.2 %collective-permute-start.37 = (f32[2,2,8,8,128]{4,3,2,1,0:T(8,128)S(1)}, f32[2,2,8,8,128]{4,3,2,1,0:T(8,128)S(1)}, u32[]{:S(2)}, u32[]{:S(2)}) collective-permute-start(f32[2,2,8,8,128]{4,3,2,1,0:T(8,128)S(1)} %get-tuple-element.108), channel_id=1, source_target_pairs={{0,3},{1,2},{2,1},{3,0},{4,7},{5,6},{6,5},{7,4},{8,11},{9,10},{10,... | collective-permute-start | bytes 393224 | tf_op jit(solution)/shard_map/ppermute | solution.py:346
  96.1 20.4 %collective-permute-start.38 = (f32[2,2,8,8,128]{4,3,2,1,0:T(8,128)S(1)}, f32[2,2,8,8,128]{4,3,2,1,0:T(8,128)S(1)}, u32[]{:S(2)}, u32[]{:S(2)}) collective-permute-start(f32[2,2,8,8,128]{4,3,2,1,0:T(8,128)S(1)} %get-tuple-element.109), channel_id=1, source_target_pairs={{0,20},{1,21},{2,22},{3,23},{4,16},{5,17},{6,18},{7,19},{8,28},{9,... | collective-permute-start | bytes 393224 | tf_op jit(solution)/shard_map/ppermute | solution.py:346
  101.6 14.9 %collective-permute-start.39 = (f32[2,2,8,8,128]{4,3,2,1,0:T(8,128)S(1)}, f32[2,2,8,8,128]{4,3,2,1,0:T(8,128)S(1)}, u32[]{:S(2)}, u32[]{:S(2)}) collective-permute-start(f32[2,2,8,8,128]{4,3,2,1,0:T(8,128)S(1)} %get-tuple-element.110), channel_id=1, source_target_pairs={{0,4},{1,5},{2,6},{3,7},{4,0},{5,1},{6,2},{7,3},{8,12},{9,13},{10,... | collective-permute-start | bytes 393224 | tf_op jit(solution)/shard_map/ppermute | solution.py:346
  105.8 17.2 %collective-permute-start.40 = (f32[2,2,8,8,128]{4,3,2,1,0:T(8,128)S(1)}, f32[2,2,8,8,128]{4,3,2,1,0:T(8,128)S(1)}, u32[]{:S(2)}, u32[]{:S(2)}) collective-permute-start(f32[2,2,8,8,128]{4,3,2,1,0:T(8,128)S(1)} %get-tuple-element.111), channel_id=1, source_target_pairs={{0,21},{1,20},{2,23},{3,22},{4,17},{5,16},{6,19},{7,18},{8,29},{9,... | collective-permute-start | bytes 393224 | tf_op jit(solution)/shard_map/ppermute | solution.py:346
  107.2 15.7 %collective-permute-start.41 = (f32[2,2,8,8,128]{4,3,2,1,0:T(8,128)S(1)}, f32[2,2,8,8,128]{4,3,2,1,0:T(8,128)S(1)}, u32[]{:S(2)}, u32[]{:S(2)}) collective-permute-start(f32[2,2,8,8,128]{4,3,2,1,0:T(8,128)S(1)} %get-tuple-element.112), channel_id=1, source_target_pairs={{0,5},{1,4},{2,7},{3,6},{4,1},{5,0},{6,3},{7,2},{8,13},{9,12},{10,... | collective-permute-start | bytes 393224 | tf_op jit(solution)/shard_map/ppermute | solution.py:346
  108.2 17.5 %collective-permute-start.42 = (f32[2,2,8,8,128]{4,3,2,1,0:T(8,128)S(1)}, f32[2,2,8,8,128]{4,3,2,1,0:T(8,128)S(1)}, u32[]{:S(2)}, u32[]{:S(2)}) collective-permute-start(f32[2,2,8,8,128]{4,3,2,1,0:T(8,128)S(1)} %get-tuple-element.113), channel_id=1, source_target_pairs={{0,22},{1,23},{2,20},{3,21},{4,18},{5,19},{6,16},{7,17},{8,30},{9,... | collective-permute-start | bytes 393224 | tf_op jit(solution)/shard_map/ppermute | solution.py:346
  116.5 13.1 %collective-permute-start.43 = (f32[2,2,8,8,128]{4,3,2,1,0:T(8,128)S(1)}, f32[2,2,8,8,128]{4,3,2,1,0:T(8,128)S(1)}, u32[]{:S(2)}, u32[]{:S(2)}) collective-permute-start(f32[2,2,8,8,128]{4,3,2,1,0:T(8,128)S(1)} %get-tuple-element.114), channel_id=1, source_target_pairs={{0,6},{1,7},{2,4},{3,5},{4,2},{5,3},{6,0},{7,1},{8,14},{9,15},{10,... | collective-permute-start | bytes 393224 | tf_op jit(solution)/shard_map/ppermute | solution.py:346
  116.5 13.1 %collective-permute-start.44 = (f32[2,2,8,8,128]{4,3,2,1,0:T(8,128)S(1)}, f32[2,2,8,8,128]{4,3,2,1,0:T(8,128)S(1)}, u32[]{:S(2)}, u32[]{:S(2)}) collective-permute-start(f32[2,2,8,8,128]{4,3,2,1,0:T(8,128)S(1)} %get-tuple-element.115), channel_id=1, source_target_pairs={{0,23},{1,22},{2,21},{3,20},{4,19},{5,18},{6,17},{7,16},{8,31},{9,... | collective-permute-start | bytes 393224 | tf_op jit(solution)/shard_map/ppermute | solution.py:346
  122.9 10.4 %collective-permute-start.46 = (f32[2,2,8,8,128]{4,3,2,1,0:T(8,128)S(1)}, f32[2,2,8,8,128]{4,3,2,1,0:T(8,128)S(1)}, u32[]{:S(2)}, u32[]{:S(2)}) collective-permute-start(f32[2,2,8,8,128]{4,3,2,1,0:T(8,128)S(1)} %get-tuple-element.117), channel_id=1, source_target_pairs={{0,24},{1,25},{2,26},{3,27},{4,28},{5,29},{6,30},{7,31},{8,16},{9,... | collective-permute-start | bytes 393224 | tf_op jit(solution)/shard_map/ppermute | solution.py:346
  125.7 10.4 %collective-permute-start.47 = (f32[2,2,8,8,128]{4,3,2,1,0:T(8,128)S(1)}, f32[2,2,8,8,128]{4,3,2,1,0:T(8,128)S(1)}, u32[]{:S(2)}, u32[]{:S(2)}) collective-permute-start(f32[2,2,8,8,128]{4,3,2,1,0:T(8,128)S(1)} %get-tuple-element.118), channel_id=1, source_target_pairs={{0,8},{1,9},{2,10},{3,11},{4,12},{5,13},{6,14},{7,15},{8,0},{9,1},... | collective-permute-start | bytes 393224 | tf_op jit(solution)/shard_map/ppermute | solution.py:346
  129.6 11.4 %collective-permute-start.49 = (f32[2,2,8,8,128]{4,3,2,1,0:T(8,128)S(1)}, f32[2,2,8,8,128]{4,3,2,1,0:T(8,128)S(1)}, u32[]{:S(2)}, u32[]{:S(2)}) collective-permute-start(f32[2,2,8,8,128]{4,3,2,1,0:T(8,128)S(1)} %get-tuple-element.120), channel_id=1, source_target_pairs={{0,9},{1,8},{2,11},{3,10},{4,13},{5,12},{6,15},{7,14},{8,1},{9,0},... | collective-permute-start | bytes 393224 | tf_op jit(solution)/shard_map/ppermute | solution.py:346
  131.6 12.4 %collective-permute-start.50 = (f32[2,2,8,8,128]{4,3,2,1,0:T(8,128)S(1)}, f32[2,2,8,8,128]{4,3,2,1,0:T(8,128)S(1)}, u32[]{:S(2)}, u32[]{:S(2)}) collective-permute-start(f32[2,2,8,8,128]{4,3,2,1,0:T(8,128)S(1)} %get-tuple-element.121), channel_id=1, source_target_pairs={{0,26},{1,27},{2,24},{3,25},{4,30},{5,31},{6,28},{7,29},{8,18},{9,... | collective-permute-start | bytes 393224 | tf_op jit(solution)/shard_map/ppermute | solution.py:346
  133.3 14.9 %collective-permute-start.51 = (f32[2,2,8,8,128]{4,3,2,1,0:T(8,128)S(1)}, f32[2,2,8,8,128]{4,3,2,1,0:T(8,128)S(1)}, u32[]{:S(2)}, u32[]{:S(2)}) collective-permute-start(f32[2,2,8,8,128]{4,3,2,1,0:T(8,128)S(1)} %get-tuple-element.122), channel_id=1, source_target_pairs={{0,10},{1,11},{2,8},{3,9},{4,14},{5,15},{6,12},{7,13},{8,2},{9,3},... | collective-permute-start | bytes 393224 | tf_op jit(solution)/shard_map/ppermute | solution.py:346
  136.1 14.1 %collective-permute-start.52 = (f32[2,2,8,8,128]{4,3,2,1,0:T(8,128)S(1)}, f32[2,2,8,8,128]{4,3,2,1,0:T(8,128)S(1)}, u32[]{:S(2)}, u32[]{:S(2)}) collective-permute-start(f32[2,2,8,8,128]{4,3,2,1,0:T(8,128)S(1)} %get-tuple-element.123), channel_id=1, source_target_pairs={{0,27},{1,26},{2,25},{3,24},{4,31},{5,30},{6,29},{7,28},{8,19},{9,... | collective-permute-start | bytes 393224 | tf_op jit(solution)/shard_map/ppermute | solution.py:346
  137.9 15.3 %collective-permute-start.53 = (f32[2,2,8,8,128]{4,3,2,1,0:T(8,128)S(1)}, f32[2,2,8,8,128]{4,3,2,1,0:T(8,128)S(1)}, u32[]{:S(2)}, u32[]{:S(2)}) collective-permute-start(f32[2,2,8,8,128]{4,3,2,1,0:T(8,128)S(1)} %get-tuple-element.124), channel_id=1, source_target_pairs={{0,11},{1,10},{2,9},{3,8},{4,15},{5,14},{6,13},{7,12},{8,3},{9,2},... | collective-permute-start | bytes 393224 | tf_op jit(solution)/shard_map/ppermute | solution.py:346
  141.0 15.6 %collective-permute-start.54 = (f32[2,2,8,8,128]{4,3,2,1,0:T(8,128)S(1)}, f32[2,2,8,8,128]{4,3,2,1,0:T(8,128)S(1)}, u32[]{:S(2)}, u32[]{:S(2)}) collective-permute-start(f32[2,2,8,8,128]{4,3,2,1,0:T(8,128)S(1)} %get-tuple-element.125), channel_id=1, source_target_pairs={{0,28},{1,29},{2,30},{3,31},{4,24},{5,25},{6,26},{7,27},{8,20},{9,... | collective-permute-start | bytes 393224 | tf_op jit(solution)/shard_map/ppermute | solution.py:346
  144.0 15.4 %collective-permute-start.55 = (f32[2,2,8,8,128]{4,3,2,1,0:T(8,128)S(1)}, f32[2,2,8,8,128]{4,3,2,1,0:T(8,128)S(1)}, u32[]{:S(2)}, u32[]{:S(2)}) collective-permute-start(f32[2,2,8,8,128]{4,3,2,1,0:T(8,128)S(1)} %get-tuple-element.126), channel_id=1, source_target_pairs={{0,12},{1,13},{2,14},{3,15},{4,8},{5,9},{6,10},{7,11},{8,4},{9,5},... | collective-permute-start | bytes 393224 | tf_op jit(solution)/shard_map/ppermute | solution.py:346
  148.2 15.0 %collective-permute-start.56 = (f32[2,2,8,8,128]{4,3,2,1,0:T(8,128)S(1)}, f32[2,2,8,8,128]{4,3,2,1,0:T(8,128)S(1)}, u32[]{:S(2)}, u32[]{:S(2)}) collective-permute-start(f32[2,2,8,8,128]{4,3,2,1,0:T(8,128)S(1)} %get-tuple-element.127), channel_id=1, source_target_pairs={{0,29},{1,28},{2,31},{3,30},{4,25},{5,24},{6,27},{7,26},{8,21},{9,... | collective-permute-start | bytes 393224 | tf_op jit(solution)/shard_map/ppermute | solution.py:346
  150.2 14.4 %collective-permute-start.57 = (f32[2,2,8,8,128]{4,3,2,1,0:T(8,128)S(1)}, f32[2,2,8,8,128]{4,3,2,1,0:T(8,128)S(1)}, u32[]{:S(2)}, u32[]{:S(2)}) collective-permute-start(f32[2,2,8,8,128]{4,3,2,1,0:T(8,128)S(1)} %get-tuple-element.128), channel_id=1, source_target_pairs={{0,13},{1,12},{2,15},{3,14},{4,9},{5,8},{6,11},{7,10},{8,5},{9,4},... | collective-permute-start | bytes 393224 | tf_op jit(solution)/shard_map/ppermute | solution.py:346
  153.2 15.9 %collective-permute-start.58 = (f32[2,2,8,8,128]{4,3,2,1,0:T(8,128)S(1)}, f32[2,2,8,8,128]{4,3,2,1,0:T(8,128)S(1)}, u32[]{:S(2)}, u32[]{:S(2)}) collective-permute-start(f32[2,2,8,8,128]{4,3,2,1,0:T(8,128)S(1)} %get-tuple-element.129), channel_id=1, source_target_pairs={{0,30},{1,31},{2,28},{3,29},{4,26},{5,27},{6,24},{7,25},{8,22},{9,... | collective-permute-start | bytes 393224 | tf_op jit(solution)/shard_map/ppermute | solution.py:346
  156.6 12.6 %collective-permute-start.59 = (f32[2,2,8,8,128]{4,3,2,1,0:T(8,128)S(1)}, f32[2,2,8,8,128]{4,3,2,1,0:T(8,128)S(1)}, u32[]{:S(2)}, u32[]{:S(2)}) collective-permute-start(f32[2,2,8,8,128]{4,3,2,1,0:T(8,128)S(1)} %get-tuple-element.130), channel_id=1, source_target_pairs={{0,14},{1,15},{2,12},{3,13},{4,10},{5,11},{6,8},{7,9},{8,6},{9,7},... | collective-permute-start | bytes 393224 | tf_op jit(solution)/shard_map/ppermute | solution.py:346
  159.3 16.2 %collective-permute-start.60 = (f32[2,2,8,8,128]{4,3,2,1,0:T(8,128)S(1)}, f32[2,2,8,8,128]{4,3,2,1,0:T(8,128)S(1)}, u32[]{:S(2)}, u32[]{:S(2)}) collective-permute-start(f32[2,2,8,8,128]{4,3,2,1,0:T(8,128)S(1)} %get-tuple-element.131), channel_id=1, source_target_pairs={{0,31},{1,30},{2,29},{3,28},{4,27},{5,26},{6,25},{7,24},{8,23},{9,... | collective-permute-start | bytes 393224 | tf_op jit(solution)/shard_map/ppermute | solution.py:346
  163.3 12.3 %collective-permute-start.61 = (f32[2,2,8,8,128]{4,3,2,1,0:T(8,128)S(1)}, f32[2,2,8,8,128]{4,3,2,1,0:T(8,128)S(1)}, u32[]{:S(2)}, u32[]{:S(2)}) collective-permute-start(f32[2,2,8,8,128]{4,3,2,1,0:T(8,128)S(1)} %get-tuple-element.132), channel_id=1, source_target_pairs={{0,15},{1,14},{2,13},{3,12},{4,11},{5,10},{6,9},{7,8},{8,7},{9,6},... | collective-permute-start | bytes 393224 | tf_op jit(solution)/shard_map/ppermute | solution.py:346
  (38 other events, 431.9 us)
where the time goes:
time: 181 us; the launch traced here: 180 us
  starting transfers between devices  98.5 us (54%)
  waiting for transfers between devices  57.9 us (32%)
  Pallas kernels  14.9 us (8%)
  local copies, waits for them, and re-layouts  7.95 us (4%)
    ppermute x62, starting transfers between devices, swap(): lax.ppermute(pieces[slot], 'kb', pairs)  98.5 us
    ppermute x62, waiting for transfers between devices, swap(): lax.ppermute(pieces[slot], 'kb', pairs)  57.9 us
    pallas_call x2, Pallas kernels, call_kernel(): pl.pallas_call(kernel, in_specs=[pl.BlockSpec(memory_space=pltpu.SMEM)] +...  10.3 us
    unnamed x17, local copies, waits for them, and re-layouts  7.87 us
    pallas_call x1, Pallas kernels, to_frequencies(): pl.pallas_call(functools.partial(frequency_kernel, order), in_specs=[pl.B...  4.64 us
  transfers between devices with their start and end apart: 62, of which 17 were waited for; matrix products, arithmetic and copies ran while one was open for 1% of the time, Pallas kernels for 0%

commit v1 on v0

--- a/solution.py
+++ b/solution.py
@@ -104,6 +104,12 @@
     return out
 
 
+def place(refs, order, slot, me):
+    if slot in order:
+        return refs[1 + order.index(slot)], ()
+    return refs[0], (slot ^ (me % refs[0].shape[0]),)
+
+
 def relative_rows(matrix_ref, me):
     parts, devices = matrix_ref.shape[:2]
     rows = [matrix_ref[part, slot ^ me] for part in range(parts) for slot in range(devices)]
@@ -126,21 +132,22 @@
             ((1, 0), s_im - c_re),
             ((1, 1), -(c_im + s_re)),
         ):
-            for out_ref, slot in zip(outs, order):
-                out_ref[where[0], where[1], e] = value[slot * rows : (slot + 1) * rows]
-
-
-def call_kernel(kernel, order, me, args, arg_specs, shape, scratch, limit, name):
-    pieces = pl.pallas_call(
+            for slot in range(devices):
+                ref, at = place(outs, order, slot, me_ref[0])
+                ref[at + (where[0], where[1], e)] = value[slot * rows : (slot + 1) * rows]
+
+
+def call_kernel(kernel, near, order, me, args, arg_specs, shape, scratch, limit, name):
+    return pl.pallas_call(
         kernel,
         in_specs=[pl.BlockSpec(memory_space=pltpu.SMEM)] + arg_specs,
-        out_specs=[pl.BlockSpec(memory_space=pltpu.VMEM)] * len(order),
-        out_shape=[jax.ShapeDtypeStruct(shape, jnp.float32)] * len(order),
+        out_specs=[pl.BlockSpec(memory_space=pltpu.VMEM)] * (1 + len(order)),
+        out_shape=[jax.ShapeDtypeStruct((near,) + shape, jnp.float32)]
+        + [jax.ShapeDtypeStruct(shape, jnp.float32)] * len(order),
         scratch_shapes=scratch,
         compiler_params=pltpu.CompilerParams(vmem_limit_bytes=limit << 20),
         name=name,
     )(me, *args)
-    return dict(zip(order, pieces))
 
 
 def to_times(green, matrix, me, order):
@@ -148,7 +155,8 @@
     shape = (2, 2, entries, matrix.shape[2], lanes)
     vmem = pl.BlockSpec(memory_space=pltpu.VMEM)
     kernel = functools.partial(times_kernel, order)
-    return call_kernel(kernel, order, me, (green, matrix), [vmem] * 2, shape, [], 40, "to_times")
+    near = matrix.shape[1] - len(order)
+    return call_kernel(kernel, near, order, me, (green, matrix), [vmem] * 2, shape, [], 40, "to_times")
 
 
 def fill_block(ref, cosine, sine):
@@ -165,9 +173,8 @@
 
 
 def middle_kernel(order, me_ref, table_ref, mirror_ref, index_ref, ch_ref, cl_ref, sh_ref, sl_ref, *refs):
-    count = len(order)
-    pieces = dict(zip(order, refs[:count]))
-    outs = dict(zip(order, refs[count : 2 * count]))
+    count = 1 + len(order)
+    pieces, outs = refs[:count], refs[count : 2 * count]
     forward, backward, mid, space, chi = refs[2 * count :]
     halves, _, side, _, entries, rows, lanes = space.shape
     plane = 2 * lanes
@@ -203,7 +210,10 @@
         columns = []
         for ri in range(2):
             for h in range(2):
-                rows_of = [pieces[2 * x + h][half, ri].reshape(entries * rows, lanes) for x in range(side)]
+                rows_of = []
+                for x in range(side):
+                    ref, at = place(pieces, order, 2 * x + h, me_ref[0])
+                    rows_of.append(ref[at + (half, ri)].reshape(entries * rows, lanes))
                 columns.append(jnp.concatenate(rows_of, axis=0))
         return split_value(jnp.concatenate(columns, axis=1))
 
@@ -239,7 +249,8 @@
         for ri in range(2):
             piece = d[:, ri * lanes : (ri + 1) * lanes].reshape(side, members, rows, lanes)
             for x in range(side):
-                outs[2 * x + h][half, ri, first : first + members] = piece[x]
+                ref, at = place(outs, order, 2 * x + h, me_ref[0])
+                ref[at + (half, ri, slice(first, first + members))] = piece[x]
 
     def collect(unit):
         whole = (side * members * rows, plane)
@@ -268,9 +279,9 @@
 
 
 def middle(pieces, table, mirror_map, me, order):
-    halves, _, entries, rows, lanes = pieces[0].shape
+    near, halves, _, entries, rows, lanes = pieces[0].shape
     plane = 2 * lanes
-    side = len(order) // 2
+    side = (near + len(order)) // 2
     components = table.shape[0]
     members = components // GROUPS
     units = halves * GROUPS
@@ -287,28 +298,34 @@
         pltpu.VMEM((halves, 2, side, 2, entries, rows, lanes), jnp.float32),
         pltpu.VMEM((units, 2, side, members, rows, plane), jnp.float32),
     ]
-    args = (table, mirror_map, index, *parts) + tuple(pieces[slot] for slot in order)
-    specs = [smem, smem, vmem] + [vmem] * (4 + len(order))
+    args = (table, mirror_map, index, *parts, *pieces)
+    specs = [smem, smem, vmem] + [vmem] * (4 + len(pieces))
     shape = (halves, 2, components, rows, lanes)
     kernel = functools.partial(middle_kernel, order)
-    return call_kernel(kernel, order, me, args, specs, shape, scratch, 40, "middle")
+    return call_kernel(kernel, near, order, me, args, specs, shape, scratch, 40, "middle")
 
 
 def frequency_kernel(order, me_ref, m_ref, *refs):
-    pieces = dict(zip(order, refs[: len(order)]))
-    out_ref, stage, sems = refs[len(order) :]
+    pieces = refs[: 1 + len(order)]
+    out_ref, stage, sems = refs[1 + len(order) :]
+    devices = m_ref.shape[1]
     components, lanes = stage.shape[1:3]
     groups = sems.shape[0]
     members = components // groups
     matrix = split_value(relative_rows(m_ref, me_ref[0]))
+
+    def gathered(half, ri, c):
+        rows_of = []
+        for slot in range(devices):
+            ref, at = place(pieces, order, slot, me_ref[0])
+            rows_of.append(ref[at + (half, ri, c)])
+        return jnp.concatenate(rows_of, axis=0)
+
     copies = []
     for group in range(groups):
         values = []
         for c in range(group * members, (group + 1) * members):
-            part = [
-                [jnp.concatenate([pieces[slot][half, ri, c] for slot in range(len(order))], axis=0) for ri in range(2)]
-                for half in range(2)
-            ]
+            part = [[gathered(half, ri, c) for ri in range(2)] for half in range(2)]
             sums = [part[0][ri] + part[1][ri] for ri in range(2)]
             differences = [part[0][ri] - part[1][ri] for ri in range(2)]
             values.append(jnp.concatenate([sums[0], -differences[1]], axis=0).T)
@@ -325,31 +342,31 @@
 
 
 def to_frequencies(pieces, matrix, me, order):
-    _, _, components, rows, lanes = pieces[0].shape
+    components, rows, lanes = pieces[0].shape[3:]
     shape = (2, components, lanes, matrix.shape[3])
     vmem = pl.BlockSpec(memory_space=pltpu.VMEM)
     return pl.pallas_call(
         functools.partial(frequency_kernel, order),
-        in_specs=[pl.BlockSpec(memory_space=pltpu.SMEM)] + [vmem] * (1 + len(order)),
+        in_specs=[pl.BlockSpec(memory_space=pltpu.SMEM)] + [vmem] * (1 + len(pieces)),
         out_specs=pl.BlockSpec(memory_space=pltpu.HBM),
         out_shape=jax.ShapeDtypeStruct(shape, jnp.float32),
         scratch_shapes=[pltpu.VMEM(shape, jnp.float32), pltpu.SemaphoreType.DMA((components // 2,))],
         compiler_params=pltpu.CompilerParams(vmem_limit_bytes=40 << 20),
         name="to_frequencies",
-    )(me, matrix, *[pieces[slot] for slot in order])
-
-
-def swap(pieces, order):
-    moved = {}
-    for slot in order:
-        pairs = [(device, device ^ slot) for device in range(len(order))]
-        moved[slot] = lax.ppermute(pieces[slot], "kb", pairs) if slot else pieces[slot]
-    return moved
-
-
-def slot_order(devices):
-    half = devices // 2
-    return [slot for near in range(half) for slot in (near + half, near)]
+    )(me, matrix, *pieces)
+
+
+def swap(pieces, order, devices):
+    near = pieces[0]
+    size = near.shape[0]
+    groups = [list(range(start, start + size)) for start in range(0, devices, size)]
+    moved = []
+    for piece, slot in zip(pieces[1:], order):
+        pairs = [(device, device ^ slot) for device in range(devices)]
+        moved.append(lax.ppermute(piece, "kb", pairs))
+    flat = near.reshape(size, -1, near.shape[-1])
+    flat = lax.all_to_all(flat, "kb", split_axis=0, concat_axis=0, tiled=True, axis_index_groups=groups)
+    return [flat.reshape(near.shape)] + moved
 
 
 def trig_pair(angle_int, period, scale):
@@ -479,10 +496,10 @@
     shape = (2, devices, pairs, count)
     forward = jnp.asarray(fermion_matrix(rows, count).reshape(shape).astype(np.float32))
     backward = jnp.asarray(boson_matrix(rows, count).reshape(shape).astype(np.float32))
-    order = slot_order(devices)
+    order = list(range(devices // 2, devices))
     me = lax.axis_index("kb").astype(jnp.int32).reshape(1)
-    pieces = swap(to_times(green, forward, me, order), order)
-    pieces = swap(middle(pieces, pair_table, mirror_map, me, order), order)
+    pieces = swap(to_times(green, forward, me, order), order, devices)
+    pieces = swap(middle(pieces, pair_table, mirror_map, me, order), order, devices)
     return to_frequencies(pieces, backward, me, order)
 
 

time: 181 us -> 214 us (1.18)
  the two profiles are of different devices: /device:TPU:0 before, /device:TPU:13 now
where the time goes in v1:
time: 214 us; the launch traced here: 213 us
  waiting for transfers between devices  96 us (45%)
  starting transfers between devices  66.6 us (31%)
  local copies, waits for them, and re-layouts  33.7 us (16%)
  Pallas kernels  16.7 us (8%)
    ppermute x32, waiting for transfers between devices, swap(): moved.append(lax.ppermute(piece, 'kb', pairs))  96 us
    ppermute x32, starting transfers between devices, swap(): moved.append(lax.ppermute(piece, 'kb', pairs))  56.8 us
    unnamed x101, local copies, waits for them, and re-layouts  33.7 us
    pallas_call x2, Pallas kernels, call_kernel(): pl.pallas_call(kernel, in_specs=[pl.BlockSpec(memory_space=pltpu.SMEM)] +...  12.1 us
    all_to_all x2, starting transfers between devices, swap(): lax.all_to_all(flat, 'kb', split_axis=0, concat_axis=0, tiled=True, axis_...  9.87 us
    pallas_call x1, Pallas kernels, to_frequencies(): pl.pallas_call(functools.partial(frequency_kernel, order), in_specs=[pl.B...  4.55 us
  transfers between devices with their start and end apart: 34, of which 25 were waited for; matrix products, arithmetic and copies ran while one was open for 0% of the time, Pallas kernels for 0%

profile of v1, /device:TPU:13, one launch (start us, length us, event | category | flops | bytes accessed | tf_op | source)
XLA Modules:
  0.0 213.5 jit_solution(6451664223734193169)
XLA Ops:
  2.9 2.9 %to_times.1 = (f32[16,2,2,4,8,128]{5,4,3,2,1,0:T(8,128)}, f32[2,2,4,8,128]{4,3,2,1,0:T(8,128)S(1)}, f32[2,2,4,8,128]{4,3,2,1,0:T(8,128)S(1)}, f32[2,2,4,8,128]{4...) custom-call(s32[1]{0:T(128)} %bitcast.me_ref, ...), custom_call_target="tpu_custom_call" | custom-call | tf_op jit(solution)/shard_map/to_times/pallas_call | solution.py:141
  5.7 5.5 %all-to-all-start = ((f32[16,128,128]{2,1,0:T(8,128)}), f32[16,128,128]{2,1,0:T(8,128)S(1)}, u32[]{:S(2)}, u32[]{:S(2)}) async-start(f32[16,128,128]{2,1,0:T(8,128)} %bitcast.3), calls=%async_computation | async-start | bytes 2097152 | tf_op jit(solution)/shard_map/all_to_all | solution.py:368
  11.2 2.3 %collective-permute-start = (f32[2,2,4,8,128]{4,3,2,1,0:T(8,128)S(1)}, f32[2,2,4,8,128]{4,3,2,1,0:T(8,128)S(1)}, u32[]{:S(2)}, u32[]{:S(2)}) collective-permute-start(f32[2,2,4,8,128]{4,3,2,1,0:T(8,128)S(1)} %get-tuple-element.40), channel_id=1, source_target_pairs={{0,16},{1,17},{2,18},{3,19},{4,20},{5,21},{6,22},{7,23},{8,24},{9,... | collective-permute-start | bytes 196616 | tf_op jit(solution)/shard_map/ppermute | solution.py:366
  14.1 3.2 %collective-permute-start.2 = (f32[2,2,4,8,128]{4,3,2,1,0:T(8,128)S(1)}, f32[2,2,4,8,128]{4,3,2,1,0:T(8,128)S(1)}, u32[]{:S(2)}, u32[]{:S(2)}) collective-permute-start(f32[2,2,4,8,128]{4,3,2,1,0:T(8,128)S(1)} %get-tuple-element.42), channel_id=1, source_target_pairs={{0,18},{1,19},{2,16},{3,17},{4,22},{5,23},{6,20},{7,21},{8,26},{9,... | collective-permute-start | bytes 196616 | tf_op jit(solution)/shard_map/ppermute | solution.py:366
  17.6 2.1 collective-permute-start.4
  19.7 7.4 %collective-permute-done.refs_1_ = f32[2,2,4,8,128]{4,3,2,1,0:T(8,128)S(1)} collective-permute-done((f32[2,2,4,8,128]{4,3,2,1,0:T(8,128)S(1)}, f32[2,2,4,8,128]{4,3,2,1,0:T(8,128)S(1)}, u32[]{:S(2)}, u32[]{:S(2)}) %collective-permute-start) | collective-permute-done | bytes 65568 | tf_op jit(solution)/shard_map/ppermute | solution.py:366
  29.3 3.2 %collective-permute-start.6 = (f32[2,2,4,8,128]{4,3,2,1,0:T(8,128)S(1)}, f32[2,2,4,8,128]{4,3,2,1,0:T(8,128)S(1)}, u32[]{:S(2)}, u32[]{:S(2)}) collective-permute-start(f32[2,2,4,8,128]{4,3,2,1,0:T(8,128)S(1)} %get-tuple-element.46), channel_id=1, source_target_pairs={{0,22},{1,23},{2,20},{3,21},{4,18},{5,19},{6,16},{7,17},{8,30},{9,... | collective-permute-start | bytes 196616 | tf_op jit(solution)/shard_map/ppermute | solution.py:366
  33.4 2.1 collective-permute-start.9
  35.7 5.9 %collective-permute-start.10 = (f32[2,2,4,8,128]{4,3,2,1,0:T(8,128)S(1)}, f32[2,2,4,8,128]{4,3,2,1,0:T(8,128)S(1)}, u32[]{:S(2)}, u32[]{:S(2)}) collective-permute-start(f32[2,2,4,8,128]{4,3,2,1,0:T(8,128)S(1)} %get-tuple-element.50), channel_id=1, source_target_pairs={{0,26},{1,27},{2,24},{3,25},{4,30},{5,31},{6,28},{7,29},{8,18},{9,... | collective-permute-start | bytes 196616 | tf_op jit(solution)/shard_map/ppermute | solution.py:366
  43.7 2.8 %collective-permute-done.8.refs_9_ = f32[2,2,4,8,128]{4,3,2,1,0:T(8,128)S(1)} collective-permute-done((f32[2,2,4,8,128]{4,3,2,1,0:T(8,128)S(1)}, f32[2,2,4,8,128]{4,3,2,1,0:T(8,128)S(1)}, u32[]{:S(2)}, u32[]{:S(2)}) %collective-permute-start.8) | collective-permute-done | bytes 65568 | tf_op jit(solution)/shard_map/ppermute | solution.py:366
  46.5 2.1 collective-permute-done.9.refs_10_
  48.6 2.3 %collective-permute-start.14 = (f32[2,2,4,8,128]{4,3,2,1,0:T(8,128)S(1)}, f32[2,2,4,8,128]{4,3,2,1,0:T(8,128)S(1)}, u32[]{:S(2)}, u32[]{:S(2)}) collective-permute-start(f32[2,2,4,8,128]{4,3,2,1,0:T(8,128)S(1)} %get-tuple-element.54), channel_id=1, source_target_pairs={{0,30},{1,31},{2,28},{3,29},{4,26},{5,27},{6,24},{7,25},{8,22},{9,... | collective-permute-start | bytes 196616 | tf_op jit(solution)/shard_map/ppermute | solution.py:366
  53.6 2.9 %collective-permute-done.11.refs_12_ = f32[2,2,4,8,128]{4,3,2,1,0:T(8,128)S(1)} collective-permute-done((f32[2,2,4,8,128]{4,3,2,1,0:T(8,128)S(1)}, f32[2,2,4,8,128]{4,3,2,1,0:T(8,128)S(1)}, u32[]{:S(2)}, u32[]{:S(2)}) %collective-permute-start.11) | collective-permute-done | bytes 65568 | tf_op jit(solution)/shard_map/ppermute | solution.py:366
  58.5 2.8 %collective-permute-done.13.refs_14_ = f32[2,2,4,8,128]{4,3,2,1,0:T(8,128)S(1)} collective-permute-done((f32[2,2,4,8,128]{4,3,2,1,0:T(8,128)S(1)}, f32[2,2,4,8,128]{4,3,2,1,0:T(8,128)S(1)}, u32[]{:S(2)}, u32[]{:S(2)}) %collective-permute-start.13) | collective-permute-done | bytes 65568 | tf_op jit(solution)/shard_map/ppermute | solution.py:366
  61.3 2.3 %collective-permute-done.14.refs_15_ = f32[2,2,4,8,128]{4,3,2,1,0:T(8,128)S(1)} collective-permute-done((f32[2,2,4,8,128]{4,3,2,1,0:T(8,128)S(1)}, f32[2,2,4,8,128]{4,3,2,1,0:T(8,128)S(1)}, u32[]{:S(2)}, u32[]{:S(2)}) %collective-permute-start.14) | collective-permute-done | bytes 65568 | tf_op jit(solution)/shard_map/ppermute | solution.py:366
  65.0 9.3 %middle.1 = (f32[16,2,2,8,8,128]{5,4,3,2,1,0:T(8,128)S(1)}, f32[2,2,8,8,128]{4,3,2,1,0:T(8,128)}, f32[2,2,8,8,128]{4,3,2,1,0:T(8,128)}, f32[2,2,8,8,128]{4,3,2,1...) custom-call(s32[1]{0:T(128)} %bitcast.me_ref, ...), custom_call_target="tpu_custom_call" | custom-call | tf_op jit(solution)/shard_map/middle/pallas_call | solution.py:141
  84.8 4.4 %all-to-all-start.1 = ((f32[16,256,128]{2,1,0:T(8,128)}), f32[16,256,128]{2,1,0:T(8,128)S(1)}, u32[]{:S(2)}, u32[]{:S(2)}) async-start(f32[16,256,128]{2,1,0:T(8,128)} %bitcast.11), calls=%async_computation.1 | async-start | bytes 4194304 | tf_op jit(solution)/shard_map/all_to_all | solution.py:368
  90.0 2.1 collective-permute-start.17
  96.2 23.2 %collective-permute-done.16.refs_1_ = f32[2,2,8,8,128]{4,3,2,1,0:T(8,128)S(1)} collective-permute-done((f32[2,2,8,8,128]{4,3,2,1,0:T(8,128)}, f32[2,2,8,8,128]{4,3,2,1,0:T(8,128)S(1)}, u32[]{:S(2)}, u32[]{:S(2)}) %collective-permute-start.16) | collective-permute-done | bytes 131104 | tf_op jit(solution)/shard_map/ppermute | solution.py:366
  119.4 3.8 %collective-permute-done.17.refs_2_ = f32[2,2,8,8,128]{4,3,2,1,0:T(8,128)S(1)} collective-permute-done((f32[2,2,8,8,128]{4,3,2,1,0:T(8,128)}, f32[2,2,8,8,128]{4,3,2,1,0:T(8,128)S(1)}, u32[]{:S(2)}, u32[]{:S(2)}) %collective-permute-start.17) | collective-permute-done | bytes 131104 | tf_op jit(solution)/shard_map/ppermute | solution.py:366
  124.6 3.8 %collective-permute-start.23 = (f32[2,2,8,8,128]{4,3,2,1,0:T(8,128)}, f32[2,2,8,8,128]{4,3,2,1,0:T(8,128)S(1)}, u32[]{:S(2)}, u32[]{:S(2)}) collective-permute-start(f32[2,2,8,8,128]{4,3,2,1,0:T(8,128)} %copy-done.43), channel_id=1, source_target_pairs={{0,23},{1,22},{2,21},{3,20},{4,19},{5,18},{6,17},{7,16},{8,31},{9,... | collective-permute-start | bytes 393224 | tf_op jit(solution)/shard_map/ppermute | solution.py:366
  131.4 15.3 %collective-permute-done.21.refs_6_ = f32[2,2,8,8,128]{4,3,2,1,0:T(8,128)S(1)} collective-permute-done((f32[2,2,8,8,128]{4,3,2,1,0:T(8,128)}, f32[2,2,8,8,128]{4,3,2,1,0:T(8,128)S(1)}, u32[]{:S(2)}, u32[]{:S(2)}) %collective-permute-start.21) | collective-permute-done | bytes 131104 | tf_op jit(solution)/shard_map/ppermute | solution.py:366
  157.0 6.3 %collective-permute-start.29 = (f32[2,2,8,8,128]{4,3,2,1,0:T(8,128)}, f32[2,2,8,8,128]{4,3,2,1,0:T(8,128)S(1)}, u32[]{:S(2)}, u32[]{:S(2)}) collective-permute-start(f32[2,2,8,8,128]{4,3,2,1,0:T(8,128)} %copy-done.37), channel_id=1, source_target_pairs={{0,29},{1,28},{2,31},{3,30},{4,25},{5,24},{6,27},{7,26},{8,21},{9,... | collective-permute-start | bytes 393224 | tf_op jit(solution)/shard_map/ppermute | solution.py:366
  163.3 7.2 %collective-permute-done.25.refs_10_ = f32[2,2,8,8,128]{4,3,2,1,0:T(8,128)S(1)} collective-permute-done((f32[2,2,8,8,128]{4,3,2,1,0:T(8,128)}, f32[2,2,8,8,128]{4,3,2,1,0:T(8,128)S(1)}, u32[]{:S(2)}, u32[]{:S(2)}) %collective-permute-start.25) | collective-permute-done | bytes 131104 | tf_op jit(solution)/shard_map/ppermute | solution.py:366
  171.2 4.3 %collective-permute-start.30 = (f32[2,2,8,8,128]{4,3,2,1,0:T(8,128)}, f32[2,2,8,8,128]{4,3,2,1,0:T(8,128)S(1)}, u32[]{:S(2)}, u32[]{:S(2)}) collective-permute-start(f32[2,2,8,8,128]{4,3,2,1,0:T(8,128)} %copy-done.36), channel_id=1, source_target_pairs={{0,30},{1,31},{2,28},{3,29},{4,26},{5,27},{6,24},{7,25},{8,22},{9,... | collective-permute-start | bytes 393224 | tf_op jit(solution)/shard_map/ppermute | solution.py:366
  175.5 3.1 %collective-permute-done.26.refs_11_ = f32[2,2,8,8,128]{4,3,2,1,0:T(8,128)S(1)} collective-permute-done((f32[2,2,8,8,128]{4,3,2,1,0:T(8,128)}, f32[2,2,8,8,128]{4,3,2,1,0:T(8,128)S(1)}, u32[]{:S(2)}, u32[]{:S(2)}) %collective-permute-start.26) | collective-permute-done | bytes 131104 | tf_op jit(solution)/shard_map/ppermute | solution.py:366
  179.3 3.0 %collective-permute-start.31 = (f32[2,2,8,8,128]{4,3,2,1,0:T(8,128)}, f32[2,2,8,8,128]{4,3,2,1,0:T(8,128)S(1)}, u32[]{:S(2)}, u32[]{:S(2)}) collective-permute-start(f32[2,2,8,8,128]{4,3,2,1,0:T(8,128)} %copy-done.35), channel_id=1, source_target_pairs={{0,31},{1,30},{2,29},{3,28},{4,27},{5,26},{6,25},{7,24},{8,23},{9,... | collective-permute-start | bytes 393224 | tf_op jit(solution)/shard_map/ppermute | solution.py:366
  183.0 2.0 collective-permute-done.28.refs_13_
  185.7 2.2 %collective-permute-done.29.refs_14_ = f32[2,2,8,8,128]{4,3,2,1,0:T(8,128)S(1)} collective-permute-done((f32[2,2,8,8,128]{4,3,2,1,0:T(8,128)}, f32[2,2,8,8,128]{4,3,2,1,0:T(8,128)S(1)}, u32[]{:S(2)}, u32[]{:S(2)}) %collective-permute-start.29) | collective-permute-done | bytes 131104 | tf_op jit(solution)/shard_map/ppermute | solution.py:366
  188.5 5.0 %collective-permute-done.30.refs_15_ = f32[2,2,8,8,128]{4,3,2,1,0:T(8,128)S(1)} collective-permute-done((f32[2,2,8,8,128]{4,3,2,1,0:T(8,128)}, f32[2,2,8,8,128]{4,3,2,1,0:T(8,128)S(1)}, u32[]{:S(2)}, u32[]{:S(2)}) %collective-permute-start.30) | collective-permute-done | bytes 131104 | tf_op jit(solution)/shard_map/ppermute | solution.py:366
  194.2 2.2 %collective-permute-done.31.refs_16_ = f32[2,2,8,8,128]{4,3,2,1,0:T(8,128)S(1)} collective-permute-done((f32[2,2,8,8,128]{4,3,2,1,0:T(8,128)}, f32[2,2,8,8,128]{4,3,2,1,0:T(8,128)S(1)}, u32[]{:S(2)}, u32[]{:S(2)}) %collective-permute-start.31) | collective-permute-done | bytes 131104 | tf_op jit(solution)/shard_map/ppermute | solution.py:366
  208.8 4.6 %to_frequencies.1 = f32[2,8,128,512]{3,2,1,0:T(8,128)} custom-call(s32[1]{0:T(128)} %bitcast.me_ref, f32[2,32,8,512]{3,2,1,0:T(8,128)S(1)} %copy-done.2, f32[16,2,2,8,8,128]{5,4,3,2,1,0:T(8,128)S(1)} %bitcast.9, f32[2,2,8,8,128]{4,3,2,1,0:T(8,128)S(1)} %collective-permute-done.16.refs_1_, f32[2,2,8,8,128]{4,3,2,1,0:T(8,128)S(1)} %collective-permute-done.17.refs_2_, ...), custom_call_target="tpu_custom_call" | custom-call | tf_op jit(solution)/shard_map/to_frequencies/pallas_call | solution.py:348
  (143 shorter events, 61.5 us)
Async XLA Ops:
  5.7 59.3 %all-to-all-start = ((f32[16,128,128]{2,1,0:T(8,128)}), f32[16,128,128]{2,1,0:T(8,128)S(1)}, u32[]{:S(2)}, u32[]{:S(2)}) async-start(f32[16,128,128]{2,1,0:T(8,128)} %bitcast.3), calls=%async_computation | async-start | bytes 2097152 | tf_op jit(solution)/shard_map/all_to_all | solution.py:368
  11.2 15.9 %collective-permute-start = (f32[2,2,4,8,128]{4,3,2,1,0:T(8,128)S(1)}, f32[2,2,4,8,128]{4,3,2,1,0:T(8,128)S(1)}, u32[]{:S(2)}, u32[]{:S(2)}) collective-permute-start(f32[2,2,4,8,128]{4,3,2,1,0:T(8,128)S(1)} %get-tuple-element.40), channel_id=1, source_target_pairs={{0,16},{1,17},{2,18},{3,19},{4,20},{5,21},{6,22},{7,23},{8,24},{9,... | collective-permute-start | bytes 196616 | tf_op jit(solution)/shard_map/ppermute | solution.py:366
  13.5 15.8 %collective-permute-start.1 = (f32[2,2,4,8,128]{4,3,2,1,0:T(8,128)S(1)}, f32[2,2,4,8,128]{4,3,2,1,0:T(8,128)S(1)}, u32[]{:S(2)}, u32[]{:S(2)}) collective-permute-start(f32[2,2,4,8,128]{4,3,2,1,0:T(8,128)S(1)} %get-tuple-element.41), channel_id=1, source_target_pairs={{0,17},{1,16},{2,19},{3,18},{4,21},{5,20},{6,23},{7,22},{8,25},{9,... | collective-permute-start | bytes 196616 | tf_op jit(solution)/shard_map/ppermute | solution.py:366
  14.1 18.4 %collective-permute-start.2 = (f32[2,2,4,8,128]{4,3,2,1,0:T(8,128)S(1)}, f32[2,2,4,8,128]{4,3,2,1,0:T(8,128)S(1)}, u32[]{:S(2)}, u32[]{:S(2)}) collective-permute-start(f32[2,2,4,8,128]{4,3,2,1,0:T(8,128)S(1)} %get-tuple-element.42), channel_id=1, source_target_pairs={{0,18},{1,19},{2,16},{3,17},{4,22},{5,23},{6,20},{7,21},{8,26},{9,... | collective-permute-start | bytes 196616 | tf_op jit(solution)/shard_map/ppermute | solution.py:366
  17.3 16.1 %collective-permute-start.3 = (f32[2,2,4,8,128]{4,3,2,1,0:T(8,128)S(1)}, f32[2,2,4,8,128]{4,3,2,1,0:T(8,128)S(1)}, u32[]{:S(2)}, u32[]{:S(2)}) collective-permute-start(f32[2,2,4,8,128]{4,3,2,1,0:T(8,128)S(1)} %get-tuple-element.43), channel_id=1, source_target_pairs={{0,19},{1,18},{2,17},{3,16},{4,23},{5,22},{6,21},{7,20},{8,27},{9,... | collective-permute-start | bytes 196616 | tf_op jit(solution)/shard_map/ppermute | solution.py:366
  17.6 15.8 %collective-permute-start.4 = (f32[2,2,4,8,128]{4,3,2,1,0:T(8,128)S(1)}, f32[2,2,4,8,128]{4,3,2,1,0:T(8,128)S(1)}, u32[]{:S(2)}, u32[]{:S(2)}) collective-permute-start(f32[2,2,4,8,128]{4,3,2,1,0:T(8,128)S(1)} %get-tuple-element.44), channel_id=1, source_target_pairs={{0,20},{1,21},{2,22},{3,23},{4,16},{5,17},{6,18},{7,19},{8,28},{9,... | collective-permute-start | bytes 196616 | tf_op jit(solution)/shard_map/ppermute | solution.py:366
  29.3 12.3 %collective-permute-start.6 = (f32[2,2,4,8,128]{4,3,2,1,0:T(8,128)S(1)}, f32[2,2,4,8,128]{4,3,2,1,0:T(8,128)S(1)}, u32[]{:S(2)}, u32[]{:S(2)}) collective-permute-start(f32[2,2,4,8,128]{4,3,2,1,0:T(8,128)S(1)} %get-tuple-element.46), channel_id=1, source_target_pairs={{0,22},{1,23},{2,20},{3,21},{4,18},{5,19},{6,16},{7,17},{8,30},{9,... | collective-permute-start | bytes 196616 | tf_op jit(solution)/shard_map/ppermute | solution.py:366
  33.4 13.1 %collective-permute-start.8 = (f32[2,2,4,8,128]{4,3,2,1,0:T(8,128)S(1)}, f32[2,2,4,8,128]{4,3,2,1,0:T(8,128)S(1)}, u32[]{:S(2)}, u32[]{:S(2)}) collective-permute-start(f32[2,2,4,8,128]{4,3,2,1,0:T(8,128)S(1)} %get-tuple-element.48), channel_id=1, source_target_pairs={{0,24},{1,25},{2,26},{3,27},{4,28},{5,29},{6,30},{7,31},{8,16},{9,... | collective-permute-start | bytes 196616 | tf_op jit(solution)/shard_map/ppermute | solution.py:366
  33.4 15.2 %collective-permute-start.9 = (f32[2,2,4,8,128]{4,3,2,1,0:T(8,128)S(1)}, f32[2,2,4,8,128]{4,3,2,1,0:T(8,128)S(1)}, u32[]{:S(2)}, u32[]{:S(2)}) collective-permute-start(f32[2,2,4,8,128]{4,3,2,1,0:T(8,128)S(1)} %get-tuple-element.49), channel_id=1, source_target_pairs={{0,25},{1,24},{2,27},{3,26},{4,29},{5,28},{6,31},{7,30},{8,17},{9,... | collective-permute-start | bytes 196616 | tf_op jit(solution)/shard_map/ppermute | solution.py:366
  35.7 16.6 %collective-permute-start.10 = (f32[2,2,4,8,128]{4,3,2,1,0:T(8,128)S(1)}, f32[2,2,4,8,128]{4,3,2,1,0:T(8,128)S(1)}, u32[]{:S(2)}, u32[]{:S(2)}) collective-permute-start(f32[2,2,4,8,128]{4,3,2,1,0:T(8,128)S(1)} %get-tuple-element.50), channel_id=1, source_target_pairs={{0,26},{1,27},{2,24},{3,25},{4,30},{5,31},{6,28},{7,29},{8,18},{9,... | collective-permute-start | bytes 196616 | tf_op jit(solution)/shard_map/ppermute | solution.py:366
  41.6 14.9 %collective-permute-start.11 = (f32[2,2,4,8,128]{4,3,2,1,0:T(8,128)S(1)}, f32[2,2,4,8,128]{4,3,2,1,0:T(8,128)S(1)}, u32[]{:S(2)}, u32[]{:S(2)}) collective-permute-start(f32[2,2,4,8,128]{4,3,2,1,0:T(8,128)S(1)} %get-tuple-element.51), channel_id=1, source_target_pairs={{0,27},{1,26},{2,25},{3,24},{4,31},{5,30},{6,29},{7,28},{8,19},{9,... | collective-permute-start | bytes 196616 | tf_op jit(solution)/shard_map/ppermute | solution.py:366
  43.6 14.9 %collective-permute-start.12 = (f32[2,2,4,8,128]{4,3,2,1,0:T(8,128)S(1)}, f32[2,2,4,8,128]{4,3,2,1,0:T(8,128)S(1)}, u32[]{:S(2)}, u32[]{:S(2)}) collective-permute-start(f32[2,2,4,8,128]{4,3,2,1,0:T(8,128)S(1)} %get-tuple-element.52), channel_id=1, source_target_pairs={{0,28},{1,29},{2,30},{3,31},{4,24},{5,25},{6,26},{7,27},{8,20},{9,... | collective-permute-start | bytes 196616 | tf_op jit(solution)/shard_map/ppermute | solution.py:366
  46.5 14.8 %collective-permute-start.13 = (f32[2,2,4,8,128]{4,3,2,1,0:T(8,128)S(1)}, f32[2,2,4,8,128]{4,3,2,1,0:T(8,128)S(1)}, u32[]{:S(2)}, u32[]{:S(2)}) collective-permute-start(f32[2,2,4,8,128]{4,3,2,1,0:T(8,128)S(1)} %get-tuple-element.53), channel_id=1, source_target_pairs={{0,29},{1,28},{2,31},{3,30},{4,25},{5,24},{6,27},{7,26},{8,21},{9,... | collective-permute-start | bytes 196616 | tf_op jit(solution)/shard_map/ppermute | solution.py:366
  48.6 15.0 %collective-permute-start.14 = (f32[2,2,4,8,128]{4,3,2,1,0:T(8,128)S(1)}, f32[2,2,4,8,128]{4,3,2,1,0:T(8,128)S(1)}, u32[]{:S(2)}, u32[]{:S(2)}) collective-permute-start(f32[2,2,4,8,128]{4,3,2,1,0:T(8,128)S(1)} %get-tuple-element.54), channel_id=1, source_target_pairs={{0,30},{1,31},{2,28},{3,29},{4,26},{5,27},{6,24},{7,25},{8,22},{9,... | collective-permute-start | bytes 196616 | tf_op jit(solution)/shard_map/ppermute | solution.py:366
  52.3 12.7 %collective-permute-start.15 = (f32[2,2,4,8,128]{4,3,2,1,0:T(8,128)S(1)}, f32[2,2,4,8,128]{4,3,2,1,0:T(8,128)S(1)}, u32[]{:S(2)}, u32[]{:S(2)}) collective-permute-start(f32[2,2,4,8,128]{4,3,2,1,0:T(8,128)S(1)} %get-tuple-element.55), channel_id=1, source_target_pairs={{0,31},{1,30},{2,29},{3,28},{4,27},{5,26},{6,25},{7,24},{8,23},{9,... | collective-permute-start | bytes 196616 | tf_op jit(solution)/shard_map/ppermute | solution.py:366
  84.8 112.2 %all-to-all-start.1 = ((f32[16,256,128]{2,1,0:T(8,128)}), f32[16,256,128]{2,1,0:T(8,128)S(1)}, u32[]{:S(2)}, u32[]{:S(2)}) async-start(f32[16,256,128]{2,1,0:T(8,128)} %bitcast.11), calls=%async_computation.1 | async-start | bytes 4194304 | tf_op jit(solution)/shard_map/all_to_all | solution.py:368
  89.2 30.2 %collective-permute-start.16 = (f32[2,2,8,8,128]{4,3,2,1,0:T(8,128)}, f32[2,2,8,8,128]{4,3,2,1,0:T(8,128)S(1)}, u32[]{:S(2)}, u32[]{:S(2)}) collective-permute-start(f32[2,2,8,8,128]{4,3,2,1,0:T(8,128)} %get-tuple-element.57), channel_id=1, source_target_pairs={{0,16},{1,17},{2,18},{3,19},{4,20},{5,21},{6,22},{7,23},{8,24},{9,... | collective-permute-start | bytes 393224 | tf_op jit(solution)/shard_map/ppermute | solution.py:366
  90.0 33.2 %collective-permute-start.17 = (f32[2,2,8,8,128]{4,3,2,1,0:T(8,128)}, f32[2,2,8,8,128]{4,3,2,1,0:T(8,128)S(1)}, u32[]{:S(2)}, u32[]{:S(2)}) collective-permute-start(f32[2,2,8,8,128]{4,3,2,1,0:T(8,128)} %get-tuple-element.58), channel_id=1, source_target_pairs={{0,17},{1,16},{2,19},{3,18},{4,21},{5,20},{6,23},{7,22},{8,25},{9,... | collective-permute-start | bytes 393224 | tf_op jit(solution)/shard_map/ppermute | solution.py:366
  92.2 32.5 %collective-permute-start.18 = (f32[2,2,8,8,128]{4,3,2,1,0:T(8,128)}, f32[2,2,8,8,128]{4,3,2,1,0:T(8,128)S(1)}, u32[]{:S(2)}, u32[]{:S(2)}) collective-permute-start(f32[2,2,8,8,128]{4,3,2,1,0:T(8,128)} %copy-done.48), channel_id=1, source_target_pairs={{0,18},{1,19},{2,16},{3,17},{4,22},{5,23},{6,20},{7,21},{8,26},{9,... | collective-permute-start | bytes 393224 | tf_op jit(solution)/shard_map/ppermute | solution.py:366
  93.8 34.6 %collective-permute-start.19 = (f32[2,2,8,8,128]{4,3,2,1,0:T(8,128)}, f32[2,2,8,8,128]{4,3,2,1,0:T(8,128)S(1)}, u32[]{:S(2)}, u32[]{:S(2)}) collective-permute-start(f32[2,2,8,8,128]{4,3,2,1,0:T(8,128)} %copy-done.47), channel_id=1, source_target_pairs={{0,19},{1,18},{2,17},{3,16},{4,23},{5,22},{6,21},{7,20},{8,27},{9,... | collective-permute-start | bytes 393224 | tf_op jit(solution)/shard_map/ppermute | solution.py:366
  95.5 34.5 %collective-permute-start.20 = (f32[2,2,8,8,128]{4,3,2,1,0:T(8,128)}, f32[2,2,8,8,128]{4,3,2,1,0:T(8,128)S(1)}, u32[]{:S(2)}, u32[]{:S(2)}) collective-permute-start(f32[2,2,8,8,128]{4,3,2,1,0:T(8,128)} %copy-done.46), channel_id=1, source_target_pairs={{0,20},{1,21},{2,22},{3,23},{4,16},{5,17},{6,18},{7,19},{8,28},{9,... | collective-permute-start | bytes 393224 | tf_op jit(solution)/shard_map/ppermute | solution.py:366
  119.4 27.2 %collective-permute-start.21 = (f32[2,2,8,8,128]{4,3,2,1,0:T(8,128)}, f32[2,2,8,8,128]{4,3,2,1,0:T(8,128)S(1)}, u32[]{:S(2)}, u32[]{:S(2)}) collective-permute-start(f32[2,2,8,8,128]{4,3,2,1,0:T(8,128)} %copy-done.45), channel_id=1, source_target_pairs={{0,21},{1,20},{2,23},{3,22},{4,17},{5,16},{6,19},{7,18},{8,29},{9,... | collective-permute-start | bytes 393224 | tf_op jit(solution)/shard_map/ppermute | solution.py:366
  123.2 26.3 %collective-permute-start.22 = (f32[2,2,8,8,128]{4,3,2,1,0:T(8,128)}, f32[2,2,8,8,128]{4,3,2,1,0:T(8,128)S(1)}, u32[]{:S(2)}, u32[]{:S(2)}) collective-permute-start(f32[2,2,8,8,128]{4,3,2,1,0:T(8,128)} %copy-done.44), channel_id=1, source_target_pairs={{0,22},{1,23},{2,20},{3,21},{4,18},{5,19},{6,16},{7,17},{8,30},{9,... | collective-permute-start | bytes 393224 | tf_op jit(solution)/shard_map/ppermute | solution.py:366
  124.6 27.6 %collective-permute-start.23 = (f32[2,2,8,8,128]{4,3,2,1,0:T(8,128)}, f32[2,2,8,8,128]{4,3,2,1,0:T(8,128)S(1)}, u32[]{:S(2)}, u32[]{:S(2)}) collective-permute-start(f32[2,2,8,8,128]{4,3,2,1,0:T(8,128)} %copy-done.43), channel_id=1, source_target_pairs={{0,23},{1,22},{2,21},{3,20},{4,19},{5,18},{6,17},{7,16},{8,31},{9,... | collective-permute-start | bytes 393224 | tf_op jit(solution)/shard_map/ppermute | solution.py:366
  129.1 27.3 %collective-permute-start.24 = (f32[2,2,8,8,128]{4,3,2,1,0:T(8,128)}, f32[2,2,8,8,128]{4,3,2,1,0:T(8,128)S(1)}, u32[]{:S(2)}, u32[]{:S(2)}) collective-permute-start(f32[2,2,8,8,128]{4,3,2,1,0:T(8,128)} %copy-done.42), channel_id=1, source_target_pairs={{0,24},{1,25},{2,26},{3,27},{4,28},{5,29},{6,30},{7,31},{8,16},{9,... | collective-permute-start | bytes 393224 | tf_op jit(solution)/shard_map/ppermute | solution.py:366
  130.6 40.0 %collective-permute-start.25 = (f32[2,2,8,8,128]{4,3,2,1,0:T(8,128)}, f32[2,2,8,8,128]{4,3,2,1,0:T(8,128)S(1)}, u32[]{:S(2)}, u32[]{:S(2)}) collective-permute-start(f32[2,2,8,8,128]{4,3,2,1,0:T(8,128)} %copy-done.41), channel_id=1, source_target_pairs={{0,25},{1,24},{2,27},{3,26},{4,29},{5,28},{6,31},{7,30},{8,17},{9,... | collective-permute-start | bytes 393224 | tf_op jit(solution)/shard_map/ppermute | solution.py:366
  147.3 31.4 %collective-permute-start.26 = (f32[2,2,8,8,128]{4,3,2,1,0:T(8,128)}, f32[2,2,8,8,128]{4,3,2,1,0:T(8,128)S(1)}, u32[]{:S(2)}, u32[]{:S(2)}) collective-permute-start(f32[2,2,8,8,128]{4,3,2,1,0:T(8,128)} %copy-done.40), channel_id=1, source_target_pairs={{0,26},{1,27},{2,24},{3,25},{4,30},{5,31},{6,28},{7,29},{8,18},{9,... | collective-permute-start | bytes 393224 | tf_op jit(solution)/shard_map/ppermute | solution.py:366
  150.1 32.3 %collective-permute-start.27 = (f32[2,2,8,8,128]{4,3,2,1,0:T(8,128)}, f32[2,2,8,8,128]{4,3,2,1,0:T(8,128)S(1)}, u32[]{:S(2)}, u32[]{:S(2)}) collective-permute-start(f32[2,2,8,8,128]{4,3,2,1,0:T(8,128)} %copy-done.39), channel_id=1, source_target_pairs={{0,27},{1,26},{2,25},{3,24},{4,31},{5,30},{6,29},{7,28},{8,19},{9,... | collective-permute-start | bytes 393224 | tf_op jit(solution)/shard_map/ppermute | solution.py:366
  152.9 32.2 %collective-permute-start.28 = (f32[2,2,8,8,128]{4,3,2,1,0:T(8,128)}, f32[2,2,8,8,128]{4,3,2,1,0:T(8,128)S(1)}, u32[]{:S(2)}, u32[]{:S(2)}) collective-permute-start(f32[2,2,8,8,128]{4,3,2,1,0:T(8,128)} %copy-done.38), channel_id=1, source_target_pairs={{0,28},{1,29},{2,30},{3,31},{4,24},{5,25},{6,26},{7,27},{8,20},{9,... | collective-permute-start | bytes 393224 | tf_op jit(solution)/shard_map/ppermute | solution.py:366
  157.0 30.9 %collective-permute-start.29 = (f32[2,2,8,8,128]{4,3,2,1,0:T(8,128)}, f32[2,2,8,8,128]{4,3,2,1,0:T(8,128)S(1)}, u32[]{:S(2)}, u32[]{:S(2)}) collective-permute-start(f32[2,2,8,8,128]{4,3,2,1,0:T(8,128)} %copy-done.37), channel_id=1, source_target_pairs={{0,29},{1,28},{2,31},{3,30},{4,25},{5,24},{6,27},{7,26},{8,21},{9,... | collective-permute-start | bytes 393224 | tf_op jit(solution)/shard_map/ppermute | solution.py:366
  171.2 22.3 %collective-permute-start.30 = (f32[2,2,8,8,128]{4,3,2,1,0:T(8,128)}, f32[2,2,8,8,128]{4,3,2,1,0:T(8,128)S(1)}, u32[]{:S(2)}, u32[]{:S(2)}) collective-permute-start(f32[2,2,8,8,128]{4,3,2,1,0:T(8,128)} %copy-done.36), channel_id=1, source_target_pairs={{0,30},{1,31},{2,28},{3,29},{4,26},{5,27},{6,24},{7,25},{8,22},{9,... | collective-permute-start | bytes 393224 | tf_op jit(solution)/shard_map/ppermute | solution.py:366
  179.3 17.0 %collective-permute-start.31 = (f32[2,2,8,8,128]{4,3,2,1,0:T(8,128)}, f32[2,2,8,8,128]{4,3,2,1,0:T(8,128)S(1)}, u32[]{:S(2)}, u32[]{:S(2)}) collective-permute-start(f32[2,2,8,8,128]{4,3,2,1,0:T(8,128)} %copy-done.35), channel_id=1, source_target_pairs={{0,31},{1,30},{2,29},{3,28},{4,27},{5,26},{6,25},{7,24},{8,23},{9,... | collective-permute-start | bytes 393224 | tf_op jit(solution)/shard_map/ppermute | solution.py:366
  (52 other events, 503.6 us)

commit v2 on v0

--- a/solution.py
+++ b/solution.py
@@ -104,18 +104,35 @@
     return out
 
 
-def relative_rows(matrix_ref, me):
-    parts, devices = matrix_ref.shape[:2]
-    rows = [matrix_ref[part, slot ^ me] for part in range(parts) for slot in range(devices)]
-    return jnp.concatenate(rows, axis=0)
-
-
-def times_kernel(order, me_ref, g_ref, m_ref, *outs):
-    _, entries, lanes, _ = g_ref.shape
-    _, devices, rows, _ = m_ref.shape
-    half = devices * rows
-    matrix = split_value(relative_rows(m_ref, me_ref[0]))
+def half_line(values, sign, parity):
+    side = len(values)
+    inner = side // 4
+    parts = [dft_line(values[b::4], sign) for b in range(4)]
+    out = [None] * (side // 2)
+    for k1 in range(inner):
+        column = [twiddle(parts[b][k1], b * k1, sign, side) for b in range(4)]
+        column = [(re * parity, im * parity) if b % 2 else (re, im) for b, (re, im) in enumerate(column)]
+        for k2, value in enumerate(dft4(column, sign)[:2]):
+            out[k1 + inner * k2] = value
+    return out
+
+
+def times_kernel(g_hbm, m_hbm, out_ref, g_ref, m_ref, stage, in_sems, m_sem, out_sems):
+    entries, lanes = g_ref.shape[1:3]
+    near, _, _, _, rows, _ = stage.shape
+    half = near * rows
+    load = pltpu.make_async_copy(m_hbm, m_ref, m_sem)
+    pieces = [
+        pltpu.make_async_copy(g_hbm.at[:, pl.ds(e, 1)], g_ref.at[:, pl.ds(e, 1)], in_sems.at[e])
+        for e in range(entries)
+    ]
+    for copy in [load] + pieces:
+        copy.start()
+    load.wait()
+    matrix = split_value(m_ref[...])
+    copies = []
     for e in range(entries):
+        pieces[e].wait()
         g = jnp.concatenate([g_ref[0, e], g_ref[1, e]], axis=0)
         d = dot3(matrix, split_value(g), ((1,), (1,)))
         c_re, c_im = d[:half, :lanes], d[:half, lanes:]
@@ -126,29 +143,36 @@
             ((1, 0), s_im - c_re),
             ((1, 1), -(c_im + s_re)),
         ):
-            for out_ref, slot in zip(outs, order):
-                out_ref[where[0], where[1], e] = value[slot * rows : (slot + 1) * rows]
-
-
-def call_kernel(kernel, order, me, args, arg_specs, shape, scratch, limit, name):
-    pieces = pl.pallas_call(
-        kernel,
-        in_specs=[pl.BlockSpec(memory_space=pltpu.SMEM)] + arg_specs,
-        out_specs=[pl.BlockSpec(memory_space=pltpu.VMEM)] * len(order),
-        out_shape=[jax.ShapeDtypeStruct(shape, jnp.float32)] * len(order),
-        scratch_shapes=scratch,
-        compiler_params=pltpu.CompilerParams(vmem_limit_bytes=limit << 20),
-        name=name,
-    )(me, *args)
-    return dict(zip(order, pieces))
-
-
-def to_times(green, matrix, me, order):
+            stage[:, where[0], where[1], e] = value.reshape(near, rows, lanes)
+        cut = pl.ds(e, 1)
+        for side in range(2):
+            target = out_ref.at[pl.ds(side * near, near), :, :, cut]
+            copies.append(pltpu.make_async_copy(stage.at[:, :, :, cut], target, out_sems.at[e, side]))
+            copies[-1].start()
+    for copy in copies:
+        copy.wait()
+
+
+def to_times(green, matrix, near):
     _, entries, lanes, _ = green.shape
-    shape = (2, 2, entries, matrix.shape[2], lanes)
-    vmem = pl.BlockSpec(memory_space=pltpu.VMEM)
-    kernel = functools.partial(times_kernel, order)
-    return call_kernel(kernel, order, me, (green, matrix), [vmem] * 2, shape, [], 40, "to_times")
+    shape = (near, 2, 2, entries, ROWS, lanes)
+    hbm = pl.BlockSpec(memory_space=pltpu.HBM)
+    return pl.pallas_call(
+        times_kernel,
+        in_specs=[hbm, hbm],
+        out_specs=hbm,
+        out_shape=jax.ShapeDtypeStruct((2 * near,) + shape[1:], jnp.float32),
+        scratch_shapes=[
+            pltpu.VMEM(green.shape, jnp.float32),
+            pltpu.VMEM(matrix.shape, jnp.float32),
+            pltpu.VMEM(shape, jnp.float32),
+            pltpu.SemaphoreType.DMA((entries,)),
+            pltpu.SemaphoreType.DMA,
+            pltpu.SemaphoreType.DMA((entries, 2)),
+        ],
+        compiler_params=pltpu.CompilerParams(vmem_limit_bytes=60 << 20),
+        name="to_times",
+    )(green, matrix)
 
 
 def fill_block(ref, cosine, sine):
@@ -164,47 +188,38 @@
         ref[plane:, re] = (-sine[:, cut]).astype(jnp.bfloat16)
 
 
-def middle_kernel(order, me_ref, table_ref, mirror_ref, index_ref, ch_ref, cl_ref, sh_ref, sl_ref, *refs):
-    count = len(order)
-    pieces = dict(zip(order, refs[:count]))
-    outs = dict(zip(order, refs[count : 2 * count]))
-    forward, backward, mid, space, chi = refs[2 * count :]
+def middle_kernel(me_ref, table_ref, mirror_ref, index_ref, ch_ref, cl_ref, sh_ref, sl_ref, x_ref, *refs):
+    outs, (forward, backward, mid, space, chi) = refs[:-5], refs[-5:]
     halves, _, side, _, entries, rows, lanes = space.shape
     plane = 2 * lanes
-    units, _, _, members, _, _ = chi.shape
-    line, core = me_ref[0] // 2, me_ref[0] % 2
+    units, _, kept, members, _, _ = chi.shape
+    me, near = me_ref[0], len(outs)
+    core, line = me % 2, me // 2 % kept
+    parity = (1 - 2 * (me // near)).astype(jnp.float32)
     row = lax.broadcasted_iota(jnp.int32, (plane, plane), 0)
     pick = (row == index_ref[...]).astype(jnp.float32).astype(jnp.bfloat16)
 
     def dot(a, b):
         return jnp.dot(a, b, preferred_element_type=jnp.float32)
 
-    def turned(value, axis):
-        first = lax.slice_in_dim(value, 0, lanes, axis=axis)
-        second = lax.slice_in_dim(value, lanes, plane, axis=axis)
-        return jnp.where(core == 0, value, jnp.concatenate([second, first], axis=axis))
+    def turned(value):
+        return jnp.where(core == 0, value, jnp.concatenate([value[:, lanes:], value[:, :lanes]], axis=1))
 
     for part, (c_ref, s_ref) in enumerate(((ch_ref, sh_ref), (cl_ref, sl_ref))):
         cosine, sine = c_ref[...].astype(jnp.float32), s_ref[...].astype(jnp.float32)
-        fill_block(forward.at[0, part], turned(cosine, 0), turned(sine, 0))
-        fill_block(backward.at[0, part], turned(cosine, 1), turned(-sine, 1))
-        fill_block(
-            forward.at[1, part], turned(dot(c_ref[...], pick), 0), turned(dot(s_ref[...], pick), 0)
-        )
-        fill_block(
-            backward.at[1, part], turned(dot(pick, c_ref[...]), 1), turned(-dot(pick, s_ref[...]), 1)
-        )
+        fill_block(forward.at[0, part], cosine, sine)
+        fill_block(backward.at[0, part], turned(cosine), turned(-sine))
+        fill_block(forward.at[1, part], dot(c_ref[...], pick), dot(s_ref[...], pick))
+        fill_block(backward.at[1, part], turned(dot(pick, c_ref[...])), turned(-dot(pick, s_ref[...])))
 
     def plane_dot(value, matrix, half, block):
         cut = slice(2 * block * lanes, 2 * (block + 1) * lanes)
         return dot3(value, (matrix[half, 0, :, cut], matrix[half, 1, :, cut]), ((1,), (0,)))
 
     def arrive(half):
-        columns = []
-        for ri in range(2):
-            for h in range(2):
-                rows_of = [pieces[2 * x + h][half, ri].reshape(entries * rows, lanes) for x in range(side)]
-                columns.append(jnp.concatenate(rows_of, axis=0))
+        columns = [
+            x_ref[:, h, half, ri].reshape(side * entries * rows, lanes) for ri in range(2) for h in range(2)
+        ]
         return split_value(jnp.concatenate(columns, axis=1))
 
     def to_plane(value, half, block):
@@ -214,7 +229,7 @@
             mid[half, block, ri] = piece.reshape(side, entries, rows, lanes)
 
     def along_line(half, block, e):
-        values = [(mid[half, block, 0, x ^ line, e], mid[half, block, 1, x ^ line, e]) for x in range(side)]
+        values = [(mid[half, block, 0, x, e], mid[half, block, 1, x, e]) for x in range(side)]
         for x, (re, im) in enumerate(dft_line(values, 1)):
             space[half, block, x, 0, e] = re
             space[half, block, x, 1, e] = im
@@ -229,7 +244,7 @@
             b_re, b_im = space[1 - half, block, other, 0, right], space[1 - half, block, other, 1, right]
             values.append((a_re * b_re - a_im * b_im, a_re * b_im + a_im * b_re))
         cut = slice(block * lanes, (block + 1) * lanes)
-        for x, (re, im) in enumerate(dft_line(values, -1)):
+        for x, (re, im) in enumerate(half_line(values, -1, parity)):
             chi[unit, 0, x ^ line, c, :, cut] = re
             chi[unit, 1, x ^ line, c, :, cut] = im
 
@@ -237,12 +252,12 @@
         half, first = unit % halves, unit // halves * members
         d = plane_dot(value, backward, half, h)
         for ri in range(2):
-            piece = d[:, ri * lanes : (ri + 1) * lanes].reshape(side, members, rows, lanes)
-            for x in range(side):
+            piece = d[:, ri * lanes : (ri + 1) * lanes].reshape(kept, members, rows, lanes)
+            for x in range(kept):
                 outs[2 * x + h][half, ri, first : first + members] = piece[x]
 
     def collect(unit):
-        whole = (side * members * rows, plane)
+        whole = (kept * members * rows, plane)
         return split_value(jnp.concatenate([chi[unit, ri].reshape(whole) for ri in range(2)], axis=1))
 
     places = [(half, block) for half in range(halves) for block in range(2)]
@@ -267,10 +282,10 @@
                 product(unit, block, c)
 
 
-def middle(pieces, table, mirror_map, me, order):
-    halves, _, entries, rows, lanes = pieces[0].shape
+def middle(x, table, mirror_map, me, near):
+    devices, halves, _, entries, rows, lanes = x.shape
     plane = 2 * lanes
-    side = len(order) // 2
+    side = devices // 2
     components = table.shape[0]
     members = components // GROUPS
     units = halves * GROUPS
@@ -280,35 +295,43 @@
     smem = pl.BlockSpec(memory_space=pltpu.SMEM)
     vmem = pl.BlockSpec(memory_space=pltpu.VMEM)
     matrices = pltpu.VMEM((halves, 2, 2 * plane, 2 * plane), jnp.bfloat16)
-    scratch = [
-        matrices,
-        matrices,
-        pltpu.VMEM((halves, 2, 2, side, entries, rows, lanes), jnp.float32),
-        pltpu.VMEM((halves, 2, side, 2, entries, rows, lanes), jnp.float32),
-        pltpu.VMEM((units, 2, side, members, rows, plane), jnp.float32),
-    ]
-    args = (table, mirror_map, index, *parts) + tuple(pieces[slot] for slot in order)
-    specs = [smem, smem, vmem] + [vmem] * (4 + len(order))
-    shape = (halves, 2, components, rows, lanes)
-    kernel = functools.partial(middle_kernel, order)
-    return call_kernel(kernel, order, me, args, specs, shape, scratch, 40, "middle")
-
-
-def frequency_kernel(order, me_ref, m_ref, *refs):
-    pieces = dict(zip(order, refs[: len(order)]))
-    out_ref, stage, sems = refs[len(order) :]
+    return pl.pallas_call(
+        middle_kernel,
+        in_specs=[smem, smem, smem] + [vmem] * 6,
+        out_specs=[vmem] * near,
+        out_shape=[jax.ShapeDtypeStruct((halves, 2, components, rows, lanes), jnp.float32)] * near,
+        scratch_shapes=[
+            matrices,
+            matrices,
+            pltpu.VMEM((halves, 2, 2, side, entries, rows, lanes), jnp.float32),
+            pltpu.VMEM((halves, 2, side, 2, entries, rows, lanes), jnp.float32),
+            pltpu.VMEM((units, 2, near // 2, members, rows, plane), jnp.float32),
+        ],
+        compiler_params=pltpu.CompilerParams(vmem_limit_bytes=28 << 20),
+        name="middle",
+    )(me, table, mirror_map, index, *parts, x.reshape((side, 2) + x.shape[1:]))
+
+
+def frequency_kernel(near, me_ref, m_ref, *refs):
+    pieces, (out_ref, stage, sems) = refs[:-3], refs[-3:]
     components, lanes = stage.shape[1:3]
     groups = sems.shape[0]
     members = components // groups
-    matrix = split_value(relative_rows(m_ref, me_ref[0]))
+    sets = len(pieces) // near
+    me = me_ref[0] % near
+    rows = [
+        m_ref[part, some * near + (slot ^ me)] for part in range(2) for some in range(sets) for slot in range(near)
+    ]
+    matrix = split_value(jnp.concatenate(rows, axis=0))
+
+    def gathered(half, ri, c):
+        return jnp.concatenate([piece[half, ri, c] for piece in pieces], axis=0)
+
     copies = []
     for group in range(groups):
         values = []
         for c in range(group * members, (group + 1) * members):
-            part = [
-                [jnp.concatenate([pieces[slot][half, ri, c] for slot in range(len(order))], axis=0) for ri in range(2)]
-                for half in range(2)
-            ]
+            part = [[gathered(half, ri, c) for ri in range(2)] for half in range(2)]
             sums = [part[0][ri] + part[1][ri] for ri in range(2)]
             differences = [part[0][ri] - part[1][ri] for ri in range(2)]
             values.append(jnp.concatenate([sums[0], -differences[1]], axis=0).T)
@@ -324,32 +347,32 @@
         copy.wait()
 
 
-def to_frequencies(pieces, matrix, me, order):
-    _, _, components, rows, lanes = pieces[0].shape
+def to_frequencies(pieces, matrix, me, near):
+    components, rows, lanes = pieces[0].shape[2:]
     shape = (2, components, lanes, matrix.shape[3])
     vmem = pl.BlockSpec(memory_space=pltpu.VMEM)
     return pl.pallas_call(
-        functools.partial(frequency_kernel, order),
-        in_specs=[pl.BlockSpec(memory_space=pltpu.SMEM)] + [vmem] * (1 + len(order)),
+        functools.partial(frequency_kernel, near),
+        in_specs=[pl.BlockSpec(memory_space=pltpu.SMEM)] + [vmem] * (1 + len(pieces)),
         out_specs=pl.BlockSpec(memory_space=pltpu.HBM),
         out_shape=jax.ShapeDtypeStruct(shape, jnp.float32),
         scratch_shapes=[pltpu.VMEM(shape, jnp.float32), pltpu.SemaphoreType.DMA((components // 2,))],
-        compiler_params=pltpu.CompilerParams(vmem_limit_bytes=40 << 20),
+        compiler_params=pltpu.CompilerParams(vmem_limit_bytes=28 << 20),
         name="to_frequencies",
-    )(me, matrix, *[pieces[slot] for slot in order])
-
-
-def swap(pieces, order):
-    moved = {}
-    for slot in order:
-        pairs = [(device, device ^ slot) for device in range(len(order))]
-        moved[slot] = lax.ppermute(pieces[slot], "kb", pairs) if slot else pieces[slot]
+    )(me, matrix, *pieces)
+
+
+def exchange(x):
+    flat = x.reshape(x.shape[0], -1, x.shape[-1])
+    return lax.all_to_all(flat, "kb", split_axis=0, concat_axis=0, tiled=True).reshape(x.shape)
+
+
+def swap(pieces, devices):
+    moved = [pieces[0]]
+    for slot in range(1, len(pieces)):
+        pairs = [(device, device ^ slot) for device in range(devices)]
+        moved.append(lax.ppermute(pieces[slot], "kb", pairs))
     return moved
-
-
-def slot_order(devices):
-    half = devices // 2
-    return [slot for near in range(half) for slot in (near + half, near)]
 
 
 def trig_pair(angle_int, period, scale):
@@ -472,18 +495,25 @@
     plane = side * side
     lanes, count = green.shape[2], green.shape[3]
     devices = side * plane // lanes
-    pairs = count // (2 * devices)
-    if lanes != LANES or pairs != ROWS or 2 * lanes != plane:
+    near = devices // 2
+    sets = count // (2 * near * ROWS)
+    if lanes != LANES or 2 * lanes != plane or sets * 2 * near * ROWS != count:
         return general(green, pair_table, mirror_map)
-    rows = np.arange(devices * pairs)
-    shape = (2, devices, pairs, count)
-    forward = jnp.asarray(fermion_matrix(rows, count).reshape(shape).astype(np.float32))
-    backward = jnp.asarray(boson_matrix(rows, count).reshape(shape).astype(np.float32))
-    order = slot_order(devices)
+    rows = np.arange(count // 2)
+    fermion = fermion_matrix(rows, count).reshape(2, sets, near * ROWS, count).swapaxes(0, 1)
+    fermion = fermion.reshape(sets, 2 * near * ROWS, count).astype(np.float32)
+    boson = boson_matrix(rows, count).reshape(2, sets * near, ROWS, count).astype(np.float32)
     me = lax.axis_index("kb").astype(jnp.int32).reshape(1)
-    pieces = swap(to_times(green, forward, me, order), order)
-    pieces = swap(middle(pieces, pair_table, mirror_map, me, order), order)
-    return to_frequencies(pieces, backward, me, order)
+    sent = []
+    for some in range(sets):
+        if sent:
+            green, sent[-1] = lax.optimization_barrier((green, sent[-1]))
+        sent.append(to_times(green, jnp.asarray(fermion[some]), near))
+    returned = []
+    for some in range(sets):
+        x, returned, sent[some + 1 :] = lax.optimization_barrier((exchange(sent[some]), returned, sent[some + 1 :]))
+        returned = returned + swap(middle(x, pair_table, mirror_map, me, near), devices)
+    return to_frequencies(returned, jnp.asarray(boson), me, near)
 
 
 def solution(mesh):

time: 181 us -> 180 us (level)
  starting transfers between devices: 98.5 us -> 42.8 us
  waiting for transfers between devices: 57.9 us -> 93.2 us
  Pallas kernels: 14.9 us -> 27.5 us
  local copies, waits for them, and re-layouts: 7.95 us -> 15.4 us
    ppermute x62 -> x30, starting transfers between devices: 98.5 us -> 31.3 us  [swap(): moved.append(lax.ppermute(pieces[slot], 'kb', pairs))]
    all_to_all x0 -> x2, waiting for transfers between devices: none -> 43.9 us  [exchange(): lax.all_to_all(flat, 'kb', split_axis=0, concat_axis=0, tiled=True)]
    pallas_call x3 -> x5, Pallas kernels: 14.9 us -> 27.5 us  [the longest x2 12.8 us: middle(): pl.pallas_call(middle_kernel, in_specs=[smem, smem, smem] + [vmem] * 6, o...]
    all_to_all x0 -> x2, starting transfers between devices: none -> 11.5 us  [exchange(): lax.all_to_all(flat, 'kb', split_axis=0, concat_axis=0, tiled=True)]
    ppermute x62 -> x30, waiting for transfers between devices: 57.9 us -> 49.3 us  [swap(): moved.append(lax.ppermute(pieces[slot], 'kb', pairs))]
    unnamed x17 -> x85, local copies, waits for them, and re-layouts: 7.87 us -> 15.4 us
  transfers between devices with their start and end apart: 62 -> 32, of which waited for: 17 -> 20; matrix products, arithmetic and copies ran while one was open for 1% -> 0% of each run, Pallas kernels for 0% -> 6%
where the time goes in v2:
time: 180 us
  waiting for transfers between devices  93.2 us (52%)
  starting transfers between devices  42.8 us (24%)
  Pallas kernels  27.5 us (15%)
  local copies, waits for them, and re-layouts  15.4 us (9%)
    ppermute x30, waiting for transfers between devices, swap(): moved.append(lax.ppermute(pieces[slot], 'kb', pairs))  49.3 us
    all_to_all x2, waiting for transfers between devices, exchange(): lax.all_to_all(flat, 'kb', split_axis=0, concat_axis=0, tiled=True)  43.9 us
    ppermute x30, starting transfers between devices, swap(): moved.append(lax.ppermute(pieces[slot], 'kb', pairs))  31.3 us
    unnamed x85, local copies, waits for them, and re-layouts  15.4 us
    pallas_call x2, Pallas kernels, middle(): pl.pallas_call(middle_kernel, in_specs=[smem, smem, smem] + [vmem] * 6, o...  12.8 us
    all_to_all x2, starting transfers between devices, exchange(): lax.all_to_all(flat, 'kb', split_axis=0, concat_axis=0, tiled=True)  11.5 us
    pallas_call x2, Pallas kernels, to_times(): pl.pallas_call(times_kernel, in_specs=[hbm, hbm], out_specs=hbm, out_shap...  9.9 us
    pallas_call x1, Pallas kernels, to_frequencies(): pl.pallas_call(functools.partial(frequency_kernel, near), in_specs=[pl.Bl...  4.81 us
  transfers between devices with their start and end apart: 32, of which 20 were waited for; matrix products, arithmetic and copies ran while one was open for 0% of the time, Pallas kernels for 6%

profile of v2, /device:TPU:0, one launch (start us, length us, event | category | flops | bytes accessed | tf_op | source)
XLA Modules:
  0.0 179.6 jit_solution(17562343077266437699)
XLA Ops:
  0.0 4.9 %to_times.2 = f32[32,2,2,4,8,128]{5,4,3,2,1,0:T(8,128)} custom-call(f32[2,4,128,512]{3,2,1,0:T(8,128)} %g_hbm.2, f32[256,512]{1,0:T(8,128)} %constant.20.clone.m_hbm), custom_call_target="tpu_custom_call" | custom-call | tf_op jit(solution)/shard_map/to_times/pallas_call | solution.py:160
  4.9 7.3 %all-to-all-start = ((f32[32,128,128]{2,1,0:T(8,128)}), f32[32,128,128]{2,1,0:T(8,128)S(1)}, u32[]{:S(2)}, u32[]{:S(2)}) async-start(f32[32,128,128]{2,1,0:T(8,128)} %bitcast.14), calls=%async_computation | async-start | bytes 4194304 | tf_op jit(solution)/shard_map/all_to_all | solution.py:367
  12.2 5.0 %to_times.3 = f32[32,2,2,4,8,128]{5,4,3,2,1,0:T(8,128)} custom-call(f32[2,4,128,512]{3,2,1,0:T(8,128)} %g_hbm.2, f32[256,512]{1,0:T(8,128)} %constant.21.clone.m_hbm), custom_call_target="tpu_custom_call" | custom-call | tf_op jit(solution)/shard_map/to_times/pallas_call | solution.py:160
  17.2 43.9 %all-to-all-done = f32[32,128,128]{2,1,0:T(8,128)S(1)} async-done(((f32[32,128,128]{2,1,0:T(8,128)}), f32[32,128,128]{2,1,0:T(8,128)S(1)}, u32[]{:S(2)}, u32[]{:S(2)}) %all-to-all-start) | async-done | bytes 2097184 | tf_op jit(solution)/shard_map/all_to_all | solution.py:367
  62.5 4.2 %all-to-all-start.1 = ((f32[32,128,128]{2,1,0:T(8,128)}), f32[32,128,128]{2,1,0:T(8,128)S(1)}, u32[]{:S(2)}, u32[]{:S(2)}) async-start(f32[32,128,128]{2,1,0:T(8,128)} %bitcast.13), calls=%async_computation.1 | async-start | bytes 4194304 | tf_op jit(solution)/shard_map/all_to_all | solution.py:367
  69.4 6.4 %middle.2 = (f32[2,2,8,8,128]{4,3,2,1,0:T(8,128)S(1)}, f32[2,2,8,8,128]{4,3,2,1,0:T(8,128)S(1)}, f32[2,2,8,8,128]{4,3,2,1,0:T(8,128)S(1)}, f32[2,2,8,8,128]{4,3,...) custom-call(s32[1]{0:T(128)} %bitcast.me_ref, ...), custom_call_target="tpu_custom_call" | custom-call | tf_op jit(solution)/shard_map/middle/pallas_call | solution.py:298
  76.7 1.7 collective-permute-start.1
  78.4 1.7 collective-permute-start.3
  80.9 2.6 %collective-permute-start.5 = (f32[2,2,8,8,128]{4,3,2,1,0:T(8,128)S(1)}, f32[2,2,8,8,128]{4,3,2,1,0:T(8,128)S(1)}, u32[]{:S(2)}, u32[]{:S(2)}) collective-permute-start(f32[2,2,8,8,128]{4,3,2,1,0:T(8,128)S(1)} %get-tuple-element.68), channel_id=1, source_target_pairs={{0,6},{1,7},{2,4},{3,5},{4,2},{5,3},{6,0},{7,1},{8,14},{9,15},{10,... | collective-permute-start | bytes 393224 | tf_op jit(solution)/shard_map/ppermute | solution.py:374
  83.5 2.3 %collective-permute-done.1.refs_2_ = f32[2,2,8,8,128]{4,3,2,1,0:T(8,128)S(1)} collective-permute-done((f32[2,2,8,8,128]{4,3,2,1,0:T(8,128)S(1)}, f32[2,2,8,8,128]{4,3,2,1,0:T(8,128)S(1)}, u32[]{:S(2)}, u32[]{:S(2)}) %collective-permute-start.1) | collective-permute-done | bytes 131104 | tf_op jit(solution)/shard_map/ppermute | solution.py:374
  86.8 2.5 %collective-permute-done.2.refs_3_ = f32[2,2,8,8,128]{4,3,2,1,0:T(8,128)S(1)} collective-permute-done((f32[2,2,8,8,128]{4,3,2,1,0:T(8,128)S(1)}, f32[2,2,8,8,128]{4,3,2,1,0:T(8,128)S(1)}, u32[]{:S(2)}, u32[]{:S(2)}) %collective-permute-start.2) | collective-permute-done | bytes 131104 | tf_op jit(solution)/shard_map/ppermute | solution.py:374
  90.6 5.2 %collective-permute-start.8 = (f32[2,2,8,8,128]{4,3,2,1,0:T(8,128)S(1)}, f32[2,2,8,8,128]{4,3,2,1,0:T(8,128)S(1)}, u32[]{:S(2)}, u32[]{:S(2)}) collective-permute-start(f32[2,2,8,8,128]{4,3,2,1,0:T(8,128)S(1)} %get-tuple-element.71), channel_id=1, source_target_pairs={{0,9},{1,8},{2,11},{3,10},{4,13},{5,12},{6,15},{7,14},{8,1},{9,0},... | collective-permute-start | bytes 393224 | tf_op jit(solution)/shard_map/ppermute | solution.py:374
  95.9 5.7 %collective-permute-done.4.refs_5_ = f32[2,2,8,8,128]{4,3,2,1,0:T(8,128)S(1)} collective-permute-done((f32[2,2,8,8,128]{4,3,2,1,0:T(8,128)S(1)}, f32[2,2,8,8,128]{4,3,2,1,0:T(8,128)S(1)}, u32[]{:S(2)}, u32[]{:S(2)}) %collective-permute-start.4) | collective-permute-done | bytes 131104 | tf_op jit(solution)/shard_map/ppermute | solution.py:374
  102.9 2.6 %collective-permute-start.10 = (f32[2,2,8,8,128]{4,3,2,1,0:T(8,128)S(1)}, f32[2,2,8,8,128]{4,3,2,1,0:T(8,128)S(1)}, u32[]{:S(2)}, u32[]{:S(2)}) collective-permute-start(f32[2,2,8,8,128]{4,3,2,1,0:T(8,128)S(1)} %get-tuple-element.73), channel_id=1, source_target_pairs={{0,11},{1,10},{2,9},{3,8},{4,15},{5,14},{6,13},{7,12},{8,3},{9,2},... | collective-permute-start | bytes 393224 | tf_op jit(solution)/shard_map/ppermute | solution.py:374
  106.8 2.7 %collective-permute-start.12 = (f32[2,2,8,8,128]{4,3,2,1,0:T(8,128)S(1)}, f32[2,2,8,8,128]{4,3,2,1,0:T(8,128)S(1)}, u32[]{:S(2)}, u32[]{:S(2)}) collective-permute-start(f32[2,2,8,8,128]{4,3,2,1,0:T(8,128)S(1)} %get-tuple-element.75), channel_id=1, source_target_pairs={{0,13},{1,12},{2,15},{3,14},{4,9},{5,8},{6,11},{7,10},{8,5},{9,4},... | collective-permute-start | bytes 393224 | tf_op jit(solution)/shard_map/ppermute | solution.py:374
  115.8 4.2 %collective-permute-done.11.refs_12_ = f32[2,2,8,8,128]{4,3,2,1,0:T(8,128)S(1)} collective-permute-done((f32[2,2,8,8,128]{4,3,2,1,0:T(8,128)S(1)}, f32[2,2,8,8,128]{4,3,2,1,0:T(8,128)S(1)}, u32[]{:S(2)}, u32[]{:S(2)}) %collective-permute-start.11) | collective-permute-done | bytes 131104 | tf_op jit(solution)/shard_map/ppermute | solution.py:374
  120.7 2.3 %collective-permute-done.12.refs_13_ = f32[2,2,8,8,128]{4,3,2,1,0:T(8,128)S(1)} collective-permute-done((f32[2,2,8,8,128]{4,3,2,1,0:T(8,128)S(1)}, f32[2,2,8,8,128]{4,3,2,1,0:T(8,128)S(1)}, u32[]{:S(2)}, u32[]{:S(2)}) %collective-permute-start.12) | collective-permute-done | bytes 131104 | tf_op jit(solution)/shard_map/ppermute | solution.py:374
  123.6 4.0 %collective-permute-done.13.refs_14_ = f32[2,2,8,8,128]{4,3,2,1,0:T(8,128)S(1)} collective-permute-done((f32[2,2,8,8,128]{4,3,2,1,0:T(8,128)S(1)}, f32[2,2,8,8,128]{4,3,2,1,0:T(8,128)S(1)}, u32[]{:S(2)}, u32[]{:S(2)}) %collective-permute-start.13) | collective-permute-done | bytes 131104 | tf_op jit(solution)/shard_map/ppermute | solution.py:374
  128.3 2.2 %collective-permute-done.14.refs_15_ = f32[2,2,8,8,128]{4,3,2,1,0:T(8,128)S(1)} collective-permute-done((f32[2,2,8,8,128]{4,3,2,1,0:T(8,128)S(1)}, f32[2,2,8,8,128]{4,3,2,1,0:T(8,128)S(1)}, u32[]{:S(2)}, u32[]{:S(2)}) %collective-permute-start.14) | collective-permute-done | bytes 131104 | tf_op jit(solution)/shard_map/ppermute | solution.py:374
  132.1 6.4 %middle.3 = (f32[2,2,8,8,128]{4,3,2,1,0:T(8,128)S(1)}, f32[2,2,8,8,128]{4,3,2,1,0:T(8,128)S(1)}, f32[2,2,8,8,128]{4,3,2,1,0:T(8,128)S(1)}, f32[2,2,8,8,128]{4,3,...) custom-call(s32[1]{0:T(128)} %bitcast.me_ref, ...), custom_call_target="tpu_custom_call" | custom-call | tf_op jit(solution)/shard_map/middle/pallas_call | solution.py:298
  140.5 1.7 collective-permute-start.19
  142.6 2.5 %collective-permute-done.16.refs_18_ = f32[2,2,8,8,128]{4,3,2,1,0:T(8,128)S(1)} collective-permute-done((f32[2,2,8,8,128]{4,3,2,1,0:T(8,128)S(1)}, f32[2,2,8,8,128]{4,3,2,1,0:T(8,128)S(1)}, u32[]{:S(2)}, u32[]{:S(2)}) %collective-permute-start.16) | collective-permute-done | bytes 131104 | tf_op jit(solution)/shard_map/ppermute | solution.py:374
  145.0 1.9 %collective-permute-done.17.refs_19_ = f32[2,2,8,8,128]{4,3,2,1,0:T(8,128)S(1)} collective-permute-done((f32[2,2,8,8,128]{4,3,2,1,0:T(8,128)S(1)}, f32[2,2,8,8,128]{4,3,2,1,0:T(8,128)S(1)}, u32[]{:S(2)}, u32[]{:S(2)}) %collective-permute-start.17) | collective-permute-done | bytes 131104 | tf_op jit(solution)/shard_map/ppermute | solution.py:374
  146.9 5.5 %collective-permute-done.18.refs_20_ = f32[2,2,8,8,128]{4,3,2,1,0:T(8,128)S(1)} collective-permute-done((f32[2,2,8,8,128]{4,3,2,1,0:T(8,128)S(1)}, f32[2,2,8,8,128]{4,3,2,1,0:T(8,128)S(1)}, u32[]{:S(2)}, u32[]{:S(2)}) %collective-permute-start.18) | collective-permute-done | bytes 131104 | tf_op jit(solution)/shard_map/ppermute | solution.py:374
  154.3 2.5 %collective-permute-start.25 = (f32[2,2,8,8,128]{4,3,2,1,0:T(8,128)S(1)}, f32[2,2,8,8,128]{4,3,2,1,0:T(8,128)S(1)}, u32[]{:S(2)}, u32[]{:S(2)}) collective-permute-start(f32[2,2,8,8,128]{4,3,2,1,0:T(8,128)S(1)} %get-tuple-element.106), channel_id=1, source_target_pairs={{0,11},{1,10},{2,9},{3,8},{4,15},{5,14},{6,13},{7,12},{8,3},{9,2},... | collective-permute-start | bytes 393224 | tf_op jit(solution)/shard_map/ppermute | solution.py:374
  156.8 2.6 %collective-permute-start.27 = (f32[2,2,8,8,128]{4,3,2,1,0:T(8,128)S(1)}, f32[2,2,8,8,128]{4,3,2,1,0:T(8,128)S(1)}, u32[]{:S(2)}, u32[]{:S(2)}) collective-permute-start(f32[2,2,8,8,128]{4,3,2,1,0:T(8,128)S(1)} %get-tuple-element.108), channel_id=1, source_target_pairs={{0,13},{1,12},{2,15},{3,14},{4,9},{5,8},{6,11},{7,10},{8,5},{9,4},... | collective-permute-start | bytes 393224 | tf_op jit(solution)/shard_map/ppermute | solution.py:374
  161.3 1.7 collective-permute-start.29
  163.2 2.8 %collective-permute-done.26.refs_28_ = f32[2,2,8,8,128]{4,3,2,1,0:T(8,128)S(1)} collective-permute-done((f32[2,2,8,8,128]{4,3,2,1,0:T(8,128)S(1)}, f32[2,2,8,8,128]{4,3,2,1,0:T(8,128)S(1)}, u32[]{:S(2)}, u32[]{:S(2)}) %collective-permute-start.26) | collective-permute-done | bytes 131104 | tf_op jit(solution)/shard_map/ppermute | solution.py:374
  166.0 1.9 %collective-permute-done.27.refs_29_ = f32[2,2,8,8,128]{4,3,2,1,0:T(8,128)S(1)} collective-permute-done((f32[2,2,8,8,128]{4,3,2,1,0:T(8,128)S(1)}, f32[2,2,8,8,128]{4,3,2,1,0:T(8,128)S(1)}, u32[]{:S(2)}, u32[]{:S(2)}) %collective-permute-start.27) | collective-permute-done | bytes 131104 | tf_op jit(solution)/shard_map/ppermute | solution.py:374
  167.9 4.6 %collective-permute-done.28.refs_30_ = f32[2,2,8,8,128]{4,3,2,1,0:T(8,128)S(1)} collective-permute-done((f32[2,2,8,8,128]{4,3,2,1,0:T(8,128)S(1)}, f32[2,2,8,8,128]{4,3,2,1,0:T(8,128)S(1)}, u32[]{:S(2)}, u32[]{:S(2)}) %collective-permute-start.28) | collective-permute-done | bytes 131104 | tf_op jit(solution)/shard_map/ppermute | solution.py:374
  172.5 1.9 %collective-permute-done.29.refs_31_ = f32[2,2,8,8,128]{4,3,2,1,0:T(8,128)S(1)} collective-permute-done((f32[2,2,8,8,128]{4,3,2,1,0:T(8,128)S(1)}, f32[2,2,8,8,128]{4,3,2,1,0:T(8,128)S(1)}, u32[]{:S(2)}, u32[]{:S(2)}) %collective-permute-start.29) | collective-permute-done | bytes 131104 | tf_op jit(solution)/shard_map/ppermute | solution.py:374
  174.6 4.8 %to_frequencies.1 = f32[2,8,128,512]{3,2,1,0:T(8,128)} custom-call(s32[1]{0:T(128)} %bitcast.me_ref, f32[2,32,8,512]{3,2,1,0:T(8,128)S(1)} %copy-done.2, f32[2,2,8,8,128]{4,3,2,1,0:T(8,128)S(1)} %copy-done.9, f32[2,2,8,8,128]{4,3,2,1,0:T(8,128)S(1)} %copy-done.11, f32[2,2,8,8,128]{4,3,2,1,0:T(8,128)S(1)} %copy-done.13, f32[2,2,8,8,128]{4,3,2,1,0:T(8,128)S(1)} %copy-done.15, ...), custom_call_target="tpu_custom_call" | custom-call | tf_op jit(solution)/shard_map/to_frequencies/pallas_call | solution.py:354
  (125 shorter events, 26.7 us)
Async XLA Ops:
  4.9 56.2 %all-to-all-start = ((f32[32,128,128]{2,1,0:T(8,128)}), f32[32,128,128]{2,1,0:T(8,128)S(1)}, u32[]{:S(2)}, u32[]{:S(2)}) async-start(f32[32,128,128]{2,1,0:T(8,128)} %bitcast.14), calls=%async_computation | async-start | bytes 4194304 | tf_op jit(solution)/shard_map/all_to_all | solution.py:367
  62.5 68.6 %all-to-all-start.1 = ((f32[32,128,128]{2,1,0:T(8,128)}), f32[32,128,128]{2,1,0:T(8,128)S(1)}, u32[]{:S(2)}, u32[]{:S(2)}) async-start(f32[32,128,128]{2,1,0:T(8,128)} %bitcast.13), calls=%async_computation.1 | async-start | bytes 4194304 | tf_op jit(solution)/shard_map/all_to_all | solution.py:367
  76.5 3.7 %collective-permute-start = (f32[2,2,8,8,128]{4,3,2,1,0:T(8,128)S(1)}, f32[2,2,8,8,128]{4,3,2,1,0:T(8,128)S(1)}, u32[]{:S(2)}, u32[]{:S(2)}) collective-permute-start(f32[2,2,8,8,128]{4,3,2,1,0:T(8,128)S(1)} %get-tuple-element.63), channel_id=1, source_target_pairs={{0,1},{1,0},{2,3},{3,2},{4,5},{5,4},{6,7},{7,6},{8,9},{9,8},{10,11... | collective-permute-start | bytes 393224 | tf_op jit(solution)/shard_map/ppermute | solution.py:374
  76.7 9.1 %collective-permute-start.1 = (f32[2,2,8,8,128]{4,3,2,1,0:T(8,128)S(1)}, f32[2,2,8,8,128]{4,3,2,1,0:T(8,128)S(1)}, u32[]{:S(2)}, u32[]{:S(2)}) collective-permute-start(f32[2,2,8,8,128]{4,3,2,1,0:T(8,128)S(1)} %get-tuple-element.64), channel_id=1, source_target_pairs={{0,2},{1,3},{2,0},{3,1},{4,6},{5,7},{6,4},{7,5},{8,10},{9,11},{10,... | collective-permute-start | bytes 393224 | tf_op jit(solution)/shard_map/ppermute | solution.py:374
  78.4 10.9 %collective-permute-start.2 = (f32[2,2,8,8,128]{4,3,2,1,0:T(8,128)S(1)}, f32[2,2,8,8,128]{4,3,2,1,0:T(8,128)S(1)}, u32[]{:S(2)}, u32[]{:S(2)}) collective-permute-start(f32[2,2,8,8,128]{4,3,2,1,0:T(8,128)S(1)} %get-tuple-element.65), channel_id=1, source_target_pairs={{0,3},{1,2},{2,1},{3,0},{4,7},{5,6},{6,5},{7,4},{8,11},{9,10},{10,... | collective-permute-start | bytes 393224 | tf_op jit(solution)/shard_map/ppermute | solution.py:374
  78.4 11.6 %collective-permute-start.3 = (f32[2,2,8,8,128]{4,3,2,1,0:T(8,128)S(1)}, f32[2,2,8,8,128]{4,3,2,1,0:T(8,128)S(1)}, u32[]{:S(2)}, u32[]{:S(2)}) collective-permute-start(f32[2,2,8,8,128]{4,3,2,1,0:T(8,128)S(1)} %get-tuple-element.66), channel_id=1, source_target_pairs={{0,4},{1,5},{2,6},{3,7},{4,0},{5,1},{6,2},{7,3},{8,12},{9,13},{10,... | collective-permute-start | bytes 393224 | tf_op jit(solution)/shard_map/ppermute | solution.py:374
  80.1 21.4 %collective-permute-start.4 = (f32[2,2,8,8,128]{4,3,2,1,0:T(8,128)S(1)}, f32[2,2,8,8,128]{4,3,2,1,0:T(8,128)S(1)}, u32[]{:S(2)}, u32[]{:S(2)}) collective-permute-start(f32[2,2,8,8,128]{4,3,2,1,0:T(8,128)S(1)} %get-tuple-element.67), channel_id=1, source_target_pairs={{0,5},{1,4},{2,7},{3,6},{4,1},{5,0},{6,3},{7,2},{8,13},{9,12},{10,... | collective-permute-start | bytes 393224 | tf_op jit(solution)/shard_map/ppermute | solution.py:374
  80.9 21.3 %collective-permute-start.5 = (f32[2,2,8,8,128]{4,3,2,1,0:T(8,128)S(1)}, f32[2,2,8,8,128]{4,3,2,1,0:T(8,128)S(1)}, u32[]{:S(2)}, u32[]{:S(2)}) collective-permute-start(f32[2,2,8,8,128]{4,3,2,1,0:T(8,128)S(1)} %get-tuple-element.68), channel_id=1, source_target_pairs={{0,6},{1,7},{2,4},{3,5},{4,2},{5,3},{6,0},{7,1},{8,14},{9,15},{10,... | collective-permute-start | bytes 393224 | tf_op jit(solution)/shard_map/ppermute | solution.py:374
  86.4 19.0 %collective-permute-start.6 = (f32[2,2,8,8,128]{4,3,2,1,0:T(8,128)S(1)}, f32[2,2,8,8,128]{4,3,2,1,0:T(8,128)S(1)}, u32[]{:S(2)}, u32[]{:S(2)}) collective-permute-start(f32[2,2,8,8,128]{4,3,2,1,0:T(8,128)S(1)} %get-tuple-element.69), channel_id=1, source_target_pairs={{0,7},{1,6},{2,5},{3,4},{4,3},{5,2},{6,1},{7,0},{8,15},{9,14},{10,... | collective-permute-start | bytes 393224 | tf_op jit(solution)/shard_map/ppermute | solution.py:374
  90.0 16.1 %collective-permute-start.7 = (f32[2,2,8,8,128]{4,3,2,1,0:T(8,128)S(1)}, f32[2,2,8,8,128]{4,3,2,1,0:T(8,128)S(1)}, u32[]{:S(2)}, u32[]{:S(2)}) collective-permute-start(f32[2,2,8,8,128]{4,3,2,1,0:T(8,128)S(1)} %get-tuple-element.70), channel_id=1, source_target_pairs={{0,8},{1,9},{2,10},{3,11},{4,12},{5,13},{6,14},{7,15},{8,0},{9,1},... | collective-permute-start | bytes 393224 | tf_op jit(solution)/shard_map/ppermute | solution.py:374
  90.6 18.8 %collective-permute-start.8 = (f32[2,2,8,8,128]{4,3,2,1,0:T(8,128)S(1)}, f32[2,2,8,8,128]{4,3,2,1,0:T(8,128)S(1)}, u32[]{:S(2)}, u32[]{:S(2)}) collective-permute-start(f32[2,2,8,8,128]{4,3,2,1,0:T(8,128)S(1)} %get-tuple-element.71), channel_id=1, source_target_pairs={{0,9},{1,8},{2,11},{3,10},{4,13},{5,12},{6,15},{7,14},{8,1},{9,0},... | collective-permute-start | bytes 393224 | tf_op jit(solution)/shard_map/ppermute | solution.py:374
  102.2 10.0 %collective-permute-start.9 = (f32[2,2,8,8,128]{4,3,2,1,0:T(8,128)S(1)}, f32[2,2,8,8,128]{4,3,2,1,0:T(8,128)S(1)}, u32[]{:S(2)}, u32[]{:S(2)}) collective-permute-start(f32[2,2,8,8,128]{4,3,2,1,0:T(8,128)S(1)} %get-tuple-element.72), channel_id=1, source_target_pairs={{0,10},{1,11},{2,8},{3,9},{4,14},{5,15},{6,12},{7,13},{8,2},{9,3},... | collective-permute-start | bytes 393224 | tf_op jit(solution)/shard_map/ppermute | solution.py:374
  102.9 12.2 %collective-permute-start.10 = (f32[2,2,8,8,128]{4,3,2,1,0:T(8,128)S(1)}, f32[2,2,8,8,128]{4,3,2,1,0:T(8,128)S(1)}, u32[]{:S(2)}, u32[]{:S(2)}) collective-permute-start(f32[2,2,8,8,128]{4,3,2,1,0:T(8,128)S(1)} %get-tuple-element.73), channel_id=1, source_target_pairs={{0,11},{1,10},{2,9},{3,8},{4,15},{5,14},{6,13},{7,12},{8,3},{9,2},... | collective-permute-start | bytes 393224 | tf_op jit(solution)/shard_map/ppermute | solution.py:374
  106.1 13.9 %collective-permute-start.11 = (f32[2,2,8,8,128]{4,3,2,1,0:T(8,128)S(1)}, f32[2,2,8,8,128]{4,3,2,1,0:T(8,128)S(1)}, u32[]{:S(2)}, u32[]{:S(2)}) collective-permute-start(f32[2,2,8,8,128]{4,3,2,1,0:T(8,128)S(1)} %get-tuple-element.74), channel_id=1, source_target_pairs={{0,12},{1,13},{2,14},{3,15},{4,8},{5,9},{6,10},{7,11},{8,4},{9,5},... | collective-permute-start | bytes 393224 | tf_op jit(solution)/shard_map/ppermute | solution.py:374
  106.8 16.2 %collective-permute-start.12 = (f32[2,2,8,8,128]{4,3,2,1,0:T(8,128)S(1)}, f32[2,2,8,8,128]{4,3,2,1,0:T(8,128)S(1)}, u32[]{:S(2)}, u32[]{:S(2)}) collective-permute-start(f32[2,2,8,8,128]{4,3,2,1,0:T(8,128)S(1)} %get-tuple-element.75), channel_id=1, source_target_pairs={{0,13},{1,12},{2,15},{3,14},{4,9},{5,8},{6,11},{7,10},{8,5},{9,4},... | collective-permute-start | bytes 393224 | tf_op jit(solution)/shard_map/ppermute | solution.py:374
  110.1 17.5 %collective-permute-start.13 = (f32[2,2,8,8,128]{4,3,2,1,0:T(8,128)S(1)}, f32[2,2,8,8,128]{4,3,2,1,0:T(8,128)S(1)}, u32[]{:S(2)}, u32[]{:S(2)}) collective-permute-start(f32[2,2,8,8,128]{4,3,2,1,0:T(8,128)S(1)} %get-tuple-element.76), channel_id=1, source_target_pairs={{0,14},{1,15},{2,12},{3,13},{4,10},{5,11},{6,8},{7,9},{8,6},{9,7},... | collective-permute-start | bytes 393224 | tf_op jit(solution)/shard_map/ppermute | solution.py:374
  112.8 17.6 %collective-permute-start.14 = (f32[2,2,8,8,128]{4,3,2,1,0:T(8,128)S(1)}, f32[2,2,8,8,128]{4,3,2,1,0:T(8,128)S(1)}, u32[]{:S(2)}, u32[]{:S(2)}) collective-permute-start(f32[2,2,8,8,128]{4,3,2,1,0:T(8,128)S(1)} %get-tuple-element.77), channel_id=1, source_target_pairs={{0,15},{1,14},{2,13},{3,12},{4,11},{5,10},{6,9},{7,8},{8,7},{9,6},... | collective-permute-start | bytes 393224 | tf_op jit(solution)/shard_map/ppermute | solution.py:374
  138.6 3.6 %collective-permute-start.15 = (f32[2,2,8,8,128]{4,3,2,1,0:T(8,128)S(1)}, f32[2,2,8,8,128]{4,3,2,1,0:T(8,128)S(1)}, u32[]{:S(2)}, u32[]{:S(2)}) collective-permute-start(f32[2,2,8,8,128]{4,3,2,1,0:T(8,128)S(1)} %get-tuple-element.96), channel_id=1, source_target_pairs={{0,1},{1,0},{2,3},{3,2},{4,5},{5,4},{6,7},{7,6},{8,9},{9,8},{10,11... | collective-permute-start | bytes 393224 | tf_op jit(solution)/shard_map/ppermute | solution.py:374
  138.7 6.3 %collective-permute-start.16 = (f32[2,2,8,8,128]{4,3,2,1,0:T(8,128)S(1)}, f32[2,2,8,8,128]{4,3,2,1,0:T(8,128)S(1)}, u32[]{:S(2)}, u32[]{:S(2)}) collective-permute-start(f32[2,2,8,8,128]{4,3,2,1,0:T(8,128)S(1)} %get-tuple-element.97), channel_id=1, source_target_pairs={{0,2},{1,3},{2,0},{3,1},{4,6},{5,7},{6,4},{7,5},{8,10},{9,11},{10,... | collective-permute-start | bytes 393224 | tf_op jit(solution)/shard_map/ppermute | solution.py:374
  139.3 7.7 %collective-permute-start.17 = (f32[2,2,8,8,128]{4,3,2,1,0:T(8,128)S(1)}, f32[2,2,8,8,128]{4,3,2,1,0:T(8,128)S(1)}, u32[]{:S(2)}, u32[]{:S(2)}) collective-permute-start(f32[2,2,8,8,128]{4,3,2,1,0:T(8,128)S(1)} %get-tuple-element.98), channel_id=1, source_target_pairs={{0,3},{1,2},{2,1},{3,0},{4,7},{5,6},{6,5},{7,4},{8,11},{9,10},{10,... | collective-permute-start | bytes 393224 | tf_op jit(solution)/shard_map/ppermute | solution.py:374
  140.5 11.9 %collective-permute-start.18 = (f32[2,2,8,8,128]{4,3,2,1,0:T(8,128)S(1)}, f32[2,2,8,8,128]{4,3,2,1,0:T(8,128)S(1)}, u32[]{:S(2)}, u32[]{:S(2)}) collective-permute-start(f32[2,2,8,8,128]{4,3,2,1,0:T(8,128)S(1)} %get-tuple-element.99), channel_id=1, source_target_pairs={{0,4},{1,5},{2,6},{3,7},{4,0},{5,1},{6,2},{7,3},{8,12},{9,13},{10,... | collective-permute-start | bytes 393224 | tf_op jit(solution)/shard_map/ppermute | solution.py:374
  140.5 13.6 %collective-permute-start.19 = (f32[2,2,8,8,128]{4,3,2,1,0:T(8,128)S(1)}, f32[2,2,8,8,128]{4,3,2,1,0:T(8,128)S(1)}, u32[]{:S(2)}, u32[]{:S(2)}) collective-permute-start(f32[2,2,8,8,128]{4,3,2,1,0:T(8,128)S(1)} %get-tuple-element.100), channel_id=1, source_target_pairs={{0,5},{1,4},{2,7},{3,6},{4,1},{5,0},{6,3},{7,2},{8,13},{9,12},{10,... | collective-permute-start | bytes 393224 | tf_op jit(solution)/shard_map/ppermute | solution.py:374
  142.2 12.0 %collective-permute-start.20 = (f32[2,2,8,8,128]{4,3,2,1,0:T(8,128)S(1)}, f32[2,2,8,8,128]{4,3,2,1,0:T(8,128)S(1)}, u32[]{:S(2)}, u32[]{:S(2)}) collective-permute-start(f32[2,2,8,8,128]{4,3,2,1,0:T(8,128)S(1)} %get-tuple-element.101), channel_id=1, source_target_pairs={{0,6},{1,7},{2,4},{3,5},{4,2},{5,3},{6,0},{7,1},{8,14},{9,15},{10,... | collective-permute-start | bytes 393224 | tf_op jit(solution)/shard_map/ppermute | solution.py:374
  145.0 11.8 %collective-permute-start.21 = (f32[2,2,8,8,128]{4,3,2,1,0:T(8,128)S(1)}, f32[2,2,8,8,128]{4,3,2,1,0:T(8,128)S(1)}, u32[]{:S(2)}, u32[]{:S(2)}) collective-permute-start(f32[2,2,8,8,128]{4,3,2,1,0:T(8,128)S(1)} %get-tuple-element.102), channel_id=1, source_target_pairs={{0,7},{1,6},{2,5},{3,4},{4,3},{5,2},{6,1},{7,0},{8,15},{9,14},{10,... | collective-permute-start | bytes 393224 | tf_op jit(solution)/shard_map/ppermute | solution.py:374
  146.9 9.9 %collective-permute-start.22 = (f32[2,2,8,8,128]{4,3,2,1,0:T(8,128)S(1)}, f32[2,2,8,8,128]{4,3,2,1,0:T(8,128)S(1)}, u32[]{:S(2)}, u32[]{:S(2)}) collective-permute-start(f32[2,2,8,8,128]{4,3,2,1,0:T(8,128)S(1)} %get-tuple-element.103), channel_id=1, source_target_pairs={{0,8},{1,9},{2,10},{3,11},{4,12},{5,13},{6,14},{7,15},{8,0},{9,1},... | collective-permute-start | bytes 393224 | tf_op jit(solution)/shard_map/ppermute | solution.py:374
  152.5 6.9 %collective-permute-start.23 = (f32[2,2,8,8,128]{4,3,2,1,0:T(8,128)S(1)}, f32[2,2,8,8,128]{4,3,2,1,0:T(8,128)S(1)}, u32[]{:S(2)}, u32[]{:S(2)}) collective-permute-start(f32[2,2,8,8,128]{4,3,2,1,0:T(8,128)S(1)} %get-tuple-element.104), channel_id=1, source_target_pairs={{0,9},{1,8},{2,11},{3,10},{4,13},{5,12},{6,15},{7,14},{8,1},{9,0},... | collective-permute-start | bytes 393224 | tf_op jit(solution)/shard_map/ppermute | solution.py:374
  154.1 7.2 %collective-permute-start.24 = (f32[2,2,8,8,128]{4,3,2,1,0:T(8,128)S(1)}, f32[2,2,8,8,128]{4,3,2,1,0:T(8,128)S(1)}, u32[]{:S(2)}, u32[]{:S(2)}) collective-permute-start(f32[2,2,8,8,128]{4,3,2,1,0:T(8,128)S(1)} %get-tuple-element.105), channel_id=1, source_target_pairs={{0,10},{1,11},{2,8},{3,9},{4,14},{5,15},{6,12},{7,13},{8,2},{9,3},... | collective-permute-start | bytes 393224 | tf_op jit(solution)/shard_map/ppermute | solution.py:374
  154.3 8.9 %collective-permute-start.25 = (f32[2,2,8,8,128]{4,3,2,1,0:T(8,128)S(1)}, f32[2,2,8,8,128]{4,3,2,1,0:T(8,128)S(1)}, u32[]{:S(2)}, u32[]{:S(2)}) collective-permute-start(f32[2,2,8,8,128]{4,3,2,1,0:T(8,128)S(1)} %get-tuple-element.106), channel_id=1, source_target_pairs={{0,11},{1,10},{2,9},{3,8},{4,15},{5,14},{6,13},{7,12},{8,3},{9,2},... | collective-permute-start | bytes 393224 | tf_op jit(solution)/shard_map/ppermute | solution.py:374
  156.8 9.2 %collective-permute-start.26 = (f32[2,2,8,8,128]{4,3,2,1,0:T(8,128)S(1)}, f32[2,2,8,8,128]{4,3,2,1,0:T(8,128)S(1)}, u32[]{:S(2)}, u32[]{:S(2)}) collective-permute-start(f32[2,2,8,8,128]{4,3,2,1,0:T(8,128)S(1)} %get-tuple-element.107), channel_id=1, source_target_pairs={{0,12},{1,13},{2,14},{3,15},{4,8},{5,9},{6,10},{7,11},{8,4},{9,5},... | collective-permute-start | bytes 393224 | tf_op jit(solution)/shard_map/ppermute | solution.py:374
  156.8 11.1 %collective-permute-start.27 = (f32[2,2,8,8,128]{4,3,2,1,0:T(8,128)S(1)}, f32[2,2,8,8,128]{4,3,2,1,0:T(8,128)S(1)}, u32[]{:S(2)}, u32[]{:S(2)}) collective-permute-start(f32[2,2,8,8,128]{4,3,2,1,0:T(8,128)S(1)} %get-tuple-element.108), channel_id=1, source_target_pairs={{0,13},{1,12},{2,15},{3,14},{4,9},{5,8},{6,11},{7,10},{8,5},{9,4},... | collective-permute-start | bytes 393224 | tf_op jit(solution)/shard_map/ppermute | solution.py:374
  159.4 13.1 %collective-permute-start.28 = (f32[2,2,8,8,128]{4,3,2,1,0:T(8,128)S(1)}, f32[2,2,8,8,128]{4,3,2,1,0:T(8,128)S(1)}, u32[]{:S(2)}, u32[]{:S(2)}) collective-permute-start(f32[2,2,8,8,128]{4,3,2,1,0:T(8,128)S(1)} %get-tuple-element.109), channel_id=1, source_target_pairs={{0,14},{1,15},{2,12},{3,13},{4,10},{5,11},{6,8},{7,9},{8,6},{9,7},... | collective-permute-start | bytes 393224 | tf_op jit(solution)/shard_map/ppermute | solution.py:374
  161.3 13.1 %collective-permute-start.29 = (f32[2,2,8,8,128]{4,3,2,1,0:T(8,128)S(1)}, f32[2,2,8,8,128]{4,3,2,1,0:T(8,128)S(1)}, u32[]{:S(2)}, u32[]{:S(2)}) collective-permute-start(f32[2,2,8,8,128]{4,3,2,1,0:T(8,128)S(1)} %get-tuple-element.110), channel_id=1, source_target_pairs={{0,15},{1,14},{2,13},{3,12},{4,11},{5,10},{6,9},{7,8},{8,7},{9,6},... | collective-permute-start | bytes 393224 | tf_op jit(solution)/shard_map/ppermute | solution.py:374
  (42 other events, 821.7 us)

commit v3 on v2

--- a/solution.py
+++ b/solution.py
@@ -117,26 +117,35 @@
     return out
 
 
-def times_kernel(g_hbm, m_hbm, out_ref, g_ref, m_ref, stage, in_sems, m_sem, out_sems):
-    entries, lanes = g_ref.shape[1:3]
-    near, _, _, _, rows, _ = stage.shape
-    half = near * rows
+def load_inputs(g_hbm, m_hbm, g_ref, m_ref, in_sems, m_sem):
     load = pltpu.make_async_copy(m_hbm, m_ref, m_sem)
     pieces = [
         pltpu.make_async_copy(g_hbm.at[:, pl.ds(e, 1)], g_ref.at[:, pl.ds(e, 1)], in_sems.at[e])
-        for e in range(entries)
+        for e in range(g_ref.shape[1])
     ]
     for copy in [load] + pieces:
         copy.start()
     load.wait()
+    return pieces
+
+
+def sums_of(matrix, g_ref, e):
+    lanes = g_ref.shape[2]
+    g = jnp.concatenate([g_ref[0, e], g_ref[1, e]], axis=0)
+    d = dot3(matrix, split_value(g), ((1,), (1,)))
+    half = d.shape[0] // 2
+    return d[:half, :lanes], d[:half, lanes:], d[half:, :lanes], d[half:, lanes:]
+
+
+def both_times_kernel(g_hbm, m_hbm, out_ref, g_ref, m_ref, stage, in_sems, m_sem, out_sems):
+    entries, lanes = g_ref.shape[1:3]
+    near, _, _, _, rows, _ = stage.shape
+    pieces = load_inputs(g_hbm, m_hbm, g_ref, m_ref, in_sems, m_sem)
     matrix = split_value(m_ref[...])
     copies = []
     for e in range(entries):
         pieces[e].wait()
-        g = jnp.concatenate([g_ref[0, e], g_ref[1, e]], axis=0)
-        d = dot3(matrix, split_value(g), ((1,), (1,)))
-        c_re, c_im = d[:half, :lanes], d[:half, lanes:]
-        s_re, s_im = d[half:, :lanes], d[half:, lanes:]
+        c_re, c_im, s_re, s_im = sums_of(matrix, g_ref, e)
         for where, value in (
             ((0, 0), c_re + s_im),
             ((0, 1), c_im - s_re),
@@ -153,15 +162,32 @@
         copy.wait()
 
 
-def to_times(green, matrix, near):
-    _, entries, lanes, _ = green.shape
-    shape = (near, 2, 2, entries, ROWS, lanes)
+def one_times_kernel(g_hbm, m_hbm, out_ref, g_ref, m_ref, stage, in_sems, m_sem, out_sems):
+    entries, lanes = g_ref.shape[1:3]
+    devices, _, _, rows, _ = stage.shape
+    pieces = load_inputs(g_hbm, m_hbm, g_ref, m_ref, in_sems, m_sem)
+    matrix = split_value(m_ref[...])
+    copies = []
+    for e in range(entries):
+        pieces[e].wait()
+        c_re, c_im, s_re, s_im = sums_of(matrix, g_ref, e)
+        stage[:, 0, e] = (c_re + s_im).reshape(devices, rows, lanes)
+        stage[:, 1, e] = (c_im - s_re).reshape(devices, rows, lanes)
+        cut = pl.ds(e, 1)
+        copies.append(pltpu.make_async_copy(stage.at[:, :, cut], out_ref.at[:, :, cut], out_sems.at[e, 0]))
+        copies[-1].start()
+    for copy in copies:
+        copy.wait()
+
+
+def to_times(kernel, green, matrix, shape, targets, name):
+    entries = green.shape[1]
     hbm = pl.BlockSpec(memory_space=pltpu.HBM)
     return pl.pallas_call(
-        times_kernel,
+        kernel,
         in_specs=[hbm, hbm],
         out_specs=hbm,
-        out_shape=jax.ShapeDtypeStruct((2 * near,) + shape[1:], jnp.float32),
+        out_shape=jax.ShapeDtypeStruct((targets,) + shape[1:], jnp.float32),
         scratch_shapes=[
             pltpu.VMEM(green.shape, jnp.float32),
             pltpu.VMEM(matrix.shape, jnp.float32),
@@ -171,7 +197,7 @@
             pltpu.SemaphoreType.DMA((entries, 2)),
         ],
         compiler_params=pltpu.CompilerParams(vmem_limit_bytes=60 << 20),
-        name="to_times",
+        name=name,
     )(green, matrix)
 
 
@@ -188,7 +214,81 @@
         ref[plane:, re] = (-sine[:, cut]).astype(jnp.bfloat16)
 
 
-def middle_kernel(me_ref, table_ref, mirror_ref, index_ref, ch_ref, cl_ref, sh_ref, sl_ref, x_ref, *refs):
+def fill_matrices(index_ref, parts, forward, backward, turned):
+    plane = parts[0].shape[0]
+    row = lax.broadcasted_iota(jnp.int32, (plane, plane), 0)
+    pick = (row == index_ref[...]).astype(jnp.float32).astype(jnp.bfloat16)
+
+    def dot(a, b):
+        return jnp.dot(a, b, preferred_element_type=jnp.float32)
+
+    for part in range(2):
+        c_ref, s_ref = parts[part], parts[2 + part]
+        cosine, sine = c_ref[...].astype(jnp.float32), s_ref[...].astype(jnp.float32)
+        fill_block(forward.at[0, part], cosine, sine)
+        fill_block(backward.at[0, part], turned(cosine), turned(-sine))
+        fill_block(forward.at[1, part], dot(c_ref[...], pick), dot(s_ref[...], pick))
+        fill_block(backward.at[1, part], turned(dot(pick, c_ref[...])), turned(-dot(pick, s_ref[...])))
+
+
+def plane_dot(value, matrix, half, block):
+    width = matrix.shape[3] // 2
+    cut = slice(block * width, (block + 1) * width)
+    return dot3(value, (matrix[half, 0, :, cut], matrix[half, 1, :, cut]), ((1,), (0,)))
+
+
+def one_middle_kernel(table_ref, mirror_ref, index_ref, ch_ref, cl_ref, sh_ref, sl_ref, x_ref, out_ref, *refs):
+    forward, backward, mid, space, other_space, chi = refs
+    _, side, _, entries, rows, lanes = space.shape
+    plane = 2 * lanes
+    groups, _, _, members, _, _ = chi.shape
+    fill_matrices(index_ref, (ch_ref, cl_ref, sh_ref, sl_ref), forward, backward, lambda value: value)
+
+    def select_dot(value, matrix, block):
+        shape = (value[0].shape[0] // rows, rows, plane)
+        first, second = (plane_dot(value, matrix, half, block).reshape(shape) for half in range(2))
+        upper = lax.broadcasted_iota(jnp.int32, shape, 1) < rows // 2
+        return jnp.where(upper, first, second)
+
+    columns = [x_ref[:, h, ri].reshape(side * entries * rows, lanes) for ri in range(2) for h in range(2)]
+    value = split_value(jnp.concatenate(columns, axis=1))
+    for block in range(2):
+        d = select_dot(value, forward, block)
+        for ri in range(2):
+            piece = d[:, :, ri * lanes : (ri + 1) * lanes]
+            mid[block, ri] = piece.reshape(side, entries, rows, lanes)
+    for block in range(2):
+        for e in range(entries):
+            values = [(mid[block, 0, x, e], mid[block, 1, x, e]) for x in range(side)]
+            for x, parts in enumerate(dft_line(values, 1)):
+                for ri in range(2):
+                    space[block, x, ri, e] = parts[ri]
+                    other_space[block, x, ri, e] = pltpu.roll(parts[ri], rows // 2, 0)
+
+    for group in range(groups):
+        for c in range(members):
+            left, right = table_ref[group * members + c, 0], table_ref[group * members + c, 1]
+            for block in range(2):
+                values = []
+                for x in range(side):
+                    other = mirror_ref[0, x]
+                    a_re, a_im = space[block, x, 0, left], space[block, x, 1, left]
+                    b_re, b_im = other_space[block, other, 0, right], other_space[block, other, 1, right]
+                    values.append((a_re * b_re - a_im * b_im, a_re * b_im + a_im * b_re))
+                cut = slice(block * lanes, (block + 1) * lanes)
+                for x, parts in enumerate(dft_line(values, -1)):
+                    for ri in range(2):
+                        chi[group, ri, x, c, :, cut] = parts[ri]
+        whole = (side * members * rows, plane)
+        value = split_value(jnp.concatenate([chi[group, ri].reshape(whole) for ri in range(2)], axis=1))
+        for h in range(2):
+            d = select_dot(value, backward, h)
+            for ri in range(2):
+                piece = d[:, :, ri * lanes : (ri + 1) * lanes].reshape(side, members, rows, lanes)
+                out_ref[:, h, ri, group * members : (group + 1) * members] = piece
+
+
+def both_middle_kernel(me_ref, table_ref, mirror_ref, index_ref, ch_ref, cl_ref, sh_ref, sl_ref, x_ref, *refs):
     outs, (forward, backward, mid, space, chi) = refs[:-5], refs[-5:]
     halves, _, side, _, entries, rows, lanes = space.shape
     plane = 2 * lanes
@@ -196,25 +296,11 @@
     me, near = me_ref[0], len(outs)
     core, line = me % 2, me // 2 % kept
     parity = (1 - 2 * (me // near)).astype(jnp.float32)
-    row = lax.broadcasted_iota(jnp.int32, (plane, plane), 0)
-    pick = (row == index_ref[...]).astype(jnp.float32).astype(jnp.bfloat16)
-
-    def dot(a, b):
-        return jnp.dot(a, b, preferred_element_type=jnp.float32)
 
     def turned(value):
         return jnp.where(core == 0, value, jnp.concatenate([value[:, lanes:], value[:, :lanes]], axis=1))
 
-    for part, (c_ref, s_ref) in enumerate(((ch_ref, sh_ref), (cl_ref, sl_ref))):
-        cosine, sine = c_ref[...].astype(jnp.float32), s_ref[...].astype(jnp.float32)
-        fill_block(forward.at[0, part], cosine, sine)
-        fill_block(backward.at[0, part], turned(cosine), turned(-sine))
-        fill_block(forward.at[1, part], dot(c_ref[...], pick), dot(s_ref[...], pick))
-        fill_block(backward.at[1, part], turned(dot(pick, c_ref[...])), turned(-dot(pick, s_ref[...])))
-
-    def plane_dot(value, matrix, half, block):
-        cut = slice(2 * block * lanes, 2 * (block + 1) * lanes)
-        return dot3(value, (matrix[half, 0, :, cut], matrix[half, 1, :, cut]), ((1,), (0,)))
+    fill_matrices(index_ref, (ch_ref, cl_ref, sh_ref, sl_ref), forward, backward, turned)
 
     def arrive(half):
         columns = [
@@ -282,47 +368,74 @@
                 product(unit, block, c)
 
 
-def middle(x, table, mirror_map, me, near):
-    devices, halves, _, entries, rows, lanes = x.shape
-    plane = 2 * lanes
-    side = devices // 2
-    components = table.shape[0]
-    members = components // GROUPS
-    units = halves * GROUPS
+def middle_inputs(table, mirror_map, x):
+    side, plane = x.shape[0] // 2, 2 * x.shape[-1]
     index = (mirror_map[1][:, None] * side + mirror_map[2][None, :]).reshape(1, plane)
     cosine, sine = plane_parts(side)
     parts = [jnp.asarray(part) for part in split_constant(cosine) + split_constant(sine)]
     smem = pl.BlockSpec(memory_space=pltpu.SMEM)
     vmem = pl.BlockSpec(memory_space=pltpu.VMEM)
-    matrices = pltpu.VMEM((halves, 2, 2 * plane, 2 * plane), jnp.bfloat16)
+    args = (table, mirror_map, index, *parts, x.reshape((side, 2) + x.shape[1:]))
+    return args, [smem, smem] + [vmem] * 6, pltpu.VMEM((2, 2, 2 * plane, 2 * plane), jnp.bfloat16)
+
+
+def one_middle(x, table, mirror_map):
+    devices, _, entries, rows, lanes = x.shape
+    side, components = devices // 2, table.shape[0]
+    args, specs, matrices = middle_inputs(table, mirror_map, x)
+    spatial = pltpu.VMEM((2, side, 2, entries, rows, lanes), jnp.float32)
+    shape = (side, 2, 2, components, rows, lanes)
+    out = pl.pallas_call(
+        one_middle_kernel,
+        in_specs=specs,
+        out_specs=pl.BlockSpec(memory_space=pltpu.VMEM),
+        out_shape=jax.ShapeDtypeStruct(shape, jnp.float32),
+        scratch_shapes=[
+            matrices,
+            matrices,
+            pltpu.VMEM((2, 2, side, entries, rows, lanes), jnp.float32),
+            spatial,
+            spatial,
+            pltpu.VMEM((GROUPS, 2, side, components // GROUPS, rows, 2 * lanes), jnp.float32),
+        ],
+        compiler_params=pltpu.CompilerParams(vmem_limit_bytes=28 << 20),
+        name="one_middle",
+    )(*args)
+    return out.reshape((devices,) + shape[2:])
+
+
+def both_middle(x, table, mirror_map, me, near):
+    devices, halves, _, entries, rows, lanes = x.shape
+    side, components = devices // 2, table.shape[0]
+    args, specs, matrices = middle_inputs(table, mirror_map, x)
+    members = components // GROUPS
     return pl.pallas_call(
-        middle_kernel,
-        in_specs=[smem, smem, smem] + [vmem] * 6,
-        out_specs=[vmem] * near,
+        both_middle_kernel,
+        in_specs=[pl.BlockSpec(memory_space=pltpu.SMEM)] + specs,
+        out_specs=[pl.BlockSpec(memory_space=pltpu.VMEM)] * near,
         out_shape=[jax.ShapeDtypeStruct((halves, 2, components, rows, lanes), jnp.float32)] * near,
         scratch_shapes=[
             matrices,
             matrices,
             pltpu.VMEM((halves, 2, 2, side, entries, rows, lanes), jnp.float32),
             pltpu.VMEM((halves, 2, side, 2, entries, rows, lanes), jnp.float32),
-            pltpu.VMEM((units, 2, near // 2, members, rows, plane), jnp.float32),
+            pltpu.VMEM((halves * GROUPS, 2, near // 2, members, rows, 2 * lanes), jnp.float32),
         ],
         compiler_params=pltpu.CompilerParams(vmem_limit_bytes=28 << 20),
-        name="middle",
-    )(me, table, mirror_map, index, *parts, x.reshape((side, 2) + x.shape[1:]))
-
-
-def frequency_kernel(near, me_ref, m_ref, *refs):
+        name="both_middle",
+    )(me, *args)
+
+
+def frequency_kernel(me_ref, both_ref, one_ref, y_ref, *refs):
     pieces, (out_ref, stage, sems) = refs[:-3], refs[-3:]
-    components, lanes = stage.shape[1:3]
+    near = len(pieces)
+    devices, _, components, rows, lanes = y_ref.shape
     groups = sems.shape[0]
     members = components // groups
-    sets = len(pieces) // near
     me = me_ref[0] % near
-    rows = [
-        m_ref[part, some * near + (slot ^ me)] for part in range(2) for some in range(sets) for slot in range(near)
-    ]
-    matrix = split_value(jnp.concatenate(rows, axis=0))
+    both = [both_ref[part, slot ^ me] for part in range(2) for slot in range(near)]
+    matrix = split_value(jnp.concatenate(both + [one_ref[...]], axis=0))
+    upper_rows = lax.broadcasted_iota(jnp.int32, (devices, rows, lanes), 1) < rows // 2
 
     def gathered(half, ri, c):
         return jnp.concatenate([piece[half, ri, c] for piece in pieces], axis=0)
@@ -334,8 +447,15 @@
             part = [[gathered(half, ri, c) for ri in range(2)] for half in range(2)]
             sums = [part[0][ri] + part[1][ri] for ri in range(2)]
             differences = [part[0][ri] - part[1][ri] for ri in range(2)]
-            values.append(jnp.concatenate([sums[0], -differences[1]], axis=0).T)
-            values.append(jnp.concatenate([sums[1], differences[0]], axis=0).T)
+            folded = []
+            for ri in range(2):
+                tile = y_ref[:, ri, c]
+                turned = pltpu.roll(tile, rows // 2, 1)
+                folded.append((tile + turned, turned - tile))
+            first = jnp.where(upper_rows, folded[0][0], -folded[1][1]).reshape(devices * rows, lanes)
+            second = jnp.where(upper_rows, folded[1][0], folded[0][1]).reshape(devices * rows, lanes)
+            values.append(jnp.concatenate([sums[0], -differences[1], first], axis=0).T)
+            values.append(jnp.concatenate([sums[1], differences[0], second], axis=0).T)
         d = dot3(split_value(jnp.concatenate(values, axis=0)), matrix, ((1,), (0,)))
         d = d.reshape(members, 2, lanes, d.shape[1])
         for ri in range(2):
@@ -347,19 +467,19 @@
         copy.wait()
 
 
-def to_frequencies(pieces, matrix, me, near):
-    components, rows, lanes = pieces[0].shape[2:]
-    shape = (2, components, lanes, matrix.shape[3])
+def to_frequencies(y, pieces, both, one, me):
+    _, _, components, _, lanes = y.shape
+    shape = (2, components, lanes, one.shape[1])
     vmem = pl.BlockSpec(memory_space=pltpu.VMEM)
     return pl.pallas_call(
-        functools.partial(frequency_kernel, near),
-        in_specs=[pl.BlockSpec(memory_space=pltpu.SMEM)] + [vmem] * (1 + len(pieces)),
+        frequency_kernel,
+        in_specs=[pl.BlockSpec(memory_space=pltpu.SMEM)] + [vmem] * (3 + len(pieces)),
         out_specs=pl.BlockSpec(memory_space=pltpu.HBM),
         out_shape=jax.ShapeDtypeStruct(shape, jnp.float32),
         scratch_shapes=[pltpu.VMEM(shape, jnp.float32), pltpu.SemaphoreType.DMA((components // 2,))],
         compiler_params=pltpu.CompilerParams(vmem_limit_bytes=28 << 20),
         name="to_frequencies",
-    )(me, matrix, *pieces)
+    )(me, both, one, y, *pieces)
 
 
 def exchange(x):
@@ -496,24 +616,31 @@
     lanes, count = green.shape[2], green.shape[3]
     devices = side * plane // lanes
     near = devices // 2
-    sets = count // (2 * near * ROWS)
-    if lanes != LANES or 2 * lanes != plane or sets * 2 * near * ROWS != count:
+    half = ROWS // 2
+    shared = near * ROWS
+    if lanes != LANES or 2 * lanes != plane or 2 * (shared + devices * half) != count:
         return general(green, pair_table, mirror_map)
-    rows = np.arange(count // 2)
-    fermion = fermion_matrix(rows, count).reshape(2, sets, near * ROWS, count).swapaxes(0, 1)
-    fermion = fermion.reshape(sets, 2 * near * ROWS, count).astype(np.float32)
-    boson = boson_matrix(rows, count).reshape(2, sets * near, ROWS, count).astype(np.float32)
     me = lax.axis_index("kb").astype(jnp.int32).reshape(1)
-    sent = []
-    for some in range(sets):
-        if sent:
-            green, sent[-1] = lax.optimization_barrier((green, sent[-1]))
-        sent.append(to_times(green, jnp.asarray(fermion[some]), near))
-    returned = []
-    for some in range(sets):
-        x, returned, sent[some + 1 :] = lax.optimization_barrier((exchange(sent[some]), returned, sent[some + 1 :]))
-        returned = returned + swap(middle(x, pair_table, mirror_map, me, near), devices)
-    return to_frequencies(returned, jnp.asarray(boson), me, near)
+    entries = green.shape[1]
+
+    rows = np.arange(shared)
+    both_fermion = fermion_matrix(rows, count).astype(np.float32)
+    both_boson = boson_matrix(rows, count).reshape(2, near, ROWS, count).astype(np.float32)
+    rows = shared + np.arange(devices * half).reshape(devices, half)
+    times = np.concatenate([rows, count - 1 - rows], axis=1).reshape(-1)
+    one_fermion = fermion_matrix(times, count).astype(np.float32)
+    one_boson = boson_matrix(rows.reshape(-1), count).reshape(2, devices, half, count).swapaxes(0, 1)
+    one_boson = one_boson.reshape(devices * ROWS, count).astype(np.float32)
+
+    shape = (devices, 2, entries, ROWS, lanes)
+    one = to_times(one_times_kernel, green, jnp.asarray(one_fermion), shape, devices, "one_times")
+    green, one = lax.optimization_barrier((green, one))
+    shape = (near, 2, 2, entries, ROWS, lanes)
+    both = to_times(both_times_kernel, green, jnp.asarray(both_fermion), shape, devices, "both_times")
+    one, both = lax.optimization_barrier((exchange(one), both))
+    one, both = lax.optimization_barrier((one_middle(one, pair_table, mirror_map), exchange(both)))
+    pieces = swap(both_middle(both, pair_table, mirror_map, me, near), devices)
+    return to_frequencies(exchange(one), pieces, jnp.asarray(both_boson), jnp.asarray(one_boson), me)
 
 
 def solution(mesh):

time: 180 us -> 180 us (level)
  waiting for transfers between devices: 93.2 us -> 79.5 us
  local copies, waits for them, and re-layouts: 15.4 us -> 27.1 us
  Pallas kernels: 27.5 us -> 30.2 us
    ppermute x30 -> x15, waiting for transfers between devices: 49.3 us -> 20.8 us  [swap(): moved.append(lax.ppermute(pieces[slot], 'kb', pairs))]
    all_to_all x2 -> x3, waiting for transfers between devices: 43.9 us -> 58.8 us  [exchange(): lax.all_to_all(flat, 'kb', split_axis=0, concat_axis=0, tiled=True)]
    unnamed x85 -> x77, local copies, waits for them, and re-layouts: 15.4 us -> 26.4 us
    ppermute x30 -> x15, starting transfers between devices: 31.3 us -> 26.5 us  [swap(): moved.append(lax.ppermute(pieces[slot], 'kb', pairs))]
    all_to_all x2 -> x3, starting transfers between devices: 11.5 us -> 15.1 us  [exchange(): lax.all_to_all(flat, 'kb', split_axis=0, concat_axis=0, tiled=True)]
    pallas_call x5, Pallas kernels: 27.5 us -> 30.2 us  [the longest x2 11.7 us: to_times(): pl.pallas_call(kernel, in_specs=[hbm, hbm], out_specs=hbm, out_shape=jax....]
  transfers between devices with their start and end apart: 32 -> 18, of which waited for: 20 -> 11; matrix products, arithmetic and copies ran while one was open for 0% -> 1% of each run, Pallas kernels for 6% -> 11%
where the time goes in v3:
time: 180 us
  waiting for transfers between devices  79.5 us (44%)
  starting transfers between devices  41.6 us (23%)
  Pallas kernels  30.2 us (17%)
  local copies, waits for them, and re-layouts  27.1 us (15%)
    all_to_all x3, waiting for transfers between devices, exchange(): lax.all_to_all(flat, 'kb', split_axis=0, concat_axis=0, tiled=True)  58.8 us
    ppermute x15, starting transfers between devices, swap(): moved.append(lax.ppermute(pieces[slot], 'kb', pairs))  26.5 us
    unnamed x77, local copies, waits for them, and re-layouts  26.4 us
    ppermute x15, waiting for transfers between devices, swap(): moved.append(lax.ppermute(pieces[slot], 'kb', pairs))  20.8 us
    all_to_all x3, starting transfers between devices, exchange(): lax.all_to_all(flat, 'kb', split_axis=0, concat_axis=0, tiled=True)  15.1 us
    pallas_call x2, Pallas kernels, to_times(): pl.pallas_call(kernel, in_specs=[hbm, hbm], out_specs=hbm, out_shape=jax....  11.7 us
    pallas_call x1, Pallas kernels, one_middle(): pl.pallas_call(one_middle_kernel, in_specs=specs, out_specs=pl.BlockSpec(...  7.58 us
    pallas_call x1, Pallas kernels, both_middle(): pl.pallas_call(both_middle_kernel, in_specs=[pl.BlockSpec(memory_space=pl...  6.38 us
  transfers between devices with their start and end apart: 18, of which 11 were waited for; matrix products, arithmetic and copies ran while one was open for 1% of the time, Pallas kernels for 11%

profile of v3, /device:TPU:0, one launch (start us, length us, event | category | flops | bytes accessed | tf_op | source)
XLA Modules:
  0.0 179.5 jit_solution(17858696884837648495)
XLA Ops:
  0.0 6.7 %one_times.1 = f32[32,2,4,8,128]{4,3,2,1,0:T(8,128)} custom-call(f32[2,4,128,512]{3,2,1,0:T(8,128)} %g_hbm.2, f32[512,512]{1,0:T(8,128)} %constant.22.clone.m_hbm), custom_call_target="tpu_custom_call" | custom-call | tf_op jit(solution)/shard_map/one_times/pallas_call | solution.py:186
  6.7 7.3 %all-to-all-start = ((f32[32,64,128]{2,1,0:T(8,128)}), f32[32,64,128]{2,1,0:T(8,128)S(1)}, u32[]{:S(2)}, u32[]{:S(2)}) async-start(f32[32,64,128]{2,1,0:T(8,128)} %bitcast.19), calls=%async_computation | async-start | bytes 2097152 | tf_op jit(solution)/shard_map/all_to_all | solution.py:487
  14.0 5.0 %both_times.1 = f32[32,2,2,4,8,128]{5,4,3,2,1,0:T(8,128)} custom-call(f32[2,4,128,512]{3,2,1,0:T(8,128)} %g_hbm.2, f32[256,512]{1,0:T(8,128)} %constant.23.clone.m_hbm), custom_call_target="tpu_custom_call" | custom-call | tf_op jit(solution)/shard_map/both_times/pallas_call | solution.py:186
  19.0 21.3 %all-to-all-done = f32[32,64,128]{2,1,0:T(8,128)S(1)} async-done(((f32[32,64,128]{2,1,0:T(8,128)}), f32[32,64,128]{2,1,0:T(8,128)S(1)}, u32[]{:S(2)}, u32[]{:S(2)}) %all-to-all-start) | async-done | bytes 1048608 | tf_op jit(solution)/shard_map/all_to_all | solution.py:487
  40.3 3.6 %all-to-all-start.1 = ((f32[32,128,128]{2,1,0:T(8,128)}), f32[32,128,128]{2,1,0:T(8,128)S(1)}, u32[]{:S(2)}, u32[]{:S(2)}) async-start(f32[32,128,128]{2,1,0:T(8,128)} %bitcast.18), calls=%async_computation.1 | async-start | bytes 4194304 | tf_op jit(solution)/shard_map/all_to_all | solution.py:487
  46.4 7.6 %one_middle.1 = f32[16,2,2,8,8,128]{5,4,3,2,1,0:T(8,128)S(1)} custom-call(s32[8,2]{1,0:T(8,128)S(1)} %copy.16.table_ref, s32[3,16]{1,0:T(4,128)S(1)} %copy-done.36, s32[1,256]{1,0:T(1,128)S(1)} %add.36.index_ref, bf16[256,256]{1,0:T(8,128)(2,1)S(1)} %copy-done.8, bf16[256,256]{1,0:T(8,128)(2,1)S(1)} %copy-done.7, bf16[256,256]{1,0:T(8,128)(2,1)S(1)} %copy-done.6, ...), custom_call_target="tpu_custom_call" | custom-call | tf_op jit(solution)/shard_map/one_middle/pallas_call | solution.py:388
  54.0 1.3 copy-done
  55.3 37.5 %all-to-all-done.1 = f32[32,128,128]{2,1,0:T(8,128)S(1)} async-done(((f32[32,128,128]{2,1,0:T(8,128)}), f32[32,128,128]{2,1,0:T(8,128)S(1)}, u32[]{:S(2)}, u32[]{:S(2)}) %all-to-all-start.1) | async-done | bytes 2097184 | tf_op jit(solution)/shard_map/all_to_all | solution.py:487
  92.8 1.3 copy-done.1
  94.2 4.2 %all-to-all-start.2 = ((f32[32,128,128]{2,1,0:T(8,128)}), f32[32,128,128]{2,1,0:T(8,128)S(1)}, u32[]{:S(2)}, u32[]{:S(2)}) async-start(f32[32,128,128]{2,1,0:T(8,128)} %bitcast.15), calls=%async_computation.2 | async-start | bytes 4194304 | tf_op jit(solution)/shard_map/all_to_all | solution.py:487
  98.4 1.6 copy-done.2
  100.0 0.9 copy-done.9
  100.9 6.4 %both_middle.1 = (f32[2,2,8,8,128]{4,3,2,1,0:T(8,128)S(1)}, f32[2,2,8,8,128]{4,3,2,1,0:T(8,128)S(1)}, f32[2,2,8,8,128]{4,3,2,1,0:T(8,128)S(1)}, f32[2,2,8,8,128]...) custom-call(s32[1]{0:T(128)} %bitcast.me_ref, ...), custom_call_target="tpu_custom_call" | custom-call | tf_op jit(solution)/shard_map/both_middle/pallas_call | solution.py:412
  108.0 1.7 collective-permute-start.1
  109.8 1.6 collective-permute-start.3
  111.5 2.6 %collective-permute-start.5 = (f32[2,2,8,8,128]{4,3,2,1,0:T(8,128)S(1)}, f32[2,2,8,8,128]{4,3,2,1,0:T(8,128)S(1)}, u32[]{:S(2)}, u32[]{:S(2)}) collective-permute-start(f32[2,2,8,8,128]{4,3,2,1,0:T(8,128)S(1)} %get-tuple-element.39), channel_id=1, source_target_pairs={{0,6},{1,7},{2,4},{3,5},{4,2},{5,3},{6,0},{7,1},{8,14},{9,15},{10,... | collective-permute-start | bytes 393224 | tf_op jit(solution)/shard_map/ppermute | solution.py:494
  114.1 3.4 %collective-permute-done.1.refs_2_ = f32[2,2,8,8,128]{4,3,2,1,0:T(8,128)S(1)} collective-permute-done((f32[2,2,8,8,128]{4,3,2,1,0:T(8,128)S(1)}, f32[2,2,8,8,128]{4,3,2,1,0:T(8,128)S(1)}, u32[]{:S(2)}, u32[]{:S(2)}) %collective-permute-start.1) | collective-permute-done | bytes 131104 | tf_op jit(solution)/shard_map/ppermute | solution.py:494
  117.9 3.1 %collective-permute-done.2.refs_3_ = f32[2,2,8,8,128]{4,3,2,1,0:T(8,128)S(1)} collective-permute-done((f32[2,2,8,8,128]{4,3,2,1,0:T(8,128)S(1)}, f32[2,2,8,8,128]{4,3,2,1,0:T(8,128)S(1)}, u32[]{:S(2)}, u32[]{:S(2)}) %collective-permute-start.2) | collective-permute-done | bytes 131104 | tf_op jit(solution)/shard_map/ppermute | solution.py:494
  121.7 5.2 %collective-permute-start.8 = (f32[2,2,8,8,128]{4,3,2,1,0:T(8,128)S(1)}, f32[2,2,8,8,128]{4,3,2,1,0:T(8,128)S(1)}, u32[]{:S(2)}, u32[]{:S(2)}) collective-permute-start(f32[2,2,8,8,128]{4,3,2,1,0:T(8,128)S(1)} %get-tuple-element.42), channel_id=1, source_target_pairs={{0,9},{1,8},{2,11},{3,10},{4,13},{5,12},{6,15},{7,14},{8,1},{9,0},... | collective-permute-start | bytes 393224 | tf_op jit(solution)/shard_map/ppermute | solution.py:494
  127.5 2.8 %collective-permute-start.9 = (f32[2,2,8,8,128]{4,3,2,1,0:T(8,128)S(1)}, f32[2,2,8,8,128]{4,3,2,1,0:T(8,128)S(1)}, u32[]{:S(2)}, u32[]{:S(2)}) collective-permute-start(f32[2,2,8,8,128]{4,3,2,1,0:T(8,128)S(1)} %get-tuple-element.43), channel_id=1, source_target_pairs={{0,10},{1,11},{2,8},{3,9},{4,14},{5,15},{6,12},{7,13},{8,2},{9,3},... | collective-permute-start | bytes 393224 | tf_op jit(solution)/shard_map/ppermute | solution.py:494
  131.0 5.9 %collective-permute-start.10 = (f32[2,2,8,8,128]{4,3,2,1,0:T(8,128)S(1)}, f32[2,2,8,8,128]{4,3,2,1,0:T(8,128)S(1)}, u32[]{:S(2)}, u32[]{:S(2)}) collective-permute-start(f32[2,2,8,8,128]{4,3,2,1,0:T(8,128)S(1)} %get-tuple-element.44), channel_id=1, source_target_pairs={{0,11},{1,10},{2,9},{3,8},{4,15},{5,14},{6,13},{7,12},{8,3},{9,2},... | collective-permute-start | bytes 393224 | tf_op jit(solution)/shard_map/ppermute | solution.py:494
  139.9 3.2 %collective-permute-start.13 = (f32[2,2,8,8,128]{4,3,2,1,0:T(8,128)S(1)}, f32[2,2,8,8,128]{4,3,2,1,0:T(8,128)S(1)}, u32[]{:S(2)}, u32[]{:S(2)}) collective-permute-start(f32[2,2,8,8,128]{4,3,2,1,0:T(8,128)S(1)} %get-tuple-element.47), channel_id=1, source_target_pairs={{0,14},{1,15},{2,12},{3,13},{4,10},{5,11},{6,8},{7,9},{8,6},{9,7},... | collective-permute-start | bytes 393224 | tf_op jit(solution)/shard_map/ppermute | solution.py:494
  143.8 2.0 %collective-permute-start.14 = (f32[2,2,8,8,128]{4,3,2,1,0:T(8,128)S(1)}, f32[2,2,8,8,128]{4,3,2,1,0:T(8,128)S(1)}, u32[]{:S(2)}, u32[]{:S(2)}) collective-permute-start(f32[2,2,8,8,128]{4,3,2,1,0:T(8,128)S(1)} %get-tuple-element.48), channel_id=1, source_target_pairs={{0,15},{1,14},{2,13},{3,12},{4,11},{5,10},{6,9},{7,8},{8,7},{9,6},... | collective-permute-start | bytes 393224 | tf_op jit(solution)/shard_map/ppermute | solution.py:494
  145.8 3.5 %collective-permute-done.10.refs_11_ = f32[2,2,8,8,128]{4,3,2,1,0:T(8,128)S(1)} collective-permute-done((f32[2,2,8,8,128]{4,3,2,1,0:T(8,128)S(1)}, f32[2,2,8,8,128]{4,3,2,1,0:T(8,128)S(1)}, u32[]{:S(2)}, u32[]{:S(2)}) %collective-permute-start.10) | collective-permute-done | bytes 131104 | tf_op jit(solution)/shard_map/ppermute | solution.py:494
  149.9 1.5 collective-permute-done.11.refs_12_
  152.1 2.3 %collective-permute-done.12.refs_13_ = f32[2,2,8,8,128]{4,3,2,1,0:T(8,128)S(1)} collective-permute-done((f32[2,2,8,8,128]{4,3,2,1,0:T(8,128)S(1)}, f32[2,2,8,8,128]{4,3,2,1,0:T(8,128)S(1)}, u32[]{:S(2)}, u32[]{:S(2)}) %collective-permute-start.12) | collective-permute-done | bytes 131104 | tf_op jit(solution)/shard_map/ppermute | solution.py:494
  155.0 4.6 %collective-permute-done.13.refs_14_ = f32[2,2,8,8,128]{4,3,2,1,0:T(8,128)S(1)} collective-permute-done((f32[2,2,8,8,128]{4,3,2,1,0:T(8,128)S(1)}, f32[2,2,8,8,128]{4,3,2,1,0:T(8,128)S(1)}, u32[]{:S(2)}, u32[]{:S(2)}) %collective-permute-start.13) | collective-permute-done | bytes 131104 | tf_op jit(solution)/shard_map/ppermute | solution.py:494
  160.2 2.2 %collective-permute-done.14.refs_15_ = f32[2,2,8,8,128]{4,3,2,1,0:T(8,128)S(1)} collective-permute-done((f32[2,2,8,8,128]{4,3,2,1,0:T(8,128)S(1)}, f32[2,2,8,8,128]{4,3,2,1,0:T(8,128)S(1)}, u32[]{:S(2)}, u32[]{:S(2)}) %collective-permute-start.14) | collective-permute-done | bytes 131104 | tf_op jit(solution)/shard_map/ppermute | solution.py:494
  167.6 0.9 copy-done.21
  173.0 0.9 copy-done.33
  173.9 0.9 copy-done.35
  174.8 4.6 %to_frequencies.1 = f32[2,8,128,512]{3,2,1,0:T(8,128)} custom-call(s32[1]{0:T(128)} %bitcast.me_ref, f32[2,16,8,512]{3,2,1,0:T(8,128)S(1)} %copy-done.4, f32[256,512]{1,0:T(8,128)S(1)} %copy-done.3, f32[32,2,8,8,128]{4,3,2,1,0:T(8,128)S(1)} %bitcast.14, f32[2,2,8,8,128]{4,3,2,1,0:T(8,128)S(1)} %copy-done.11, ...), custom_call_target="tpu_custom_call" | custom-call | tf_op jit(solution)/shard_map/to_frequencies/pallas_call | solution.py:474
  (89 shorter events, 21.8 us)
Async XLA Ops:
  6.7 33.5 %all-to-all-start = ((f32[32,64,128]{2,1,0:T(8,128)}), f32[32,64,128]{2,1,0:T(8,128)S(1)}, u32[]{:S(2)}, u32[]{:S(2)}) async-start(f32[32,64,128]{2,1,0:T(8,128)} %bitcast.19), calls=%async_computation | async-start | bytes 2097152 | tf_op jit(solution)/shard_map/all_to_all | solution.py:487
  40.2 3.7 %copy-start.37 = (s32[8,2]{0,1:T(2,128)S(1)}, s32[8,2]{0,1:T(2,128)}, u32[]{:S(2)}) copy-start(s32[8,2]{0,1:T(2,128)} %param.16) | copy-start | bytes 196
  40.2 3.8 %copy-start.36 = (s32[3,16]{1,0:T(4,128)S(1)}, s32[3,16]{1,0:T(4,128)}, u32[]{:S(2)}) copy-start(s32[3,16]{1,0:T(4,128)} %mirror_ref.3) | copy-start | bytes 580
  40.2 5.2 %copy-start.5 = (bf16[256,256]{1,0:T(8,128)(2,1)S(1)}, bf16[256,256]{1,0:T(8,128)(2,1)}, u32[]{:S(2)}) copy-start(bf16[256,256]{1,0:T(8,128)(2,1)} %constant.27.clone.sl_ref) | copy-start | bytes 393220
  40.3 5.2 %copy-start.6 = (bf16[256,256]{1,0:T(8,128)(2,1)S(1)}, bf16[256,256]{1,0:T(8,128)(2,1)}, u32[]{:S(2)}) copy-start(bf16[256,256]{1,0:T(8,128)(2,1)} %constant.26.clone.sh_ref) | copy-start | bytes 393220
  40.3 5.2 %copy-start.7 = (bf16[256,256]{1,0:T(8,128)(2,1)S(1)}, bf16[256,256]{1,0:T(8,128)(2,1)}, u32[]{:S(2)}) copy-start(bf16[256,256]{1,0:T(8,128)(2,1)} %constant.25.clone.cl_ref) | copy-start | bytes 393220
  40.3 52.5 %all-to-all-start.1 = ((f32[32,128,128]{2,1,0:T(8,128)}), f32[32,128,128]{2,1,0:T(8,128)S(1)}, u32[]{:S(2)}, u32[]{:S(2)}) async-start(f32[32,128,128]{2,1,0:T(8,128)} %bitcast.18), calls=%async_computation.1 | async-start | bytes 4194304 | tf_op jit(solution)/shard_map/all_to_all | solution.py:487
  45.5 0.9 copy-start.8
  54.0 1.3 copy-start
  92.8 1.4 copy-start.1
  94.1 68.9 %copy-start.3 = (f32[256,512]{1,0:T(8,128)S(1)}, f32[256,512]{1,0:T(8,128)}, u32[]{:S(2)}) copy-start(f32[256,512]{1,0:T(8,128)} %constant.29.clone.one_ref) | copy-start | bytes 1572868
  94.2 68.9 %copy-start.4 = (f32[2,16,8,512]{3,2,1,0:T(8,128)S(1)}, f32[2,16,8,512]{3,2,1,0:T(8,128)}, u32[]{:S(2)}) copy-start(f32[2,16,8,512]{3,2,1,0:T(8,128)} %constant.28.clone.both_ref) | copy-start | bytes 1572868
  94.2 68.9 %all-to-all-start.2 = ((f32[32,128,128]{2,1,0:T(8,128)}), f32[32,128,128]{2,1,0:T(8,128)S(1)}, u32[]{:S(2)}, u32[]{:S(2)}) async-start(f32[32,128,128]{2,1,0:T(8,128)} %bitcast.15), calls=%async_computation.2 | async-start | bytes 4194304 | tf_op jit(solution)/shard_map/all_to_all | solution.py:487
  98.4 1.6 copy-start.2
  99.9 0.9 copy-start.9
  107.9 3.6 %collective-permute-start = (f32[2,2,8,8,128]{4,3,2,1,0:T(8,128)S(1)}, f32[2,2,8,8,128]{4,3,2,1,0:T(8,128)S(1)}, u32[]{:S(2)}, u32[]{:S(2)}) collective-permute-start(f32[2,2,8,8,128]{4,3,2,1,0:T(8,128)S(1)} %get-tuple-element.34), channel_id=1, source_target_pairs={{0,1},{1,0},{2,3},{3,2},{4,5},{5,4},{6,7},{7,6},{8,9},{9,8},{10,11... | collective-permute-start | bytes 393224 | tf_op jit(solution)/shard_map/ppermute | solution.py:494
  108.0 9.5 %collective-permute-start.1 = (f32[2,2,8,8,128]{4,3,2,1,0:T(8,128)S(1)}, f32[2,2,8,8,128]{4,3,2,1,0:T(8,128)S(1)}, u32[]{:S(2)}, u32[]{:S(2)}) collective-permute-start(f32[2,2,8,8,128]{4,3,2,1,0:T(8,128)S(1)} %get-tuple-element.35), channel_id=1, source_target_pairs={{0,2},{1,3},{2,0},{3,1},{4,6},{5,7},{6,4},{7,5},{8,10},{9,11},{10,... | collective-permute-start | bytes 393224 | tf_op jit(solution)/shard_map/ppermute | solution.py:494
  109.7 11.3 %collective-permute-start.2 = (f32[2,2,8,8,128]{4,3,2,1,0:T(8,128)S(1)}, f32[2,2,8,8,128]{4,3,2,1,0:T(8,128)S(1)}, u32[]{:S(2)}, u32[]{:S(2)}) collective-permute-start(f32[2,2,8,8,128]{4,3,2,1,0:T(8,128)S(1)} %get-tuple-element.36), channel_id=1, source_target_pairs={{0,3},{1,2},{2,1},{3,0},{4,7},{5,6},{6,5},{7,4},{8,11},{9,10},{10,... | collective-permute-start | bytes 393224 | tf_op jit(solution)/shard_map/ppermute | solution.py:494
  109.8 11.2 %collective-permute-start.3 = (f32[2,2,8,8,128]{4,3,2,1,0:T(8,128)S(1)}, f32[2,2,8,8,128]{4,3,2,1,0:T(8,128)S(1)}, u32[]{:S(2)}, u32[]{:S(2)}) collective-permute-start(f32[2,2,8,8,128]{4,3,2,1,0:T(8,128)S(1)} %get-tuple-element.37), channel_id=1, source_target_pairs={{0,4},{1,5},{2,6},{3,7},{4,0},{5,1},{6,2},{7,3},{8,12},{9,13},{10,... | collective-permute-start | bytes 393224 | tf_op jit(solution)/shard_map/ppermute | solution.py:494
  111.4 15.5 %collective-permute-start.4 = (f32[2,2,8,8,128]{4,3,2,1,0:T(8,128)S(1)}, f32[2,2,8,8,128]{4,3,2,1,0:T(8,128)S(1)}, u32[]{:S(2)}, u32[]{:S(2)}) collective-permute-start(f32[2,2,8,8,128]{4,3,2,1,0:T(8,128)S(1)} %get-tuple-element.38), channel_id=1, source_target_pairs={{0,5},{1,4},{2,7},{3,6},{4,1},{5,0},{6,3},{7,2},{8,13},{9,12},{10,... | collective-permute-start | bytes 393224 | tf_op jit(solution)/shard_map/ppermute | solution.py:494
  111.5 18.9 %collective-permute-start.5 = (f32[2,2,8,8,128]{4,3,2,1,0:T(8,128)S(1)}, f32[2,2,8,8,128]{4,3,2,1,0:T(8,128)S(1)}, u32[]{:S(2)}, u32[]{:S(2)}) collective-permute-start(f32[2,2,8,8,128]{4,3,2,1,0:T(8,128)S(1)} %get-tuple-element.39), channel_id=1, source_target_pairs={{0,6},{1,7},{2,4},{3,5},{4,2},{5,3},{6,0},{7,1},{8,14},{9,15},{10,... | collective-permute-start | bytes 393224 | tf_op jit(solution)/shard_map/ppermute | solution.py:494
  117.5 19.5 %collective-permute-start.6 = (f32[2,2,8,8,128]{4,3,2,1,0:T(8,128)S(1)}, f32[2,2,8,8,128]{4,3,2,1,0:T(8,128)S(1)}, u32[]{:S(2)}, u32[]{:S(2)}) collective-permute-start(f32[2,2,8,8,128]{4,3,2,1,0:T(8,128)S(1)} %get-tuple-element.40), channel_id=1, source_target_pairs={{0,7},{1,6},{2,5},{3,4},{4,3},{5,2},{6,1},{7,0},{8,15},{9,14},{10,... | collective-permute-start | bytes 393224 | tf_op jit(solution)/shard_map/ppermute | solution.py:494
  121.0 16.6 %collective-permute-start.7 = (f32[2,2,8,8,128]{4,3,2,1,0:T(8,128)S(1)}, f32[2,2,8,8,128]{4,3,2,1,0:T(8,128)S(1)}, u32[]{:S(2)}, u32[]{:S(2)}) collective-permute-start(f32[2,2,8,8,128]{4,3,2,1,0:T(8,128)S(1)} %get-tuple-element.41), channel_id=1, source_target_pairs={{0,8},{1,9},{2,10},{3,11},{4,12},{5,13},{6,14},{7,15},{8,0},{9,1},... | collective-permute-start | bytes 393224 | tf_op jit(solution)/shard_map/ppermute | solution.py:494
  121.7 17.6 %collective-permute-start.8 = (f32[2,2,8,8,128]{4,3,2,1,0:T(8,128)S(1)}, f32[2,2,8,8,128]{4,3,2,1,0:T(8,128)S(1)}, u32[]{:S(2)}, u32[]{:S(2)}) collective-permute-start(f32[2,2,8,8,128]{4,3,2,1,0:T(8,128)S(1)} %get-tuple-element.42), channel_id=1, source_target_pairs={{0,9},{1,8},{2,11},{3,10},{4,13},{5,12},{6,15},{7,14},{8,1},{9,0},... | collective-permute-start | bytes 393224 | tf_op jit(solution)/shard_map/ppermute | solution.py:494
  127.5 15.6 %collective-permute-start.9 = (f32[2,2,8,8,128]{4,3,2,1,0:T(8,128)S(1)}, f32[2,2,8,8,128]{4,3,2,1,0:T(8,128)S(1)}, u32[]{:S(2)}, u32[]{:S(2)}) collective-permute-start(f32[2,2,8,8,128]{4,3,2,1,0:T(8,128)S(1)} %get-tuple-element.43), channel_id=1, source_target_pairs={{0,10},{1,11},{2,8},{3,9},{4,14},{5,15},{6,12},{7,13},{8,2},{9,3},... | collective-permute-start | bytes 393224 | tf_op jit(solution)/shard_map/ppermute | solution.py:494
  131.0 18.2 %collective-permute-start.10 = (f32[2,2,8,8,128]{4,3,2,1,0:T(8,128)S(1)}, f32[2,2,8,8,128]{4,3,2,1,0:T(8,128)S(1)}, u32[]{:S(2)}, u32[]{:S(2)}) collective-permute-start(f32[2,2,8,8,128]{4,3,2,1,0:T(8,128)S(1)} %get-tuple-element.44), channel_id=1, source_target_pairs={{0,11},{1,10},{2,9},{3,8},{4,15},{5,14},{6,13},{7,12},{8,3},{9,2},... | collective-permute-start | bytes 393224 | tf_op jit(solution)/shard_map/ppermute | solution.py:494
  137.6 13.8 %collective-permute-start.11 = (f32[2,2,8,8,128]{4,3,2,1,0:T(8,128)S(1)}, f32[2,2,8,8,128]{4,3,2,1,0:T(8,128)S(1)}, u32[]{:S(2)}, u32[]{:S(2)}) collective-permute-start(f32[2,2,8,8,128]{4,3,2,1,0:T(8,128)S(1)} %get-tuple-element.45), channel_id=1, source_target_pairs={{0,12},{1,13},{2,14},{3,15},{4,8},{5,9},{6,10},{7,11},{8,4},{9,5},... | collective-permute-start | bytes 393224 | tf_op jit(solution)/shard_map/ppermute | solution.py:494
  138.2 16.1 %collective-permute-start.12 = (f32[2,2,8,8,128]{4,3,2,1,0:T(8,128)S(1)}, f32[2,2,8,8,128]{4,3,2,1,0:T(8,128)S(1)}, u32[]{:S(2)}, u32[]{:S(2)}) collective-permute-start(f32[2,2,8,8,128]{4,3,2,1,0:T(8,128)S(1)} %get-tuple-element.46), channel_id=1, source_target_pairs={{0,13},{1,12},{2,15},{3,14},{4,9},{5,8},{6,11},{7,10},{8,5},{9,4},... | collective-permute-start | bytes 393224 | tf_op jit(solution)/shard_map/ppermute | solution.py:494
  139.9 19.7 %collective-permute-start.13 = (f32[2,2,8,8,128]{4,3,2,1,0:T(8,128)S(1)}, f32[2,2,8,8,128]{4,3,2,1,0:T(8,128)S(1)}, u32[]{:S(2)}, u32[]{:S(2)}) collective-permute-start(f32[2,2,8,8,128]{4,3,2,1,0:T(8,128)S(1)} %get-tuple-element.47), channel_id=1, source_target_pairs={{0,14},{1,15},{2,12},{3,13},{4,10},{5,11},{6,8},{7,9},{8,6},{9,7},... | collective-permute-start | bytes 393224 | tf_op jit(solution)/shard_map/ppermute | solution.py:494
  143.8 18.6 %collective-permute-start.14 = (f32[2,2,8,8,128]{4,3,2,1,0:T(8,128)S(1)}, f32[2,2,8,8,128]{4,3,2,1,0:T(8,128)S(1)}, u32[]{:S(2)}, u32[]{:S(2)}) collective-permute-start(f32[2,2,8,8,128]{4,3,2,1,0:T(8,128)S(1)} %get-tuple-element.48), channel_id=1, source_target_pairs={{0,15},{1,14},{2,13},{3,12},{4,11},{5,10},{6,9},{7,8},{8,7},{9,6},... | collective-permute-start | bytes 393224 | tf_op jit(solution)/shard_map/ppermute | solution.py:494
  163.0 0.9 copy-start.11
  165.7 0.9 copy-start.17
  (24 other events, 18.4 us)

commit v4 on v3

--- a/solution.py
+++ b/solution.py
@@ -238,7 +238,7 @@
 
 
 def one_middle_kernel(table_ref, mirror_ref, index_ref, ch_ref, cl_ref, sh_ref, sl_ref, x_ref, out_ref, *refs):
-    forward, backward, mid, space, other_space, chi = refs
+    forward, backward, mid, space, other_space, chi, stage, sems = refs
     _, side, _, entries, rows, lanes = space.shape
     plane = 2 * lanes
     groups, _, _, members, _, _ = chi.shape
@@ -265,6 +265,7 @@
                     space[block, x, ri, e] = parts[ri]
                     other_space[block, x, ri, e] = pltpu.roll(parts[ri], rows // 2, 0)
 
+    copies = []
     for group in range(groups):
         for c in range(members):
             left, right = table_ref[group * members + c, 0], table_ref[group * members + c, 1]
@@ -285,7 +286,12 @@
             d = select_dot(value, backward, h)
             for ri in range(2):
                 piece = d[:, :, ri * lanes : (ri + 1) * lanes].reshape(side, members, rows, lanes)
-                out_ref[:, h, ri, group * members : (group + 1) * members] = piece
+                stage[group, :, h, ri] = piece
+        target = out_ref.at[:, :, :, pl.ds(group * members, members)]
+        copies.append(pltpu.make_async_copy(stage.at[group], target, sems.at[group]))
+        copies[-1].start()
+    for copy in copies:
+        copy.wait()
 
 
 def both_middle_kernel(me_ref, table_ref, mirror_ref, index_ref, ch_ref, cl_ref, sh_ref, sl_ref, x_ref, *refs):
@@ -388,7 +394,7 @@
     out = pl.pallas_call(
         one_middle_kernel,
         in_specs=specs,
-        out_specs=pl.BlockSpec(memory_space=pltpu.VMEM),
+        out_specs=pl.BlockSpec(memory_space=pltpu.HBM),
         out_shape=jax.ShapeDtypeStruct(shape, jnp.float32),
         scratch_shapes=[
             matrices,
@@ -397,8 +403,10 @@
             spatial,
             spatial,
             pltpu.VMEM((GROUPS, 2, side, components // GROUPS, rows, 2 * lanes), jnp.float32),
+            pltpu.VMEM((GROUPS, side, 2, 2, components // GROUPS, rows, lanes), jnp.float32),
+            pltpu.SemaphoreType.DMA((GROUPS,)),
         ],
-        compiler_params=pltpu.CompilerParams(vmem_limit_bytes=28 << 20),
+        compiler_params=pltpu.CompilerParams(vmem_limit_bytes=61 << 20),
         name="one_middle",
     )(*args)
     return out.reshape((devices,) + shape[2:])
@@ -421,21 +429,19 @@
             pltpu.VMEM((halves, 2, side, 2, entries, rows, lanes), jnp.float32),
             pltpu.VMEM((halves * GROUPS, 2, near // 2, members, rows, 2 * lanes), jnp.float32),
         ],
-        compiler_params=pltpu.CompilerParams(vmem_limit_bytes=28 << 20),
+        compiler_params=pltpu.CompilerParams(vmem_limit_bytes=60 << 20),
         name="both_middle",
     )(me, *args)
 
 
-def frequency_kernel(me_ref, both_ref, one_ref, y_ref, *refs):
+def both_frequency_kernel(me_ref, m_ref, *refs):
     pieces, (out_ref, stage, sems) = refs[:-3], refs[-3:]
     near = len(pieces)
-    devices, _, components, rows, lanes = y_ref.shape
+    components, lanes = stage.shape[1:3]
     groups = sems.shape[0]
     members = components // groups
     me = me_ref[0] % near
-    both = [both_ref[part, slot ^ me] for part in range(2) for slot in range(near)]
-    matrix = split_value(jnp.concatenate(both + [one_ref[...]], axis=0))
-    upper_rows = lax.broadcasted_iota(jnp.int32, (devices, rows, lanes), 1) < rows // 2
+    matrix = split_value(jnp.concatenate([m_ref[part, slot ^ me] for part in range(2) for slot in range(near)], axis=0))
 
     def gathered(half, ri, c):
         return jnp.concatenate([piece[half, ri, c] for piece in pieces], axis=0)
@@ -447,15 +453,8 @@
             part = [[gathered(half, ri, c) for ri in range(2)] for half in range(2)]
             sums = [part[0][ri] + part[1][ri] for ri in range(2)]
             differences = [part[0][ri] - part[1][ri] for ri in range(2)]
-            folded = []
-            for ri in range(2):
-                tile = y_ref[:, ri, c]
-                turned = pltpu.roll(tile, rows // 2, 1)
-                folded.append((tile + turned, turned - tile))
-            first = jnp.where(upper_rows, folded[0][0], -folded[1][1]).reshape(devices * rows, lanes)
-            second = jnp.where(upper_rows, folded[1][0], folded[0][1]).reshape(devices * rows, lanes)
-            values.append(jnp.concatenate([sums[0], -differences[1], first], axis=0).T)
-            values.append(jnp.concatenate([sums[1], differences[0], second], axis=0).T)
+            values.append(jnp.concatenate([sums[0], -differences[1]], axis=0).T)
+            values.append(jnp.concatenate([sums[1], differences[0]], axis=0).T)
         d = dot3(split_value(jnp.concatenate(values, axis=0)), matrix, ((1,), (0,)))
         d = d.reshape(members, 2, lanes, d.shape[1])
         for ri in range(2):
@@ -467,19 +466,77 @@
         copy.wait()
 
 
-def to_frequencies(y, pieces, both, one, me):
-    _, _, components, _, lanes = y.shape
-    shape = (2, components, lanes, one.shape[1])
+def both_frequencies(pieces, matrix, me):
+    _, _, components, _, lanes = pieces[0].shape
+    shape = (2, components, lanes, matrix.shape[3])
     vmem = pl.BlockSpec(memory_space=pltpu.VMEM)
     return pl.pallas_call(
-        frequency_kernel,
-        in_specs=[pl.BlockSpec(memory_space=pltpu.SMEM)] + [vmem] * (3 + len(pieces)),
+        both_frequency_kernel,
+        in_specs=[pl.BlockSpec(memory_space=pltpu.SMEM)] + [vmem] * (1 + len(pieces)),
         out_specs=pl.BlockSpec(memory_space=pltpu.HBM),
         out_shape=jax.ShapeDtypeStruct(shape, jnp.float32),
         scratch_shapes=[pltpu.VMEM(shape, jnp.float32), pltpu.SemaphoreType.DMA((components // 2,))],
-        compiler_params=pltpu.CompilerParams(vmem_limit_bytes=28 << 20),
-        name="to_frequencies",
-    )(me, both, one, y, *pieces)
+        compiler_params=pltpu.CompilerParams(vmem_limit_bytes=60 << 20),
+        name="both_frequencies",
+    )(me, matrix, *pieces)
+
+
+def one_frequency_kernel(y_ref, m_ref, earlier_hbm, out_ref, earlier, stage, in_sems, sems):
+    devices, _, components, rows, lanes = y_ref.shape
+    groups = sems.shape[0]
+    members = components // groups
+    cuts = [pl.ds(group * members, members) for group in range(groups)]
+    loads = [
+        pltpu.make_async_copy(earlier_hbm.at[:, cut], earlier.at[:, cut], in_sems.at[group])
+        for group, cut in enumerate(cuts)
+    ]
+    for copy in loads:
+        copy.start()
+    matrix = split_value(m_ref[...])
+    upper_rows = lax.broadcasted_iota(jnp.int32, (devices, rows, lanes), 1) < rows // 2
+    copies = []
+    for group, cut in enumerate(cuts):
+        values = []
+        for c in range(group * members, (group + 1) * members):
+            folded = []
+            for ri in range(2):
+                tile = y_ref[:, ri, c]
+                turned = pltpu.roll(tile, rows // 2, 1)
+                folded.append((tile + turned, turned - tile))
+            first = jnp.where(upper_rows, folded[0][0], -folded[1][1])
+            second = jnp.where(upper_rows, folded[1][0], folded[0][1])
+            values.append(first.reshape(devices * rows, lanes).T)
+            values.append(second.reshape(devices * rows, lanes).T)
+        d = dot3(split_value(jnp.concatenate(values, axis=0)), matrix, ((1,), (0,)))
+        d = d.reshape(members, 2, lanes, d.shape[1])
+        loads[group].wait()
+        for ri in range(2):
+            own = slice(group * members, (group + 1) * members)
+            stage[ri, own] = earlier[ri, own] + d[:, ri]
+        copies.append(pltpu.make_async_copy(stage.at[:, cut], out_ref.at[:, cut], sems.at[group]))
+        copies[-1].start()
+    for copy in copies:
+        copy.wait()
+
+
+def one_frequencies(y, matrix, earlier):
+    vmem = pl.BlockSpec(memory_space=pltpu.VMEM)
+    hbm = pl.BlockSpec(memory_space=pltpu.HBM)
+    groups = earlier.shape[1] // 2
+    return pl.pallas_call(
+        one_frequency_kernel,
+        in_specs=[vmem, vmem, hbm],
+        out_specs=hbm,
+        out_shape=jax.ShapeDtypeStruct(earlier.shape, jnp.float32),
+        scratch_shapes=[
+            pltpu.VMEM(earlier.shape, jnp.float32),
+            pltpu.VMEM(earlier.shape, jnp.float32),
+            pltpu.SemaphoreType.DMA((groups,)),
+            pltpu.SemaphoreType.DMA((groups,)),
+        ],
+        compiler_params=pltpu.CompilerParams(vmem_limit_bytes=60 << 20),
+        name="one_frequencies",
+    )(y, matrix, earlier)
 
 
 def exchange(x):
@@ -632,15 +689,17 @@
     one_boson = boson_matrix(rows.reshape(-1), count).reshape(2, devices, half, count).swapaxes(0, 1)
     one_boson = one_boson.reshape(devices * ROWS, count).astype(np.float32)
 
+    shape = (near, 2, 2, entries, ROWS, lanes)
+    both = to_times(both_times_kernel, green, jnp.asarray(both_fermion), shape, devices, "both_times")
+    green, both = lax.optimization_barrier((green, both))
     shape = (devices, 2, entries, ROWS, lanes)
     one = to_times(one_times_kernel, green, jnp.asarray(one_fermion), shape, devices, "one_times")
-    green, one = lax.optimization_barrier((green, one))
-    shape = (near, 2, 2, entries, ROWS, lanes)
-    both = to_times(both_times_kernel, green, jnp.asarray(both_fermion), shape, devices, "both_times")
-    one, both = lax.optimization_barrier((exchange(one), both))
-    one, both = lax.optimization_barrier((one_middle(one, pair_table, mirror_map), exchange(both)))
-    pieces = swap(both_middle(both, pair_table, mirror_map, me, near), devices)
-    return to_frequencies(exchange(one), pieces, jnp.asarray(both_boson), jnp.asarray(one_boson), me)
+    both, one = lax.optimization_barrier((exchange(both), one))
+    pieces = list(both_middle(both, pair_table, mirror_map, me, near))
+    one, pieces[0] = lax.optimization_barrier((exchange(one), pieces[0]))
+    one = exchange(one_middle(one, pair_table, mirror_map))
+    earlier = both_frequencies(swap(pieces, devices), jnp.asarray(both_boson), me)
+    return one_frequencies(one, jnp.asarray(one_boson), earlier)
 
 
 def solution(mesh):

time: 180 us -> 184 us (1.022)
  local copies, waits for them, and re-layouts: 27.1 us -> 4.45 us
  waiting for transfers between devices: 79.5 us -> 101 us
  Pallas kernels: 30.2 us -> 41.1 us
  starting transfers between devices: 41.6 us -> 35.9 us
    unnamed x77 -> x61, local copies, waits for them, and re-layouts: 26.4 us -> 3.77 us
    ppermute x15, waiting for transfers between devices: 20.8 us -> 43.4 us  [swap(): moved.append(lax.ppermute(pieces[slot], 'kb', pairs))]
    pallas_call x1 -> x2, Pallas kernels: 4.59 us -> 11 us  [the longest x1 6.36 us: one_frequencies(): pl.pallas_call(one_frequency_kernel, in_specs=[vmem, vmem, hbm], out_spec...]
    ppermute x15, starting transfers between devices: 26.5 us -> 20.5 us  [swap(): moved.append(lax.ppermute(pieces[slot], 'kb', pairs))]
    pallas_call x1, Pallas kernels: 6.38 us -> 9 us  [both_middle(): pl.pallas_call(both_middle_kernel, in_specs=[pl.BlockSpec(memory_space=pl...]
    pallas_call x1, Pallas kernels: 7.58 us -> 9.52 us  [one_middle(): pl.pallas_call(one_middle_kernel, in_specs=specs, out_specs=pl.BlockSpec(...]
  transfers between devices with their start and end apart: 18 -> 18, of which waited for: 11 -> 14; matrix products, arithmetic and copies ran while one was open for 1% -> 1% of each run, Pallas kernels for 11% -> 11%
where the time goes in v4:
time: 184 us; the launch traced here: 183 us
  waiting for transfers between devices  101 us (55%)
  Pallas kernels  41.1 us (22%)
  starting transfers between devices  35.9 us (20%)
  local copies, waits for them, and re-layouts  4.45 us (2%)
    all_to_all x3, waiting for transfers between devices, exchange(): lax.all_to_all(flat, 'kb', split_axis=0, concat_axis=0, tiled=True)  57.8 us
    ppermute x15, waiting for transfers between devices, swap(): moved.append(lax.ppermute(pieces[slot], 'kb', pairs))  43.4 us
    ppermute x15, starting transfers between devices, swap(): moved.append(lax.ppermute(pieces[slot], 'kb', pairs))  20.5 us
    all_to_all x3, starting transfers between devices, exchange(): lax.all_to_all(flat, 'kb', split_axis=0, concat_axis=0, tiled=True)  15.3 us
    pallas_call x2, Pallas kernels, to_times(): pl.pallas_call(kernel, in_specs=[hbm, hbm], out_specs=hbm, out_shape=jax....  11.6 us
    pallas_call x1, Pallas kernels, one_middle(): pl.pallas_call(one_middle_kernel, in_specs=specs, out_specs=pl.BlockSpec(...  9.52 us
    pallas_call x1, Pallas kernels, both_middle(): pl.pallas_call(both_middle_kernel, in_specs=[pl.BlockSpec(memory_space=pl...  9 us
    pallas_call x1, Pallas kernels, one_frequencies(): pl.pallas_call(one_frequency_kernel, in_specs=[vmem, vmem, hbm], out_spec...  6.36 us
  transfers between devices with their start and end apart: 18, of which 14 were waited for; matrix products, arithmetic and copies ran while one was open for 1% of the time, Pallas kernels for 11%

profile of v4, /device:TPU:0, one launch (start us, length us, event | category | flops | bytes accessed | tf_op | source)
XLA Modules:
  0.0 183.2 jit_solution(5690428272712673096)
XLA Ops:
  0.0 4.9 %both_times.1 = f32[32,2,2,4,8,128]{5,4,3,2,1,0:T(8,128)} custom-call(f32[2,4,128,512]{3,2,1,0:T(8,128)} %g_hbm.2, f32[256,512]{1,0:T(8,128)} %constant.22.clone.m_hbm), custom_call_target="tpu_custom_call" | custom-call | tf_op jit(solution)/shard_map/both_times/pallas_call | solution.py:186
  4.9 7.3 %all-to-all-start = ((f32[32,128,128]{2,1,0:T(8,128)}), f32[32,128,128]{2,1,0:T(8,128)S(1)}, u32[]{:S(2)}, u32[]{:S(2)}) async-start(f32[32,128,128]{2,1,0:T(8,128)} %bitcast.15), calls=%async_computation | async-start | bytes 4194304 | tf_op jit(solution)/shard_map/all_to_all | solution.py:544
  12.2 6.7 %one_times.1 = f32[32,2,4,8,128]{4,3,2,1,0:T(8,128)} custom-call(f32[2,4,128,512]{3,2,1,0:T(8,128)} %g_hbm.2, f32[512,512]{1,0:T(8,128)} %constant.23.clone.m_hbm), custom_call_target="tpu_custom_call" | custom-call | tf_op jit(solution)/shard_map/one_times/pallas_call | solution.py:186
  19.0 42.1 %all-to-all-done = f32[32,128,128]{2,1,0:T(8,128)S(1)} async-done(((f32[32,128,128]{2,1,0:T(8,128)}), f32[32,128,128]{2,1,0:T(8,128)S(1)}, u32[]{:S(2)}, u32[]{:S(2)}) %all-to-all-start) | async-done | bytes 2097184 | tf_op jit(solution)/shard_map/all_to_all | solution.py:544
  61.1 4.2 %all-to-all-start.1 = ((f32[32,64,128]{2,1,0:T(8,128)}), f32[32,64,128]{2,1,0:T(8,128)S(1)}, u32[]{:S(2)}, u32[]{:S(2)}) async-start(f32[32,64,128]{2,1,0:T(8,128)} %bitcast.18), calls=%async_computation.1 | async-start | bytes 2097152 | tf_op jit(solution)/shard_map/all_to_all | solution.py:544
  66.8 9.0 %both_middle.1 = (f32[2,2,8,8,128]{4,3,2,1,0:T(8,128)}, f32[2,2,8,8,128]{4,3,2,1,0:T(8,128)}, f32[2,2,8,8,128]{4,3,2,1,0:T(8,128)}, f32[2,2,8,8,128]{4,3,2,1,0:T...) custom-call(s32[1]{0:T(128)} %bitcast.6.me_ref, ...), custom_call_target="tpu_custom_call" | custom-call | tf_op jit(solution)/shard_map/both_middle/pallas_call | solution.py:420
  75.8 15.6 %all-to-all-done.1 = f32[32,64,128]{2,1,0:T(8,128)S(1)} async-done(((f32[32,64,128]{2,1,0:T(8,128)}), f32[32,64,128]{2,1,0:T(8,128)S(1)}, u32[]{:S(2)}, u32[]{:S(2)}) %all-to-all-start.1) | async-done | bytes 1048608 | tf_op jit(solution)/shard_map/all_to_all | solution.py:544
  91.4 1.0 copy-done.2
  92.4 9.5 %one_middle.1 = f32[16,2,2,8,8,128]{5,4,3,2,1,0:T(8,128)} custom-call(s32[8,2]{1,0:T(8,128)} %copy.17.table_ref, s32[3,16]{1,0:T(4,128)} %mirror_ref.3, s32[1,256]{1,0:T(1,128)} %add.36.index_ref, bf16[256,256]{1,0:T(8,128)(2,1)} %constant.24.clone.ch_ref, bf16[256,256]{1,0:T(8,128)(2,1)} %constant.25.clone.cl_ref, bf16[256,256]{1,0:T(8,128)(2,1)} %constant.26.clone.sh_ref, ...), custom_call_target="tpu_custom_call" | custom-call | tf_op jit(solution)/shard_map/one_middle/pallas_call | solution.py:394
  102.0 3.9 %all-to-all-start.2 = ((f32[32,128,128]{2,1,0:T(8,128)}), f32[32,128,128]{2,1,0:T(8,128)S(1)}, u32[]{:S(2)}, u32[]{:S(2)}) async-start(f32[32,128,128]{2,1,0:T(8,128)} %bitcast.13), calls=%async_computation.2 | async-start | bytes 4194304 | tf_op jit(solution)/shard_map/all_to_all | solution.py:544
  106.0 1.7 collective-permute-start.1
  107.8 1.5 collective-permute-start.3
  109.5 2.6 %collective-permute-start.5 = (f32[2,2,8,8,128]{4,3,2,1,0:T(8,128)S(1)}, f32[2,2,8,8,128]{4,3,2,1,0:T(8,128)S(1)}, u32[]{:S(2)}, u32[]{:S(2)}) collective-permute-start(f32[2,2,8,8,128]{4,3,2,1,0:T(8,128)S(1)} %copy-done.24), channel_id=1, source_target_pairs={{0,6},{1,7},{2,4},{3,5},{4,2},{5,3},{6,0},{7,1},{8,14},{9,15},{10,... | collective-permute-start | bytes 393224 | tf_op jit(solution)/shard_map/ppermute | solution.py:551
  112.1 12.9 %collective-permute-done.1.refs_2_ = f32[2,2,8,8,128]{4,3,2,1,0:T(8,128)S(1)} collective-permute-done((f32[2,2,8,8,128]{4,3,2,1,0:T(8,128)S(1)}, f32[2,2,8,8,128]{4,3,2,1,0:T(8,128)S(1)}, u32[]{:S(2)}, u32[]{:S(2)}) %collective-permute-start.1) | collective-permute-done | bytes 131104 | tf_op jit(solution)/shard_map/ppermute | solution.py:551
  125.4 4.5 %collective-permute-done.2.refs_3_ = f32[2,2,8,8,128]{4,3,2,1,0:T(8,128)S(1)} collective-permute-done((f32[2,2,8,8,128]{4,3,2,1,0:T(8,128)S(1)}, f32[2,2,8,8,128]{4,3,2,1,0:T(8,128)S(1)}, u32[]{:S(2)}, u32[]{:S(2)}) %collective-permute-start.2) | collective-permute-done | bytes 131104 | tf_op jit(solution)/shard_map/ppermute | solution.py:551
  129.9 3.9 %collective-permute-start.8 = (f32[2,2,8,8,128]{4,3,2,1,0:T(8,128)S(1)}, f32[2,2,8,8,128]{4,3,2,1,0:T(8,128)S(1)}, u32[]{:S(2)}, u32[]{:S(2)}) collective-permute-start(f32[2,2,8,8,128]{4,3,2,1,0:T(8,128)S(1)} %copy-done.21), channel_id=1, source_target_pairs={{0,9},{1,8},{2,11},{3,10},{4,13},{5,12},{6,15},{7,14},{8,1},{9,0},... | collective-permute-start | bytes 393224 | tf_op jit(solution)/shard_map/ppermute | solution.py:551
  134.0 3.8 %collective-permute-done.5.refs_6_ = f32[2,2,8,8,128]{4,3,2,1,0:T(8,128)S(1)} collective-permute-done((f32[2,2,8,8,128]{4,3,2,1,0:T(8,128)S(1)}, f32[2,2,8,8,128]{4,3,2,1,0:T(8,128)S(1)}, u32[]{:S(2)}, u32[]{:S(2)}) %collective-permute-start.5) | collective-permute-done | bytes 131104 | tf_op jit(solution)/shard_map/ppermute | solution.py:551
  137.8 2.2 %collective-permute-done.6.refs_7_ = f32[2,2,8,8,128]{4,3,2,1,0:T(8,128)S(1)} collective-permute-done((f32[2,2,8,8,128]{4,3,2,1,0:T(8,128)S(1)}, f32[2,2,8,8,128]{4,3,2,1,0:T(8,128)S(1)}, u32[]{:S(2)}, u32[]{:S(2)}) %collective-permute-start.6) | collective-permute-done | bytes 131104 | tf_op jit(solution)/shard_map/ppermute | solution.py:551
  139.9 2.5 %collective-permute-start.11 = (f32[2,2,8,8,128]{4,3,2,1,0:T(8,128)}, f32[2,2,8,8,128]{4,3,2,1,0:T(8,128)S(1)}, u32[]{:S(2)}, u32[]{:S(2)}) collective-permute-start(f32[2,2,8,8,128]{4,3,2,1,0:T(8,128)} %get-tuple-element.45), channel_id=1, source_target_pairs={{0,12},{1,13},{2,14},{3,15},{4,8},{5,9},{6,10},{7,11},{8,4},{9,5},... | collective-permute-start | bytes 393224 | tf_op jit(solution)/shard_map/ppermute | solution.py:551
  142.5 1.5 collective-permute-done.7.refs_8_
  143.9 2.0 %collective-permute-start.12 = (f32[2,2,8,8,128]{4,3,2,1,0:T(8,128)}, f32[2,2,8,8,128]{4,3,2,1,0:T(8,128)S(1)}, u32[]{:S(2)}, u32[]{:S(2)}) collective-permute-start(f32[2,2,8,8,128]{4,3,2,1,0:T(8,128)} %get-tuple-element.46), channel_id=1, source_target_pairs={{0,13},{1,12},{2,15},{3,14},{4,9},{5,8},{6,11},{7,10},{8,5},{9,4},... | collective-permute-start | bytes 393224 | tf_op jit(solution)/shard_map/ppermute | solution.py:551
  145.9 0.8 collective-permute-done.8.refs_9_
  146.7 3.2 %collective-permute-start.13 = (f32[2,2,8,8,128]{4,3,2,1,0:T(8,128)}, f32[2,2,8,8,128]{4,3,2,1,0:T(8,128)S(1)}, u32[]{:S(2)}, u32[]{:S(2)}) collective-permute-start(f32[2,2,8,8,128]{4,3,2,1,0:T(8,128)} %get-tuple-element.47), channel_id=1, source_target_pairs={{0,14},{1,15},{2,12},{3,13},{4,10},{5,11},{6,8},{7,9},{8,6},{9,7},... | collective-permute-start | bytes 393224 | tf_op jit(solution)/shard_map/ppermute | solution.py:551
  150.2 2.3 %collective-permute-start.14 = (f32[2,2,8,8,128]{4,3,2,1,0:T(8,128)}, f32[2,2,8,8,128]{4,3,2,1,0:T(8,128)S(1)}, u32[]{:S(2)}, u32[]{:S(2)}) collective-permute-start(f32[2,2,8,8,128]{4,3,2,1,0:T(8,128)} %get-tuple-element.48), channel_id=1, source_target_pairs={{0,15},{1,14},{2,13},{3,12},{4,11},{5,10},{6,9},{7,8},{8,7},{9,6},... | collective-permute-start | bytes 393224 | tf_op jit(solution)/shard_map/ppermute | solution.py:551
  152.4 4.1 %collective-permute-done.10.refs_11_ = f32[2,2,8,8,128]{4,3,2,1,0:T(8,128)S(1)} collective-permute-done((f32[2,2,8,8,128]{4,3,2,1,0:T(8,128)}, f32[2,2,8,8,128]{4,3,2,1,0:T(8,128)S(1)}, u32[]{:S(2)}, u32[]{:S(2)}) %collective-permute-start.10) | collective-permute-done | bytes 131104 | tf_op jit(solution)/shard_map/ppermute | solution.py:551
  156.5 2.3 %collective-permute-done.11.refs_12_ = f32[2,2,8,8,128]{4,3,2,1,0:T(8,128)S(1)} collective-permute-done((f32[2,2,8,8,128]{4,3,2,1,0:T(8,128)}, f32[2,2,8,8,128]{4,3,2,1,0:T(8,128)S(1)}, u32[]{:S(2)}, u32[]{:S(2)}) %collective-permute-start.11) | collective-permute-done | bytes 131104 | tf_op jit(solution)/shard_map/ppermute | solution.py:551
  158.9 2.9 %collective-permute-done.12.refs_13_ = f32[2,2,8,8,128]{4,3,2,1,0:T(8,128)S(1)} collective-permute-done((f32[2,2,8,8,128]{4,3,2,1,0:T(8,128)}, f32[2,2,8,8,128]{4,3,2,1,0:T(8,128)S(1)}, u32[]{:S(2)}, u32[]{:S(2)}) %collective-permute-start.12) | collective-permute-done | bytes 131104 | tf_op jit(solution)/shard_map/ppermute | solution.py:551
  161.8 5.2 %collective-permute-done.13.refs_14_ = f32[2,2,8,8,128]{4,3,2,1,0:T(8,128)S(1)} collective-permute-done((f32[2,2,8,8,128]{4,3,2,1,0:T(8,128)}, f32[2,2,8,8,128]{4,3,2,1,0:T(8,128)S(1)}, u32[]{:S(2)}, u32[]{:S(2)}) %collective-permute-start.13) | collective-permute-done | bytes 131104 | tf_op jit(solution)/shard_map/ppermute | solution.py:551
  167.0 2.8 %collective-permute-done.14.refs_15_ = f32[2,2,8,8,128]{4,3,2,1,0:T(8,128)S(1)} collective-permute-done((f32[2,2,8,8,128]{4,3,2,1,0:T(8,128)}, f32[2,2,8,8,128]{4,3,2,1,0:T(8,128)S(1)}, u32[]{:S(2)}, u32[]{:S(2)}) %collective-permute-start.14) | collective-permute-done | bytes 131104 | tf_op jit(solution)/shard_map/ppermute | solution.py:551
  170.6 4.6 %both_frequencies.1.earlier_hbm = f32[2,8,128,512]{3,2,1,0:T(8,128)} custom-call(s32[1]{0:T(128)} %bitcast.6.me_ref, f32[2,16,8,512]{3,2,1,0:T(8,128)} %constant.28.clone.m_ref, f32[2,2,8,8,128]{4,3,2,1,0:T(8,128)} %get-tuple-element.33.refs_0_, f32[2,2,8,8,128]{4,3,2,1,0:T(8,128)} %copy-done.3, f32[2,2,8,8,128]{4,3,2,1,0:T(8,128)} %copy-done.4, ...), custom_call_target="tpu_custom_call" | custom-call | tf_op jit(solution)/shard_map/both_frequencies/pallas_call | solution.py:473
  175.3 1.4 copy-done.1
  176.6 6.4 %one_frequencies.1 = f32[2,8,128,512]{3,2,1,0:T(8,128)} custom-call(f32[32,2,8,8,128]{4,3,2,1,0:T(8,128)} %bitcast.16, f32[256,512]{1,0:T(8,128)} %constant.29.clone.m_ref, f32[2,8,128,512]{3,2,1,0:T(8,128)} %both_frequencies.1.earlier_hbm), custom_call_target="tpu_custom_call" | custom-call | tf_op jit(solution)/shard_map/one_frequencies/pallas_call | solution.py:526
  (74 shorter events, 3.2 us)
Async XLA Ops:
  4.9 56.2 %all-to-all-start = ((f32[32,128,128]{2,1,0:T(8,128)}), f32[32,128,128]{2,1,0:T(8,128)S(1)}, u32[]{:S(2)}, u32[]{:S(2)}) async-start(f32[32,128,128]{2,1,0:T(8,128)} %bitcast.15), calls=%async_computation | async-start | bytes 4194304 | tf_op jit(solution)/shard_map/all_to_all | solution.py:544
  19.0 46.4 %copy-start.19 = (s32[8,2]{0,1:T(2,128)S(1)}, s32[8,2]{0,1:T(2,128)}, u32[]{:S(2)}) copy-start(s32[8,2]{0,1:T(2,128)} %param.16) | copy-start | bytes 196
  19.0 47.0 %copy-start.18 = (s32[3,16]{1,0:T(4,128)S(1)}, s32[3,16]{1,0:T(4,128)}, u32[]{:S(2)}) copy-start(s32[3,16]{1,0:T(4,128)} %mirror_ref.3) | copy-start | bytes 580
  61.1 30.3 %all-to-all-start.1 = ((f32[32,64,128]{2,1,0:T(8,128)}), f32[32,64,128]{2,1,0:T(8,128)S(1)}, u32[]{:S(2)}, u32[]{:S(2)}) async-start(f32[32,64,128]{2,1,0:T(8,128)} %bitcast.18), calls=%async_computation.1 | async-start | bytes 2097152 | tf_op jit(solution)/shard_map/all_to_all | solution.py:544
  102.0 27.9 %copy-start.22 = (f32[2,2,8,8,128]{4,3,2,1,0:T(8,128)S(1)}, f32[2,2,8,8,128]{4,3,2,1,0:T(8,128)}, u32[]{:S(2)}) copy-start(f32[2,2,8,8,128]{4,3,2,1,0:T(8,128)} %get-tuple-element.41) | copy-start | bytes 393220
  102.0 27.9 %copy-start.21 = (f32[2,2,8,8,128]{4,3,2,1,0:T(8,128)S(1)}, f32[2,2,8,8,128]{4,3,2,1,0:T(8,128)}, u32[]{:S(2)}) copy-start(f32[2,2,8,8,128]{4,3,2,1,0:T(8,128)} %get-tuple-element.42) | copy-start | bytes 393220
  102.0 31.9 %copy-start.20 = (f32[2,2,8,8,128]{4,3,2,1,0:T(8,128)S(1)}, f32[2,2,8,8,128]{4,3,2,1,0:T(8,128)}, u32[]{:S(2)}) copy-start(f32[2,2,8,8,128]{4,3,2,1,0:T(8,128)} %get-tuple-element.43) | copy-start | bytes 393220
  102.0 73.2 %all-to-all-start.2 = ((f32[32,128,128]{2,1,0:T(8,128)}), f32[32,128,128]{2,1,0:T(8,128)S(1)}, u32[]{:S(2)}, u32[]{:S(2)}) async-start(f32[32,128,128]{2,1,0:T(8,128)} %bitcast.13), calls=%async_computation.2 | async-start | bytes 4194304 | tf_op jit(solution)/shard_map/all_to_all | solution.py:544
  105.9 3.7 %collective-permute-start = (f32[2,2,8,8,128]{4,3,2,1,0:T(8,128)S(1)}, f32[2,2,8,8,128]{4,3,2,1,0:T(8,128)S(1)}, u32[]{:S(2)}, u32[]{:S(2)}) collective-permute-start(f32[2,2,8,8,128]{4,3,2,1,0:T(8,128)S(1)} %copy-done.29), channel_id=1, source_target_pairs={{0,1},{1,0},{2,3},{3,2},{4,5},{5,4},{6,7},{7,6},{8,9},{9,8},{10,11... | collective-permute-start | bytes 393224 | tf_op jit(solution)/shard_map/ppermute | solution.py:551
  106.0 19.1 %collective-permute-start.1 = (f32[2,2,8,8,128]{4,3,2,1,0:T(8,128)S(1)}, f32[2,2,8,8,128]{4,3,2,1,0:T(8,128)S(1)}, u32[]{:S(2)}, u32[]{:S(2)}) collective-permute-start(f32[2,2,8,8,128]{4,3,2,1,0:T(8,128)S(1)} %copy-done.28), channel_id=1, source_target_pairs={{0,2},{1,3},{2,0},{3,1},{4,6},{5,7},{6,4},{7,5},{8,10},{9,11},{10,... | collective-permute-start | bytes 393224 | tf_op jit(solution)/shard_map/ppermute | solution.py:551
  107.7 22.2 %collective-permute-start.2 = (f32[2,2,8,8,128]{4,3,2,1,0:T(8,128)S(1)}, f32[2,2,8,8,128]{4,3,2,1,0:T(8,128)S(1)}, u32[]{:S(2)}, u32[]{:S(2)}) collective-permute-start(f32[2,2,8,8,128]{4,3,2,1,0:T(8,128)S(1)} %copy-done.27), channel_id=1, source_target_pairs={{0,3},{1,2},{2,1},{3,0},{4,7},{5,6},{6,5},{7,4},{8,11},{9,10},{10,... | collective-permute-start | bytes 393224 | tf_op jit(solution)/shard_map/ppermute | solution.py:551
  107.8 22.1 %collective-permute-start.3 = (f32[2,2,8,8,128]{4,3,2,1,0:T(8,128)S(1)}, f32[2,2,8,8,128]{4,3,2,1,0:T(8,128)S(1)}, u32[]{:S(2)}, u32[]{:S(2)}) collective-permute-start(f32[2,2,8,8,128]{4,3,2,1,0:T(8,128)S(1)} %copy-done.26), channel_id=1, source_target_pairs={{0,4},{1,5},{2,6},{3,7},{4,0},{5,1},{6,2},{7,3},{8,12},{9,13},{10,... | collective-permute-start | bytes 393224 | tf_op jit(solution)/shard_map/ppermute | solution.py:551
  109.4 24.5 %collective-permute-start.4 = (f32[2,2,8,8,128]{4,3,2,1,0:T(8,128)S(1)}, f32[2,2,8,8,128]{4,3,2,1,0:T(8,128)S(1)}, u32[]{:S(2)}, u32[]{:S(2)}) collective-permute-start(f32[2,2,8,8,128]{4,3,2,1,0:T(8,128)S(1)} %copy-done.25), channel_id=1, source_target_pairs={{0,5},{1,4},{2,7},{3,6},{4,1},{5,0},{6,3},{7,2},{8,13},{9,12},{10,... | collective-permute-start | bytes 393224 | tf_op jit(solution)/shard_map/ppermute | solution.py:551
  109.5 60.3 %copy-start.3 = (f32[2,2,8,8,128]{4,3,2,1,0:T(8,128)}, f32[2,2,8,8,128]{4,3,2,1,0:T(8,128)S(1)}, u32[]{:S(2)}) copy-start(f32[2,2,8,8,128]{4,3,2,1,0:T(8,128)S(1)} %collective-permute-done.refs_1_) | copy-start | bytes 393220
  109.5 28.2 %collective-permute-start.5 = (f32[2,2,8,8,128]{4,3,2,1,0:T(8,128)S(1)}, f32[2,2,8,8,128]{4,3,2,1,0:T(8,128)S(1)}, u32[]{:S(2)}, u32[]{:S(2)}) collective-permute-start(f32[2,2,8,8,128]{4,3,2,1,0:T(8,128)S(1)} %copy-done.24), channel_id=1, source_target_pairs={{0,6},{1,7},{2,4},{3,5},{4,2},{5,3},{6,0},{7,1},{8,14},{9,15},{10,... | collective-permute-start | bytes 393224 | tf_op jit(solution)/shard_map/ppermute | solution.py:551
  125.0 44.8 %copy-start.4 = (f32[2,2,8,8,128]{4,3,2,1,0:T(8,128)}, f32[2,2,8,8,128]{4,3,2,1,0:T(8,128)S(1)}, u32[]{:S(2)}) copy-start(f32[2,2,8,8,128]{4,3,2,1,0:T(8,128)S(1)} %collective-permute-done.1.refs_2_) | copy-start | bytes 393220
  125.0 14.9 %collective-permute-start.6 = (f32[2,2,8,8,128]{4,3,2,1,0:T(8,128)S(1)}, f32[2,2,8,8,128]{4,3,2,1,0:T(8,128)S(1)}, u32[]{:S(2)}, u32[]{:S(2)}) collective-permute-start(f32[2,2,8,8,128]{4,3,2,1,0:T(8,128)S(1)} %copy-done.23), channel_id=1, source_target_pairs={{0,7},{1,6},{2,5},{3,4},{4,3},{5,2},{6,1},{7,0},{8,15},{9,14},{10,... | collective-permute-start | bytes 393224 | tf_op jit(solution)/shard_map/ppermute | solution.py:551
  129.9 40.0 %copy-start.5 = (f32[2,2,8,8,128]{4,3,2,1,0:T(8,128)}, f32[2,2,8,8,128]{4,3,2,1,0:T(8,128)S(1)}, u32[]{:S(2)}) copy-start(f32[2,2,8,8,128]{4,3,2,1,0:T(8,128)S(1)} %collective-permute-done.2.refs_3_) | copy-start | bytes 393220
  129.9 14.0 %collective-permute-start.7 = (f32[2,2,8,8,128]{4,3,2,1,0:T(8,128)S(1)}, f32[2,2,8,8,128]{4,3,2,1,0:T(8,128)S(1)}, u32[]{:S(2)}, u32[]{:S(2)}) collective-permute-start(f32[2,2,8,8,128]{4,3,2,1,0:T(8,128)S(1)} %copy-done.22), channel_id=1, source_target_pairs={{0,8},{1,9},{2,10},{3,11},{4,12},{5,13},{6,14},{7,15},{8,0},{9,1},... | collective-permute-start | bytes 393224 | tf_op jit(solution)/shard_map/ppermute | solution.py:551
  129.9 40.0 %copy-start.6 = (f32[2,2,8,8,128]{4,3,2,1,0:T(8,128)}, f32[2,2,8,8,128]{4,3,2,1,0:T(8,128)S(1)}, u32[]{:S(2)}) copy-start(f32[2,2,8,8,128]{4,3,2,1,0:T(8,128)S(1)} %collective-permute-done.3.refs_4_) | copy-start | bytes 393220
  129.9 16.8 %collective-permute-start.8 = (f32[2,2,8,8,128]{4,3,2,1,0:T(8,128)S(1)}, f32[2,2,8,8,128]{4,3,2,1,0:T(8,128)S(1)}, u32[]{:S(2)}, u32[]{:S(2)}) collective-permute-start(f32[2,2,8,8,128]{4,3,2,1,0:T(8,128)S(1)} %copy-done.21), channel_id=1, source_target_pairs={{0,9},{1,8},{2,11},{3,10},{4,13},{5,12},{6,15},{7,14},{8,1},{9,0},... | collective-permute-start | bytes 393224 | tf_op jit(solution)/shard_map/ppermute | solution.py:551
  133.9 36.0 %copy-start.7 = (f32[2,2,8,8,128]{4,3,2,1,0:T(8,128)}, f32[2,2,8,8,128]{4,3,2,1,0:T(8,128)S(1)}, u32[]{:S(2)}) copy-start(f32[2,2,8,8,128]{4,3,2,1,0:T(8,128)S(1)} %collective-permute-done.4.refs_5_) | copy-start | bytes 393220
  133.9 16.3 %collective-permute-start.9 = (f32[2,2,8,8,128]{4,3,2,1,0:T(8,128)S(1)}, f32[2,2,8,8,128]{4,3,2,1,0:T(8,128)S(1)}, u32[]{:S(2)}, u32[]{:S(2)}) collective-permute-start(f32[2,2,8,8,128]{4,3,2,1,0:T(8,128)S(1)} %copy-done.20), channel_id=1, source_target_pairs={{0,10},{1,11},{2,8},{3,9},{4,14},{5,15},{6,12},{7,13},{8,2},{9,3},... | collective-permute-start | bytes 393224 | tf_op jit(solution)/shard_map/ppermute | solution.py:551
  137.7 32.1 %copy-start.8 = (f32[2,2,8,8,128]{4,3,2,1,0:T(8,128)}, f32[2,2,8,8,128]{4,3,2,1,0:T(8,128)S(1)}, u32[]{:S(2)}) copy-start(f32[2,2,8,8,128]{4,3,2,1,0:T(8,128)S(1)} %collective-permute-done.5.refs_6_) | copy-start | bytes 393220
  137.7 18.8 %collective-permute-start.10 = (f32[2,2,8,8,128]{4,3,2,1,0:T(8,128)}, f32[2,2,8,8,128]{4,3,2,1,0:T(8,128)S(1)}, u32[]{:S(2)}, u32[]{:S(2)}) collective-permute-start(f32[2,2,8,8,128]{4,3,2,1,0:T(8,128)} %get-tuple-element.44), channel_id=1, source_target_pairs={{0,11},{1,10},{2,9},{3,8},{4,15},{5,14},{6,13},{7,12},{8,3},{9,2},... | collective-permute-start | bytes 393224 | tf_op jit(solution)/shard_map/ppermute | solution.py:551
  139.9 29.9 %copy-start.9 = (f32[2,2,8,8,128]{4,3,2,1,0:T(8,128)}, f32[2,2,8,8,128]{4,3,2,1,0:T(8,128)S(1)}, u32[]{:S(2)}) copy-start(f32[2,2,8,8,128]{4,3,2,1,0:T(8,128)S(1)} %collective-permute-done.6.refs_7_) | copy-start | bytes 393220
  139.9 18.9 %collective-permute-start.11 = (f32[2,2,8,8,128]{4,3,2,1,0:T(8,128)}, f32[2,2,8,8,128]{4,3,2,1,0:T(8,128)S(1)}, u32[]{:S(2)}, u32[]{:S(2)}) collective-permute-start(f32[2,2,8,8,128]{4,3,2,1,0:T(8,128)} %get-tuple-element.45), channel_id=1, source_target_pairs={{0,12},{1,13},{2,14},{3,15},{4,8},{5,9},{6,10},{7,11},{8,4},{9,5},... | collective-permute-start | bytes 393224 | tf_op jit(solution)/shard_map/ppermute | solution.py:551
  143.9 26.0 %copy-start.10 = (f32[2,2,8,8,128]{4,3,2,1,0:T(8,128)}, f32[2,2,8,8,128]{4,3,2,1,0:T(8,128)S(1)}, u32[]{:S(2)}) copy-start(f32[2,2,8,8,128]{4,3,2,1,0:T(8,128)S(1)} %collective-permute-done.7.refs_8_) | copy-start | bytes 393220
  143.9 17.8 %collective-permute-start.12 = (f32[2,2,8,8,128]{4,3,2,1,0:T(8,128)}, f32[2,2,8,8,128]{4,3,2,1,0:T(8,128)S(1)}, u32[]{:S(2)}, u32[]{:S(2)}) collective-permute-start(f32[2,2,8,8,128]{4,3,2,1,0:T(8,128)} %get-tuple-element.46), channel_id=1, source_target_pairs={{0,13},{1,12},{2,15},{3,14},{4,9},{5,8},{6,11},{7,10},{8,5},{9,4},... | collective-permute-start | bytes 393224 | tf_op jit(solution)/shard_map/ppermute | solution.py:551
  146.7 23.2 %copy-start.11 = (f32[2,2,8,8,128]{4,3,2,1,0:T(8,128)}, f32[2,2,8,8,128]{4,3,2,1,0:T(8,128)S(1)}, u32[]{:S(2)}) copy-start(f32[2,2,8,8,128]{4,3,2,1,0:T(8,128)S(1)} %collective-permute-done.8.refs_9_) | copy-start | bytes 393220
  146.7 20.3 %collective-permute-start.13 = (f32[2,2,8,8,128]{4,3,2,1,0:T(8,128)}, f32[2,2,8,8,128]{4,3,2,1,0:T(8,128)S(1)}, u32[]{:S(2)}, u32[]{:S(2)}) collective-permute-start(f32[2,2,8,8,128]{4,3,2,1,0:T(8,128)} %get-tuple-element.47), channel_id=1, source_target_pairs={{0,14},{1,15},{2,12},{3,13},{4,10},{5,11},{6,8},{7,9},{8,6},{9,7},... | collective-permute-start | bytes 393224 | tf_op jit(solution)/shard_map/ppermute | solution.py:551
  150.2 19.7 %collective-permute-start.14 = (f32[2,2,8,8,128]{4,3,2,1,0:T(8,128)}, f32[2,2,8,8,128]{4,3,2,1,0:T(8,128)S(1)}, u32[]{:S(2)}, u32[]{:S(2)}) collective-permute-start(f32[2,2,8,8,128]{4,3,2,1,0:T(8,128)} %get-tuple-element.48), channel_id=1, source_target_pairs={{0,15},{1,14},{2,13},{3,12},{4,11},{5,10},{6,9},{7,8},{8,7},{9,6},... | collective-permute-start | bytes 393224 | tf_op jit(solution)/shard_map/ppermute | solution.py:551
  (16 other events, 121.7 us)

commit v5 on v4

--- a/solution.py
+++ b/solution.py
@@ -244,18 +244,28 @@
     groups, _, _, members, _, _ = chi.shape
     fill_matrices(index_ref, (ch_ref, cl_ref, sh_ref, sl_ref), forward, backward, lambda value: value)
 
-    def select_dot(value, matrix, block):
-        shape = (value[0].shape[0] // rows, rows, plane)
-        first, second = (plane_dot(value, matrix, half, block).reshape(shape) for half in range(2))
-        upper = lax.broadcasted_iota(jnp.int32, shape, 1) < rows // 2
-        return jnp.where(upper, first, second)
-
-    columns = [x_ref[:, h, ri].reshape(side * entries * rows, lanes) for ri in range(2) for h in range(2)]
-    value = split_value(jnp.concatenate(columns, axis=1))
+    def paired(first, second):
+        upper = lax.broadcasted_iota(jnp.int32, first.shape, 1) < rows // 2
+        turned = [pltpu.roll(part, rows // 2, 1) for part in (first, second)]
+        return jnp.where(upper, first, turned[1]), jnp.where(upper, turned[0], second)
+
+    def halves_of(columns):
+        value = jnp.concatenate(columns, axis=1)
+        count, width = value.shape
+        value = value.reshape(count // (2 * rows), 2, rows, width)
+        parts = paired(value[:, 0], value[:, 1])
+        return [split_value(part.reshape(count // 2, width)) for part in parts]
+
+    def halves_dot(parts, matrix, block):
+        shape = (parts[0][0].shape[0] // rows, rows, plane)
+        d = paired(*(plane_dot(parts[half], matrix, half, block).reshape(shape) for half in range(2)))
+        return jnp.concatenate([part.reshape(shape[0], 1, rows, plane) for part in d], axis=1)
+
+    parts = halves_of([x_ref[:, h, ri].reshape(side * entries * rows, lanes) for ri in range(2) for h in range(2)])
     for block in range(2):
-        d = select_dot(value, forward, block)
+        d = halves_dot(parts, forward, block)
         for ri in range(2):
-            piece = d[:, :, ri * lanes : (ri + 1) * lanes]
+            piece = d[:, :, :, ri * lanes : (ri + 1) * lanes]
             mid[block, ri] = piece.reshape(side, entries, rows, lanes)
     for block in range(2):
         for e in range(entries):
@@ -281,11 +291,11 @@
                     for ri in range(2):
                         chi[group, ri, x, c, :, cut] = parts[ri]
         whole = (side * members * rows, plane)
-        value = split_value(jnp.concatenate([chi[group, ri].reshape(whole) for ri in range(2)], axis=1))
+        parts = halves_of([chi[group, ri].reshape(whole) for ri in range(2)])
         for h in range(2):
-            d = select_dot(value, backward, h)
+            d = halves_dot(parts, backward, h)
             for ri in range(2):
-                piece = d[:, :, ri * lanes : (ri + 1) * lanes].reshape(side, members, rows, lanes)
+                piece = d[:, :, :, ri * lanes : (ri + 1) * lanes].reshape(side, members, rows, lanes)
                 stage[group, :, h, ri] = piece
         target = out_ref.at[:, :, :, pl.ds(group * members, members)]
         copies.append(pltpu.make_async_copy(stage.at[group], target, sems.at[group]))
@@ -406,7 +416,7 @@
             pltpu.VMEM((GROUPS, side, 2, 2, components // GROUPS, rows, lanes), jnp.float32),
             pltpu.SemaphoreType.DMA((GROUPS,)),
         ],
-        compiler_params=pltpu.CompilerParams(vmem_limit_bytes=61 << 20),
+        compiler_params=pltpu.CompilerParams(vmem_limit_bytes=44 << 20),
         name="one_middle",
     )(*args)
     return out.reshape((devices,) + shape[2:])
@@ -544,12 +554,10 @@
     return lax.all_to_all(flat, "kb", split_axis=0, concat_axis=0, tiled=True).reshape(x.shape)
 
 
-def swap(pieces, devices):
-    moved = [pieces[0]]
-    for slot in range(1, len(pieces)):
-        pairs = [(device, device ^ slot) for device in range(devices)]
-        moved.append(lax.ppermute(pieces[slot], "kb", pairs))
-    return moved
+def swap(piece, slot, devices):
+    if slot == 0:
+        return piece
+    return lax.ppermute(piece, "kb", [(device, device ^ slot) for device in range(devices)])
 
 
 def trig_pair(angle_int, period, scale):
@@ -695,10 +703,12 @@
     shape = (devices, 2, entries, ROWS, lanes)
     one = to_times(one_times_kernel, green, jnp.asarray(one_fermion), shape, devices, "one_times")
     both, one = lax.optimization_barrier((exchange(both), one))
-    pieces = list(both_middle(both, pair_table, mirror_map, me, near))
-    one, pieces[0] = lax.optimization_barrier((exchange(one), pieces[0]))
+    pieces = both_middle(both, pair_table, mirror_map, me, near)
+    early = [swap(piece, slot, devices) for slot, piece in enumerate(pieces[: near // 2 + 1])]
+    one, early = lax.optimization_barrier((exchange(one), early))
     one = exchange(one_middle(one, pair_table, mirror_map))
-    earlier = both_frequencies(swap(pieces, devices), jnp.asarray(both_boson), me)
+    late = [swap(pieces[slot], slot, devices) for slot in range(len(early), near)]
+    earlier = both_frequencies(early + late, jnp.asarray(both_boson), me)
     return one_frequencies(one, jnp.asarray(one_boson), earlier)
 
 

time: 184 us -> 178 us (0.967)
  waiting for transfers between devices: 101 us -> 96.7 us
  Pallas kernels: 41.1 us -> 38.2 us
  starting transfers between devices: 35.9 us -> 38.3 us
    all_to_all x3, waiting for transfers between devices: 57.8 us -> 42.1 us  [exchange(): lax.all_to_all(flat, 'kb', split_axis=0, concat_axis=0, tiled=True)]
    ppermute x15, waiting for transfers between devices: 43.4 us -> 54.5 us  [swap(): lax.ppermute(piece, 'kb', [(device, device ^ slot) for device in range(de...]
    pallas_call x1, Pallas kernels: 9.52 us -> 6.63 us  [one_middle(): pl.pallas_call(one_middle_kernel, in_specs=specs, out_specs=pl.BlockSpec(...]
    unnamed x61 -> x57, local copies, waits for them, and re-layouts: 3.77 us -> 2.75 us
  transfers between devices with their start and end apart: 18 -> 18, of which waited for: 14 -> 9; matrix products, arithmetic and copies ran while one was open for 1% -> 1% of each run, Pallas kernels for 11% -> 11%
where the time goes in v5:
time: 178 us; the launch traced here: 177 us
  waiting for transfers between devices  96.7 us (54%)
  starting transfers between devices  38.3 us (22%)
  Pallas kernels  38.2 us (21%)
  local copies, waits for them, and re-layouts  3.38 us (2%)
    ppermute x15, waiting for transfers between devices, swap(): lax.ppermute(piece, 'kb', [(device, device ^ slot) for device in range(de...  54.5 us
    all_to_all x3, waiting for transfers between devices, exchange(): lax.all_to_all(flat, 'kb', split_axis=0, concat_axis=0, tiled=True)  42.1 us
    ppermute x15, starting transfers between devices, swap(): lax.ppermute(piece, 'kb', [(device, device ^ slot) for device in range(de...  22.2 us
    all_to_all x3, starting transfers between devices, exchange(): lax.all_to_all(flat, 'kb', split_axis=0, concat_axis=0, tiled=True)  16.1 us
    pallas_call x2, Pallas kernels, to_times(): pl.pallas_call(kernel, in_specs=[hbm, hbm], out_specs=hbm, out_shape=jax....  11.6 us
    pallas_call x1, Pallas kernels, both_middle(): pl.pallas_call(both_middle_kernel, in_specs=[pl.BlockSpec(memory_space=pl...  8.94 us
    pallas_call x1, Pallas kernels, one_middle(): pl.pallas_call(one_middle_kernel, in_specs=specs, out_specs=pl.BlockSpec(...  6.63 us
    pallas_call x1, Pallas kernels, one_frequencies(): pl.pallas_call(one_frequency_kernel, in_specs=[vmem, vmem, hbm], out_spec...  6.36 us
  transfers between devices with their start and end apart: 18, of which 9 were waited for; matrix products, arithmetic and copies ran while one was open for 1% of the time, Pallas kernels for 11%

profile of v5, /device:TPU:0, one launch (start us, length us, event | category | flops | bytes accessed | tf_op | source)
XLA Modules:
  0.0 177.2 jit_solution(4712155717404738484)
XLA Ops:
  0.0 4.9 %both_times.1 = f32[32,2,2,4,8,128]{5,4,3,2,1,0:T(8,128)} custom-call(f32[2,4,128,512]{3,2,1,0:T(8,128)} %g_hbm.2, f32[256,512]{1,0:T(8,128)} %constant.22.clone.m_hbm), custom_call_target="tpu_custom_call" | custom-call | tf_op jit(solution)/shard_map/both_times/pallas_call | solution.py:186
  4.9 7.4 %all-to-all-start = ((f32[32,128,128]{2,1,0:T(8,128)}), f32[32,128,128]{2,1,0:T(8,128)}, u32[]{:S(2)}, u32[]{:S(2)}) async-start(f32[32,128,128]{2,1,0:T(8,128)} %bitcast.14), calls=%async_computation | async-start | bytes 4194304 | tf_op jit(solution)/shard_map/all_to_all | solution.py:554
  12.3 6.7 %one_times.1 = f32[32,2,4,8,128]{4,3,2,1,0:T(8,128)} custom-call(f32[2,4,128,512]{3,2,1,0:T(8,128)} %g_hbm.2, f32[512,512]{1,0:T(8,128)} %constant.23.clone.m_hbm), custom_call_target="tpu_custom_call" | custom-call | tf_op jit(solution)/shard_map/one_times/pallas_call | solution.py:186
  19.1 42.1 %all-to-all-done = f32[32,128,128]{2,1,0:T(8,128)} async-done(((f32[32,128,128]{2,1,0:T(8,128)}), f32[32,128,128]{2,1,0:T(8,128)}, u32[]{:S(2)}, u32[]{:S(2)}) %all-to-all-start) | async-done | bytes 2097184 | tf_op jit(solution)/shard_map/all_to_all | solution.py:554
  61.2 4.2 %all-to-all-start.1 = ((f32[32,64,128]{2,1,0:T(8,128)}), f32[32,64,128]{2,1,0:T(8,128)S(1)}, u32[]{:S(2)}, u32[]{:S(2)}) async-start(f32[32,64,128]{2,1,0:T(8,128)} %bitcast.16), calls=%async_computation.1 | async-start | bytes 2097152 | tf_op jit(solution)/shard_map/all_to_all | solution.py:554
  65.5 0.7 copy.17.table_ref
  66.8 8.9 %both_middle.1 = (f32[2,2,8,8,128]{4,3,2,1,0:T(8,128)}, f32[2,2,8,8,128]{4,3,2,1,0:T(8,128)}, f32[2,2,8,8,128]{4,3,2,1,0:T(8,128)}, f32[2,2,8,8,128]{4,3,2,1,0:T...) custom-call(s32[1]{0:T(128)} %bitcast.6.me_ref, ...), custom_call_target="tpu_custom_call" | custom-call | tf_op jit(solution)/shard_map/both_middle/pallas_call | solution.py:430
  75.9 1.7 collective-permute-start.1
  77.7 1.6 collective-permute-start.3
  79.4 2.6 %collective-permute-start.5 = (f32[2,2,8,8,128]{4,3,2,1,0:T(8,128)}, f32[2,2,8,8,128]{4,3,2,1,0:T(8,128)S(1)}, u32[]{:S(2)}, u32[]{:S(2)}) collective-permute-start(f32[2,2,8,8,128]{4,3,2,1,0:T(8,128)} %get-tuple-element.45), channel_id=1, source_target_pairs={{0,6},{1,7},{2,4},{3,5},{4,2},{5,3},{6,0},{7,1},{8,14},{9,15},{10,... | collective-permute-start | bytes 393224 | tf_op jit(solution)/shard_map/ppermute | solution.py:560
  82.0 1.9 %collective-permute-done.1.refs_2_ = f32[2,2,8,8,128]{4,3,2,1,0:T(8,128)S(1)} collective-permute-done((f32[2,2,8,8,128]{4,3,2,1,0:T(8,128)}, f32[2,2,8,8,128]{4,3,2,1,0:T(8,128)S(1)}, u32[]{:S(2)}, u32[]{:S(2)}) %collective-permute-start.1) | collective-permute-done | bytes 131104 | tf_op jit(solution)/shard_map/ppermute | solution.py:560
  83.9 1.4 collective-permute-start.6
  85.3 1.2 collective-permute-done.2.refs_3_
  86.5 2.2 %collective-permute-start.7 = (f32[2,2,8,8,128]{4,3,2,1,0:T(8,128)}, f32[2,2,8,8,128]{4,3,2,1,0:T(8,128)S(1)}, u32[]{:S(2)}, u32[]{:S(2)}) collective-permute-start(f32[2,2,8,8,128]{4,3,2,1,0:T(8,128)} %get-tuple-element.47), channel_id=1, source_target_pairs={{0,8},{1,9},{2,10},{3,11},{4,12},{5,13},{6,14},{7,15},{8,0},{9,1},... | collective-permute-start | bytes 393224 | tf_op jit(solution)/shard_map/ppermute | solution.py:560
  88.6 6.3 %collective-permute-done.4.refs_5_ = f32[2,2,8,8,128]{4,3,2,1,0:T(8,128)S(1)} collective-permute-done((f32[2,2,8,8,128]{4,3,2,1,0:T(8,128)}, f32[2,2,8,8,128]{4,3,2,1,0:T(8,128)S(1)}, u32[]{:S(2)}, u32[]{:S(2)}) %collective-permute-start.4) | collective-permute-done | bytes 131104 | tf_op jit(solution)/shard_map/ppermute | solution.py:560
  95.0 6.6 %one_middle.1 = f32[16,2,2,8,8,128]{5,4,3,2,1,0:T(8,128)} custom-call(s32[8,2]{1,0:T(8,128)S(1)} %copy-done.4, s32[3,16]{1,0:T(4,128)S(1)} %copy-done.6, s32[1,256]{1,0:T(1,128)S(1)} %copy-done.7, bf16[256,256]{1,0:T(8,128)(2,1)S(1)} %copy-done.3, bf16[256,256]{1,0:T(8,128)(2,1)S(1)} %copy-done.2, bf16[256,256]{1,0:T(8,128)(2,1)S(1)} %copy-done.1, ...), custom_call_target="tpu_custom_call" | custom-call | tf_op jit(solution)/shard_map/one_middle/pallas_call | solution.py:404
  101.8 4.5 %all-to-all-start.2 = ((f32[32,128,128]{2,1,0:T(8,128)}), f32[32,128,128]{2,1,0:T(8,128)S(1)}, u32[]{:S(2)}, u32[]{:S(2)}) async-start(f32[32,128,128]{2,1,0:T(8,128)} %bitcast.9), calls=%async_computation.2 | async-start | bytes 4194304 | tf_op jit(solution)/shard_map/all_to_all | solution.py:554
  106.3 1.4 collective-permute-start.8
  107.6 1.5 collective-permute-start.9
  109.1 1.1 collective-permute-start.10
  110.2 1.5 collective-permute-start.11
  111.7 1.2 collective-permute-start.12
  112.9 31.5 %collective-permute-done.8.refs_9_ = f32[2,2,8,8,128]{4,3,2,1,0:T(8,128)S(1)} collective-permute-done((f32[2,2,8,8,128]{4,3,2,1,0:T(8,128)}, f32[2,2,8,8,128]{4,3,2,1,0:T(8,128)S(1)}, u32[]{:S(2)}, u32[]{:S(2)}) %collective-permute-start.8) | collective-permute-done | bytes 131104 | tf_op jit(solution)/shard_map/ppermute | solution.py:560
  144.4 3.1 %collective-permute-start.13 = (f32[2,2,8,8,128]{4,3,2,1,0:T(8,128)S(1)}, f32[2,2,8,8,128]{4,3,2,1,0:T(8,128)S(1)}, u32[]{:S(2)}, u32[]{:S(2)}) collective-permute-start(f32[2,2,8,8,128]{4,3,2,1,0:T(8,128)S(1)} %copy-done.26), channel_id=1, source_target_pairs={{0,14},{1,15},{2,12},{3,13},{4,10},{5,11},{6,8},{7,9},{8,6},{9,7},... | collective-permute-start | bytes 393224 | tf_op jit(solution)/shard_map/ppermute | solution.py:560
  147.5 2.7 %collective-permute-start.14 = (f32[2,2,8,8,128]{4,3,2,1,0:T(8,128)S(1)}, f32[2,2,8,8,128]{4,3,2,1,0:T(8,128)S(1)}, u32[]{:S(2)}, u32[]{:S(2)}) collective-permute-start(f32[2,2,8,8,128]{4,3,2,1,0:T(8,128)S(1)} %copy-done.25), channel_id=1, source_target_pairs={{0,15},{1,14},{2,13},{3,12},{4,11},{5,10},{6,9},{7,8},{8,7},{9,6},... | collective-permute-start | bytes 393224 | tf_op jit(solution)/shard_map/ppermute | solution.py:560
  150.2 3.7 %collective-permute-done.11.refs_12_ = f32[2,2,8,8,128]{4,3,2,1,0:T(8,128)S(1)} collective-permute-done((f32[2,2,8,8,128]{4,3,2,1,0:T(8,128)}, f32[2,2,8,8,128]{4,3,2,1,0:T(8,128)S(1)}, u32[]{:S(2)}, u32[]{:S(2)}) %collective-permute-start.11) | collective-permute-done | bytes 131104 | tf_op jit(solution)/shard_map/ppermute | solution.py:560
  154.0 3.1 %collective-permute-done.12.refs_13_ = f32[2,2,8,8,128]{4,3,2,1,0:T(8,128)S(1)} collective-permute-done((f32[2,2,8,8,128]{4,3,2,1,0:T(8,128)S(1)}, f32[2,2,8,8,128]{4,3,2,1,0:T(8,128)S(1)}, u32[]{:S(2)}, u32[]{:S(2)}) %collective-permute-start.12) | collective-permute-done | bytes 131104 | tf_op jit(solution)/shard_map/ppermute | solution.py:560
  157.1 5.0 %collective-permute-done.13.refs_14_ = f32[2,2,8,8,128]{4,3,2,1,0:T(8,128)S(1)} collective-permute-done((f32[2,2,8,8,128]{4,3,2,1,0:T(8,128)S(1)}, f32[2,2,8,8,128]{4,3,2,1,0:T(8,128)S(1)}, u32[]{:S(2)}, u32[]{:S(2)}) %collective-permute-start.13) | collective-permute-done | bytes 131104 | tf_op jit(solution)/shard_map/ppermute | solution.py:560
  162.1 1.9 %collective-permute-done.14.refs_15_ = f32[2,2,8,8,128]{4,3,2,1,0:T(8,128)S(1)} collective-permute-done((f32[2,2,8,8,128]{4,3,2,1,0:T(8,128)S(1)}, f32[2,2,8,8,128]{4,3,2,1,0:T(8,128)S(1)}, u32[]{:S(2)}, u32[]{:S(2)}) %collective-permute-start.14) | collective-permute-done | bytes 131104 | tf_op jit(solution)/shard_map/ppermute | solution.py:560
  164.6 4.7 %both_frequencies.1.earlier_hbm = f32[2,8,128,512]{3,2,1,0:T(8,128)} custom-call(s32[1]{0:T(128)} %bitcast.6.me_ref, f32[2,16,8,512]{3,2,1,0:T(8,128)} %constant.28.clone.m_ref, f32[2,2,8,8,128]{4,3,2,1,0:T(8,128)} %get-tuple-element.49.refs_0_, f32[2,2,8,8,128]{4,3,2,1,0:T(8,128)} %copy-done.9, f32[2,2,8,8,128]{4,3,2,1,0:T(8,128)} %copy-done.10, ...), custom_call_target="tpu_custom_call" | custom-call | tf_op jit(solution)/shard_map/both_frequencies/pallas_call | solution.py:483
  169.3 1.3 copy-done.8
  170.6 6.4 %one_frequencies.1 = f32[2,8,128,512]{3,2,1,0:T(8,128)} custom-call(f32[32,2,8,8,128]{4,3,2,1,0:T(8,128)} %bitcast.15, f32[256,512]{1,0:T(8,128)} %constant.29.clone.m_ref, f32[2,8,128,512]{3,2,1,0:T(8,128)} %both_frequencies.1.earlier_hbm), custom_call_target="tpu_custom_call" | custom-call | tf_op jit(solution)/shard_map/one_frequencies/pallas_call | solution.py:536
  (70 shorter events, 1.8 us)
Async XLA Ops:
  4.9 56.3 %all-to-all-start = ((f32[32,128,128]{2,1,0:T(8,128)}), f32[32,128,128]{2,1,0:T(8,128)}, u32[]{:S(2)}, u32[]{:S(2)}) async-start(f32[32,128,128]{2,1,0:T(8,128)} %bitcast.14), calls=%async_computation | async-start | bytes 4194304 | tf_op jit(solution)/shard_map/all_to_all | solution.py:554
  19.1 46.4 %copy-start.24 = (s32[8,2]{0,1:T(2,128)S(1)}, s32[8,2]{0,1:T(2,128)}, u32[]{:S(2)}) copy-start(s32[8,2]{0,1:T(2,128)} %param.16) | copy-start | bytes 196
  19.1 47.1 %copy-start.5 = (s32[3,16]{1,0:T(4,128)S(1)}, s32[3,16]{1,0:T(4,128)}, u32[]{:S(2)}) copy-start(s32[3,16]{1,0:T(4,128)} %mirror_ref.3) | copy-start | bytes 580
  61.2 33.7 %copy-start = (bf16[256,256]{1,0:T(8,128)(2,1)S(1)}, bf16[256,256]{1,0:T(8,128)(2,1)}, u32[]{:S(2)}) copy-start(bf16[256,256]{1,0:T(8,128)(2,1)} %constant.27.clone.sl_ref) | copy-start | bytes 393220
  61.2 33.7 %copy-start.1 = (bf16[256,256]{1,0:T(8,128)(2,1)S(1)}, bf16[256,256]{1,0:T(8,128)(2,1)}, u32[]{:S(2)}) copy-start(bf16[256,256]{1,0:T(8,128)(2,1)} %constant.26.clone.sh_ref) | copy-start | bytes 393220
  61.2 33.7 %copy-start.2 = (bf16[256,256]{1,0:T(8,128)(2,1)S(1)}, bf16[256,256]{1,0:T(8,128)(2,1)}, u32[]{:S(2)}) copy-start(bf16[256,256]{1,0:T(8,128)(2,1)} %constant.25.clone.cl_ref) | copy-start | bytes 393220
  61.2 33.7 %copy-start.3 = (bf16[256,256]{1,0:T(8,128)(2,1)S(1)}, bf16[256,256]{1,0:T(8,128)(2,1)}, u32[]{:S(2)}) copy-start(bf16[256,256]{1,0:T(8,128)(2,1)} %constant.24.clone.ch_ref) | copy-start | bytes 393220
  61.2 33.7 %copy-start.6 = (s32[3,16]{1,0:T(4,128)S(1)}, s32[3,16]{1,0:T(4,128)}, u32[]{:S(2)}) copy-start(s32[3,16]{1,0:T(4,128)} %mirror_ref.3) | copy-start | bytes 580
  61.2 33.7 %all-to-all-start.1 = ((f32[32,64,128]{2,1,0:T(8,128)}), f32[32,64,128]{2,1,0:T(8,128)S(1)}, u32[]{:S(2)}, u32[]{:S(2)}) async-start(f32[32,64,128]{2,1,0:T(8,128)} %bitcast.16), calls=%async_computation.1 | async-start | bytes 2097152 | tf_op jit(solution)/shard_map/all_to_all | solution.py:554
  66.1 28.9 %copy-start.4 = (s32[8,2]{1,0:T(8,128)S(1)}, s32[8,2]{1,0:T(8,128)}, u32[]{:S(2)}) copy-start(s32[8,2]{1,0:T(8,128)} %copy.17.table_ref) | copy-start | bytes 196
  66.8 28.2 %copy-start.7 = (s32[1,256]{1,0:T(1,128)S(1)}, s32[1,256]{1,0:T(1,128)}, u32[]{:S(2)}) copy-start(s32[1,256]{1,0:T(1,128)} %add.36.index_ref) | copy-start | bytes 3076
  75.8 3.6 %collective-permute-start = (f32[2,2,8,8,128]{4,3,2,1,0:T(8,128)}, f32[2,2,8,8,128]{4,3,2,1,0:T(8,128)S(1)}, u32[]{:S(2)}, u32[]{:S(2)}) collective-permute-start(f32[2,2,8,8,128]{4,3,2,1,0:T(8,128)} %get-tuple-element.40), channel_id=1, source_target_pairs={{0,1},{1,0},{2,3},{3,2},{4,5},{5,4},{6,7},{7,6},{8,9},{9,8},{10,11... | collective-permute-start | bytes 393224 | tf_op jit(solution)/shard_map/ppermute | solution.py:560
  75.9 8.0 %collective-permute-start.1 = (f32[2,2,8,8,128]{4,3,2,1,0:T(8,128)}, f32[2,2,8,8,128]{4,3,2,1,0:T(8,128)S(1)}, u32[]{:S(2)}, u32[]{:S(2)}) collective-permute-start(f32[2,2,8,8,128]{4,3,2,1,0:T(8,128)} %get-tuple-element.41), channel_id=1, source_target_pairs={{0,2},{1,3},{2,0},{3,1},{4,6},{5,7},{6,4},{7,5},{8,10},{9,11},{10,... | collective-permute-start | bytes 393224 | tf_op jit(solution)/shard_map/ppermute | solution.py:560
  77.6 8.9 %collective-permute-start.2 = (f32[2,2,8,8,128]{4,3,2,1,0:T(8,128)}, f32[2,2,8,8,128]{4,3,2,1,0:T(8,128)S(1)}, u32[]{:S(2)}, u32[]{:S(2)}) collective-permute-start(f32[2,2,8,8,128]{4,3,2,1,0:T(8,128)} %get-tuple-element.42), channel_id=1, source_target_pairs={{0,3},{1,2},{2,1},{3,0},{4,7},{5,6},{6,5},{7,4},{8,11},{9,10},{10,... | collective-permute-start | bytes 393224 | tf_op jit(solution)/shard_map/ppermute | solution.py:560
  77.7 10.9 %collective-permute-start.3 = (f32[2,2,8,8,128]{4,3,2,1,0:T(8,128)}, f32[2,2,8,8,128]{4,3,2,1,0:T(8,128)S(1)}, u32[]{:S(2)}, u32[]{:S(2)}) collective-permute-start(f32[2,2,8,8,128]{4,3,2,1,0:T(8,128)} %get-tuple-element.43), channel_id=1, source_target_pairs={{0,4},{1,5},{2,6},{3,7},{4,0},{5,1},{6,2},{7,3},{8,12},{9,13},{10,... | collective-permute-start | bytes 393224 | tf_op jit(solution)/shard_map/ppermute | solution.py:560
  79.3 15.6 %collective-permute-start.4 = (f32[2,2,8,8,128]{4,3,2,1,0:T(8,128)}, f32[2,2,8,8,128]{4,3,2,1,0:T(8,128)S(1)}, u32[]{:S(2)}, u32[]{:S(2)}) collective-permute-start(f32[2,2,8,8,128]{4,3,2,1,0:T(8,128)} %get-tuple-element.44), channel_id=1, source_target_pairs={{0,5},{1,4},{2,7},{3,6},{4,1},{5,0},{6,3},{7,2},{8,13},{9,12},{10,... | collective-permute-start | bytes 393224 | tf_op jit(solution)/shard_map/ppermute | solution.py:560
  79.4 22.3 %copy-start.9 = (f32[2,2,8,8,128]{4,3,2,1,0:T(8,128)}, f32[2,2,8,8,128]{4,3,2,1,0:T(8,128)S(1)}, u32[]{:S(2)}) copy-start(f32[2,2,8,8,128]{4,3,2,1,0:T(8,128)S(1)} %collective-permute-done.refs_1_) | copy-start | bytes 393220
  79.4 15.5 %collective-permute-start.5 = (f32[2,2,8,8,128]{4,3,2,1,0:T(8,128)}, f32[2,2,8,8,128]{4,3,2,1,0:T(8,128)S(1)}, u32[]{:S(2)}, u32[]{:S(2)}) collective-permute-start(f32[2,2,8,8,128]{4,3,2,1,0:T(8,128)} %get-tuple-element.45), channel_id=1, source_target_pairs={{0,6},{1,7},{2,4},{3,5},{4,2},{5,3},{6,0},{7,1},{8,14},{9,15},{10,... | collective-permute-start | bytes 393224 | tf_op jit(solution)/shard_map/ppermute | solution.py:560
  83.9 17.8 %copy-start.10 = (f32[2,2,8,8,128]{4,3,2,1,0:T(8,128)}, f32[2,2,8,8,128]{4,3,2,1,0:T(8,128)S(1)}, u32[]{:S(2)}) copy-start(f32[2,2,8,8,128]{4,3,2,1,0:T(8,128)S(1)} %collective-permute-done.1.refs_2_) | copy-start | bytes 393220
  83.9 11.0 %collective-permute-start.6 = (f32[2,2,8,8,128]{4,3,2,1,0:T(8,128)}, f32[2,2,8,8,128]{4,3,2,1,0:T(8,128)S(1)}, u32[]{:S(2)}, u32[]{:S(2)}) collective-permute-start(f32[2,2,8,8,128]{4,3,2,1,0:T(8,128)} %get-tuple-element.46), channel_id=1, source_target_pairs={{0,7},{1,6},{2,5},{3,4},{4,3},{5,2},{6,1},{7,0},{8,15},{9,14},{10,... | collective-permute-start | bytes 393224 | tf_op jit(solution)/shard_map/ppermute | solution.py:560
  86.5 8.5 %collective-permute-start.7 = (f32[2,2,8,8,128]{4,3,2,1,0:T(8,128)}, f32[2,2,8,8,128]{4,3,2,1,0:T(8,128)S(1)}, u32[]{:S(2)}, u32[]{:S(2)}) collective-permute-start(f32[2,2,8,8,128]{4,3,2,1,0:T(8,128)} %get-tuple-element.47), channel_id=1, source_target_pairs={{0,8},{1,9},{2,10},{3,11},{4,12},{5,13},{6,14},{7,15},{8,0},{9,1},... | collective-permute-start | bytes 393224 | tf_op jit(solution)/shard_map/ppermute | solution.py:560
  101.7 42.8 %copy-start.26 = (f32[2,2,8,8,128]{4,3,2,1,0:T(8,128)S(1)}, f32[2,2,8,8,128]{4,3,2,1,0:T(8,128)}, u32[]{:S(2)}) copy-start(f32[2,2,8,8,128]{4,3,2,1,0:T(8,128)} %get-tuple-element.63) | copy-start | bytes 393220
  101.7 45.8 %copy-start.25 = (f32[2,2,8,8,128]{4,3,2,1,0:T(8,128)S(1)}, f32[2,2,8,8,128]{4,3,2,1,0:T(8,128)}, u32[]{:S(2)}) copy-start(f32[2,2,8,8,128]{4,3,2,1,0:T(8,128)} %get-tuple-element.64) | copy-start | bytes 393220
  101.8 67.5 %all-to-all-start.2 = ((f32[32,128,128]{2,1,0:T(8,128)}), f32[32,128,128]{2,1,0:T(8,128)S(1)}, u32[]{:S(2)}, u32[]{:S(2)}) async-start(f32[32,128,128]{2,1,0:T(8,128)} %bitcast.9), calls=%async_computation.2 | async-start | bytes 4194304 | tf_op jit(solution)/shard_map/all_to_all | solution.py:554
  106.3 38.1 %collective-permute-start.8 = (f32[2,2,8,8,128]{4,3,2,1,0:T(8,128)}, f32[2,2,8,8,128]{4,3,2,1,0:T(8,128)S(1)}, u32[]{:S(2)}, u32[]{:S(2)}) collective-permute-start(f32[2,2,8,8,128]{4,3,2,1,0:T(8,128)} %get-tuple-element.58), channel_id=1, source_target_pairs={{0,9},{1,8},{2,11},{3,10},{4,13},{5,12},{6,15},{7,14},{8,1},{9,0},... | collective-permute-start | bytes 393224 | tf_op jit(solution)/shard_map/ppermute | solution.py:560
  107.6 39.8 %collective-permute-start.9 = (f32[2,2,8,8,128]{4,3,2,1,0:T(8,128)}, f32[2,2,8,8,128]{4,3,2,1,0:T(8,128)S(1)}, u32[]{:S(2)}, u32[]{:S(2)}) collective-permute-start(f32[2,2,8,8,128]{4,3,2,1,0:T(8,128)} %get-tuple-element.59), channel_id=1, source_target_pairs={{0,10},{1,11},{2,8},{3,9},{4,14},{5,15},{6,12},{7,13},{8,2},{9,3},... | collective-permute-start | bytes 393224 | tf_op jit(solution)/shard_map/ppermute | solution.py:560
  109.1 41.1 %collective-permute-start.10 = (f32[2,2,8,8,128]{4,3,2,1,0:T(8,128)}, f32[2,2,8,8,128]{4,3,2,1,0:T(8,128)S(1)}, u32[]{:S(2)}, u32[]{:S(2)}) collective-permute-start(f32[2,2,8,8,128]{4,3,2,1,0:T(8,128)} %get-tuple-element.60), channel_id=1, source_target_pairs={{0,11},{1,10},{2,9},{3,8},{4,15},{5,14},{6,13},{7,12},{8,3},{9,2},... | collective-permute-start | bytes 393224 | tf_op jit(solution)/shard_map/ppermute | solution.py:560
  110.2 43.7 %collective-permute-start.11 = (f32[2,2,8,8,128]{4,3,2,1,0:T(8,128)}, f32[2,2,8,8,128]{4,3,2,1,0:T(8,128)S(1)}, u32[]{:S(2)}, u32[]{:S(2)}) collective-permute-start(f32[2,2,8,8,128]{4,3,2,1,0:T(8,128)} %get-tuple-element.61), channel_id=1, source_target_pairs={{0,12},{1,13},{2,14},{3,15},{4,8},{5,9},{6,10},{7,11},{8,4},{9,5},... | collective-permute-start | bytes 393224 | tf_op jit(solution)/shard_map/ppermute | solution.py:560
  111.7 45.4 %collective-permute-start.12 = (f32[2,2,8,8,128]{4,3,2,1,0:T(8,128)S(1)}, f32[2,2,8,8,128]{4,3,2,1,0:T(8,128)S(1)}, u32[]{:S(2)}, u32[]{:S(2)}) collective-permute-start(f32[2,2,8,8,128]{4,3,2,1,0:T(8,128)S(1)} %copy-done.27), channel_id=1, source_target_pairs={{0,13},{1,12},{2,15},{3,14},{4,9},{5,8},{6,11},{7,10},{8,5},{9,4},... | collective-permute-start | bytes 393224 | tf_op jit(solution)/shard_map/ppermute | solution.py:560
  144.4 19.5 %copy-start.17 = (f32[2,2,8,8,128]{4,3,2,1,0:T(8,128)}, f32[2,2,8,8,128]{4,3,2,1,0:T(8,128)S(1)}, u32[]{:S(2)}) copy-start(f32[2,2,8,8,128]{4,3,2,1,0:T(8,128)S(1)} %collective-permute-done.8.refs_9_) | copy-start | bytes 393220
  144.4 17.6 %collective-permute-start.13 = (f32[2,2,8,8,128]{4,3,2,1,0:T(8,128)S(1)}, f32[2,2,8,8,128]{4,3,2,1,0:T(8,128)S(1)}, u32[]{:S(2)}, u32[]{:S(2)}) collective-permute-start(f32[2,2,8,8,128]{4,3,2,1,0:T(8,128)S(1)} %copy-done.26), channel_id=1, source_target_pairs={{0,14},{1,15},{2,12},{3,13},{4,10},{5,11},{6,8},{7,9},{8,6},{9,7},... | collective-permute-start | bytes 393224 | tf_op jit(solution)/shard_map/ppermute | solution.py:560
  147.5 16.4 %collective-permute-start.14 = (f32[2,2,8,8,128]{4,3,2,1,0:T(8,128)S(1)}, f32[2,2,8,8,128]{4,3,2,1,0:T(8,128)S(1)}, u32[]{:S(2)}, u32[]{:S(2)}) collective-permute-start(f32[2,2,8,8,128]{4,3,2,1,0:T(8,128)S(1)} %copy-done.25), channel_id=1, source_target_pairs={{0,15},{1,14},{2,13},{3,12},{4,11},{5,10},{6,9},{7,8},{8,7},{9,6},... | collective-permute-start | bytes 393224 | tf_op jit(solution)/shard_map/ppermute | solution.py:560
  (14 other events, 116.6 us)

commit v6 on v3

--- a/solution.py
+++ b/solution.py
@@ -214,10 +214,14 @@
         ref[plane:, re] = (-sine[:, cut]).astype(jnp.bfloat16)
 
 
-def fill_matrices(index_ref, parts, forward, backward, turned):
+def fill_matrices(mirror_ref, parts, forward, backward, turned):
     plane = parts[0].shape[0]
+    side = mirror_ref.shape[1]
     row = lax.broadcasted_iota(jnp.int32, (plane, plane), 0)
-    pick = (row == index_ref[...]).astype(jnp.float32).astype(jnp.bfloat16)
+    column = lax.broadcasted_iota(jnp.int32, (plane, plane), 1)
+    upper = (mirror_ref[1, 0] - column // side) & (side - 1)
+    lower = (mirror_ref[2, 0] - column % side) & (side - 1)
+    pick = (row == upper * side + lower).astype(jnp.float32).astype(jnp.bfloat16)
 
     def dot(a, b):
         return jnp.dot(a, b, preferred_element_type=jnp.float32)
@@ -237,25 +241,35 @@
     return dot3(value, (matrix[half, 0, :, cut], matrix[half, 1, :, cut]), ((1,), (0,)))
 
 
-def one_middle_kernel(table_ref, mirror_ref, index_ref, ch_ref, cl_ref, sh_ref, sl_ref, x_ref, out_ref, *refs):
-    forward, backward, mid, space, other_space, chi = refs
+def one_middle_kernel(table_ref, mirror_ref, ch_ref, cl_ref, sh_ref, sl_ref, x_ref, out_ref, *refs):
+    forward, backward, mid, space, other_space, chi, stage, sems = refs
     _, side, _, entries, rows, lanes = space.shape
     plane = 2 * lanes
     groups, _, _, members, _, _ = chi.shape
-    fill_matrices(index_ref, (ch_ref, cl_ref, sh_ref, sl_ref), forward, backward, lambda value: value)
-
-    def select_dot(value, matrix, block):
-        shape = (value[0].shape[0] // rows, rows, plane)
-        first, second = (plane_dot(value, matrix, half, block).reshape(shape) for half in range(2))
-        upper = lax.broadcasted_iota(jnp.int32, shape, 1) < rows // 2
-        return jnp.where(upper, first, second)
-
-    columns = [x_ref[:, h, ri].reshape(side * entries * rows, lanes) for ri in range(2) for h in range(2)]
-    value = split_value(jnp.concatenate(columns, axis=1))
+    fill_matrices(mirror_ref, (ch_ref, cl_ref, sh_ref, sl_ref), forward, backward, lambda value: value)
+
+    def paired(first, second):
+        upper = lax.broadcasted_iota(jnp.int32, first.shape, 1) < rows // 2
+        turned = [pltpu.roll(part, rows // 2, 1) for part in (first, second)]
+        return jnp.where(upper, first, turned[1]), jnp.where(upper, turned[0], second)
+
+    def halves_of(columns):
+        value = jnp.concatenate(columns, axis=1)
+        count, width = value.shape
+        value = value.reshape(count // (2 * rows), 2, rows, width)
+        parts = paired(value[:, 0], value[:, 1])
+        return [split_value(part.reshape(count // 2, width)) for part in parts]
+
+    def halves_dot(parts, matrix, block):
+        shape = (parts[0][0].shape[0] // rows, rows, plane)
+        d = paired(*(plane_dot(parts[half], matrix, half, block).reshape(shape) for half in range(2)))
+        return jnp.concatenate([part.reshape(shape[0], 1, rows, plane) for part in d], axis=1)
+
+    parts = halves_of([x_ref[:, h, ri].reshape(side * entries * rows, lanes) for ri in range(2) for h in range(2)])
     for block in range(2):
-        d = select_dot(value, forward, block)
+        d = halves_dot(parts, forward, block)
         for ri in range(2):
-            piece = d[:, :, ri * lanes : (ri + 1) * lanes]
+            piece = d[:, :, :, ri * lanes : (ri + 1) * lanes]
             mid[block, ri] = piece.reshape(side, entries, rows, lanes)
     for block in range(2):
         for e in range(entries):
@@ -265,9 +279,10 @@
                     space[block, x, ri, e] = parts[ri]
                     other_space[block, x, ri, e] = pltpu.roll(parts[ri], rows // 2, 0)
 
+    copies = []
     for group in range(groups):
         for c in range(members):
-            left, right = table_ref[group * members + c, 0], table_ref[group * members + c, 1]
+            left, right = table_ref[0, group * members + c], table_ref[1, group * members + c]
             for block in range(2):
                 values = []
                 for x in range(side):
@@ -280,15 +295,20 @@
                     for ri in range(2):
                         chi[group, ri, x, c, :, cut] = parts[ri]
         whole = (side * members * rows, plane)
-        value = split_value(jnp.concatenate([chi[group, ri].reshape(whole) for ri in range(2)], axis=1))
+        parts = halves_of([chi[group, ri].reshape(whole) for ri in range(2)])
         for h in range(2):
-            d = select_dot(value, backward, h)
+            d = halves_dot(parts, backward, h)
             for ri in range(2):
-                piece = d[:, :, ri * lanes : (ri + 1) * lanes].reshape(side, members, rows, lanes)
-                out_ref[:, h, ri, group * members : (group + 1) * members] = piece
-
-
-def both_middle_kernel(me_ref, table_ref, mirror_ref, index_ref, ch_ref, cl_ref, sh_ref, sl_ref, x_ref, *refs):
+                piece = d[:, :, :, ri * lanes : (ri + 1) * lanes].reshape(side, members, rows, lanes)
+                stage[group, :, h, ri] = piece
+        target = out_ref.at[:, :, :, pl.ds(group * members, members)]
+        copies.append(pltpu.make_async_copy(stage.at[group], target, sems.at[group]))
+        copies[-1].start()
+    for copy in copies:
+        copy.wait()
+
+
+def both_middle_kernel(me_ref, table_ref, mirror_ref, ch_ref, cl_ref, sh_ref, sl_ref, x_ref, *refs):
     outs, (forward, backward, mid, space, chi) = refs[:-5], refs[-5:]
     halves, _, side, _, entries, rows, lanes = space.shape
     plane = 2 * lanes
@@ -300,7 +320,7 @@
     def turned(value):
         return jnp.where(core == 0, value, jnp.concatenate([value[:, lanes:], value[:, :lanes]], axis=1))
 
-    fill_matrices(index_ref, (ch_ref, cl_ref, sh_ref, sl_ref), forward, backward, turned)
+    fill_matrices(mirror_ref, (ch_ref, cl_ref, sh_ref, sl_ref), forward, backward, turned)
 
     def arrive(half):
         columns = [
@@ -322,7 +342,7 @@
 
     def product(unit, block, c):
         half, first = unit % halves, unit // halves * members
-        left, right = table_ref[first + c, 0], table_ref[first + c, 1]
+        left, right = table_ref[0, first + c], table_ref[1, first + c]
         values = []
         for x in range(side):
             other = mirror_ref[0, x]
@@ -370,13 +390,12 @@
 
 def middle_inputs(table, mirror_map, x):
     side, plane = x.shape[0] // 2, 2 * x.shape[-1]
-    index = (mirror_map[1][:, None] * side + mirror_map[2][None, :]).reshape(1, plane)
     cosine, sine = plane_parts(side)
     parts = [jnp.asarray(part) for part in split_constant(cosine) + split_constant(sine)]
     smem = pl.BlockSpec(memory_space=pltpu.SMEM)
     vmem = pl.BlockSpec(memory_space=pltpu.VMEM)
-    args = (table, mirror_map, index, *parts, x.reshape((side, 2) + x.shape[1:]))
-    return args, [smem, smem] + [vmem] * 6, pltpu.VMEM((2, 2, 2 * plane, 2 * plane), jnp.bfloat16)
+    args = (table.T, mirror_map, *parts, x.reshape((side, 2) + x.shape[1:]))
+    return args, [smem, smem] + [vmem] * 5, pltpu.VMEM((2, 2, 2 * plane, 2 * plane), jnp.bfloat16)
 
 
 def one_middle(x, table, mirror_map):
@@ -388,7 +407,7 @@
     out = pl.pallas_call(
         one_middle_kernel,
         in_specs=specs,
-        out_specs=pl.BlockSpec(memory_space=pltpu.VMEM),
+        out_specs=pl.BlockSpec(memory_space=pltpu.HBM),
         out_shape=jax.ShapeDtypeStruct(shape, jnp.float32),
         scratch_shapes=[
             matrices,
@@ -397,8 +416,10 @@
             spatial,
             spatial,
             pltpu.VMEM((GROUPS, 2, side, components // GROUPS, rows, 2 * lanes), jnp.float32),
+            pltpu.VMEM((GROUPS, side, 2, 2, components // GROUPS, rows, lanes), jnp.float32),
+            pltpu.SemaphoreType.DMA((GROUPS,)),
         ],
-        compiler_params=pltpu.CompilerParams(vmem_limit_bytes=28 << 20),
+        compiler_params=pltpu.CompilerParams(vmem_limit_bytes=44 << 20),
         name="one_middle",
     )(*args)
     return out.reshape((devices,) + shape[2:])
@@ -421,30 +442,32 @@
             pltpu.VMEM((halves, 2, side, 2, entries, rows, lanes), jnp.float32),
             pltpu.VMEM((halves * GROUPS, 2, near // 2, members, rows, 2 * lanes), jnp.float32),
         ],
-        compiler_params=pltpu.CompilerParams(vmem_limit_bytes=28 << 20),
+        compiler_params=pltpu.CompilerParams(vmem_limit_bytes=60 << 20),
         name="both_middle",
     )(me, *args)
 
 
 def frequency_kernel(me_ref, both_ref, one_ref, y_ref, *refs):
-    pieces, (out_ref, stage, sems) = refs[:-3], refs[-3:]
+    pieces, (out_ref, held, stage, in_sems, sems) = refs[:-5], refs[-5:]
     near = len(pieces)
     devices, _, components, rows, lanes = y_ref.shape
     groups = sems.shape[0]
     members = components // groups
+    loads = [pltpu.make_async_copy(piece, held.at[slot], in_sems.at[slot]) for slot, piece in enumerate(pieces)]
+    for copy in loads:
+        copy.start()
     me = me_ref[0] % near
     both = [both_ref[part, slot ^ me] for part in range(2) for slot in range(near)]
     matrix = split_value(jnp.concatenate(both + [one_ref[...]], axis=0))
     upper_rows = lax.broadcasted_iota(jnp.int32, (devices, rows, lanes), 1) < rows // 2
-
-    def gathered(half, ri, c):
-        return jnp.concatenate([piece[half, ri, c] for piece in pieces], axis=0)
+    for copy in loads:
+        copy.wait()
 
     copies = []
     for group in range(groups):
         values = []
         for c in range(group * members, (group + 1) * members):
-            part = [[gathered(half, ri, c) for ri in range(2)] for half in range(2)]
+            part = [[held[:, half, ri, c].reshape(near * rows, lanes) for ri in range(2)] for half in range(2)]
             sums = [part[0][ri] + part[1][ri] for ri in range(2)]
             differences = [part[0][ri] - part[1][ri] for ri in range(2)]
             folded = []
@@ -471,13 +494,19 @@
     _, _, components, _, lanes = y.shape
     shape = (2, components, lanes, one.shape[1])
     vmem = pl.BlockSpec(memory_space=pltpu.VMEM)
+    hbm = pl.BlockSpec(memory_space=pltpu.HBM)
     return pl.pallas_call(
         frequency_kernel,
-        in_specs=[pl.BlockSpec(memory_space=pltpu.SMEM)] + [vmem] * (3 + len(pieces)),
-        out_specs=pl.BlockSpec(memory_space=pltpu.HBM),
+        in_specs=[pl.BlockSpec(memory_space=pltpu.SMEM)] + [vmem] * 3 + [hbm] * len(pieces),
+        out_specs=hbm,
         out_shape=jax.ShapeDtypeStruct(shape, jnp.float32),
-        scratch_shapes=[pltpu.VMEM(shape, jnp.float32), pltpu.SemaphoreType.DMA((components // 2,))],
-        compiler_params=pltpu.CompilerParams(vmem_limit_bytes=28 << 20),
+        scratch_shapes=[
+            pltpu.VMEM((len(pieces),) + pieces[0].shape, jnp.float32),
+            pltpu.VMEM(shape, jnp.float32),
+            pltpu.SemaphoreType.DMA((len(pieces),)),
+            pltpu.SemaphoreType.DMA((components // 2,)),
+        ],
+        compiler_params=pltpu.CompilerParams(vmem_limit_bytes=60 << 20),
         name="to_frequencies",
     )(me, both, one, y, *pieces)
 
@@ -487,12 +516,10 @@
     return lax.all_to_all(flat, "kb", split_axis=0, concat_axis=0, tiled=True).reshape(x.shape)
 
 
-def swap(pieces, devices):
-    moved = [pieces[0]]
-    for slot in range(1, len(pieces)):
-        pairs = [(device, device ^ slot) for device in range(devices)]
-        moved.append(lax.ppermute(pieces[slot], "kb", pairs))
-    return moved
+def swap(piece, slot, devices):
+    if slot == 0:
+        return piece
+    return lax.ppermute(piece, "kb", [(device, device ^ slot) for device in range(devices)])
 
 
 def trig_pair(angle_int, period, scale):
@@ -632,15 +659,22 @@
     one_boson = boson_matrix(rows.reshape(-1), count).reshape(2, devices, half, count).swapaxes(0, 1)
     one_boson = one_boson.reshape(devices * ROWS, count).astype(np.float32)
 
+    shape = (near, 2, 2, entries, ROWS, lanes)
+    both = to_times(both_times_kernel, green, jnp.asarray(both_fermion), shape, devices, "both_times")
+    green, both = lax.optimization_barrier((green, both))
     shape = (devices, 2, entries, ROWS, lanes)
     one = to_times(one_times_kernel, green, jnp.asarray(one_fermion), shape, devices, "one_times")
-    green, one = lax.optimization_barrier((green, one))
-    shape = (near, 2, 2, entries, ROWS, lanes)
-    both = to_times(both_times_kernel, green, jnp.asarray(both_fermion), shape, devices, "both_times")
-    one, both = lax.optimization_barrier((exchange(one), both))
-    one, both = lax.optimization_barrier((one_middle(one, pair_table, mirror_map), exchange(both)))
-    pieces = swap(both_middle(both, pair_table, mirror_map, me, near), devices)
-    return to_frequencies(exchange(one), pieces, jnp.asarray(both_boson), jnp.asarray(one_boson), me)
+    both, one = lax.optimization_barrier((exchange(both), one))
+    pieces = both_middle(both, pair_table, mirror_map, me, near)
+    middle_slot, quarter = near // 2, near // 4
+    order = list(range(middle_slot, middle_slot + quarter)) + list(range(1, quarter + 1))
+    early = [swap(pieces[slot], slot, devices) for slot in order]
+    one, early = lax.optimization_barrier((exchange(one), early))
+    one = exchange(one_middle(one, pair_table, mirror_map))
+    rest = [slot for slot in reversed(range(near)) if slot not in order]
+    moved = dict(zip(order, early)) | {slot: swap(pieces[slot], slot, devices) for slot in rest}
+    pieces = [moved[slot] for slot in range(near)]
+    return to_frequencies(one, pieces, jnp.asarray(both_boson), jnp.asarray(one_boson), me)
 
 
 def solution(mesh):

time: 180 us -> 175 us (0.972)
  local copies, waits for them, and re-layouts: 27.1 us -> 2.71 us
  waiting for transfers between devices: 79.5 us -> 95.2 us
  Pallas kernels: 30.2 us -> 35.4 us
  starting transfers between devices: 41.6 us -> 39.6 us
    ppermute x15, waiting for transfers between devices: 20.8 us -> 52.7 us  [swap(): lax.ppermute(piece, 'kb', [(device, device ^ slot) for device in range(de...]
    unnamed x77 -> x52, local copies, waits for them, and re-layouts: 26.4 us -> 2.71 us
    all_to_all x3, waiting for transfers between devices: 58.8 us -> 42.5 us  [exchange(): lax.all_to_all(flat, 'kb', split_axis=0, concat_axis=0, tiled=True)]
    ppermute x15, starting transfers between devices: 26.5 us -> 22.5 us  [swap(): lax.ppermute(piece, 'kb', [(device, device ^ slot) for device in range(de...]
    pallas_call x1, Pallas kernels: 4.59 us -> 8.27 us  [to_frequencies(): pl.pallas_call(frequency_kernel, in_specs=[pl.BlockSpec(memory_space=pltp...]
    pallas_call x1, Pallas kernels: 6.38 us -> 8.93 us  [both_middle(): pl.pallas_call(both_middle_kernel, in_specs=[pl.BlockSpec(memory_space=pl...]
    all_to_all x3, starting transfers between devices: 15.1 us -> 17.1 us  [exchange(): lax.all_to_all(flat, 'kb', split_axis=0, concat_axis=0, tiled=True)]
  transfers between devices with their start and end apart: 18 -> 18, of which waited for: 11 -> 13; matrix products, arithmetic and copies ran while one was open for 1% -> 0% of each run, Pallas kernels for 11% -> 9%
where the time goes in v6:
time: 175 us; the launch traced here: 173 us
  waiting for transfers between devices  95.2 us (54%)
  starting transfers between devices  39.6 us (23%)
  Pallas kernels  35.4 us (20%)
  local copies, waits for them, and re-layouts  2.71 us (2%)
    ppermute x15, waiting for transfers between devices, swap(): lax.ppermute(piece, 'kb', [(device, device ^ slot) for device in range(de...  52.7 us
    all_to_all x3, waiting for transfers between devices, exchange(): lax.all_to_all(flat, 'kb', split_axis=0, concat_axis=0, tiled=True)  42.5 us
    ppermute x15, starting transfers between devices, swap(): lax.ppermute(piece, 'kb', [(device, device ^ slot) for device in range(de...  22.5 us
    all_to_all x3, starting transfers between devices, exchange(): lax.all_to_all(flat, 'kb', split_axis=0, concat_axis=0, tiled=True)  17.1 us
    pallas_call x2, Pallas kernels, to_times(): pl.pallas_call(kernel, in_specs=[hbm, hbm], out_specs=hbm, out_shape=jax....  11.6 us
    pallas_call x1, Pallas kernels, both_middle(): pl.pallas_call(both_middle_kernel, in_specs=[pl.BlockSpec(memory_space=pl...  8.93 us
    pallas_call x1, Pallas kernels, to_frequencies(): pl.pallas_call(frequency_kernel, in_specs=[pl.BlockSpec(memory_space=pltp...  8.27 us
    pallas_call x1, Pallas kernels, one_middle(): pl.pallas_call(one_middle_kernel, in_specs=specs, out_specs=pl.BlockSpec(...  6.58 us
  transfers between devices with their start and end apart: 18, of which 13 were waited for; matrix products, arithmetic and copies ran while one was open for 0% of the time, Pallas kernels for 9%

profile of v6, /device:TPU:0, one launch (start us, length us, event | category | flops | bytes accessed | tf_op | source)
XLA Modules:
  0.0 173.4 jit_solution(8397068087765818913)
XLA Ops:
  0.0 4.9 %both_times.1 = f32[32,2,2,4,8,128]{5,4,3,2,1,0:T(8,128)} custom-call(f32[2,4,128,512]{3,2,1,0:T(8,128)} %g_hbm.2, f32[256,512]{1,0:T(8,128)} %constant.20.clone.m_hbm), custom_call_target="tpu_custom_call" | custom-call | tf_op jit(solution)/shard_map/both_times/pallas_call | solution.py:186
  4.9 7.3 %all-to-all-start = ((f32[32,128,128]{2,1,0:T(8,128)}), f32[32,128,128]{2,1,0:T(8,128)S(1)}, u32[]{:S(2)}, u32[]{:S(2)}) async-start(f32[32,128,128]{2,1,0:T(8,128)} %bitcast.15), calls=%async_computation | async-start | bytes 4194304 | tf_op jit(solution)/shard_map/all_to_all | solution.py:516
  12.2 6.7 %one_times.1 = f32[32,2,4,8,128]{4,3,2,1,0:T(8,128)} custom-call(f32[2,4,128,512]{3,2,1,0:T(8,128)} %g_hbm.2, f32[512,512]{1,0:T(8,128)} %constant.21.clone.m_hbm), custom_call_target="tpu_custom_call" | custom-call | tf_op jit(solution)/shard_map/one_times/pallas_call | solution.py:186
  18.9 42.2 %all-to-all-done = f32[32,128,128]{2,1,0:T(8,128)S(1)} async-done(((f32[32,128,128]{2,1,0:T(8,128)}), f32[32,128,128]{2,1,0:T(8,128)S(1)}, u32[]{:S(2)}, u32[]{:S(2)}) %all-to-all-start) | async-done | bytes 2097184 | tf_op jit(solution)/shard_map/all_to_all | solution.py:516
  61.1 1.3 copy-done.7
  62.5 4.2 %all-to-all-start.1 = ((f32[32,64,128]{2,1,0:T(8,128)}), f32[32,64,128]{2,1,0:T(8,128)S(1)}, u32[]{:S(2)}, u32[]{:S(2)}) async-start(f32[32,64,128]{2,1,0:T(8,128)} %bitcast.16), calls=%async_computation.1 | async-start | bytes 2097152 | tf_op jit(solution)/shard_map/all_to_all | solution.py:516
  66.7 8.9 %both_middle.1 = (f32[2,2,8,8,128]{4,3,2,1,0:T(8,128)}, f32[2,2,8,8,128]{4,3,2,1,0:T(8,128)}, f32[2,2,8,8,128]{4,3,2,1,0:T(8,128)}, f32[2,2,8,8,128]{4,3,2,1,0:T...) custom-call(s32[1]{0:T(128)} %bitcast.me_ref, ...), custom_call_target="tpu_custom_call" | custom-call | tf_op jit(solution)/shard_map/both_middle/pallas_call | solution.py:433
  75.6 1.7 collective-permute-start
  77.3 2.4 %collective-permute-start.2 = (f32[2,2,8,8,128]{4,3,2,1,0:T(8,128)}, f32[2,2,8,8,128]{4,3,2,1,0:T(8,128)S(1)}, u32[]{:S(2)}, u32[]{:S(2)}) collective-permute-start(f32[2,2,8,8,128]{4,3,2,1,0:T(8,128)} %get-tuple-element.40), channel_id=1, source_target_pairs={{0,10},{1,11},{2,8},{3,9},{4,14},{5,15},{6,12},{7,13},{8,2},{9,3},... | collective-permute-start | bytes 393224 | tf_op jit(solution)/shard_map/ppermute | solution.py:522
  80.3 7.2 %collective-permute-done.refs_8_ = f32[2,2,8,8,128]{4,3,2,1,0:T(8,128)S(1)} collective-permute-done((f32[2,2,8,8,128]{4,3,2,1,0:T(8,128)}, f32[2,2,8,8,128]{4,3,2,1,0:T(8,128)S(1)}, u32[]{:S(2)}, u32[]{:S(2)}) %collective-permute-start) | collective-permute-done | bytes 131104 | tf_op jit(solution)/shard_map/ppermute | solution.py:522
  87.5 1.7 collective-permute-start.5
  89.2 1.1 collective-permute-done.1.refs_9_
  90.3 2.2 %collective-permute-start.6 = (f32[2,2,8,8,128]{4,3,2,1,0:T(8,128)}, f32[2,2,8,8,128]{4,3,2,1,0:T(8,128)S(1)}, u32[]{:S(2)}, u32[]{:S(2)}) collective-permute-start(f32[2,2,8,8,128]{4,3,2,1,0:T(8,128)} %get-tuple-element.44), channel_id=1, source_target_pairs={{0,3},{1,2},{2,1},{3,0},{4,7},{5,6},{6,5},{7,4},{8,11},{9,10},{10,... | collective-permute-start | bytes 393224 | tf_op jit(solution)/shard_map/ppermute | solution.py:522
  92.4 3.7 %collective-permute-done.2.refs_10_ = f32[2,2,8,8,128]{4,3,2,1,0:T(8,128)S(1)} collective-permute-done((f32[2,2,8,8,128]{4,3,2,1,0:T(8,128)}, f32[2,2,8,8,128]{4,3,2,1,0:T(8,128)S(1)}, u32[]{:S(2)}, u32[]{:S(2)}) %collective-permute-start.2) | collective-permute-done | bytes 131104 | tf_op jit(solution)/shard_map/ppermute | solution.py:522
  96.1 1.3 collective-permute-start.7
  98.0 1.9 %collective-permute-done.5.refs_2_ = f32[2,2,8,8,128]{4,3,2,1,0:T(8,128)S(1)} collective-permute-done((f32[2,2,8,8,128]{4,3,2,1,0:T(8,128)}, f32[2,2,8,8,128]{4,3,2,1,0:T(8,128)S(1)}, u32[]{:S(2)}, u32[]{:S(2)}) %collective-permute-start.5) | collective-permute-done | bytes 131104 | tf_op jit(solution)/shard_map/ppermute | solution.py:522
  99.9 1.5 collective-permute-done.6.refs_3_
  101.4 6.6 %one_middle.1 = f32[16,2,2,8,8,128]{5,4,3,2,1,0:T(8,128)} custom-call(s32[2,8]{1,0:T(2,128)S(1)} %bitcast.12, s32[3,16]{1,0:T(4,128)S(1)} %copy-done.4, bf16[256,256]{1,0:T(8,128)(2,1)S(1)} %copy-done.3, bf16[256,256]{1,0:T(8,128)(2,1)S(1)} %copy-done.2, bf16[256,256]{1,0:T(8,128)(2,1)S(1)} %copy-done.1, bf16[256,256]{1,0:T(8,128)(2,1)S(1)} %copy-done, ...), custom_call_target="tpu_custom_call" | custom-call | tf_op jit(solution)/shard_map/one_middle/pallas_call | solution.py:407
  108.1 5.6 %all-to-all-start.2 = ((f32[32,128,128]{2,1,0:T(8,128)}), f32[32,128,128]{2,1,0:T(8,128)S(1)}, u32[]{:S(2)}, u32[]{:S(2)}) async-start(f32[32,128,128]{2,1,0:T(8,128)} %bitcast.8), calls=%async_computation.2 | async-start | bytes 4194304 | tf_op jit(solution)/shard_map/all_to_all | solution.py:516
  113.7 1.4 collective-permute-start.8
  115.1 1.5 collective-permute-start.9
  116.6 1.1 collective-permute-start.10
  117.7 1.5 collective-permute-start.11
  119.2 1.2 collective-permute-start.12
  120.4 17.2 %collective-permute-done.8.refs_5_ = f32[2,2,8,8,128]{4,3,2,1,0:T(8,128)S(1)} collective-permute-done((f32[2,2,8,8,128]{4,3,2,1,0:T(8,128)}, f32[2,2,8,8,128]{4,3,2,1,0:T(8,128)S(1)}, u32[]{:S(2)}, u32[]{:S(2)}) %collective-permute-start.8) | collective-permute-done | bytes 131104 | tf_op jit(solution)/shard_map/ppermute | solution.py:522
  137.6 5.9 %collective-permute-start.13 = (f32[2,2,8,8,128]{4,3,2,1,0:T(8,128)S(1)}, f32[2,2,8,8,128]{4,3,2,1,0:T(8,128)S(1)}, u32[]{:S(2)}, u32[]{:S(2)}) collective-permute-start(f32[2,2,8,8,128]{4,3,2,1,0:T(8,128)S(1)} %copy-done.24), channel_id=1, source_target_pairs={{0,14},{1,15},{2,12},{3,13},{4,10},{5,11},{6,8},{7,9},{8,6},{9,7},... | collective-permute-start | bytes 393224 | tf_op jit(solution)/shard_map/ppermute | solution.py:522
  143.7 8.4 %collective-permute-done.11.refs_12_ = f32[2,2,8,8,128]{4,3,2,1,0:T(8,128)S(1)} collective-permute-done((f32[2,2,8,8,128]{4,3,2,1,0:T(8,128)}, f32[2,2,8,8,128]{4,3,2,1,0:T(8,128)S(1)}, u32[]{:S(2)}, u32[]{:S(2)}) %collective-permute-start.11) | collective-permute-done | bytes 131104 | tf_op jit(solution)/shard_map/ppermute | solution.py:522
  152.1 3.9 %collective-permute-done.12.refs_13_ = f32[2,2,8,8,128]{4,3,2,1,0:T(8,128)S(1)} collective-permute-done((f32[2,2,8,8,128]{4,3,2,1,0:T(8,128)S(1)}, f32[2,2,8,8,128]{4,3,2,1,0:T(8,128)S(1)}, u32[]{:S(2)}, u32[]{:S(2)}) %collective-permute-start.12) | collective-permute-done | bytes 131104 | tf_op jit(solution)/shard_map/ppermute | solution.py:522
  156.0 4.5 %collective-permute-done.13.refs_14_ = f32[2,2,8,8,128]{4,3,2,1,0:T(8,128)S(1)} collective-permute-done((f32[2,2,8,8,128]{4,3,2,1,0:T(8,128)S(1)}, f32[2,2,8,8,128]{4,3,2,1,0:T(8,128)S(1)}, u32[]{:S(2)}, u32[]{:S(2)}) %collective-permute-start.13) | collective-permute-done | bytes 131104 | tf_op jit(solution)/shard_map/ppermute | solution.py:522
  160.6 2.7 %collective-permute-done.14.refs_15_ = f32[2,2,8,8,128]{4,3,2,1,0:T(8,128)S(1)} collective-permute-done((f32[2,2,8,8,128]{4,3,2,1,0:T(8,128)S(1)}, f32[2,2,8,8,128]{4,3,2,1,0:T(8,128)S(1)}, u32[]{:S(2)}, u32[]{:S(2)}) %collective-permute-start.14) | collective-permute-done | bytes 131104 | tf_op jit(solution)/shard_map/ppermute | solution.py:522
  163.9 1.0 copy-done.6
  164.9 8.3 %to_frequencies.1 = f32[2,8,128,512]{3,2,1,0:T(8,128)} custom-call(s32[1]{0:T(128)} %bitcast.me_ref, f32[2,16,8,512]{3,2,1,0:T(8,128)} %constant.26.clone.both_ref, f32[256,512]{1,0:T(8,128)} %constant.27.clone.one_ref, f32[32,2,8,8,128]{4,3,2,1,0:T(8,128)} %bitcast.13, f32[2,2,8,8,128]{4,3,2,1,0:T(8,128)} %get-tuple-element.47.refs_0_, ...), custom_call_target="tpu_custom_call" | custom-call | tf_op jit(solution)/shard_map/to_frequencies/pallas_call | solution.py:498
  (61 shorter events, 2.0 us)
Async XLA Ops:
  4.9 56.2 %all-to-all-start = ((f32[32,128,128]{2,1,0:T(8,128)}), f32[32,128,128]{2,1,0:T(8,128)S(1)}, u32[]{:S(2)}, u32[]{:S(2)}) async-start(f32[32,128,128]{2,1,0:T(8,128)} %bitcast.15), calls=%async_computation | async-start | bytes 4194304 | tf_op jit(solution)/shard_map/all_to_all | solution.py:516
  62.4 39.0 %copy-start = (bf16[256,256]{1,0:T(8,128)(2,1)S(1)}, bf16[256,256]{1,0:T(8,128)(2,1)}, u32[]{:S(2)}) copy-start(bf16[256,256]{1,0:T(8,128)(2,1)} %constant.25.clone.sl_ref) | copy-start | bytes 393220
  62.4 39.0 %copy-start.1 = (bf16[256,256]{1,0:T(8,128)(2,1)S(1)}, bf16[256,256]{1,0:T(8,128)(2,1)}, u32[]{:S(2)}) copy-start(bf16[256,256]{1,0:T(8,128)(2,1)} %constant.24.clone.sh_ref) | copy-start | bytes 393220
  62.4 39.0 %copy-start.2 = (bf16[256,256]{1,0:T(8,128)(2,1)S(1)}, bf16[256,256]{1,0:T(8,128)(2,1)}, u32[]{:S(2)}) copy-start(bf16[256,256]{1,0:T(8,128)(2,1)} %constant.23.clone.cl_ref) | copy-start | bytes 393220
  62.4 39.0 %copy-start.3 = (bf16[256,256]{1,0:T(8,128)(2,1)S(1)}, bf16[256,256]{1,0:T(8,128)(2,1)}, u32[]{:S(2)}) copy-start(bf16[256,256]{1,0:T(8,128)(2,1)} %constant.22.clone.ch_ref) | copy-start | bytes 393220
  62.4 39.0 %copy-start.4 = (s32[3,16]{1,0:T(4,128)S(1)}, s32[3,16]{1,0:T(4,128)}, u32[]{:S(2)}) copy-start(s32[3,16]{1,0:T(4,128)} %mirror_ref.3) | copy-start | bytes 580
  62.5 39.0 %copy-start.5 = (s32[8,2]{0,1:T(2,128)S(1)}, s32[8,2]{0,1:T(2,128)}, u32[]{:S(2)}) copy-start(s32[8,2]{0,1:T(2,128)} %param.16) | copy-start | bytes 196
  62.5 38.9 %all-to-all-start.1 = ((f32[32,64,128]{2,1,0:T(8,128)}), f32[32,64,128]{2,1,0:T(8,128)S(1)}, u32[]{:S(2)}, u32[]{:S(2)}) async-start(f32[32,64,128]{2,1,0:T(8,128)} %bitcast.16), calls=%async_computation.1 | async-start | bytes 2097152 | tf_op jit(solution)/shard_map/all_to_all | solution.py:516
  75.6 11.9 %collective-permute-start = (f32[2,2,8,8,128]{4,3,2,1,0:T(8,128)}, f32[2,2,8,8,128]{4,3,2,1,0:T(8,128)S(1)}, u32[]{:S(2)}, u32[]{:S(2)}) collective-permute-start(f32[2,2,8,8,128]{4,3,2,1,0:T(8,128)} %get-tuple-element.38), channel_id=1, source_target_pairs={{0,8},{1,9},{2,10},{3,11},{4,12},{5,13},{6,14},{7,15},{8,0},{9,1},... | collective-permute-start | bytes 393224 | tf_op jit(solution)/shard_map/ppermute | solution.py:522
  77.3 13.0 %collective-permute-start.1 = (f32[2,2,8,8,128]{4,3,2,1,0:T(8,128)}, f32[2,2,8,8,128]{4,3,2,1,0:T(8,128)S(1)}, u32[]{:S(2)}, u32[]{:S(2)}) collective-permute-start(f32[2,2,8,8,128]{4,3,2,1,0:T(8,128)} %get-tuple-element.39), channel_id=1, source_target_pairs={{0,9},{1,8},{2,11},{3,10},{4,13},{5,12},{6,15},{7,14},{8,1},{9,0},... | collective-permute-start | bytes 393224 | tf_op jit(solution)/shard_map/ppermute | solution.py:522
  77.3 18.8 %collective-permute-start.2 = (f32[2,2,8,8,128]{4,3,2,1,0:T(8,128)}, f32[2,2,8,8,128]{4,3,2,1,0:T(8,128)S(1)}, u32[]{:S(2)}, u32[]{:S(2)}) collective-permute-start(f32[2,2,8,8,128]{4,3,2,1,0:T(8,128)} %get-tuple-element.40), channel_id=1, source_target_pairs={{0,10},{1,11},{2,8},{3,9},{4,14},{5,15},{6,12},{7,13},{8,2},{9,3},... | collective-permute-start | bytes 393224 | tf_op jit(solution)/shard_map/ppermute | solution.py:522
  79.7 18.3 %collective-permute-start.3 = (f32[2,2,8,8,128]{4,3,2,1,0:T(8,128)}, f32[2,2,8,8,128]{4,3,2,1,0:T(8,128)S(1)}, u32[]{:S(2)}, u32[]{:S(2)}) collective-permute-start(f32[2,2,8,8,128]{4,3,2,1,0:T(8,128)} %get-tuple-element.41), channel_id=1, source_target_pairs={{0,11},{1,10},{2,9},{3,8},{4,15},{5,14},{6,13},{7,12},{8,3},{9,2},... | collective-permute-start | bytes 393224 | tf_op jit(solution)/shard_map/ppermute | solution.py:522
  80.0 17.9 %collective-permute-start.4 = (f32[2,2,8,8,128]{4,3,2,1,0:T(8,128)}, f32[2,2,8,8,128]{4,3,2,1,0:T(8,128)S(1)}, u32[]{:S(2)}, u32[]{:S(2)}) collective-permute-start(f32[2,2,8,8,128]{4,3,2,1,0:T(8,128)} %get-tuple-element.42), channel_id=1, source_target_pairs={{0,1},{1,0},{2,3},{3,2},{4,5},{5,4},{6,7},{7,6},{8,9},{9,8},{10,11... | collective-permute-start | bytes 393224 | tf_op jit(solution)/shard_map/ppermute | solution.py:522
  87.5 20.6 %copy-start.8 = (f32[2,2,8,8,128]{4,3,2,1,0:T(8,128)}, f32[2,2,8,8,128]{4,3,2,1,0:T(8,128)S(1)}, u32[]{:S(2)}) copy-start(f32[2,2,8,8,128]{4,3,2,1,0:T(8,128)S(1)} %collective-permute-done.refs_8_) | copy-start | bytes 393220
  87.5 12.4 %collective-permute-start.5 = (f32[2,2,8,8,128]{4,3,2,1,0:T(8,128)}, f32[2,2,8,8,128]{4,3,2,1,0:T(8,128)S(1)}, u32[]{:S(2)}, u32[]{:S(2)}) collective-permute-start(f32[2,2,8,8,128]{4,3,2,1,0:T(8,128)} %get-tuple-element.43), channel_id=1, source_target_pairs={{0,2},{1,3},{2,0},{3,1},{4,6},{5,7},{6,4},{7,5},{8,10},{9,11},{10,... | collective-permute-start | bytes 393224 | tf_op jit(solution)/shard_map/ppermute | solution.py:522
  90.3 17.8 %copy-start.9 = (f32[2,2,8,8,128]{4,3,2,1,0:T(8,128)}, f32[2,2,8,8,128]{4,3,2,1,0:T(8,128)S(1)}, u32[]{:S(2)}) copy-start(f32[2,2,8,8,128]{4,3,2,1,0:T(8,128)S(1)} %collective-permute-done.1.refs_9_) | copy-start | bytes 393220
  90.3 11.1 %collective-permute-start.6 = (f32[2,2,8,8,128]{4,3,2,1,0:T(8,128)}, f32[2,2,8,8,128]{4,3,2,1,0:T(8,128)S(1)}, u32[]{:S(2)}, u32[]{:S(2)}) collective-permute-start(f32[2,2,8,8,128]{4,3,2,1,0:T(8,128)} %get-tuple-element.44), channel_id=1, source_target_pairs={{0,3},{1,2},{2,1},{3,0},{4,7},{5,6},{6,5},{7,4},{8,11},{9,10},{10,... | collective-permute-start | bytes 393224 | tf_op jit(solution)/shard_map/ppermute | solution.py:522
  96.1 12.0 %copy-start.10 = (f32[2,2,8,8,128]{4,3,2,1,0:T(8,128)}, f32[2,2,8,8,128]{4,3,2,1,0:T(8,128)S(1)}, u32[]{:S(2)}) copy-start(f32[2,2,8,8,128]{4,3,2,1,0:T(8,128)S(1)} %collective-permute-done.2.refs_10_) | copy-start | bytes 393220
  96.1 5.3 %collective-permute-start.7 = (f32[2,2,8,8,128]{4,3,2,1,0:T(8,128)}, f32[2,2,8,8,128]{4,3,2,1,0:T(8,128)S(1)}, u32[]{:S(2)}, u32[]{:S(2)}) collective-permute-start(f32[2,2,8,8,128]{4,3,2,1,0:T(8,128)} %get-tuple-element.45), channel_id=1, source_target_pairs={{0,4},{1,5},{2,6},{3,7},{4,0},{5,1},{6,2},{7,3},{8,12},{9,13},{10,... | collective-permute-start | bytes 393224 | tf_op jit(solution)/shard_map/ppermute | solution.py:522
  108.0 29.6 %copy-start.24 = (f32[2,2,8,8,128]{4,3,2,1,0:T(8,128)S(1)}, f32[2,2,8,8,128]{4,3,2,1,0:T(8,128)}, u32[]{:S(2)}) copy-start(f32[2,2,8,8,128]{4,3,2,1,0:T(8,128)} %get-tuple-element.61) | copy-start | bytes 393220
  108.1 35.5 %copy-start.23 = (f32[2,2,8,8,128]{4,3,2,1,0:T(8,128)S(1)}, f32[2,2,8,8,128]{4,3,2,1,0:T(8,128)}, u32[]{:S(2)}) copy-start(f32[2,2,8,8,128]{4,3,2,1,0:T(8,128)} %get-tuple-element.62) | copy-start | bytes 393220
  108.1 55.4 %all-to-all-start.2 = ((f32[32,128,128]{2,1,0:T(8,128)}), f32[32,128,128]{2,1,0:T(8,128)S(1)}, u32[]{:S(2)}, u32[]{:S(2)}) async-start(f32[32,128,128]{2,1,0:T(8,128)} %bitcast.8), calls=%async_computation.2 | async-start | bytes 4194304 | tf_op jit(solution)/shard_map/all_to_all | solution.py:516
  113.7 23.9 %collective-permute-start.8 = (f32[2,2,8,8,128]{4,3,2,1,0:T(8,128)}, f32[2,2,8,8,128]{4,3,2,1,0:T(8,128)S(1)}, u32[]{:S(2)}, u32[]{:S(2)}) collective-permute-start(f32[2,2,8,8,128]{4,3,2,1,0:T(8,128)} %get-tuple-element.52), channel_id=1, source_target_pairs={{0,5},{1,4},{2,7},{3,6},{4,1},{5,0},{6,3},{7,2},{8,13},{9,12},{10,... | collective-permute-start | bytes 393224 | tf_op jit(solution)/shard_map/ppermute | solution.py:522
  115.1 28.5 %collective-permute-start.9 = (f32[2,2,8,8,128]{4,3,2,1,0:T(8,128)}, f32[2,2,8,8,128]{4,3,2,1,0:T(8,128)S(1)}, u32[]{:S(2)}, u32[]{:S(2)}) collective-permute-start(f32[2,2,8,8,128]{4,3,2,1,0:T(8,128)} %get-tuple-element.53), channel_id=1, source_target_pairs={{0,6},{1,7},{2,4},{3,5},{4,2},{5,3},{6,0},{7,1},{8,14},{9,15},{10,... | collective-permute-start | bytes 393224 | tf_op jit(solution)/shard_map/ppermute | solution.py:522
  116.6 27.1 %collective-permute-start.10 = (f32[2,2,8,8,128]{4,3,2,1,0:T(8,128)}, f32[2,2,8,8,128]{4,3,2,1,0:T(8,128)S(1)}, u32[]{:S(2)}, u32[]{:S(2)}) collective-permute-start(f32[2,2,8,8,128]{4,3,2,1,0:T(8,128)} %get-tuple-element.54), channel_id=1, source_target_pairs={{0,7},{1,6},{2,5},{3,4},{4,3},{5,2},{6,1},{7,0},{8,15},{9,14},{10,... | collective-permute-start | bytes 393224 | tf_op jit(solution)/shard_map/ppermute | solution.py:522
  117.7 34.4 %collective-permute-start.11 = (f32[2,2,8,8,128]{4,3,2,1,0:T(8,128)}, f32[2,2,8,8,128]{4,3,2,1,0:T(8,128)S(1)}, u32[]{:S(2)}, u32[]{:S(2)}) collective-permute-start(f32[2,2,8,8,128]{4,3,2,1,0:T(8,128)} %get-tuple-element.59), channel_id=1, source_target_pairs={{0,12},{1,13},{2,14},{3,15},{4,8},{5,9},{6,10},{7,11},{8,4},{9,5},... | collective-permute-start | bytes 393224 | tf_op jit(solution)/shard_map/ppermute | solution.py:522
  119.2 36.9 %collective-permute-start.12 = (f32[2,2,8,8,128]{4,3,2,1,0:T(8,128)S(1)}, f32[2,2,8,8,128]{4,3,2,1,0:T(8,128)S(1)}, u32[]{:S(2)}, u32[]{:S(2)}) collective-permute-start(f32[2,2,8,8,128]{4,3,2,1,0:T(8,128)S(1)} %copy-done.25), channel_id=1, source_target_pairs={{0,13},{1,12},{2,15},{3,14},{4,9},{5,8},{6,11},{7,10},{8,5},{9,4},... | collective-permute-start | bytes 393224 | tf_op jit(solution)/shard_map/ppermute | solution.py:522
  137.6 26.0 %copy-start.16 = (f32[2,2,8,8,128]{4,3,2,1,0:T(8,128)}, f32[2,2,8,8,128]{4,3,2,1,0:T(8,128)S(1)}, u32[]{:S(2)}) copy-start(f32[2,2,8,8,128]{4,3,2,1,0:T(8,128)S(1)} %collective-permute-done.8.refs_5_) | copy-start | bytes 393220
  137.6 23.0 %collective-permute-start.13 = (f32[2,2,8,8,128]{4,3,2,1,0:T(8,128)S(1)}, f32[2,2,8,8,128]{4,3,2,1,0:T(8,128)S(1)}, u32[]{:S(2)}, u32[]{:S(2)}) collective-permute-start(f32[2,2,8,8,128]{4,3,2,1,0:T(8,128)S(1)} %copy-done.24), channel_id=1, source_target_pairs={{0,14},{1,15},{2,12},{3,13},{4,10},{5,11},{6,8},{7,9},{8,6},{9,7},... | collective-permute-start | bytes 393224 | tf_op jit(solution)/shard_map/ppermute | solution.py:522
  143.6 20.0 %copy-start.17 = (f32[2,2,8,8,128]{4,3,2,1,0:T(8,128)}, f32[2,2,8,8,128]{4,3,2,1,0:T(8,128)S(1)}, u32[]{:S(2)}) copy-start(f32[2,2,8,8,128]{4,3,2,1,0:T(8,128)S(1)} %collective-permute-done.9.refs_6_) | copy-start | bytes 393220
  143.6 19.7 %collective-permute-start.14 = (f32[2,2,8,8,128]{4,3,2,1,0:T(8,128)S(1)}, f32[2,2,8,8,128]{4,3,2,1,0:T(8,128)S(1)}, u32[]{:S(2)}, u32[]{:S(2)}) collective-permute-start(f32[2,2,8,8,128]{4,3,2,1,0:T(8,128)S(1)} %copy-done.23), channel_id=1, source_target_pairs={{0,15},{1,14},{2,13},{3,12},{4,11},{5,10},{6,9},{7,8},{8,7},{9,6},... | collective-permute-start | bytes 393224 | tf_op jit(solution)/shard_map/ppermute | solution.py:522
  143.7 19.9 %copy-start.18 = (f32[2,2,8,8,128]{4,3,2,1,0:T(8,128)}, f32[2,2,8,8,128]{4,3,2,1,0:T(8,128)S(1)}, u32[]{:S(2)}) copy-start(f32[2,2,8,8,128]{4,3,2,1,0:T(8,128)S(1)} %collective-permute-done.10.refs_7_) | copy-start | bytes 393220
  (12 other events, 78.6 us)

commit v7 on v6

--- a/solution.py
+++ b/solution.py
@@ -196,7 +196,7 @@
             pltpu.SemaphoreType.DMA,
             pltpu.SemaphoreType.DMA((entries, 2)),
         ],
-        compiler_params=pltpu.CompilerParams(vmem_limit_bytes=60 << 20),
+        compiler_params=pltpu.CompilerParams(vmem_limit_bytes=63 << 20),
         name=name,
     )(green, matrix)
 
@@ -447,40 +447,57 @@
     )(me, *args)
 
 
-def frequency_kernel(me_ref, both_ref, one_ref, y_ref, *refs):
-    pieces, (out_ref, held, stage, in_sems, sems) = refs[:-5], refs[-5:]
+def frequency_kernel(me_ref, y_ref, both_hbm, one_hbm, *refs):
+    pieces, (out_ref, both_ref, one_ref, held, stage, m_sems, in_sems, sems) = refs[:-8], refs[-8:]
     near = len(pieces)
     devices, _, components, rows, lanes = y_ref.shape
     groups = sems.shape[0]
     members = components // groups
+    matrices = [
+        pltpu.make_async_copy(one_hbm, one_ref, m_sems.at[0]),
+        pltpu.make_async_copy(both_hbm, both_ref, m_sems.at[1]),
+    ]
     loads = [pltpu.make_async_copy(piece, held.at[slot], in_sems.at[slot]) for slot, piece in enumerate(pieces)]
-    for copy in loads:
+    for copy in matrices + loads:
         copy.start()
     me = me_ref[0] % near
-    both = [both_ref[part, slot ^ me] for part in range(2) for slot in range(near)]
-    matrix = split_value(jnp.concatenate(both + [one_ref[...]], axis=0))
     upper_rows = lax.broadcasted_iota(jnp.int32, (devices, rows, lanes), 1) < rows // 2
-    for copy in loads:
-        copy.wait()
-
-    copies = []
-    for group in range(groups):
+
+    def one_part(group):
+        values = []
+        for c in range(group * members, (group + 1) * members):
+            folded = []
+            for ri in range(2):
+                tile = y_ref[:, ri, c]
+                turned = pltpu.roll(tile, rows // 2, 1)
+                folded.append((tile + turned, turned - tile))
+            first = jnp.where(upper_rows, folded[0][0], -folded[1][1])
+            second = jnp.where(upper_rows, folded[1][0], folded[0][1])
+            values.append(first.reshape(devices * rows, lanes).T)
+            values.append(second.reshape(devices * rows, lanes).T)
+        return dot3(split_value(jnp.concatenate(values, axis=0)), one, ((1,), (0,)))
+
+    def both_part(group):
         values = []
         for c in range(group * members, (group + 1) * members):
             part = [[held[:, half, ri, c].reshape(near * rows, lanes) for ri in range(2)] for half in range(2)]
             sums = [part[0][ri] + part[1][ri] for ri in range(2)]
             differences = [part[0][ri] - part[1][ri] for ri in range(2)]
-            folded = []
-            for ri in range(2):
-                tile = y_ref[:, ri, c]
-                turned = pltpu.roll(tile, rows // 2, 1)
-                folded.append((tile + turned, turned - tile))
-            first = jnp.where(upper_rows, folded[0][0], -folded[1][1]).reshape(devices * rows, lanes)
-            second = jnp.where(upper_rows, folded[1][0], folded[0][1]).reshape(devices * rows, lanes)
-            values.append(jnp.concatenate([sums[0], -differences[1], first], axis=0).T)
-            values.append(jnp.concatenate([sums[1], differences[0], second], axis=0).T)
-        d = dot3(split_value(jnp.concatenate(values, axis=0)), matrix, ((1,), (0,)))
-        d = d.reshape(members, 2, lanes, d.shape[1])
+            values.append(jnp.concatenate([sums[0], -differences[1]], axis=0).T)
+            values.append(jnp.concatenate([sums[1], differences[0]], axis=0).T)
+        return dot3(split_value(jnp.concatenate(values, axis=0)), both, ((1,), (0,)))
+
+    copies = []
+    matrices[0].wait()
+    one = split_value(one_ref[...])
+    for group in range(groups):
+        d = one_part(group)
+        if group == 0:
+            for copy in matrices[1:] + loads:
+                copy.wait()
+            ordered = [both_ref[part, slot ^ me] for part in range(2) for slot in range(near)]
+            both = split_value(jnp.concatenate(ordered, axis=0))
+        d = (d + both_part(group)).reshape(members, 2, lanes, d.shape[1])
         for ri in range(2):
             stage[ri, group * members : (group + 1) * members] = d[:, ri]
         cut = pl.ds(group * members, members)
@@ -495,20 +512,24 @@
     shape = (2, components, lanes, one.shape[1])
     vmem = pl.BlockSpec(memory_space=pltpu.VMEM)
     hbm = pl.BlockSpec(memory_space=pltpu.HBM)
+    kept = y.size * 4 + (96 << 10)
     return pl.pallas_call(
         frequency_kernel,
-        in_specs=[pl.BlockSpec(memory_space=pltpu.SMEM)] + [vmem] * 3 + [hbm] * len(pieces),
+        in_specs=[pl.BlockSpec(memory_space=pltpu.SMEM), vmem] + [hbm] * (2 + len(pieces)),
         out_specs=hbm,
         out_shape=jax.ShapeDtypeStruct(shape, jnp.float32),
         scratch_shapes=[
+            pltpu.VMEM(both.shape, jnp.float32),
+            pltpu.VMEM(one.shape, jnp.float32),
             pltpu.VMEM((len(pieces),) + pieces[0].shape, jnp.float32),
             pltpu.VMEM(shape, jnp.float32),
+            pltpu.SemaphoreType.DMA((2,)),
             pltpu.SemaphoreType.DMA((len(pieces),)),
             pltpu.SemaphoreType.DMA((components // 2,)),
         ],
-        compiler_params=pltpu.CompilerParams(vmem_limit_bytes=60 << 20),
+        compiler_params=pltpu.CompilerParams(vmem_limit_bytes=(64 << 20) - kept),
         name="to_frequencies",
-    )(me, both, one, y, *pieces)
+    )(me, y, both, one, *pieces)
 
 
 def exchange(x):
@@ -667,7 +688,7 @@
     both, one = lax.optimization_barrier((exchange(both), one))
     pieces = both_middle(both, pair_table, mirror_map, me, near)
     middle_slot, quarter = near // 2, near // 4
-    order = list(range(middle_slot, middle_slot + quarter)) + list(range(1, quarter + 1))
+    order = list(range(middle_slot, middle_slot + quarter)) + [1]
     early = [swap(pieces[slot], slot, devices) for slot in order]
     one, early = lax.optimization_barrier((exchange(one), early))
     one = exchange(one_middle(one, pair_table, mirror_map))

time: 175 us -> 171 us (0.977)
  starting transfers between devices: 39.6 us -> 31.8 us
  waiting for transfers between devices: 95.2 us -> 100 us
    ppermute x15, starting transfers between devices: 22.5 us -> 16.1 us  [swap(): lax.ppermute(piece, 'kb', [(device, device ^ slot) for device in range(de...]
    ppermute x15, waiting for transfers between devices: 52.7 us -> 58.1 us  [swap(): lax.ppermute(piece, 'kb', [(device, device ^ slot) for device in range(de...]
where the time goes in v7:
time: 171 us
  waiting for transfers between devices  100 us (58%)
  Pallas kernels  35.6 us (21%)
  starting transfers between devices  31.8 us (19%)
  local copies, waits for them, and re-layouts  2.73 us (2%)
    ppermute x15, waiting for transfers between devices, swap(): lax.ppermute(piece, 'kb', [(device, device ^ slot) for device in range(de...  58.1 us
    all_to_all x3, waiting for transfers between devices, exchange(): lax.all_to_all(flat, 'kb', split_axis=0, concat_axis=0, tiled=True)  42.2 us
    ppermute x15, starting transfers between devices, swap(): lax.ppermute(piece, 'kb', [(device, device ^ slot) for device in range(de...  16.1 us
    all_to_all x3, starting transfers between devices, exchange(): lax.all_to_all(flat, 'kb', split_axis=0, concat_axis=0, tiled=True)  15.8 us
    pallas_call x2, Pallas kernels, to_times(): pl.pallas_call(kernel, in_specs=[hbm, hbm], out_specs=hbm, out_shape=jax....  11.6 us
    pallas_call x1, Pallas kernels, both_middle(): pl.pallas_call(both_middle_kernel, in_specs=[pl.BlockSpec(memory_space=pl...  8.96 us
    pallas_call x1, Pallas kernels, to_frequencies(): pl.pallas_call(frequency_kernel, in_specs=[pl.BlockSpec(memory_space=pltp...  8.4 us
    pallas_call x1, Pallas kernels, one_middle(): pl.pallas_call(one_middle_kernel, in_specs=specs, out_specs=pl.BlockSpec(...  6.59 us
  transfers between devices with their start and end apart: 18, of which 13 were waited for; matrix products, arithmetic and copies ran while one was open for 0% of the time, Pallas kernels for 9%

profile of v7, /device:TPU:0, one launch (start us, length us, event | category | flops | bytes accessed | tf_op | source)
XLA Modules:
  0.0 170.9 jit_solution(11288259480525100597)
XLA Ops:
  0.0 4.9 %both_times.1 = f32[32,2,2,4,8,128]{5,4,3,2,1,0:T(8,128)} custom-call(f32[2,4,128,512]{3,2,1,0:T(8,128)} %g_hbm.2, f32[256,512]{1,0:T(8,128)} %constant.20.clone.m_hbm), custom_call_target="tpu_custom_call" | custom-call | tf_op jit(solution)/shard_map/both_times/pallas_call | solution.py:186
  4.9 7.4 %all-to-all-start = ((f32[32,128,128]{2,1,0:T(8,128)}), f32[32,128,128]{2,1,0:T(8,128)}, u32[]{:S(2)}, u32[]{:S(2)}) async-start(f32[32,128,128]{2,1,0:T(8,128)} %bitcast.14), calls=%async_computation | async-start | bytes 4194304 | tf_op jit(solution)/shard_map/all_to_all | solution.py:537
  12.3 6.7 %one_times.1 = f32[32,2,4,8,128]{4,3,2,1,0:T(8,128)} custom-call(f32[2,4,128,512]{3,2,1,0:T(8,128)} %g_hbm.2, f32[512,512]{1,0:T(8,128)} %constant.21.clone.m_hbm), custom_call_target="tpu_custom_call" | custom-call | tf_op jit(solution)/shard_map/one_times/pallas_call | solution.py:186
  19.1 42.2 %all-to-all-done = f32[32,128,128]{2,1,0:T(8,128)} async-done(((f32[32,128,128]{2,1,0:T(8,128)}), f32[32,128,128]{2,1,0:T(8,128)}, u32[]{:S(2)}, u32[]{:S(2)}) %all-to-all-start) | async-done | bytes 2097184 | tf_op jit(solution)/shard_map/all_to_all | solution.py:537
  61.3 4.2 %all-to-all-start.1 = ((f32[32,64,128]{2,1,0:T(8,128)}), f32[32,64,128]{2,1,0:T(8,128)S(1)}, u32[]{:S(2)}, u32[]{:S(2)}) async-start(f32[32,64,128]{2,1,0:T(8,128)} %bitcast.15), calls=%async_computation.1 | async-start | bytes 2097152 | tf_op jit(solution)/shard_map/all_to_all | solution.py:537
  65.5 9.0 %both_middle.1 = (f32[2,2,8,8,128]{4,3,2,1,0:T(8,128)}, f32[2,2,8,8,128]{4,3,2,1,0:T(8,128)}, f32[2,2,8,8,128]{4,3,2,1,0:T(8,128)}, f32[2,2,8,8,128]{4,3,2,1,0:T...) custom-call(s32[1]{0:T(128)} %bitcast.me_ref, ...), custom_call_target="tpu_custom_call" | custom-call | tf_op jit(solution)/shard_map/both_middle/pallas_call | solution.py:433
  74.4 1.6 collective-permute-start
  76.1 2.4 %collective-permute-start.2 = (f32[2,2,8,8,128]{4,3,2,1,0:T(8,128)}, f32[2,2,8,8,128]{4,3,2,1,0:T(8,128)S(1)}, u32[]{:S(2)}, u32[]{:S(2)}) collective-permute-start(f32[2,2,8,8,128]{4,3,2,1,0:T(8,128)} %get-tuple-element.37), channel_id=1, source_target_pairs={{0,10},{1,11},{2,8},{3,9},{4,14},{5,15},{6,12},{7,13},{8,2},{9,3},... | collective-permute-start | bytes 393224 | tf_op jit(solution)/shard_map/ppermute | solution.py:543
  78.5 0.4 collective-permute-start.3
  79.1 7.1 %collective-permute-done.refs_8_ = f32[2,2,8,8,128]{4,3,2,1,0:T(8,128)S(1)} collective-permute-done((f32[2,2,8,8,128]{4,3,2,1,0:T(8,128)}, f32[2,2,8,8,128]{4,3,2,1,0:T(8,128)S(1)}, u32[]{:S(2)}, u32[]{:S(2)}) %collective-permute-start) | collective-permute-done | bytes 131104 | tf_op jit(solution)/shard_map/ppermute | solution.py:543
  86.3 2.8 %collective-permute-done.1.refs_9_ = f32[2,2,8,8,128]{4,3,2,1,0:T(8,128)S(1)} collective-permute-done((f32[2,2,8,8,128]{4,3,2,1,0:T(8,128)}, f32[2,2,8,8,128]{4,3,2,1,0:T(8,128)S(1)}, u32[]{:S(2)}, u32[]{:S(2)}) %collective-permute-start.1) | collective-permute-done | bytes 131104 | tf_op jit(solution)/shard_map/ppermute | solution.py:543
  89.1 5.7 %collective-permute-done.2.refs_10_ = f32[2,2,8,8,128]{4,3,2,1,0:T(8,128)S(1)} collective-permute-done((f32[2,2,8,8,128]{4,3,2,1,0:T(8,128)}, f32[2,2,8,8,128]{4,3,2,1,0:T(8,128)S(1)}, u32[]{:S(2)}, u32[]{:S(2)}) %collective-permute-start.2) | collective-permute-done | bytes 131104 | tf_op jit(solution)/shard_map/ppermute | solution.py:543
  94.8 1.9 %collective-permute-done.3.refs_11_ = f32[2,2,8,8,128]{4,3,2,1,0:T(8,128)S(1)} collective-permute-done((f32[2,2,8,8,128]{4,3,2,1,0:T(8,128)}, f32[2,2,8,8,128]{4,3,2,1,0:T(8,128)S(1)}, u32[]{:S(2)}, u32[]{:S(2)}) %collective-permute-start.3) | collective-permute-done | bytes 131104 | tf_op jit(solution)/shard_map/ppermute | solution.py:543
  96.7 0.6 copy-done.10
  97.4 6.6 %one_middle.1 = f32[16,2,2,8,8,128]{5,4,3,2,1,0:T(8,128)} custom-call(s32[2,8]{1,0:T(2,128)S(1)} %bitcast.12, s32[3,16]{1,0:T(4,128)S(1)} %copy-done.4, bf16[256,256]{1,0:T(8,128)(2,1)S(1)} %copy-done.3, bf16[256,256]{1,0:T(8,128)(2,1)S(1)} %copy-done.2, bf16[256,256]{1,0:T(8,128)(2,1)S(1)} %copy-done.1, bf16[256,256]{1,0:T(8,128)(2,1)S(1)} %copy-done, ...), custom_call_target="tpu_custom_call" | custom-call | tf_op jit(solution)/shard_map/one_middle/pallas_call | solution.py:407
  104.1 4.1 %all-to-all-start.2 = ((f32[32,128,128]{2,1,0:T(8,128)}), f32[32,128,128]{2,1,0:T(8,128)S(1)}, u32[]{:S(2)}, u32[]{:S(2)}) async-start(f32[32,128,128]{2,1,0:T(8,128)} %bitcast.8), calls=%async_computation.2 | async-start | bytes 4194304 | tf_op jit(solution)/shard_map/all_to_all | solution.py:537
  108.2 1.6 collective-permute-start.5
  109.9 1.5 collective-permute-start.7
  111.4 0.4 collective-permute-start.8
  111.8 2.5 %collective-permute-start.9 = (f32[2,2,8,8,128]{4,3,2,1,0:T(8,128)S(1)}, f32[2,2,8,8,128]{4,3,2,1,0:T(8,128)S(1)}, u32[]{:S(2)}, u32[]{:S(2)}) collective-permute-start(f32[2,2,8,8,128]{4,3,2,1,0:T(8,128)S(1)} %copy-done.25), channel_id=1, source_target_pairs={{0,6},{1,7},{2,4},{3,5},{4,2},{5,3},{6,0},{7,1},{8,14},{9,15},{10,... | collective-permute-start | bytes 393224 | tf_op jit(solution)/shard_map/ppermute | solution.py:543
  114.2 13.1 %collective-permute-done.5.refs_2_ = f32[2,2,8,8,128]{4,3,2,1,0:T(8,128)S(1)} collective-permute-done((f32[2,2,8,8,128]{4,3,2,1,0:T(8,128)S(1)}, f32[2,2,8,8,128]{4,3,2,1,0:T(8,128)S(1)}, u32[]{:S(2)}, u32[]{:S(2)}) %collective-permute-start.5) | collective-permute-done | bytes 131104 | tf_op jit(solution)/shard_map/ppermute | solution.py:543
  127.7 4.5 %collective-permute-done.6.refs_3_ = f32[2,2,8,8,128]{4,3,2,1,0:T(8,128)S(1)} collective-permute-done((f32[2,2,8,8,128]{4,3,2,1,0:T(8,128)S(1)}, f32[2,2,8,8,128]{4,3,2,1,0:T(8,128)S(1)}, u32[]{:S(2)}, u32[]{:S(2)}) %collective-permute-start.6) | collective-permute-done | bytes 131104 | tf_op jit(solution)/shard_map/ppermute | solution.py:543
  132.3 4.8 %collective-permute-start.12 = (f32[2,2,8,8,128]{4,3,2,1,0:T(8,128)S(1)}, f32[2,2,8,8,128]{4,3,2,1,0:T(8,128)S(1)}, u32[]{:S(2)}, u32[]{:S(2)}) collective-permute-start(f32[2,2,8,8,128]{4,3,2,1,0:T(8,128)S(1)} %copy-done.22), channel_id=1, source_target_pairs={{0,13},{1,12},{2,15},{3,14},{4,9},{5,8},{6,11},{7,10},{8,5},{9,4},... | collective-permute-start | bytes 393224 | tf_op jit(solution)/shard_map/ppermute | solution.py:543
  137.4 3.4 %collective-permute-done.9.refs_6_ = f32[2,2,8,8,128]{4,3,2,1,0:T(8,128)S(1)} collective-permute-done((f32[2,2,8,8,128]{4,3,2,1,0:T(8,128)S(1)}, f32[2,2,8,8,128]{4,3,2,1,0:T(8,128)S(1)}, u32[]{:S(2)}, u32[]{:S(2)}) %collective-permute-start.9) | collective-permute-done | bytes 131104 | tf_op jit(solution)/shard_map/ppermute | solution.py:543
  140.8 3.7 %collective-permute-done.10.refs_7_ = f32[2,2,8,8,128]{4,3,2,1,0:T(8,128)S(1)} collective-permute-done((f32[2,2,8,8,128]{4,3,2,1,0:T(8,128)S(1)}, f32[2,2,8,8,128]{4,3,2,1,0:T(8,128)S(1)}, u32[]{:S(2)}, u32[]{:S(2)}) %collective-permute-start.10) | collective-permute-done | bytes 131104 | tf_op jit(solution)/shard_map/ppermute | solution.py:543
  144.5 2.0 %collective-permute-done.11.refs_12_ = f32[2,2,8,8,128]{4,3,2,1,0:T(8,128)S(1)} collective-permute-done((f32[2,2,8,8,128]{4,3,2,1,0:T(8,128)S(1)}, f32[2,2,8,8,128]{4,3,2,1,0:T(8,128)S(1)}, u32[]{:S(2)}, u32[]{:S(2)}) %collective-permute-start.11) | collective-permute-done | bytes 131104 | tf_op jit(solution)/shard_map/ppermute | solution.py:543
  146.5 7.6 %collective-permute-done.12.refs_13_ = f32[2,2,8,8,128]{4,3,2,1,0:T(8,128)S(1)} collective-permute-done((f32[2,2,8,8,128]{4,3,2,1,0:T(8,128)S(1)}, f32[2,2,8,8,128]{4,3,2,1,0:T(8,128)S(1)}, u32[]{:S(2)}, u32[]{:S(2)}) %collective-permute-start.12) | collective-permute-done | bytes 131104 | tf_op jit(solution)/shard_map/ppermute | solution.py:543
  154.1 0.9 collective-permute-done.13.refs_14_
  155.1 0.6 copy-done.19
  155.7 5.3 %collective-permute-done.14.refs_15_ = f32[2,2,8,8,128]{4,3,2,1,0:T(8,128)} collective-permute-done((f32[2,2,8,8,128]{4,3,2,1,0:T(8,128)S(1)}, f32[2,2,8,8,128]{4,3,2,1,0:T(8,128)}, u32[]{:S(2)}, u32[]{:S(2)}) %collective-permute-start.14) | collective-permute-done | bytes 131104 | tf_op jit(solution)/shard_map/ppermute | solution.py:543
  161.0 1.3 copy-done.6
  162.4 8.4 %to_frequencies.1 = f32[2,8,128,512]{3,2,1,0:T(8,128)} custom-call(s32[1]{0:T(128)} %bitcast.me_ref, f32[32,2,8,8,128]{4,3,2,1,0:T(8,128)} %bitcast.13, f32[2,16,8,512]{3,2,1,0:T(8,128)} %constant.26.clone.both_hbm, f32[256,512]{1,0:T(8,128)} %constant.27.clone.one_hbm, f32[2,2,8,8,128]{4,3,2,1,0:T(8,128)} %get-tuple-element.41.refs_0_, ...), custom_call_target="tpu_custom_call" | custom-call | tf_op jit(solution)/shard_map/to_frequencies/pallas_call | solution.py:516
  (69 shorter events, 0.9 us)
Async XLA Ops:
  4.9 56.3 %all-to-all-start = ((f32[32,128,128]{2,1,0:T(8,128)}), f32[32,128,128]{2,1,0:T(8,128)}, u32[]{:S(2)}, u32[]{:S(2)}) async-start(f32[32,128,128]{2,1,0:T(8,128)} %bitcast.14), calls=%async_computation | async-start | bytes 4194304 | tf_op jit(solution)/shard_map/all_to_all | solution.py:537
  61.2 36.1 %copy-start = (bf16[256,256]{1,0:T(8,128)(2,1)S(1)}, bf16[256,256]{1,0:T(8,128)(2,1)}, u32[]{:S(2)}) copy-start(bf16[256,256]{1,0:T(8,128)(2,1)} %constant.25.clone.sl_ref) | copy-start | bytes 393220
  61.2 36.1 %copy-start.1 = (bf16[256,256]{1,0:T(8,128)(2,1)S(1)}, bf16[256,256]{1,0:T(8,128)(2,1)}, u32[]{:S(2)}) copy-start(bf16[256,256]{1,0:T(8,128)(2,1)} %constant.24.clone.sh_ref) | copy-start | bytes 393220
  61.2 36.1 %copy-start.2 = (bf16[256,256]{1,0:T(8,128)(2,1)S(1)}, bf16[256,256]{1,0:T(8,128)(2,1)}, u32[]{:S(2)}) copy-start(bf16[256,256]{1,0:T(8,128)(2,1)} %constant.23.clone.cl_ref) | copy-start | bytes 393220
  61.2 36.1 %copy-start.3 = (bf16[256,256]{1,0:T(8,128)(2,1)S(1)}, bf16[256,256]{1,0:T(8,128)(2,1)}, u32[]{:S(2)}) copy-start(bf16[256,256]{1,0:T(8,128)(2,1)} %constant.22.clone.ch_ref) | copy-start | bytes 393220
  61.2 36.1 %copy-start.4 = (s32[3,16]{1,0:T(4,128)S(1)}, s32[3,16]{1,0:T(4,128)}, u32[]{:S(2)}) copy-start(s32[3,16]{1,0:T(4,128)} %mirror_ref.3) | copy-start | bytes 580
  61.2 36.1 %copy-start.5 = (s32[8,2]{0,1:T(2,128)S(1)}, s32[8,2]{0,1:T(2,128)}, u32[]{:S(2)}) copy-start(s32[8,2]{0,1:T(2,128)} %param.16) | copy-start | bytes 196
  61.3 36.1 %all-to-all-start.1 = ((f32[32,64,128]{2,1,0:T(8,128)}), f32[32,64,128]{2,1,0:T(8,128)S(1)}, u32[]{:S(2)}, u32[]{:S(2)}) async-start(f32[32,64,128]{2,1,0:T(8,128)} %bitcast.15), calls=%async_computation.1 | async-start | bytes 2097152 | tf_op jit(solution)/shard_map/all_to_all | solution.py:537
  74.4 11.8 %collective-permute-start = (f32[2,2,8,8,128]{4,3,2,1,0:T(8,128)}, f32[2,2,8,8,128]{4,3,2,1,0:T(8,128)S(1)}, u32[]{:S(2)}, u32[]{:S(2)}) collective-permute-start(f32[2,2,8,8,128]{4,3,2,1,0:T(8,128)} %get-tuple-element.35), channel_id=1, source_target_pairs={{0,8},{1,9},{2,10},{3,11},{4,12},{5,13},{6,14},{7,15},{8,0},{9,1},... | collective-permute-start | bytes 393224 | tf_op jit(solution)/shard_map/ppermute | solution.py:543
  76.1 13.0 %collective-permute-start.1 = (f32[2,2,8,8,128]{4,3,2,1,0:T(8,128)}, f32[2,2,8,8,128]{4,3,2,1,0:T(8,128)S(1)}, u32[]{:S(2)}, u32[]{:S(2)}) collective-permute-start(f32[2,2,8,8,128]{4,3,2,1,0:T(8,128)} %get-tuple-element.36), channel_id=1, source_target_pairs={{0,9},{1,8},{2,11},{3,10},{4,13},{5,12},{6,15},{7,14},{8,1},{9,0},... | collective-permute-start | bytes 393224 | tf_op jit(solution)/shard_map/ppermute | solution.py:543
  76.1 18.7 %collective-permute-start.2 = (f32[2,2,8,8,128]{4,3,2,1,0:T(8,128)}, f32[2,2,8,8,128]{4,3,2,1,0:T(8,128)S(1)}, u32[]{:S(2)}, u32[]{:S(2)}) collective-permute-start(f32[2,2,8,8,128]{4,3,2,1,0:T(8,128)} %get-tuple-element.37), channel_id=1, source_target_pairs={{0,10},{1,11},{2,8},{3,9},{4,14},{5,15},{6,12},{7,13},{8,2},{9,3},... | collective-permute-start | bytes 393224 | tf_op jit(solution)/shard_map/ppermute | solution.py:543
  78.5 18.2 %collective-permute-start.3 = (f32[2,2,8,8,128]{4,3,2,1,0:T(8,128)}, f32[2,2,8,8,128]{4,3,2,1,0:T(8,128)S(1)}, u32[]{:S(2)}, u32[]{:S(2)}) collective-permute-start(f32[2,2,8,8,128]{4,3,2,1,0:T(8,128)} %get-tuple-element.38), channel_id=1, source_target_pairs={{0,11},{1,10},{2,9},{3,8},{4,15},{5,14},{6,13},{7,12},{8,3},{9,2},... | collective-permute-start | bytes 393224 | tf_op jit(solution)/shard_map/ppermute | solution.py:543
  78.9 18.5 %collective-permute-start.4 = (f32[2,2,8,8,128]{4,3,2,1,0:T(8,128)}, f32[2,2,8,8,128]{4,3,2,1,0:T(8,128)}, u32[]{:S(2)}, u32[]{:S(2)}) collective-permute-start(f32[2,2,8,8,128]{4,3,2,1,0:T(8,128)} %get-tuple-element.39), channel_id=1, source_target_pairs={{0,1},{1,0},{2,3},{3,2},{4,5},{5,4},{6,7},{7,6},{8,9},{9,8},{10,11... | collective-permute-start | bytes 393224 | tf_op jit(solution)/shard_map/ppermute | solution.py:543
  104.0 23.4 %copy-start.24 = (f32[2,2,8,8,128]{4,3,2,1,0:T(8,128)S(1)}, f32[2,2,8,8,128]{4,3,2,1,0:T(8,128)}, u32[]{:S(2)}) copy-start(f32[2,2,8,8,128]{4,3,2,1,0:T(8,128)} %get-tuple-element.48) | copy-start | bytes 393220
  104.0 28.2 %copy-start.23 = (f32[2,2,8,8,128]{4,3,2,1,0:T(8,128)S(1)}, f32[2,2,8,8,128]{4,3,2,1,0:T(8,128)}, u32[]{:S(2)}) copy-start(f32[2,2,8,8,128]{4,3,2,1,0:T(8,128)} %get-tuple-element.53) | copy-start | bytes 393220
  104.0 28.2 %copy-start.22 = (f32[2,2,8,8,128]{4,3,2,1,0:T(8,128)S(1)}, f32[2,2,8,8,128]{4,3,2,1,0:T(8,128)}, u32[]{:S(2)}) copy-start(f32[2,2,8,8,128]{4,3,2,1,0:T(8,128)} %get-tuple-element.54) | copy-start | bytes 393220
  104.1 33.1 %copy-start.21 = (f32[2,2,8,8,128]{4,3,2,1,0:T(8,128)S(1)}, f32[2,2,8,8,128]{4,3,2,1,0:T(8,128)}, u32[]{:S(2)}) copy-start(f32[2,2,8,8,128]{4,3,2,1,0:T(8,128)} %get-tuple-element.55) | copy-start | bytes 393220
  104.1 36.7 %copy-start.20 = (f32[2,2,8,8,128]{4,3,2,1,0:T(8,128)S(1)}, f32[2,2,8,8,128]{4,3,2,1,0:T(8,128)}, u32[]{:S(2)}) copy-start(f32[2,2,8,8,128]{4,3,2,1,0:T(8,128)} %get-tuple-element.56) | copy-start | bytes 393220
  104.1 56.9 %all-to-all-start.2 = ((f32[32,128,128]{2,1,0:T(8,128)}), f32[32,128,128]{2,1,0:T(8,128)S(1)}, u32[]{:S(2)}, u32[]{:S(2)}) async-start(f32[32,128,128]{2,1,0:T(8,128)} %bitcast.8), calls=%async_computation.2 | async-start | bytes 4194304 | tf_op jit(solution)/shard_map/all_to_all | solution.py:537
  108.2 19.2 %collective-permute-start.5 = (f32[2,2,8,8,128]{4,3,2,1,0:T(8,128)S(1)}, f32[2,2,8,8,128]{4,3,2,1,0:T(8,128)S(1)}, u32[]{:S(2)}, u32[]{:S(2)}) collective-permute-start(f32[2,2,8,8,128]{4,3,2,1,0:T(8,128)S(1)} %copy-done.29), channel_id=1, source_target_pairs={{0,2},{1,3},{2,0},{3,1},{4,6},{5,7},{6,4},{7,5},{8,10},{9,11},{10,... | collective-permute-start | bytes 393224 | tf_op jit(solution)/shard_map/ppermute | solution.py:543
  109.8 22.4 %collective-permute-start.6 = (f32[2,2,8,8,128]{4,3,2,1,0:T(8,128)S(1)}, f32[2,2,8,8,128]{4,3,2,1,0:T(8,128)S(1)}, u32[]{:S(2)}, u32[]{:S(2)}) collective-permute-start(f32[2,2,8,8,128]{4,3,2,1,0:T(8,128)S(1)} %copy-done.28), channel_id=1, source_target_pairs={{0,3},{1,2},{2,1},{3,0},{4,7},{5,6},{6,5},{7,4},{8,11},{9,10},{10,... | collective-permute-start | bytes 393224 | tf_op jit(solution)/shard_map/ppermute | solution.py:543
  109.9 22.4 %collective-permute-start.7 = (f32[2,2,8,8,128]{4,3,2,1,0:T(8,128)S(1)}, f32[2,2,8,8,128]{4,3,2,1,0:T(8,128)S(1)}, u32[]{:S(2)}, u32[]{:S(2)}) collective-permute-start(f32[2,2,8,8,128]{4,3,2,1,0:T(8,128)S(1)} %copy-done.27), channel_id=1, source_target_pairs={{0,4},{1,5},{2,6},{3,7},{4,0},{5,1},{6,2},{7,3},{8,12},{9,13},{10,... | collective-permute-start | bytes 393224 | tf_op jit(solution)/shard_map/ppermute | solution.py:543
  111.4 25.7 %collective-permute-start.8 = (f32[2,2,8,8,128]{4,3,2,1,0:T(8,128)S(1)}, f32[2,2,8,8,128]{4,3,2,1,0:T(8,128)S(1)}, u32[]{:S(2)}, u32[]{:S(2)}) collective-permute-start(f32[2,2,8,8,128]{4,3,2,1,0:T(8,128)S(1)} %copy-done.26), channel_id=1, source_target_pairs={{0,5},{1,4},{2,7},{3,6},{4,1},{5,0},{6,3},{7,2},{8,13},{9,12},{10,... | collective-permute-start | bytes 393224 | tf_op jit(solution)/shard_map/ppermute | solution.py:543
  111.8 29.0 %collective-permute-start.9 = (f32[2,2,8,8,128]{4,3,2,1,0:T(8,128)S(1)}, f32[2,2,8,8,128]{4,3,2,1,0:T(8,128)S(1)}, u32[]{:S(2)}, u32[]{:S(2)}) collective-permute-start(f32[2,2,8,8,128]{4,3,2,1,0:T(8,128)S(1)} %copy-done.25), channel_id=1, source_target_pairs={{0,6},{1,7},{2,4},{3,5},{4,2},{5,3},{6,0},{7,1},{8,14},{9,15},{10,... | collective-permute-start | bytes 393224 | tf_op jit(solution)/shard_map/ppermute | solution.py:543
  127.4 27.6 %copy-start.11 = (f32[2,2,8,8,128]{4,3,2,1,0:T(8,128)}, f32[2,2,8,8,128]{4,3,2,1,0:T(8,128)S(1)}, u32[]{:S(2)}) copy-start(f32[2,2,8,8,128]{4,3,2,1,0:T(8,128)S(1)} %collective-permute-done.5.refs_2_) | copy-start | bytes 393220
  127.4 17.1 %collective-permute-start.10 = (f32[2,2,8,8,128]{4,3,2,1,0:T(8,128)S(1)}, f32[2,2,8,8,128]{4,3,2,1,0:T(8,128)S(1)}, u32[]{:S(2)}, u32[]{:S(2)}) collective-permute-start(f32[2,2,8,8,128]{4,3,2,1,0:T(8,128)S(1)} %copy-done.24), channel_id=1, source_target_pairs={{0,7},{1,6},{2,5},{3,4},{4,3},{5,2},{6,1},{7,0},{8,15},{9,14},{10,... | collective-permute-start | bytes 393224 | tf_op jit(solution)/shard_map/ppermute | solution.py:543
  132.2 22.8 %copy-start.12 = (f32[2,2,8,8,128]{4,3,2,1,0:T(8,128)}, f32[2,2,8,8,128]{4,3,2,1,0:T(8,128)S(1)}, u32[]{:S(2)}) copy-start(f32[2,2,8,8,128]{4,3,2,1,0:T(8,128)S(1)} %collective-permute-done.6.refs_3_) | copy-start | bytes 393220
  132.3 14.2 %collective-permute-start.11 = (f32[2,2,8,8,128]{4,3,2,1,0:T(8,128)S(1)}, f32[2,2,8,8,128]{4,3,2,1,0:T(8,128)S(1)}, u32[]{:S(2)}, u32[]{:S(2)}) collective-permute-start(f32[2,2,8,8,128]{4,3,2,1,0:T(8,128)S(1)} %copy-done.23), channel_id=1, source_target_pairs={{0,12},{1,13},{2,14},{3,15},{4,8},{5,9},{6,10},{7,11},{8,4},{9,5},... | collective-permute-start | bytes 393224 | tf_op jit(solution)/shard_map/ppermute | solution.py:543
  132.3 22.8 %copy-start.13 = (f32[2,2,8,8,128]{4,3,2,1,0:T(8,128)}, f32[2,2,8,8,128]{4,3,2,1,0:T(8,128)S(1)}, u32[]{:S(2)}) copy-start(f32[2,2,8,8,128]{4,3,2,1,0:T(8,128)S(1)} %collective-permute-done.7.refs_4_) | copy-start | bytes 393220
  132.3 21.8 %collective-permute-start.12 = (f32[2,2,8,8,128]{4,3,2,1,0:T(8,128)S(1)}, f32[2,2,8,8,128]{4,3,2,1,0:T(8,128)S(1)}, u32[]{:S(2)}, u32[]{:S(2)}) collective-permute-start(f32[2,2,8,8,128]{4,3,2,1,0:T(8,128)S(1)} %copy-done.22), channel_id=1, source_target_pairs={{0,13},{1,12},{2,15},{3,14},{4,9},{5,8},{6,11},{7,10},{8,5},{9,4},... | collective-permute-start | bytes 393224 | tf_op jit(solution)/shard_map/ppermute | solution.py:543
  137.1 17.9 %collective-permute-start.13 = (f32[2,2,8,8,128]{4,3,2,1,0:T(8,128)S(1)}, f32[2,2,8,8,128]{4,3,2,1,0:T(8,128)S(1)}, u32[]{:S(2)}, u32[]{:S(2)}) collective-permute-start(f32[2,2,8,8,128]{4,3,2,1,0:T(8,128)S(1)} %copy-done.21), channel_id=1, source_target_pairs={{0,14},{1,15},{2,12},{3,13},{4,10},{5,11},{6,8},{7,9},{8,6},{9,7},... | collective-permute-start | bytes 393224 | tf_op jit(solution)/shard_map/ppermute | solution.py:543
  140.8 20.2 %collective-permute-start.14 = (f32[2,2,8,8,128]{4,3,2,1,0:T(8,128)S(1)}, f32[2,2,8,8,128]{4,3,2,1,0:T(8,128)}, u32[]{:S(2)}, u32[]{:S(2)}) collective-permute-start(f32[2,2,8,8,128]{4,3,2,1,0:T(8,128)S(1)} %copy-done.20), channel_id=1, source_target_pairs={{0,15},{1,14},{2,13},{3,12},{4,11},{5,10},{6,9},{7,8},{8,7},{9,6},... | collective-permute-start | bytes 393224 | tf_op jit(solution)/shard_map/ppermute | solution.py:543
  (16 other events, 105.8 us)

commit v8 on v7

--- a/solution.py
+++ b/solution.py
@@ -447,21 +447,52 @@
     )(me, *args)
 
 
-def frequency_kernel(me_ref, y_ref, both_hbm, one_hbm, *refs):
-    pieces, (out_ref, both_ref, one_ref, held, stage, m_sems, in_sems, sems) = refs[:-8], refs[-8:]
+def prepare_kernel(me_ref, both_ref, one_ref, out_ref):
+    near = both_ref.shape[1]
+    me = me_ref[0] % near
+    ordered = [both_ref[part, slot ^ me] for part in range(2) for slot in range(near)]
+    for part, value in enumerate(split_value(jnp.concatenate([one_ref[...]] + ordered, axis=0))):
+        out_ref[part] = value
+
+
+def prepare(me, both, one):
+    smem = pl.BlockSpec(memory_space=pltpu.SMEM)
+    vmem = pl.BlockSpec(memory_space=pltpu.VMEM)
+    depth = both.size // both.shape[3] + one.shape[0]
+    return pl.pallas_call(
+        prepare_kernel,
+        in_specs=[smem, vmem, vmem],
+        out_specs=vmem,
+        out_shape=jax.ShapeDtypeStruct((2, depth, one.shape[1]), jnp.bfloat16),
+        compiler_params=pltpu.CompilerParams(vmem_limit_bytes=63 << 20),
+        name="prepare",
+    )(me, both, one)
+
+
+def frequency_kernel(order, y_hbm, m_hbm, *refs):
+    pieces, (out_ref, y_ref, m_ref, held, stage, y_sems, m_sems, in_sems, sems) = refs[:-9], refs[-9:]
     near = len(pieces)
     devices, _, components, rows, lanes = y_ref.shape
     groups = sems.shape[0]
     members = components // groups
+    depth = devices * rows
+    cuts = [pl.ds(group * members, members) for group in range(groups)]
     matrices = [
-        pltpu.make_async_copy(one_hbm, one_ref, m_sems.at[0]),
-        pltpu.make_async_copy(both_hbm, both_ref, m_sems.at[1]),
+        pltpu.make_async_copy(m_hbm.at[:, pl.ds(start, depth)], m_ref.at[:, pl.ds(start, depth)], m_sems.at[part])
+        for part, start in enumerate((0, depth))
     ]
-    loads = [pltpu.make_async_copy(piece, held.at[slot], in_sems.at[slot]) for slot, piece in enumerate(pieces)]
-    for copy in matrices + loads:
+    blocks = [
+        pltpu.make_async_copy(y_hbm.at[:, :, cut], y_ref.at[:, :, cut], y_sems.at[group])
+        for group, cut in enumerate(cuts)
+    ]
+    loads = [pltpu.make_async_copy(piece, held.at[slot], in_sems.at[slot]) for slot, piece in zip(order, pieces)]
+    for copy in [matrices[0], blocks[0], matrices[1]] + loads + blocks[1:]:
         copy.start()
-    me = me_ref[0] % near
     upper_rows = lax.broadcasted_iota(jnp.int32, (devices, rows, lanes), 1) < rows // 2
+
+    def part_of(values, start):
+        matrix = [m_ref[part, start : start + depth] for part in range(2)]
+        return dot3(split_value(jnp.concatenate(values, axis=0)), matrix, ((1,), (0,)))
 
     def one_part(group):
         values = []
@@ -475,7 +506,7 @@
             second = jnp.where(upper_rows, folded[1][0], folded[0][1])
             values.append(first.reshape(devices * rows, lanes).T)
             values.append(second.reshape(devices * rows, lanes).T)
-        return dot3(split_value(jnp.concatenate(values, axis=0)), one, ((1,), (0,)))
+        return part_of(values, 0)
 
     def both_part(group):
         values = []
@@ -485,51 +516,48 @@
             differences = [part[0][ri] - part[1][ri] for ri in range(2)]
             values.append(jnp.concatenate([sums[0], -differences[1]], axis=0).T)
             values.append(jnp.concatenate([sums[1], differences[0]], axis=0).T)
-        return dot3(split_value(jnp.concatenate(values, axis=0)), both, ((1,), (0,)))
+        return part_of(values, depth)
 
     copies = []
     matrices[0].wait()
-    one = split_value(one_ref[...])
     for group in range(groups):
+        blocks[group].wait()
         d = one_part(group)
         if group == 0:
             for copy in matrices[1:] + loads:
                 copy.wait()
-            ordered = [both_ref[part, slot ^ me] for part in range(2) for slot in range(near)]
-            both = split_value(jnp.concatenate(ordered, axis=0))
         d = (d + both_part(group)).reshape(members, 2, lanes, d.shape[1])
         for ri in range(2):
             stage[ri, group * members : (group + 1) * members] = d[:, ri]
-        cut = pl.ds(group * members, members)
-        copies.append(pltpu.make_async_copy(stage.at[:, cut], out_ref.at[:, cut], sems.at[group]))
+        copies.append(pltpu.make_async_copy(stage.at[:, cuts[group]], out_ref.at[:, cuts[group]], sems.at[group]))
         copies[-1].start()
     for copy in copies:
         copy.wait()
 
 
-def to_frequencies(y, pieces, both, one, me):
+def to_frequencies(y, pieces, order, matrix):
     _, _, components, _, lanes = y.shape
-    shape = (2, components, lanes, one.shape[1])
-    vmem = pl.BlockSpec(memory_space=pltpu.VMEM)
+    shape = (2, components, lanes, matrix.shape[2])
     hbm = pl.BlockSpec(memory_space=pltpu.HBM)
-    kept = y.size * 4 + (96 << 10)
+    groups = components // 2
     return pl.pallas_call(
-        frequency_kernel,
-        in_specs=[pl.BlockSpec(memory_space=pltpu.SMEM), vmem] + [hbm] * (2 + len(pieces)),
+        functools.partial(frequency_kernel, order),
+        in_specs=[hbm] * (2 + len(pieces)),
         out_specs=hbm,
         out_shape=jax.ShapeDtypeStruct(shape, jnp.float32),
         scratch_shapes=[
-            pltpu.VMEM(both.shape, jnp.float32),
-            pltpu.VMEM(one.shape, jnp.float32),
+            pltpu.VMEM(y.shape, jnp.float32),
+            pltpu.VMEM(matrix.shape, jnp.bfloat16),
             pltpu.VMEM((len(pieces),) + pieces[0].shape, jnp.float32),
             pltpu.VMEM(shape, jnp.float32),
+            pltpu.SemaphoreType.DMA((groups,)),
             pltpu.SemaphoreType.DMA((2,)),
             pltpu.SemaphoreType.DMA((len(pieces),)),
-            pltpu.SemaphoreType.DMA((components // 2,)),
+            pltpu.SemaphoreType.DMA((groups,)),
         ],
-        compiler_params=pltpu.CompilerParams(vmem_limit_bytes=(64 << 20) - kept),
+        compiler_params=pltpu.CompilerParams(vmem_limit_bytes=63 << 20),
         name="to_frequencies",
-    )(me, y, both, one, *pieces)
+    )(y, matrix, *pieces)
 
 
 def exchange(x):
@@ -691,11 +719,12 @@
     order = list(range(middle_slot, middle_slot + quarter)) + [1]
     early = [swap(pieces[slot], slot, devices) for slot in order]
     one, early = lax.optimization_barrier((exchange(one), early))
-    one = exchange(one_middle(one, pair_table, mirror_map))
-    rest = [slot for slot in reversed(range(near)) if slot not in order]
-    moved = dict(zip(order, early)) | {slot: swap(pieces[slot], slot, devices) for slot in rest}
-    pieces = [moved[slot] for slot in range(near)]
-    return to_frequencies(one, pieces, jnp.asarray(both_boson), jnp.asarray(one_boson), me)
+    one = one_middle(one, pair_table, mirror_map)
+    one, both_boson, one_boson = lax.optimization_barrier((one, jnp.asarray(both_boson), jnp.asarray(one_boson)))
+    matrix = prepare(me, both_boson, one_boson)
+    rest = [slot for slot in reversed(range(1, near)) if slot not in order]
+    late = [swap(pieces[slot], slot, devices) for slot in rest]
+    return to_frequencies(exchange(one), [pieces[0]] + early + late, [0] + order + rest, matrix)
 
 
 def solution(mesh):

time: 171 us -> 179 us (1.047); the launches traced: 171 us -> 176 us
  waiting for transfers between devices: 100 us -> 106 us
  local copies, waits for them, and re-layouts: 2.73 us -> 0.09 us
  Pallas kernels: 35.6 us -> 37.7 us
    ppermute x15, waiting for transfers between devices: 58.1 us -> 63.4 us  [swap(): lax.ppermute(piece, 'kb', [(device, device ^ slot) for device in range(de...]
    unnamed x60 -> x46, local copies, waits for them, and re-layouts: 2.73 us -> 0.09 us
    pallas_call x1 -> x2, Pallas kernels: 8.4 us -> 10.5 us  [the longest x1 8.17 us: to_frequencies(): pl.pallas_call(functools.partial(frequency_kernel, order), in_specs=[hbm]...]
  transfers between devices with their start and end apart: 18 -> 18, of which waited for: 13 -> 11; matrix products, arithmetic and copies ran while one was open for 0% -> 0% of each run, Pallas kernels for 9% -> 10%
where the time goes in v8:
time: 179 us; the launch traced here: 176 us
  waiting for transfers between devices  106 us (59%)
  Pallas kernels  37.7 us (21%)
  starting transfers between devices  32.2 us (18%)
    ppermute x15, waiting for transfers between devices, swap(): lax.ppermute(piece, 'kb', [(device, device ^ slot) for device in range(de...  63.4 us
    all_to_all x3, waiting for transfers between devices, exchange(): lax.all_to_all(flat, 'kb', split_axis=0, concat_axis=0, tiled=True)  42.2 us
    ppermute x15, starting transfers between devices, swap(): lax.ppermute(piece, 'kb', [(device, device ^ slot) for device in range(de...  16.3 us
    all_to_all x3, starting transfers between devices, exchange(): lax.all_to_all(flat, 'kb', split_axis=0, concat_axis=0, tiled=True)  15.9 us
    pallas_call x2, Pallas kernels, to_times(): pl.pallas_call(kernel, in_specs=[hbm, hbm], out_specs=hbm, out_shape=jax....  11.6 us
    pallas_call x1, Pallas kernels, both_middle(): pl.pallas_call(both_middle_kernel, in_specs=[pl.BlockSpec(memory_space=pl...  8.98 us
    pallas_call x1, Pallas kernels, to_frequencies(): pl.pallas_call(functools.partial(frequency_kernel, order), in_specs=[hbm]...  8.17 us
    pallas_call x1, Pallas kernels, one_middle(): pl.pallas_call(one_middle_kernel, in_specs=specs, out_specs=pl.BlockSpec(...  6.59 us
  transfers between devices with their start and end apart: 18, of which 11 were waited for; matrix products, arithmetic and copies ran while one was open for 0% of the time, Pallas kernels for 10%

profile of v8, /device:TPU:0, one launch (start us, length us, event | category | flops | bytes accessed | tf_op | source)
XLA Modules:
  0.0 176.0 jit_solution(13615184300511635225)
XLA Ops:
  0.0 4.9 %both_times.1 = f32[32,2,2,4,8,128]{5,4,3,2,1,0:T(8,128)} custom-call(f32[2,4,128,512]{3,2,1,0:T(8,128)} %g_hbm.2, f32[256,512]{1,0:T(8,128)} %constant.20.clone.m_hbm), custom_call_target="tpu_custom_call" | custom-call | tf_op jit(solution)/shard_map/both_times/pallas_call | solution.py:186
  4.9 7.4 %all-to-all-start = ((f32[32,128,128]{2,1,0:T(8,128)}), f32[32,128,128]{2,1,0:T(8,128)}, u32[]{:S(2)}, u32[]{:S(2)}) async-start(f32[32,128,128]{2,1,0:T(8,128)} %bitcast.14), calls=%async_computation | async-start | bytes 4194304 | tf_op jit(solution)/shard_map/all_to_all | solution.py:565
  12.3 6.7 %one_times.1 = f32[32,2,4,8,128]{4,3,2,1,0:T(8,128)} custom-call(f32[2,4,128,512]{3,2,1,0:T(8,128)} %g_hbm.2, f32[512,512]{1,0:T(8,128)} %constant.21.clone.m_hbm), custom_call_target="tpu_custom_call" | custom-call | tf_op jit(solution)/shard_map/one_times/pallas_call | solution.py:186
  19.1 42.2 %all-to-all-done = f32[32,128,128]{2,1,0:T(8,128)} async-done(((f32[32,128,128]{2,1,0:T(8,128)}), f32[32,128,128]{2,1,0:T(8,128)}, u32[]{:S(2)}, u32[]{:S(2)}) %all-to-all-start) | async-done | bytes 2097184 | tf_op jit(solution)/shard_map/all_to_all | solution.py:565
  61.3 4.2 %all-to-all-start.1 = ((f32[32,64,128]{2,1,0:T(8,128)}), f32[32,64,128]{2,1,0:T(8,128)S(1)}, u32[]{:S(2)}, u32[]{:S(2)}) async-start(f32[32,64,128]{2,1,0:T(8,128)} %bitcast.15), calls=%async_computation.1 | async-start | bytes 2097152 | tf_op jit(solution)/shard_map/all_to_all | solution.py:565
  65.5 9.0 %both_middle.1 = (f32[2,2,8,8,128]{4,3,2,1,0:T(8,128)}, f32[2,2,8,8,128]{4,3,2,1,0:T(8,128)}, f32[2,2,8,8,128]{4,3,2,1,0:T(8,128)}, f32[2,2,8,8,128]{4,3,2,1,0:T...) custom-call(s32[1]{0:T(128)} %bitcast.5.me_ref, ...), custom_call_target="tpu_custom_call" | custom-call | tf_op jit(solution)/shard_map/both_middle/pallas_call | solution.py:433
  74.4 1.6 collective-permute-start
  76.1 2.4 %collective-permute-start.2 = (f32[2,2,8,8,128]{4,3,2,1,0:T(8,128)}, f32[2,2,8,8,128]{4,3,2,1,0:T(8,128)S(1)}, u32[]{:S(2)}, u32[]{:S(2)}) collective-permute-start(f32[2,2,8,8,128]{4,3,2,1,0:T(8,128)} %get-tuple-element.40), channel_id=1, source_target_pairs={{0,10},{1,11},{2,8},{3,9},{4,14},{5,15},{6,12},{7,13},{8,2},{9,3},... | collective-permute-start | bytes 393224 | tf_op jit(solution)/shard_map/ppermute | solution.py:571
  78.5 0.4 collective-permute-start.3
  78.9 0.2 collective-permute-start.4
  79.1 7.1 %collective-permute-done.refs_1_ = f32[2,2,8,8,128]{4,3,2,1,0:T(8,128)S(1)} collective-permute-done((f32[2,2,8,8,128]{4,3,2,1,0:T(8,128)}, f32[2,2,8,8,128]{4,3,2,1,0:T(8,128)S(1)}, u32[]{:S(2)}, u32[]{:S(2)}) %collective-permute-start) | collective-permute-done | bytes 131104 | tf_op jit(solution)/shard_map/ppermute | solution.py:571
  86.3 2.8 %collective-permute-done.1.refs_2_ = f32[2,2,8,8,128]{4,3,2,1,0:T(8,128)S(1)} collective-permute-done((f32[2,2,8,8,128]{4,3,2,1,0:T(8,128)}, f32[2,2,8,8,128]{4,3,2,1,0:T(8,128)S(1)}, u32[]{:S(2)}, u32[]{:S(2)}) %collective-permute-start.1) | collective-permute-done | bytes 131104 | tf_op jit(solution)/shard_map/ppermute | solution.py:571
  89.1 5.7 %collective-permute-done.2.refs_3_ = f32[2,2,8,8,128]{4,3,2,1,0:T(8,128)S(1)} collective-permute-done((f32[2,2,8,8,128]{4,3,2,1,0:T(8,128)}, f32[2,2,8,8,128]{4,3,2,1,0:T(8,128)S(1)}, u32[]{:S(2)}, u32[]{:S(2)}) %collective-permute-start.2) | collective-permute-done | bytes 131104 | tf_op jit(solution)/shard_map/ppermute | solution.py:571
  94.8 1.9 %collective-permute-done.3.refs_4_ = f32[2,2,8,8,128]{4,3,2,1,0:T(8,128)S(1)} collective-permute-done((f32[2,2,8,8,128]{4,3,2,1,0:T(8,128)}, f32[2,2,8,8,128]{4,3,2,1,0:T(8,128)S(1)}, u32[]{:S(2)}, u32[]{:S(2)}) %collective-permute-start.3) | collective-permute-done | bytes 131104 | tf_op jit(solution)/shard_map/ppermute | solution.py:571
  96.7 6.6 %one_middle.1 = f32[16,2,2,8,8,128]{5,4,3,2,1,0:T(8,128)} custom-call(s32[2,8]{1,0:T(2,128)S(1)} %bitcast.13, s32[3,16]{1,0:T(4,128)S(1)} %copy-done.4, bf16[256,256]{1,0:T(8,128)(2,1)S(1)} %copy-done.3, bf16[256,256]{1,0:T(8,128)(2,1)S(1)} %copy-done.2, bf16[256,256]{1,0:T(8,128)(2,1)S(1)} %copy-done.1, bf16[256,256]{1,0:T(8,128)(2,1)S(1)} %copy-done, ...), custom_call_target="tpu_custom_call" | custom-call | tf_op jit(solution)/shard_map/one_middle/pallas_call | solution.py:407
  103.4 4.3 %all-to-all-start.2 = ((f32[32,128,128]{2,1,0:T(8,128)}), f32[32,128,128]{2,1,0:T(8,128)}, u32[]{:S(2)}, u32[]{:S(2)}) async-start(f32[32,128,128]{2,1,0:T(8,128)} %bitcast.9), calls=%async_computation.2 | async-start | bytes 4194304 | tf_op jit(solution)/shard_map/all_to_all | solution.py:565
  107.7 3.1 %collective-permute-start.5 = (f32[2,2,8,8,128]{4,3,2,1,0:T(8,128)S(1)}, f32[2,2,8,8,128]{4,3,2,1,0:T(8,128)S(1)}, u32[]{:S(2)}, u32[]{:S(2)}) collective-permute-start(f32[2,2,8,8,128]{4,3,2,1,0:T(8,128)S(1)} %copy-done.22), channel_id=1, source_target_pairs={{0,15},{1,14},{2,13},{3,12},{4,11},{5,10},{6,9},{7,8},{8,7},{9,6},... | collective-permute-start | bytes 393224 | tf_op jit(solution)/shard_map/ppermute | solution.py:571
  110.8 0.4 collective-permute-start.6
  111.2 2.3 %collective-permute-start.7 = (f32[2,2,8,8,128]{4,3,2,1,0:T(8,128)S(1)}, f32[2,2,8,8,128]{4,3,2,1,0:T(8,128)S(1)}, u32[]{:S(2)}, u32[]{:S(2)}) collective-permute-start(f32[2,2,8,8,128]{4,3,2,1,0:T(8,128)S(1)} %copy-done.20), channel_id=1, source_target_pairs={{0,13},{1,12},{2,15},{3,14},{4,9},{5,8},{6,11},{7,10},{8,5},{9,4},... | collective-permute-start | bytes 393224 | tf_op jit(solution)/shard_map/ppermute | solution.py:571
  113.4 0.5 collective-permute-start.8
  114.0 2.2 %collective-permute-start.9 = (f32[2,2,8,8,128]{4,3,2,1,0:T(8,128)S(1)}, f32[2,2,8,8,128]{4,3,2,1,0:T(8,128)S(1)}, u32[]{:S(2)}, u32[]{:S(2)}) collective-permute-start(f32[2,2,8,8,128]{4,3,2,1,0:T(8,128)S(1)} %copy-done.18), channel_id=1, source_target_pairs={{0,7},{1,6},{2,5},{3,4},{4,3},{5,2},{6,1},{7,0},{8,15},{9,14},{10,... | collective-permute-start | bytes 393224 | tf_op jit(solution)/shard_map/ppermute | solution.py:571
  116.1 29.8 %collective-permute-done.5.refs_6_ = f32[2,2,8,8,128]{4,3,2,1,0:T(8,128)S(1)} collective-permute-done((f32[2,2,8,8,128]{4,3,2,1,0:T(8,128)S(1)}, f32[2,2,8,8,128]{4,3,2,1,0:T(8,128)S(1)}, u32[]{:S(2)}, u32[]{:S(2)}) %collective-permute-start.5) | collective-permute-done | bytes 131104 | tf_op jit(solution)/shard_map/ppermute | solution.py:571
  145.9 2.0 %collective-permute-start.10 = (f32[2,2,8,8,128]{4,3,2,1,0:T(8,128)}, f32[2,2,8,8,128]{4,3,2,1,0:T(8,128)S(1)}, u32[]{:S(2)}, u32[]{:S(2)}) collective-permute-start(f32[2,2,8,8,128]{4,3,2,1,0:T(8,128)} %get-tuple-element.58), channel_id=1, source_target_pairs={{0,6},{1,7},{2,4},{3,5},{4,2},{5,3},{6,0},{7,1},{8,14},{9,15},{10,... | collective-permute-start | bytes 393224 | tf_op jit(solution)/shard_map/ppermute | solution.py:571
  147.9 1.4 collective-permute-done.6.refs_7_
  149.3 5.4 %collective-permute-done.7.refs_8_ = f32[2,2,8,8,128]{4,3,2,1,0:T(8,128)S(1)} collective-permute-done((f32[2,2,8,8,128]{4,3,2,1,0:T(8,128)S(1)}, f32[2,2,8,8,128]{4,3,2,1,0:T(8,128)S(1)}, u32[]{:S(2)}, u32[]{:S(2)}) %collective-permute-start.7) | collective-permute-done | bytes 131104 | tf_op jit(solution)/shard_map/ppermute | solution.py:571
  154.8 0.2 collective-permute-start.12
  155.0 4.4 %collective-permute-done.8.refs_9_ = f32[2,2,8,8,128]{4,3,2,1,0:T(8,128)S(1)} collective-permute-done((f32[2,2,8,8,128]{4,3,2,1,0:T(8,128)S(1)}, f32[2,2,8,8,128]{4,3,2,1,0:T(8,128)S(1)}, u32[]{:S(2)}, u32[]{:S(2)}) %collective-permute-start.8) | collective-permute-done | bytes 131104 | tf_op jit(solution)/shard_map/ppermute | solution.py:571
  159.3 1.1 collective-permute-start.14
  160.4 2.3 %prepare.1.m_hbm = bf16[2,512,512]{2,1,0:T(8,128)(2,1)} custom-call(s32[1]{0:T(128)} %bitcast.5.me_ref, f32[2,16,8,512]{3,2,1,0:T(8,128)} %constant.26.clone.both_ref, f32[256,512]{1,0:T(8,128)} %constant.27.clone.one_ref), custom_call_target="tpu_custom_call" | custom-call | tf_op jit(solution)/shard_map/prepare/pallas_call | solution.py:462
  162.8 2.6 %collective-permute-done.13.refs_14_ = f32[2,2,8,8,128]{4,3,2,1,0:T(8,128)} collective-permute-done((f32[2,2,8,8,128]{4,3,2,1,0:T(8,128)}, f32[2,2,8,8,128]{4,3,2,1,0:T(8,128)}, u32[]{:S(2)}, u32[]{:S(2)}) %collective-permute-start.13) | collective-permute-done | bytes 131104 | tf_op jit(solution)/shard_map/ppermute | solution.py:571
  165.4 2.2 %collective-permute-done.14.refs_15_ = f32[2,2,8,8,128]{4,3,2,1,0:T(8,128)} collective-permute-done((f32[2,2,8,8,128]{4,3,2,1,0:T(8,128)}, f32[2,2,8,8,128]{4,3,2,1,0:T(8,128)}, u32[]{:S(2)}, u32[]{:S(2)}) %collective-permute-start.14) | collective-permute-done | bytes 131104 | tf_op jit(solution)/shard_map/ppermute | solution.py:571
  167.6 8.2 %to_frequencies.1 = f32[2,8,128,512]{3,2,1,0:T(8,128)} custom-call(f32[32,2,8,8,128]{4,3,2,1,0:T(8,128)} %bitcast.10.y_hbm, bf16[2,512,512]{2,1,0:T(8,128)(2,1)} %prepare.1.m_hbm, f32[2,2,8,8,128]{4,3,2,1,0:T(8,128)} %get-tuple-element.47.refs_0_, f32[2,2,8,8,128]{4,3,2,1,0:T(8,128)} %copy-done.6, f32[2,2,8,8,128]{4,3,2,1,0:T(8,128)} %copy-done.7, ...), custom_call_target="tpu_custom_call" | custom-call | tf_op jit(solution)/shard_map/to_frequencies/pallas_call | solution.py:543
  (56 shorter events, 0.1 us)
Async XLA Ops:
  4.9 56.3 %all-to-all-start = ((f32[32,128,128]{2,1,0:T(8,128)}), f32[32,128,128]{2,1,0:T(8,128)}, u32[]{:S(2)}, u32[]{:S(2)}) async-start(f32[32,128,128]{2,1,0:T(8,128)} %bitcast.14), calls=%async_computation | async-start | bytes 4194304 | tf_op jit(solution)/shard_map/all_to_all | solution.py:565
  61.2 35.5 %copy-start = (bf16[256,256]{1,0:T(8,128)(2,1)S(1)}, bf16[256,256]{1,0:T(8,128)(2,1)}, u32[]{:S(2)}) copy-start(bf16[256,256]{1,0:T(8,128)(2,1)} %constant.25.clone.sl_ref) | copy-start | bytes 393220
  61.2 35.5 %copy-start.1 = (bf16[256,256]{1,0:T(8,128)(2,1)S(1)}, bf16[256,256]{1,0:T(8,128)(2,1)}, u32[]{:S(2)}) copy-start(bf16[256,256]{1,0:T(8,128)(2,1)} %constant.24.clone.sh_ref) | copy-start | bytes 393220
  61.2 35.5 %copy-start.2 = (bf16[256,256]{1,0:T(8,128)(2,1)S(1)}, bf16[256,256]{1,0:T(8,128)(2,1)}, u32[]{:S(2)}) copy-start(bf16[256,256]{1,0:T(8,128)(2,1)} %constant.23.clone.cl_ref) | copy-start | bytes 393220
  61.2 35.5 %copy-start.3 = (bf16[256,256]{1,0:T(8,128)(2,1)S(1)}, bf16[256,256]{1,0:T(8,128)(2,1)}, u32[]{:S(2)}) copy-start(bf16[256,256]{1,0:T(8,128)(2,1)} %constant.22.clone.ch_ref) | copy-start | bytes 393220
  61.2 35.5 %copy-start.4 = (s32[3,16]{1,0:T(4,128)S(1)}, s32[3,16]{1,0:T(4,128)}, u32[]{:S(2)}) copy-start(s32[3,16]{1,0:T(4,128)} %mirror_ref.3) | copy-start | bytes 580
  61.2 35.5 %copy-start.5 = (s32[8,2]{0,1:T(2,128)S(1)}, s32[8,2]{0,1:T(2,128)}, u32[]{:S(2)}) copy-start(s32[8,2]{0,1:T(2,128)} %param.16) | copy-start | bytes 196
  61.3 35.4 %all-to-all-start.1 = ((f32[32,64,128]{2,1,0:T(8,128)}), f32[32,64,128]{2,1,0:T(8,128)S(1)}, u32[]{:S(2)}, u32[]{:S(2)}) async-start(f32[32,64,128]{2,1,0:T(8,128)} %bitcast.15), calls=%async_computation.1 | async-start | bytes 2097152 | tf_op jit(solution)/shard_map/all_to_all | solution.py:565
  74.4 11.8 %collective-permute-start = (f32[2,2,8,8,128]{4,3,2,1,0:T(8,128)}, f32[2,2,8,8,128]{4,3,2,1,0:T(8,128)S(1)}, u32[]{:S(2)}, u32[]{:S(2)}) collective-permute-start(f32[2,2,8,8,128]{4,3,2,1,0:T(8,128)} %get-tuple-element.38), channel_id=1, source_target_pairs={{0,8},{1,9},{2,10},{3,11},{4,12},{5,13},{6,14},{7,15},{8,0},{9,1},... | collective-permute-start | bytes 393224 | tf_op jit(solution)/shard_map/ppermute | solution.py:571
  76.1 13.0 %collective-permute-start.1 = (f32[2,2,8,8,128]{4,3,2,1,0:T(8,128)}, f32[2,2,8,8,128]{4,3,2,1,0:T(8,128)S(1)}, u32[]{:S(2)}, u32[]{:S(2)}) collective-permute-start(f32[2,2,8,8,128]{4,3,2,1,0:T(8,128)} %get-tuple-element.39), channel_id=1, source_target_pairs={{0,9},{1,8},{2,11},{3,10},{4,13},{5,12},{6,15},{7,14},{8,1},{9,0},... | collective-permute-start | bytes 393224 | tf_op jit(solution)/shard_map/ppermute | solution.py:571
  76.1 18.7 %collective-permute-start.2 = (f32[2,2,8,8,128]{4,3,2,1,0:T(8,128)}, f32[2,2,8,8,128]{4,3,2,1,0:T(8,128)S(1)}, u32[]{:S(2)}, u32[]{:S(2)}) collective-permute-start(f32[2,2,8,8,128]{4,3,2,1,0:T(8,128)} %get-tuple-element.40), channel_id=1, source_target_pairs={{0,10},{1,11},{2,8},{3,9},{4,14},{5,15},{6,12},{7,13},{8,2},{9,3},... | collective-permute-start | bytes 393224 | tf_op jit(solution)/shard_map/ppermute | solution.py:571
  78.5 18.2 %collective-permute-start.3 = (f32[2,2,8,8,128]{4,3,2,1,0:T(8,128)}, f32[2,2,8,8,128]{4,3,2,1,0:T(8,128)S(1)}, u32[]{:S(2)}, u32[]{:S(2)}) collective-permute-start(f32[2,2,8,8,128]{4,3,2,1,0:T(8,128)} %get-tuple-element.41), channel_id=1, source_target_pairs={{0,11},{1,10},{2,9},{3,8},{4,15},{5,14},{6,13},{7,12},{8,3},{9,2},... | collective-permute-start | bytes 393224 | tf_op jit(solution)/shard_map/ppermute | solution.py:571
  78.9 17.8 %collective-permute-start.4 = (f32[2,2,8,8,128]{4,3,2,1,0:T(8,128)}, f32[2,2,8,8,128]{4,3,2,1,0:T(8,128)S(1)}, u32[]{:S(2)}, u32[]{:S(2)}) collective-permute-start(f32[2,2,8,8,128]{4,3,2,1,0:T(8,128)} %get-tuple-element.42), channel_id=1, source_target_pairs={{0,1},{1,0},{2,3},{3,2},{4,5},{5,4},{6,7},{7,6},{8,9},{9,8},{10,11... | collective-permute-start | bytes 393224 | tf_op jit(solution)/shard_map/ppermute | solution.py:571
  86.3 17.1 %copy-start.6 = (f32[2,2,8,8,128]{4,3,2,1,0:T(8,128)}, f32[2,2,8,8,128]{4,3,2,1,0:T(8,128)S(1)}, u32[]{:S(2)}) copy-start(f32[2,2,8,8,128]{4,3,2,1,0:T(8,128)S(1)} %collective-permute-done.refs_1_) | copy-start | bytes 393220
  89.1 14.3 %copy-start.7 = (f32[2,2,8,8,128]{4,3,2,1,0:T(8,128)}, f32[2,2,8,8,128]{4,3,2,1,0:T(8,128)S(1)}, u32[]{:S(2)}) copy-start(f32[2,2,8,8,128]{4,3,2,1,0:T(8,128)S(1)} %collective-permute-done.1.refs_2_) | copy-start | bytes 393220
  94.8 8.6 %copy-start.8 = (f32[2,2,8,8,128]{4,3,2,1,0:T(8,128)}, f32[2,2,8,8,128]{4,3,2,1,0:T(8,128)S(1)}, u32[]{:S(2)}) copy-start(f32[2,2,8,8,128]{4,3,2,1,0:T(8,128)S(1)} %collective-permute-done.2.refs_3_) | copy-start | bytes 393220
  103.4 10.1 %copy-start.19 = (f32[2,2,8,8,128]{4,3,2,1,0:T(8,128)S(1)}, f32[2,2,8,8,128]{4,3,2,1,0:T(8,128)}, u32[]{:S(2)}) copy-start(f32[2,2,8,8,128]{4,3,2,1,0:T(8,128)} %get-tuple-element.56) | copy-start | bytes 393220
  103.4 10.6 %copy-start.18 = (f32[2,2,8,8,128]{4,3,2,1,0:T(8,128)S(1)}, f32[2,2,8,8,128]{4,3,2,1,0:T(8,128)}, u32[]{:S(2)}) copy-start(f32[2,2,8,8,128]{4,3,2,1,0:T(8,128)} %get-tuple-element.57) | copy-start | bytes 393220
  103.4 64.1 %all-to-all-start.2 = ((f32[32,128,128]{2,1,0:T(8,128)}), f32[32,128,128]{2,1,0:T(8,128)}, u32[]{:S(2)}, u32[]{:S(2)}) async-start(f32[32,128,128]{2,1,0:T(8,128)} %bitcast.9), calls=%async_computation.2 | async-start | bytes 4194304 | tf_op jit(solution)/shard_map/all_to_all | solution.py:565
  107.7 38.2 %collective-permute-start.5 = (f32[2,2,8,8,128]{4,3,2,1,0:T(8,128)S(1)}, f32[2,2,8,8,128]{4,3,2,1,0:T(8,128)S(1)}, u32[]{:S(2)}, u32[]{:S(2)}) collective-permute-start(f32[2,2,8,8,128]{4,3,2,1,0:T(8,128)S(1)} %copy-done.22), channel_id=1, source_target_pairs={{0,15},{1,14},{2,13},{3,12},{4,11},{5,10},{6,9},{7,8},{8,7},{9,6},... | collective-permute-start | bytes 393224 | tf_op jit(solution)/shard_map/ppermute | solution.py:571
  110.8 38.5 %collective-permute-start.6 = (f32[2,2,8,8,128]{4,3,2,1,0:T(8,128)S(1)}, f32[2,2,8,8,128]{4,3,2,1,0:T(8,128)S(1)}, u32[]{:S(2)}, u32[]{:S(2)}) collective-permute-start(f32[2,2,8,8,128]{4,3,2,1,0:T(8,128)S(1)} %copy-done.21), channel_id=1, source_target_pairs={{0,14},{1,15},{2,12},{3,13},{4,10},{5,11},{6,8},{7,9},{8,6},{9,7},... | collective-permute-start | bytes 393224 | tf_op jit(solution)/shard_map/ppermute | solution.py:571
  111.2 43.6 %collective-permute-start.7 = (f32[2,2,8,8,128]{4,3,2,1,0:T(8,128)S(1)}, f32[2,2,8,8,128]{4,3,2,1,0:T(8,128)S(1)}, u32[]{:S(2)}, u32[]{:S(2)}) collective-permute-start(f32[2,2,8,8,128]{4,3,2,1,0:T(8,128)S(1)} %copy-done.20), channel_id=1, source_target_pairs={{0,13},{1,12},{2,15},{3,14},{4,9},{5,8},{6,11},{7,10},{8,5},{9,4},... | collective-permute-start | bytes 393224 | tf_op jit(solution)/shard_map/ppermute | solution.py:571
  113.4 45.9 %collective-permute-start.8 = (f32[2,2,8,8,128]{4,3,2,1,0:T(8,128)S(1)}, f32[2,2,8,8,128]{4,3,2,1,0:T(8,128)S(1)}, u32[]{:S(2)}, u32[]{:S(2)}) collective-permute-start(f32[2,2,8,8,128]{4,3,2,1,0:T(8,128)S(1)} %copy-done.19), channel_id=1, source_target_pairs={{0,12},{1,13},{2,14},{3,15},{4,8},{5,9},{6,10},{7,11},{8,4},{9,5},... | collective-permute-start | bytes 393224 | tf_op jit(solution)/shard_map/ppermute | solution.py:571
  114.0 45.4 %collective-permute-start.9 = (f32[2,2,8,8,128]{4,3,2,1,0:T(8,128)S(1)}, f32[2,2,8,8,128]{4,3,2,1,0:T(8,128)S(1)}, u32[]{:S(2)}, u32[]{:S(2)}) collective-permute-start(f32[2,2,8,8,128]{4,3,2,1,0:T(8,128)S(1)} %copy-done.18), channel_id=1, source_target_pairs={{0,7},{1,6},{2,5},{3,4},{4,3},{5,2},{6,1},{7,0},{8,15},{9,14},{10,... | collective-permute-start | bytes 393224 | tf_op jit(solution)/shard_map/ppermute | solution.py:571
  145.9 21.7 %copy-start.11 = (f32[2,2,8,8,128]{4,3,2,1,0:T(8,128)}, f32[2,2,8,8,128]{4,3,2,1,0:T(8,128)S(1)}, u32[]{:S(2)}) copy-start(f32[2,2,8,8,128]{4,3,2,1,0:T(8,128)S(1)} %collective-permute-done.5.refs_6_) | copy-start | bytes 393220
  145.9 16.8 %collective-permute-start.10 = (f32[2,2,8,8,128]{4,3,2,1,0:T(8,128)}, f32[2,2,8,8,128]{4,3,2,1,0:T(8,128)S(1)}, u32[]{:S(2)}, u32[]{:S(2)}) collective-permute-start(f32[2,2,8,8,128]{4,3,2,1,0:T(8,128)} %get-tuple-element.58), channel_id=1, source_target_pairs={{0,6},{1,7},{2,4},{3,5},{4,2},{5,3},{6,0},{7,1},{8,14},{9,15},{10,... | collective-permute-start | bytes 393224 | tf_op jit(solution)/shard_map/ppermute | solution.py:571
  149.3 18.2 %copy-start.12 = (f32[2,2,8,8,128]{4,3,2,1,0:T(8,128)}, f32[2,2,8,8,128]{4,3,2,1,0:T(8,128)S(1)}, u32[]{:S(2)}) copy-start(f32[2,2,8,8,128]{4,3,2,1,0:T(8,128)S(1)} %collective-permute-done.6.refs_7_) | copy-start | bytes 393220
  149.3 13.4 %collective-permute-start.11 = (f32[2,2,8,8,128]{4,3,2,1,0:T(8,128)}, f32[2,2,8,8,128]{4,3,2,1,0:T(8,128)S(1)}, u32[]{:S(2)}, u32[]{:S(2)}) collective-permute-start(f32[2,2,8,8,128]{4,3,2,1,0:T(8,128)} %get-tuple-element.59), channel_id=1, source_target_pairs={{0,5},{1,4},{2,7},{3,6},{4,1},{5,0},{6,3},{7,2},{8,13},{9,12},{10,... | collective-permute-start | bytes 393224 | tf_op jit(solution)/shard_map/ppermute | solution.py:571
  154.8 12.8 %copy-start.13 = (f32[2,2,8,8,128]{4,3,2,1,0:T(8,128)}, f32[2,2,8,8,128]{4,3,2,1,0:T(8,128)S(1)}, u32[]{:S(2)}) copy-start(f32[2,2,8,8,128]{4,3,2,1,0:T(8,128)S(1)} %collective-permute-done.7.refs_8_) | copy-start | bytes 393220
  154.8 8.0 %collective-permute-start.12 = (f32[2,2,8,8,128]{4,3,2,1,0:T(8,128)}, f32[2,2,8,8,128]{4,3,2,1,0:T(8,128)}, u32[]{:S(2)}, u32[]{:S(2)}) collective-permute-start(f32[2,2,8,8,128]{4,3,2,1,0:T(8,128)} %get-tuple-element.60), channel_id=1, source_target_pairs={{0,4},{1,5},{2,6},{3,7},{4,0},{5,1},{6,2},{7,3},{8,12},{9,13},{10,... | collective-permute-start | bytes 393224 | tf_op jit(solution)/shard_map/ppermute | solution.py:571
  159.3 6.0 %collective-permute-start.13 = (f32[2,2,8,8,128]{4,3,2,1,0:T(8,128)}, f32[2,2,8,8,128]{4,3,2,1,0:T(8,128)}, u32[]{:S(2)}, u32[]{:S(2)}) collective-permute-start(f32[2,2,8,8,128]{4,3,2,1,0:T(8,128)} %get-tuple-element.61), channel_id=1, source_target_pairs={{0,3},{1,2},{2,1},{3,0},{4,7},{5,6},{6,5},{7,4},{8,11},{9,10},{10,... | collective-permute-start | bytes 393224 | tf_op jit(solution)/shard_map/ppermute | solution.py:571
  159.3 8.2 %collective-permute-start.14 = (f32[2,2,8,8,128]{4,3,2,1,0:T(8,128)}, f32[2,2,8,8,128]{4,3,2,1,0:T(8,128)}, u32[]{:S(2)}, u32[]{:S(2)}) collective-permute-start(f32[2,2,8,8,128]{4,3,2,1,0:T(8,128)} %get-tuple-element.62), channel_id=1, source_target_pairs={{0,2},{1,3},{2,0},{3,1},{4,6},{5,7},{6,4},{7,5},{8,10},{9,11},{10,... | collective-permute-start | bytes 393224 | tf_op jit(solution)/shard_map/ppermute | solution.py:571
  (9 other events, 59.4 us)

commit v9 on v8

--- a/solution.py
+++ b/solution.py
@@ -420,6 +420,7 @@
             pltpu.SemaphoreType.DMA((GROUPS,)),
         ],
         compiler_params=pltpu.CompilerParams(vmem_limit_bytes=44 << 20),
+        cost_estimate=pl.CostEstimate(flops=6_000_000_000, bytes_accessed=12_000_000, transcendentals=0),
         name="one_middle",
     )(*args)
     return out.reshape((devices,) + shape[2:])
@@ -485,8 +486,15 @@
         pltpu.make_async_copy(y_hbm.at[:, :, cut], y_ref.at[:, :, cut], y_sems.at[group])
         for group, cut in enumerate(cuts)
     ]
-    loads = [pltpu.make_async_copy(piece, held.at[slot], in_sems.at[slot]) for slot, piece in zip(order, pieces)]
-    for copy in [matrices[0], blocks[0], matrices[1]] + loads + blocks[1:]:
+    spans = [pl.ds(part * components // 2, components // 2) for part in range(2)]
+    loads = [
+        [
+            pltpu.make_async_copy(piece.at[:, :, span], held.at[slot, :, :, span], in_sems.at[part, slot])
+            for slot, piece in zip(order, pieces)
+        ]
+        for part, span in enumerate(spans)
+    ]
+    for copy in [matrices[0], blocks[0], matrices[1]] + loads[0] + blocks[1:] + loads[1]:
         copy.start()
     upper_rows = lax.broadcasted_iota(jnp.int32, (devices, rows, lanes), 1) < rows // 2
 
@@ -524,7 +532,9 @@
         blocks[group].wait()
         d = one_part(group)
         if group == 0:
-            for copy in matrices[1:] + loads:
+            matrices[1].wait()
+        if group % (groups // 2) == 0:
+            for copy in loads[group // (groups // 2)]:
                 copy.wait()
         d = (d + both_part(group)).reshape(members, 2, lanes, d.shape[1])
         for ri in range(2):
@@ -552,7 +562,7 @@
             pltpu.VMEM(shape, jnp.float32),
             pltpu.SemaphoreType.DMA((groups,)),
             pltpu.SemaphoreType.DMA((2,)),
-            pltpu.SemaphoreType.DMA((len(pieces),)),
+            pltpu.SemaphoreType.DMA((2, len(pieces))),
             pltpu.SemaphoreType.DMA((groups,)),
         ],
         compiler_params=pltpu.CompilerParams(vmem_limit_bytes=63 << 20),
@@ -715,16 +725,23 @@
     one = to_times(one_times_kernel, green, jnp.asarray(one_fermion), shape, devices, "one_times")
     both, one = lax.optimization_barrier((exchange(both), one))
     pieces = both_middle(both, pair_table, mirror_map, me, near)
-    middle_slot, quarter = near // 2, near // 4
-    order = list(range(middle_slot, middle_slot + quarter)) + [1]
-    early = [swap(pieces[slot], slot, devices) for slot in order]
-    one, early = lax.optimization_barrier((exchange(one), early))
-    one = one_middle(one, pair_table, mirror_map)
-    one, both_boson, one_boson = lax.optimization_barrier((one, jnp.asarray(both_boson), jnp.asarray(one_boson)))
-    matrix = prepare(me, both_boson, one_boson)
-    rest = [slot for slot in reversed(range(1, near)) if slot not in order]
-    late = [swap(pieces[slot], slot, devices) for slot in rest]
-    return to_frequencies(exchange(one), [pieces[0]] + early + late, [0] + order + rest, matrix)
+    first = near // 2
+    early = list(range(first, first + near // 4)) + [1]
+    beside = [first + near // 4, first + near // 4 + 1, 2, 3]
+    late = [slot for slot in range(1, near) if slot not in early + beside]
+    moved = {0: pieces[0]}
+
+    one, arrived = lax.optimization_barrier((exchange(one), [swap(pieces[slot], slot, devices) for slot in early]))
+    moved |= zip(early, arrived)
+    arrived = [swap(pieces[slot], slot, devices) for slot in beside]
+    one, arrived, both_boson, one_boson = lax.optimization_barrier(
+        (one_middle(one, pair_table, mirror_map), arrived, jnp.asarray(both_boson), jnp.asarray(one_boson))
+    )
+    moved |= zip(beside, arrived)
+    matrix, sent = lax.optimization_barrier((prepare(me, both_boson, one_boson), [pieces[slot] for slot in late]))
+    moved |= zip(late, [swap(piece, slot, devices) for slot, piece in zip(late, sent)])
+    order = [0] + early + beside + late
+    return to_frequencies(exchange(one), [moved[slot] for slot in order], order, matrix)
 
 
 def solution(mesh):

time: 179 us -> 169 us (0.944); the launches traced: 176 us -> 168 us
  waiting for transfers between devices: 106 us -> 92.3 us
  starting transfers between devices: 32.2 us -> 36.7 us
    ppermute x15, waiting for transfers between devices: 63.4 us -> 44.1 us  [swap(): lax.ppermute(piece, 'kb', [(device, device ^ slot) for device in range(de...]
    all_to_all x3, waiting for transfers between devices: 42.2 us -> 48.2 us  [exchange(): lax.all_to_all(flat, 'kb', split_axis=0, concat_axis=0, tiled=True)]
    ppermute x15, starting transfers between devices: 16.3 us -> 19.6 us  [swap(): lax.ppermute(piece, 'kb', [(device, device ^ slot) for device in range(de...]
  transfers between devices with their start and end apart: 18 -> 18, of which waited for: 11 -> 9; matrix products, arithmetic and copies ran while one was open for 0% -> 0% of each run, Pallas kernels for 10% -> 15%
where the time goes in v9:
time: 169 us; the launch traced here: 168 us
  waiting for transfers between devices  92.3 us (55%)
  Pallas kernels  38 us (22%)
  starting transfers between devices  36.7 us (22%)
    all_to_all x3, waiting for transfers between devices, exchange(): lax.all_to_all(flat, 'kb', split_axis=0, concat_axis=0, tiled=True)  48.2 us
    ppermute x15, waiting for transfers between devices, swap(): lax.ppermute(piece, 'kb', [(device, device ^ slot) for device in range(de...  44.1 us
    ppermute x15, starting transfers between devices, swap(): lax.ppermute(piece, 'kb', [(device, device ^ slot) for device in range(de...  19.6 us
    all_to_all x3, starting transfers between devices, exchange(): lax.all_to_all(flat, 'kb', split_axis=0, concat_axis=0, tiled=True)  17 us
    pallas_call x2, Pallas kernels, to_times(): pl.pallas_call(kernel, in_specs=[hbm, hbm], out_specs=hbm, out_shape=jax....  11.6 us
    pallas_call x1, Pallas kernels, both_middle(): pl.pallas_call(both_middle_kernel, in_specs=[pl.BlockSpec(memory_space=pl...  8.94 us
    pallas_call x1, Pallas kernels, to_frequencies(): pl.pallas_call(functools.partial(frequency_kernel, order), in_specs=[hbm]...  8.47 us
    pallas_call x1, Pallas kernels, one_middle(): pl.pallas_call(one_middle_kernel, in_specs=specs, out_specs=pl.BlockSpec(...  6.58 us
  transfers between devices with their start and end apart: 18, of which 9 were waited for; matrix products, arithmetic and copies ran while one was open for 0% of the time, Pallas kernels for 15%

profile of v9, /device:TPU:0, one launch (start us, length us, event | category | flops | bytes accessed | tf_op | source)
XLA Modules:
  0.0 168.3 jit_solution(5251787183360266011)
XLA Ops:
  0.0 4.9 %both_times.1 = f32[32,2,2,4,8,128]{5,4,3,2,1,0:T(8,128)} custom-call(f32[2,4,128,512]{3,2,1,0:T(8,128)} %g_hbm.2, f32[256,512]{1,0:T(8,128)} %constant.20.clone.m_hbm), custom_call_target="tpu_custom_call" | custom-call | tf_op jit(solution)/shard_map/both_times/pallas_call | solution.py:186
  4.9 7.4 %all-to-all-start = ((f32[32,128,128]{2,1,0:T(8,128)}), f32[32,128,128]{2,1,0:T(8,128)}, u32[]{:S(2)}, u32[]{:S(2)}) async-start(f32[32,128,128]{2,1,0:T(8,128)} %bitcast.14), calls=%async_computation | async-start | bytes 4194304 | tf_op jit(solution)/shard_map/all_to_all | solution.py:575
  12.3 6.7 %one_times.1 = f32[32,2,4,8,128]{4,3,2,1,0:T(8,128)} custom-call(f32[2,4,128,512]{3,2,1,0:T(8,128)} %g_hbm.2, f32[512,512]{1,0:T(8,128)} %constant.21.clone.m_hbm), custom_call_target="tpu_custom_call" | custom-call | tf_op jit(solution)/shard_map/one_times/pallas_call | solution.py:186
  19.1 42.2 %all-to-all-done = f32[32,128,128]{2,1,0:T(8,128)} async-done(((f32[32,128,128]{2,1,0:T(8,128)}), f32[32,128,128]{2,1,0:T(8,128)}, u32[]{:S(2)}, u32[]{:S(2)}) %all-to-all-start) | async-done | bytes 2097184 | tf_op jit(solution)/shard_map/all_to_all | solution.py:575
  61.3 4.2 %all-to-all-start.1 = ((f32[32,64,128]{2,1,0:T(8,128)}), f32[32,64,128]{2,1,0:T(8,128)S(1)}, u32[]{:S(2)}, u32[]{:S(2)}) async-start(f32[32,64,128]{2,1,0:T(8,128)} %bitcast.15), calls=%async_computation.1 | async-start | bytes 2097152 | tf_op jit(solution)/shard_map/all_to_all | solution.py:575
  65.5 8.9 %both_middle.1 = (f32[2,2,8,8,128]{4,3,2,1,0:T(8,128)}, f32[2,2,8,8,128]{4,3,2,1,0:T(8,128)}, f32[2,2,8,8,128]{4,3,2,1,0:T(8,128)}, f32[2,2,8,8,128]{4,3,2,1,0:T...) custom-call(s32[1]{0:T(128)} %bitcast.5.me_ref, ...), custom_call_target="tpu_custom_call" | custom-call | tf_op jit(solution)/shard_map/both_middle/pallas_call | solution.py:434
  74.4 1.7 collective-permute-start
  76.1 2.4 %collective-permute-start.2 = (f32[2,2,8,8,128]{4,3,2,1,0:T(8,128)}, f32[2,2,8,8,128]{4,3,2,1,0:T(8,128)S(1)}, u32[]{:S(2)}, u32[]{:S(2)}) collective-permute-start(f32[2,2,8,8,128]{4,3,2,1,0:T(8,128)} %get-tuple-element.51), channel_id=1, source_target_pairs={{0,10},{1,11},{2,8},{3,9},{4,14},{5,15},{6,12},{7,13},{8,2},{9,3},... | collective-permute-start | bytes 393224 | tf_op jit(solution)/shard_map/ppermute | solution.py:581
  78.5 0.4 collective-permute-start.3
  78.8 0.3 collective-permute-start.4
  79.1 7.1 %collective-permute-done.refs_1_ = f32[2,2,8,8,128]{4,3,2,1,0:T(8,128)S(1)} collective-permute-done((f32[2,2,8,8,128]{4,3,2,1,0:T(8,128)}, f32[2,2,8,8,128]{4,3,2,1,0:T(8,128)S(1)}, u32[]{:S(2)}, u32[]{:S(2)}) %collective-permute-start) | collective-permute-done | bytes 131104 | tf_op jit(solution)/shard_map/ppermute | solution.py:581
  86.3 3.5 %collective-permute-start.5 = (f32[2,2,8,8,128]{4,3,2,1,0:T(8,128)}, f32[2,2,8,8,128]{4,3,2,1,0:T(8,128)S(1)}, u32[]{:S(2)}, u32[]{:S(2)}) collective-permute-start(f32[2,2,8,8,128]{4,3,2,1,0:T(8,128)} %get-tuple-element.55), channel_id=1, source_target_pairs={{0,12},{1,13},{2,14},{3,15},{4,8},{5,9},{6,10},{7,11},{8,4},{9,5},... | collective-permute-start | bytes 393224 | tf_op jit(solution)/shard_map/ppermute | solution.py:581
  89.7 2.5 %collective-permute-start.6 = (f32[2,2,8,8,128]{4,3,2,1,0:T(8,128)}, f32[2,2,8,8,128]{4,3,2,1,0:T(8,128)S(1)}, u32[]{:S(2)}, u32[]{:S(2)}) collective-permute-start(f32[2,2,8,8,128]{4,3,2,1,0:T(8,128)} %get-tuple-element.56), channel_id=1, source_target_pairs={{0,13},{1,12},{2,15},{3,14},{4,9},{5,8},{6,11},{7,10},{8,5},{9,4},... | collective-permute-start | bytes 393224 | tf_op jit(solution)/shard_map/ppermute | solution.py:581
  92.3 2.5 %collective-permute-done.2.refs_3_ = f32[2,2,8,8,128]{4,3,2,1,0:T(8,128)S(1)} collective-permute-done((f32[2,2,8,8,128]{4,3,2,1,0:T(8,128)}, f32[2,2,8,8,128]{4,3,2,1,0:T(8,128)S(1)}, u32[]{:S(2)}, u32[]{:S(2)}) %collective-permute-start.2) | collective-permute-done | bytes 131104 | tf_op jit(solution)/shard_map/ppermute | solution.py:581
  94.8 0.4 collective-permute-start.7
  95.2 1.4 collective-permute-done.3.refs_4_
  96.7 0.8 collective-permute-start.8
  97.5 6.6 %one_middle.1 = f32[16,2,2,8,8,128]{5,4,3,2,1,0:T(8,128)} custom-call(s32[2,8]{1,0:T(2,128)S(1)} %bitcast.13, s32[3,16]{1,0:T(4,128)S(1)} %copy-done.4, bf16[256,256]{1,0:T(8,128)(2,1)S(1)} %copy-done.3, bf16[256,256]{1,0:T(8,128)(2,1)S(1)} %copy-done.2, bf16[256,256]{1,0:T(8,128)(2,1)S(1)} %copy-done.1, bf16[256,256]{1,0:T(8,128)(2,1)S(1)} %copy-done, ...), custom_call_target="tpu_custom_call" | custom-call | flops 6000000000 | bytes 12000000 | tf_op jit(solution)/shard_map/one_middle/pallas_call | solution.py:407
  104.2 0.6 copy-done.11
  104.9 0.1 copy-done.14
  105.0 5.4 %all-to-all-start.2 = ((f32[32,128,128]{2,1,0:T(8,128)}), f32[32,128,128]{2,1,0:T(8,128)}, u32[]{:S(2)}, u32[]{:S(2)}) async-start(f32[32,128,128]{2,1,0:T(8,128)} %bitcast.9), calls=%async_computation.2 | async-start | bytes 4194304 | tf_op jit(solution)/shard_map/all_to_all | solution.py:575
  110.4 2.4 %prepare.1.m_hbm = bf16[2,512,512]{2,1,0:T(8,128)(2,1)} custom-call(s32[1]{0:T(128)} %bitcast.5.me_ref, f32[2,16,8,512]{3,2,1,0:T(8,128)} %constant.26.clone.both_ref, f32[256,512]{1,0:T(8,128)} %constant.27.clone.one_ref), custom_call_target="tpu_custom_call" | custom-call | tf_op jit(solution)/shard_map/prepare/pallas_call | solution.py:463
  112.8 1.5 collective-permute-start.9
  114.3 2.4 %collective-permute-start.11 = (f32[2,2,8,8,128]{4,3,2,1,0:T(8,128)}, f32[2,2,8,8,128]{4,3,2,1,0:T(8,128)S(1)}, u32[]{:S(2)}, u32[]{:S(2)}) collective-permute-start(f32[2,2,8,8,128]{4,3,2,1,0:T(8,128)} %get-tuple-element.81), channel_id=1, source_target_pairs={{0,6},{1,7},{2,4},{3,5},{4,2},{5,3},{6,0},{7,1},{8,14},{9,15},{10,... | collective-permute-start | bytes 393224 | tf_op jit(solution)/shard_map/ppermute | solution.py:581
  116.7 0.5 collective-permute-start.12
  117.2 3.3 %collective-permute-start.13 = (f32[2,2,8,8,128]{4,3,2,1,0:T(8,128)}, f32[2,2,8,8,128]{4,3,2,1,0:T(8,128)S(1)}, u32[]{:S(2)}, u32[]{:S(2)}) collective-permute-start(f32[2,2,8,8,128]{4,3,2,1,0:T(8,128)} %get-tuple-element.83), channel_id=1, source_target_pairs={{0,14},{1,15},{2,12},{3,13},{4,10},{5,11},{6,8},{7,9},{8,6},{9,7},... | collective-permute-start | bytes 393224 | tf_op jit(solution)/shard_map/ppermute | solution.py:581
  120.5 24.5 %collective-permute-done.9.refs_10_ = f32[2,2,8,8,128]{4,3,2,1,0:T(8,128)S(1)} collective-permute-done((f32[2,2,8,8,128]{4,3,2,1,0:T(8,128)S(1)}, f32[2,2,8,8,128]{4,3,2,1,0:T(8,128)S(1)}, u32[]{:S(2)}, u32[]{:S(2)}) %collective-permute-start.9) | collective-permute-done | bytes 131104 | tf_op jit(solution)/shard_map/ppermute | solution.py:581
  145.0 2.2 %collective-permute-done.10.refs_11_ = f32[2,2,8,8,128]{4,3,2,1,0:T(8,128)S(1)} collective-permute-done((f32[2,2,8,8,128]{4,3,2,1,0:T(8,128)}, f32[2,2,8,8,128]{4,3,2,1,0:T(8,128)S(1)}, u32[]{:S(2)}, u32[]{:S(2)}) %collective-permute-start.10) | collective-permute-done | bytes 131104 | tf_op jit(solution)/shard_map/ppermute | solution.py:581
  147.2 1.6 collective-permute-done.13.refs_14_
  148.8 4.7 %collective-permute-done.14.refs_15_ = f32[2,2,8,8,128]{4,3,2,1,0:T(8,128)S(1)} collective-permute-done((f32[2,2,8,8,128]{4,3,2,1,0:T(8,128)S(1)}, f32[2,2,8,8,128]{4,3,2,1,0:T(8,128)S(1)}, u32[]{:S(2)}, u32[]{:S(2)}) %collective-permute-start.14) | collective-permute-done | bytes 131104 | tf_op jit(solution)/shard_map/ppermute | solution.py:581
  153.5 6.1 %all-to-all-done.2 = f32[32,128,128]{2,1,0:T(8,128)} async-done(((f32[32,128,128]{2,1,0:T(8,128)}), f32[32,128,128]{2,1,0:T(8,128)}, u32[]{:S(2)}, u32[]{:S(2)}) %all-to-all-start.2) | async-done | bytes 2097184 | tf_op jit(solution)/shard_map/all_to_all | solution.py:575
  159.6 8.5 %to_frequencies.1 = f32[2,8,128,512]{3,2,1,0:T(8,128)} custom-call(f32[32,2,8,8,128]{4,3,2,1,0:T(8,128)} %bitcast.10.y_hbm, bf16[2,512,512]{2,1,0:T(8,128)(2,1)} %prepare.1.m_hbm, f32[2,2,8,8,128]{4,3,2,1,0:T(8,128)} %get-tuple-element.69.refs_0_, f32[2,2,8,8,128]{4,3,2,1,0:T(8,128)} %copy-done.6, f32[2,2,8,8,128]{4,3,2,1,0:T(8,128)} %copy-done.7, ...), custom_call_target="tpu_custom_call" | custom-call | tf_op jit(solution)/shard_map/to_frequencies/pallas_call | solution.py:553
  (56 shorter events, 0.2 us)
Async XLA Ops:
  4.9 56.3 %all-to-all-start = ((f32[32,128,128]{2,1,0:T(8,128)}), f32[32,128,128]{2,1,0:T(8,128)}, u32[]{:S(2)}, u32[]{:S(2)}) async-start(f32[32,128,128]{2,1,0:T(8,128)} %bitcast.14), calls=%async_computation | async-start | bytes 4194304 | tf_op jit(solution)/shard_map/all_to_all | solution.py:575
  61.2 36.2 %copy-start = (bf16[256,256]{1,0:T(8,128)(2,1)S(1)}, bf16[256,256]{1,0:T(8,128)(2,1)}, u32[]{:S(2)}) copy-start(bf16[256,256]{1,0:T(8,128)(2,1)} %constant.25.clone.sl_ref) | copy-start | bytes 393220
  61.2 36.3 %copy-start.1 = (bf16[256,256]{1,0:T(8,128)(2,1)S(1)}, bf16[256,256]{1,0:T(8,128)(2,1)}, u32[]{:S(2)}) copy-start(bf16[256,256]{1,0:T(8,128)(2,1)} %constant.24.clone.sh_ref) | copy-start | bytes 393220
  61.2 36.3 %copy-start.2 = (bf16[256,256]{1,0:T(8,128)(2,1)S(1)}, bf16[256,256]{1,0:T(8,128)(2,1)}, u32[]{:S(2)}) copy-start(bf16[256,256]{1,0:T(8,128)(2,1)} %constant.23.clone.cl_ref) | copy-start | bytes 393220
  61.2 36.3 %copy-start.3 = (bf16[256,256]{1,0:T(8,128)(2,1)S(1)}, bf16[256,256]{1,0:T(8,128)(2,1)}, u32[]{:S(2)}) copy-start(bf16[256,256]{1,0:T(8,128)(2,1)} %constant.22.clone.ch_ref) | copy-start | bytes 393220
  61.2 36.3 %copy-start.4 = (s32[3,16]{1,0:T(4,128)S(1)}, s32[3,16]{1,0:T(4,128)}, u32[]{:S(2)}) copy-start(s32[3,16]{1,0:T(4,128)} %mirror_ref.3) | copy-start | bytes 580
  61.2 36.3 %copy-start.5 = (s32[8,2]{0,1:T(2,128)S(1)}, s32[8,2]{0,1:T(2,128)}, u32[]{:S(2)}) copy-start(s32[8,2]{0,1:T(2,128)} %param.16) | copy-start | bytes 196
  61.3 36.2 %all-to-all-start.1 = ((f32[32,64,128]{2,1,0:T(8,128)}), f32[32,64,128]{2,1,0:T(8,128)S(1)}, u32[]{:S(2)}, u32[]{:S(2)}) async-start(f32[32,64,128]{2,1,0:T(8,128)} %bitcast.15), calls=%async_computation.1 | async-start | bytes 2097152 | tf_op jit(solution)/shard_map/all_to_all | solution.py:575
  74.4 11.8 %collective-permute-start = (f32[2,2,8,8,128]{4,3,2,1,0:T(8,128)}, f32[2,2,8,8,128]{4,3,2,1,0:T(8,128)S(1)}, u32[]{:S(2)}, u32[]{:S(2)}) collective-permute-start(f32[2,2,8,8,128]{4,3,2,1,0:T(8,128)} %get-tuple-element.49), channel_id=1, source_target_pairs={{0,8},{1,9},{2,10},{3,11},{4,12},{5,13},{6,14},{7,15},{8,0},{9,1},... | collective-permute-start | bytes 393224 | tf_op jit(solution)/shard_map/ppermute | solution.py:581
  76.1 13.7 %collective-permute-start.1 = (f32[2,2,8,8,128]{4,3,2,1,0:T(8,128)}, f32[2,2,8,8,128]{4,3,2,1,0:T(8,128)S(1)}, u32[]{:S(2)}, u32[]{:S(2)}) collective-permute-start(f32[2,2,8,8,128]{4,3,2,1,0:T(8,128)} %get-tuple-element.50), channel_id=1, source_target_pairs={{0,9},{1,8},{2,11},{3,10},{4,13},{5,12},{6,15},{7,14},{8,1},{9,0},... | collective-permute-start | bytes 393224 | tf_op jit(solution)/shard_map/ppermute | solution.py:581
  76.1 18.7 %collective-permute-start.2 = (f32[2,2,8,8,128]{4,3,2,1,0:T(8,128)}, f32[2,2,8,8,128]{4,3,2,1,0:T(8,128)S(1)}, u32[]{:S(2)}, u32[]{:S(2)}) collective-permute-start(f32[2,2,8,8,128]{4,3,2,1,0:T(8,128)} %get-tuple-element.51), channel_id=1, source_target_pairs={{0,10},{1,11},{2,8},{3,9},{4,14},{5,15},{6,12},{7,13},{8,2},{9,3},... | collective-permute-start | bytes 393224 | tf_op jit(solution)/shard_map/ppermute | solution.py:581
  78.5 18.2 %collective-permute-start.3 = (f32[2,2,8,8,128]{4,3,2,1,0:T(8,128)}, f32[2,2,8,8,128]{4,3,2,1,0:T(8,128)S(1)}, u32[]{:S(2)}, u32[]{:S(2)}) collective-permute-start(f32[2,2,8,8,128]{4,3,2,1,0:T(8,128)} %get-tuple-element.52), channel_id=1, source_target_pairs={{0,11},{1,10},{2,9},{3,8},{4,15},{5,14},{6,13},{7,12},{8,3},{9,2},... | collective-permute-start | bytes 393224 | tf_op jit(solution)/shard_map/ppermute | solution.py:581
  78.8 18.6 %collective-permute-start.4 = (f32[2,2,8,8,128]{4,3,2,1,0:T(8,128)}, f32[2,2,8,8,128]{4,3,2,1,0:T(8,128)S(1)}, u32[]{:S(2)}, u32[]{:S(2)}) collective-permute-start(f32[2,2,8,8,128]{4,3,2,1,0:T(8,128)} %get-tuple-element.53), channel_id=1, source_target_pairs={{0,1},{1,0},{2,3},{3,2},{4,5},{5,4},{6,7},{7,6},{8,9},{9,8},{10,11... | collective-permute-start | bytes 393224 | tf_op jit(solution)/shard_map/ppermute | solution.py:581
  86.3 17.9 %copy-start.6 = (f32[2,2,8,8,128]{4,3,2,1,0:T(8,128)}, f32[2,2,8,8,128]{4,3,2,1,0:T(8,128)S(1)}, u32[]{:S(2)}) copy-start(f32[2,2,8,8,128]{4,3,2,1,0:T(8,128)S(1)} %collective-permute-done.refs_1_) | copy-start | bytes 393220
  86.3 17.9 %collective-permute-start.5 = (f32[2,2,8,8,128]{4,3,2,1,0:T(8,128)}, f32[2,2,8,8,128]{4,3,2,1,0:T(8,128)S(1)}, u32[]{:S(2)}, u32[]{:S(2)}) collective-permute-start(f32[2,2,8,8,128]{4,3,2,1,0:T(8,128)} %get-tuple-element.55), channel_id=1, source_target_pairs={{0,12},{1,13},{2,14},{3,15},{4,8},{5,9},{6,10},{7,11},{8,4},{9,5},... | collective-permute-start | bytes 393224 | tf_op jit(solution)/shard_map/ppermute | solution.py:581
  89.7 14.4 %copy-start.7 = (f32[2,2,8,8,128]{4,3,2,1,0:T(8,128)}, f32[2,2,8,8,128]{4,3,2,1,0:T(8,128)S(1)}, u32[]{:S(2)}) copy-start(f32[2,2,8,8,128]{4,3,2,1,0:T(8,128)S(1)} %collective-permute-done.1.refs_2_) | copy-start | bytes 393220
  89.7 14.4 %collective-permute-start.6 = (f32[2,2,8,8,128]{4,3,2,1,0:T(8,128)}, f32[2,2,8,8,128]{4,3,2,1,0:T(8,128)S(1)}, u32[]{:S(2)}, u32[]{:S(2)}) collective-permute-start(f32[2,2,8,8,128]{4,3,2,1,0:T(8,128)} %get-tuple-element.56), channel_id=1, source_target_pairs={{0,13},{1,12},{2,15},{3,14},{4,9},{5,8},{6,11},{7,10},{8,5},{9,4},... | collective-permute-start | bytes 393224 | tf_op jit(solution)/shard_map/ppermute | solution.py:581
  94.8 9.4 %collective-permute-start.7 = (f32[2,2,8,8,128]{4,3,2,1,0:T(8,128)}, f32[2,2,8,8,128]{4,3,2,1,0:T(8,128)S(1)}, u32[]{:S(2)}, u32[]{:S(2)}) collective-permute-start(f32[2,2,8,8,128]{4,3,2,1,0:T(8,128)} %get-tuple-element.57), channel_id=1, source_target_pairs={{0,2},{1,3},{2,0},{3,1},{4,6},{5,7},{6,4},{7,5},{8,10},{9,11},{10,... | collective-permute-start | bytes 393224 | tf_op jit(solution)/shard_map/ppermute | solution.py:581
  96.7 7.6 %collective-permute-start.8 = (f32[2,2,8,8,128]{4,3,2,1,0:T(8,128)}, f32[2,2,8,8,128]{4,3,2,1,0:T(8,128)S(1)}, u32[]{:S(2)}, u32[]{:S(2)}) collective-permute-start(f32[2,2,8,8,128]{4,3,2,1,0:T(8,128)} %get-tuple-element.58), channel_id=1, source_target_pairs={{0,3},{1,2},{2,1},{3,0},{4,7},{5,6},{6,5},{7,4},{8,11},{9,10},{10,... | collective-permute-start | bytes 393224 | tf_op jit(solution)/shard_map/ppermute | solution.py:581
  105.0 54.6 %all-to-all-start.2 = ((f32[32,128,128]{2,1,0:T(8,128)}), f32[32,128,128]{2,1,0:T(8,128)}, u32[]{:S(2)}, u32[]{:S(2)}) async-start(f32[32,128,128]{2,1,0:T(8,128)} %bitcast.9), calls=%async_computation.2 | async-start | bytes 4194304 | tf_op jit(solution)/shard_map/all_to_all | solution.py:575
  110.4 34.6 %copy-start.21 = (f32[2,2,8,8,128]{4,3,2,1,0:T(8,128)S(1)}, f32[2,2,8,8,128]{4,3,2,1,0:T(8,128)}, u32[]{:S(2)}) copy-start(f32[2,2,8,8,128]{4,3,2,1,0:T(8,128)} %get-tuple-element.84) | copy-start | bytes 393220
  112.8 32.2 %collective-permute-start.9 = (f32[2,2,8,8,128]{4,3,2,1,0:T(8,128)S(1)}, f32[2,2,8,8,128]{4,3,2,1,0:T(8,128)S(1)}, u32[]{:S(2)}, u32[]{:S(2)}) collective-permute-start(f32[2,2,8,8,128]{4,3,2,1,0:T(8,128)S(1)} %copy-done.22), channel_id=1, source_target_pairs={{0,4},{1,5},{2,6},{3,7},{4,0},{5,1},{6,2},{7,3},{8,12},{9,13},{10,... | collective-permute-start | bytes 393224 | tf_op jit(solution)/shard_map/ppermute | solution.py:581
  114.3 32.9 %collective-permute-start.10 = (f32[2,2,8,8,128]{4,3,2,1,0:T(8,128)}, f32[2,2,8,8,128]{4,3,2,1,0:T(8,128)S(1)}, u32[]{:S(2)}, u32[]{:S(2)}) collective-permute-start(f32[2,2,8,8,128]{4,3,2,1,0:T(8,128)} %get-tuple-element.80), channel_id=1, source_target_pairs={{0,5},{1,4},{2,7},{3,6},{4,1},{5,0},{6,3},{7,2},{8,13},{9,12},{10,... | collective-permute-start | bytes 393224 | tf_op jit(solution)/shard_map/ppermute | solution.py:581
  114.3 32.9 %collective-permute-start.11 = (f32[2,2,8,8,128]{4,3,2,1,0:T(8,128)}, f32[2,2,8,8,128]{4,3,2,1,0:T(8,128)S(1)}, u32[]{:S(2)}, u32[]{:S(2)}) collective-permute-start(f32[2,2,8,8,128]{4,3,2,1,0:T(8,128)} %get-tuple-element.81), channel_id=1, source_target_pairs={{0,6},{1,7},{2,4},{3,5},{4,2},{5,3},{6,0},{7,1},{8,14},{9,15},{10,... | collective-permute-start | bytes 393224 | tf_op jit(solution)/shard_map/ppermute | solution.py:581
  116.7 30.5 %collective-permute-start.12 = (f32[2,2,8,8,128]{4,3,2,1,0:T(8,128)}, f32[2,2,8,8,128]{4,3,2,1,0:T(8,128)S(1)}, u32[]{:S(2)}, u32[]{:S(2)}) collective-permute-start(f32[2,2,8,8,128]{4,3,2,1,0:T(8,128)} %get-tuple-element.82), channel_id=1, source_target_pairs={{0,7},{1,6},{2,5},{3,4},{4,3},{5,2},{6,1},{7,0},{8,15},{9,14},{10,... | collective-permute-start | bytes 393224 | tf_op jit(solution)/shard_map/ppermute | solution.py:581
  117.2 31.6 %collective-permute-start.13 = (f32[2,2,8,8,128]{4,3,2,1,0:T(8,128)}, f32[2,2,8,8,128]{4,3,2,1,0:T(8,128)S(1)}, u32[]{:S(2)}, u32[]{:S(2)}) collective-permute-start(f32[2,2,8,8,128]{4,3,2,1,0:T(8,128)} %get-tuple-element.83), channel_id=1, source_target_pairs={{0,14},{1,15},{2,12},{3,13},{4,10},{5,11},{6,8},{7,9},{8,6},{9,7},... | collective-permute-start | bytes 393224 | tf_op jit(solution)/shard_map/ppermute | solution.py:581
  145.0 14.6 %copy-start.15 = (f32[2,2,8,8,128]{4,3,2,1,0:T(8,128)}, f32[2,2,8,8,128]{4,3,2,1,0:T(8,128)S(1)}, u32[]{:S(2)}) copy-start(f32[2,2,8,8,128]{4,3,2,1,0:T(8,128)S(1)} %collective-permute-done.9.refs_10_) | copy-start | bytes 393220
  145.0 8.5 %collective-permute-start.14 = (f32[2,2,8,8,128]{4,3,2,1,0:T(8,128)S(1)}, f32[2,2,8,8,128]{4,3,2,1,0:T(8,128)S(1)}, u32[]{:S(2)}, u32[]{:S(2)}) collective-permute-start(f32[2,2,8,8,128]{4,3,2,1,0:T(8,128)S(1)} %copy-done.21), channel_id=1, source_target_pairs={{0,15},{1,14},{2,13},{3,12},{4,11},{5,10},{6,9},{7,8},{8,7},{9,6},... | collective-permute-start | bytes 393224 | tf_op jit(solution)/shard_map/ppermute | solution.py:581
  147.2 12.4 %copy-start.16 = (f32[2,2,8,8,128]{4,3,2,1,0:T(8,128)}, f32[2,2,8,8,128]{4,3,2,1,0:T(8,128)S(1)}, u32[]{:S(2)}) copy-start(f32[2,2,8,8,128]{4,3,2,1,0:T(8,128)S(1)} %collective-permute-done.10.refs_11_) | copy-start | bytes 393220
  147.2 12.4 %copy-start.17 = (f32[2,2,8,8,128]{4,3,2,1,0:T(8,128)}, f32[2,2,8,8,128]{4,3,2,1,0:T(8,128)S(1)}, u32[]{:S(2)}) copy-start(f32[2,2,8,8,128]{4,3,2,1,0:T(8,128)S(1)} %collective-permute-done.11.refs_12_) | copy-start | bytes 393220
  147.2 12.4 %copy-start.18 = (f32[2,2,8,8,128]{4,3,2,1,0:T(8,128)}, f32[2,2,8,8,128]{4,3,2,1,0:T(8,128)S(1)}, u32[]{:S(2)}) copy-start(f32[2,2,8,8,128]{4,3,2,1,0:T(8,128)S(1)} %collective-permute-done.12.refs_13_) | copy-start | bytes 393220
  148.8 10.8 %copy-start.19 = (f32[2,2,8,8,128]{4,3,2,1,0:T(8,128)}, f32[2,2,8,8,128]{4,3,2,1,0:T(8,128)S(1)}, u32[]{:S(2)}) copy-start(f32[2,2,8,8,128]{4,3,2,1,0:T(8,128)S(1)} %collective-permute-done.13.refs_14_) | copy-start | bytes 393220
  (9 other events, 34.9 us)

commit v10 on v9

--- a/solution.py
+++ b/solution.py
@@ -498,45 +498,37 @@
         copy.start()
     upper_rows = lax.broadcasted_iota(jnp.int32, (devices, rows, lanes), 1) < rows // 2
 
-    def part_of(values, start):
-        matrix = [m_ref[part, start : start + depth] for part in range(2)]
-        return dot3(split_value(jnp.concatenate(values, axis=0)), matrix, ((1,), (0,)))
-
-    def one_part(group):
-        values = []
-        for c in range(group * members, (group + 1) * members):
-            folded = []
-            for ri in range(2):
-                tile = y_ref[:, ri, c]
-                turned = pltpu.roll(tile, rows // 2, 1)
-                folded.append((tile + turned, turned - tile))
-            first = jnp.where(upper_rows, folded[0][0], -folded[1][1])
-            second = jnp.where(upper_rows, folded[1][0], folded[0][1])
-            values.append(first.reshape(devices * rows, lanes).T)
-            values.append(second.reshape(devices * rows, lanes).T)
-        return part_of(values, 0)
-
-    def both_part(group):
-        values = []
-        for c in range(group * members, (group + 1) * members):
-            part = [[held[:, half, ri, c].reshape(near * rows, lanes) for ri in range(2)] for half in range(2)]
-            sums = [part[0][ri] + part[1][ri] for ri in range(2)]
-            differences = [part[0][ri] - part[1][ri] for ri in range(2)]
-            values.append(jnp.concatenate([sums[0], -differences[1]], axis=0).T)
-            values.append(jnp.concatenate([sums[1], differences[0]], axis=0).T)
-        return part_of(values, depth)
+    def one_values(c):
+        folded = []
+        for ri in range(2):
+            tile = y_ref[:, ri, c]
+            turned = pltpu.roll(tile, rows // 2, 1)
+            folded.append((tile + turned, turned - tile))
+        first = jnp.where(upper_rows, folded[0][0], -folded[1][1])
+        second = jnp.where(upper_rows, folded[1][0], folded[0][1])
+        return first.reshape(depth, lanes), second.reshape(depth, lanes)
+
+    def both_values(c):
+        part = [[held[:, half, ri, c].reshape(near * rows, lanes) for ri in range(2)] for half in range(2)]
+        sums = [part[0][ri] + part[1][ri] for ri in range(2)]
+        differences = [part[0][ri] - part[1][ri] for ri in range(2)]
+        return [sums[0], -differences[1]], [sums[1], differences[0]]
 
     copies = []
-    matrices[0].wait()
+    for copy in matrices:
+        copy.wait()
+    matrix = (m_ref[0], m_ref[1])
     for group in range(groups):
         blocks[group].wait()
-        d = one_part(group)
-        if group == 0:
-            matrices[1].wait()
         if group % (groups // 2) == 0:
             for copy in loads[group // (groups // 2)]:
                 copy.wait()
-        d = (d + both_part(group)).reshape(members, 2, lanes, d.shape[1])
+        values = []
+        for c in range(group * members, (group + 1) * members):
+            for one, both in zip(one_values(c), both_values(c)):
+                values.append(jnp.concatenate([one] + both, axis=0).T)
+        d = dot3(split_value(jnp.concatenate(values, axis=0)), matrix, ((1,), (0,)))
+        d = d.reshape(members, 2, lanes, d.shape[1])
         for ri in range(2):
             stage[ri, group * members : (group + 1) * members] = d[:, ri]
         copies.append(pltpu.make_async_copy(stage.at[:, cuts[group]], out_ref.at[:, cuts[group]], sems.at[group]))
@@ -725,9 +717,9 @@
     one = to_times(one_times_kernel, green, jnp.asarray(one_fermion), shape, devices, "one_times")
     both, one = lax.optimization_barrier((exchange(both), one))
     pieces = both_middle(both, pair_table, mirror_map, me, near)
-    first = near // 2
-    early = list(range(first, first + near // 4)) + [1]
-    beside = [first + near // 4, first + near // 4 + 1, 2, 3]
+    first, count = near // 2, 3 * near // 16
+    early = list(range(first, first + count)) + [1, 2]
+    beside = list(range(first + count, first + 2 * count)) + [3, 4]
     late = [slot for slot in range(1, near) if slot not in early + beside]
     moved = {0: pieces[0]}
 

time: 169 us -> 169 us (level)
  waiting for transfers between devices: 92.3 us -> 94 us
  transfers between devices with their start and end apart: 18 -> 18, of which waited for: 9 -> 10; matrix products, arithmetic and copies ran while one was open for 0% -> 0% of each run, Pallas kernels for 15% -> 15%
where the time goes in v10:
time: 169 us; the launch traced here: 168 us
  waiting for transfers between devices  94 us (56%)
  Pallas kernels  37.8 us (22%)
  starting transfers between devices  35.3 us (21%)
    all_to_all x3, waiting for transfers between devices, exchange(): lax.all_to_all(flat, 'kb', split_axis=0, concat_axis=0, tiled=True)  49.8 us
    ppermute x15, waiting for transfers between devices, swap(): lax.ppermute(piece, 'kb', [(device, device ^ slot) for device in range(de...  44.1 us
    ppermute x15, starting transfers between devices, swap(): lax.ppermute(piece, 'kb', [(device, device ^ slot) for device in range(de...  19.3 us
    all_to_all x3, starting transfers between devices, exchange(): lax.all_to_all(flat, 'kb', split_axis=0, concat_axis=0, tiled=True)  16 us
    pallas_call x2, Pallas kernels, to_times(): pl.pallas_call(kernel, in_specs=[hbm, hbm], out_specs=hbm, out_shape=jax....  11.6 us
    pallas_call x1, Pallas kernels, both_middle(): pl.pallas_call(both_middle_kernel, in_specs=[pl.BlockSpec(memory_space=pl...  8.94 us
    pallas_call x1, Pallas kernels, to_frequencies(): pl.pallas_call(functools.partial(frequency_kernel, order), in_specs=[hbm]...  8.34 us
    pallas_call x1, Pallas kernels, one_middle(): pl.pallas_call(one_middle_kernel, in_specs=specs, out_specs=pl.BlockSpec(...  6.59 us
  transfers between devices with their start and end apart: 18, of which 10 were waited for; matrix products, arithmetic and copies ran while one was open for 0% of the time, Pallas kernels for 15%

profile of v10, /device:TPU:0, one launch (start us, length us, event | category | flops | bytes accessed | tf_op | source)
XLA Modules:
  0.0 168.3 jit_solution(11054357735851101546)
XLA Ops:
  0.0 4.9 %both_times.1 = f32[32,2,2,4,8,128]{5,4,3,2,1,0:T(8,128)} custom-call(f32[2,4,128,512]{3,2,1,0:T(8,128)} %g_hbm.2, f32[256,512]{1,0:T(8,128)} %constant.20.clone.m_hbm), custom_call_target="tpu_custom_call" | custom-call | tf_op jit(solution)/shard_map/both_times/pallas_call | solution.py:186
  4.9 7.4 %all-to-all-start = ((f32[32,128,128]{2,1,0:T(8,128)}), f32[32,128,128]{2,1,0:T(8,128)}, u32[]{:S(2)}, u32[]{:S(2)}) async-start(f32[32,128,128]{2,1,0:T(8,128)} %bitcast.14), calls=%async_computation | async-start | bytes 4194304 | tf_op jit(solution)/shard_map/all_to_all | solution.py:567
  12.3 6.7 %one_times.1 = f32[32,2,4,8,128]{4,3,2,1,0:T(8,128)} custom-call(f32[2,4,128,512]{3,2,1,0:T(8,128)} %g_hbm.2, f32[512,512]{1,0:T(8,128)} %constant.21.clone.m_hbm), custom_call_target="tpu_custom_call" | custom-call | tf_op jit(solution)/shard_map/one_times/pallas_call | solution.py:186
  19.1 42.2 %all-to-all-done = f32[32,128,128]{2,1,0:T(8,128)} async-done(((f32[32,128,128]{2,1,0:T(8,128)}), f32[32,128,128]{2,1,0:T(8,128)}, u32[]{:S(2)}, u32[]{:S(2)}) %all-to-all-start) | async-done | bytes 2097184 | tf_op jit(solution)/shard_map/all_to_all | solution.py:567
  61.3 4.2 %all-to-all-start.1 = ((f32[32,64,128]{2,1,0:T(8,128)}), f32[32,64,128]{2,1,0:T(8,128)S(1)}, u32[]{:S(2)}, u32[]{:S(2)}) async-start(f32[32,64,128]{2,1,0:T(8,128)} %bitcast.15), calls=%async_computation.1 | async-start | bytes 2097152 | tf_op jit(solution)/shard_map/all_to_all | solution.py:567
  65.5 8.9 %both_middle.1 = (f32[2,2,8,8,128]{4,3,2,1,0:T(8,128)}, f32[2,2,8,8,128]{4,3,2,1,0:T(8,128)}, f32[2,2,8,8,128]{4,3,2,1,0:T(8,128)}, f32[2,2,8,8,128]{4,3,2,1,0:T...) custom-call(s32[1]{0:T(128)} %bitcast.5.me_ref, ...), custom_call_target="tpu_custom_call" | custom-call | tf_op jit(solution)/shard_map/both_middle/pallas_call | solution.py:434
  74.4 1.6 collective-permute-start
  76.0 2.4 %collective-permute-start.2 = (f32[2,2,8,8,128]{4,3,2,1,0:T(8,128)}, f32[2,2,8,8,128]{4,3,2,1,0:T(8,128)S(1)}, u32[]{:S(2)}, u32[]{:S(2)}) collective-permute-start(f32[2,2,8,8,128]{4,3,2,1,0:T(8,128)} %get-tuple-element.51), channel_id=1, source_target_pairs={{0,10},{1,11},{2,8},{3,9},{4,14},{5,15},{6,12},{7,13},{8,2},{9,3},... | collective-permute-start | bytes 393224 | tf_op jit(solution)/shard_map/ppermute | solution.py:573
  78.8 0.6 collective-permute-start.4
  79.4 6.9 %collective-permute-done.refs_1_ = f32[2,2,8,8,128]{4,3,2,1,0:T(8,128)S(1)} collective-permute-done((f32[2,2,8,8,128]{4,3,2,1,0:T(8,128)}, f32[2,2,8,8,128]{4,3,2,1,0:T(8,128)S(1)}, u32[]{:S(2)}, u32[]{:S(2)}) %collective-permute-start) | collective-permute-done | bytes 131104 | tf_op jit(solution)/shard_map/ppermute | solution.py:573
  86.3 2.3 %collective-permute-start.5 = (f32[2,2,8,8,128]{4,3,2,1,0:T(8,128)}, f32[2,2,8,8,128]{4,3,2,1,0:T(8,128)S(1)}, u32[]{:S(2)}, u32[]{:S(2)}) collective-permute-start(f32[2,2,8,8,128]{4,3,2,1,0:T(8,128)} %get-tuple-element.55), channel_id=1, source_target_pairs={{0,11},{1,10},{2,9},{3,8},{4,15},{5,14},{6,13},{7,12},{8,3},{9,2},... | collective-permute-start | bytes 393224 | tf_op jit(solution)/shard_map/ppermute | solution.py:573
  88.6 0.5 collective-permute-done.1.refs_2_
  89.1 2.5 %collective-permute-start.6 = (f32[2,2,8,8,128]{4,3,2,1,0:T(8,128)}, f32[2,2,8,8,128]{4,3,2,1,0:T(8,128)S(1)}, u32[]{:S(2)}, u32[]{:S(2)}) collective-permute-start(f32[2,2,8,8,128]{4,3,2,1,0:T(8,128)} %get-tuple-element.56), channel_id=1, source_target_pairs={{0,12},{1,13},{2,14},{3,15},{4,8},{5,9},{6,10},{7,11},{8,4},{9,5},... | collective-permute-start | bytes 393224 | tf_op jit(solution)/shard_map/ppermute | solution.py:573
  91.6 3.2 %collective-permute-done.2.refs_3_ = f32[2,2,8,8,128]{4,3,2,1,0:T(8,128)S(1)} collective-permute-done((f32[2,2,8,8,128]{4,3,2,1,0:T(8,128)}, f32[2,2,8,8,128]{4,3,2,1,0:T(8,128)S(1)}, u32[]{:S(2)}, u32[]{:S(2)}) %collective-permute-start.2) | collective-permute-done | bytes 131104 | tf_op jit(solution)/shard_map/ppermute | solution.py:573
  95.1 1.5 collective-permute-start.8
  96.6 0.4 collective-permute-start.9
  97.0 6.6 %one_middle.1 = f32[16,2,2,8,8,128]{5,4,3,2,1,0:T(8,128)} custom-call(s32[2,8]{1,0:T(2,128)S(1)} %bitcast.13, s32[3,16]{1,0:T(4,128)S(1)} %copy-done.4, bf16[256,256]{1,0:T(8,128)(2,1)S(1)} %copy-done.3, bf16[256,256]{1,0:T(8,128)(2,1)S(1)} %copy-done.2, bf16[256,256]{1,0:T(8,128)(2,1)S(1)} %copy-done.1, bf16[256,256]{1,0:T(8,128)(2,1)S(1)} %copy-done, ...), custom_call_target="tpu_custom_call" | custom-call | flops 6000000000 | bytes 12000000 | tf_op jit(solution)/shard_map/one_middle/pallas_call | solution.py:407
  103.7 1.9 %collective-permute-done.9.refs_10_ = f32[2,2,8,8,128]{4,3,2,1,0:T(8,128)S(1)} collective-permute-done((f32[2,2,8,8,128]{4,3,2,1,0:T(8,128)}, f32[2,2,8,8,128]{4,3,2,1,0:T(8,128)S(1)}, u32[]{:S(2)}, u32[]{:S(2)}) %collective-permute-start.9) | collective-permute-done | bytes 131104 | tf_op jit(solution)/shard_map/ppermute | solution.py:573
  105.6 0.6 copy-done.15
  106.3 4.3 %all-to-all-start.2 = ((f32[32,128,128]{2,1,0:T(8,128)}), f32[32,128,128]{2,1,0:T(8,128)}, u32[]{:S(2)}, u32[]{:S(2)}) async-start(f32[32,128,128]{2,1,0:T(8,128)} %bitcast.9), calls=%async_computation.2 | async-start | bytes 4194304 | tf_op jit(solution)/shard_map/all_to_all | solution.py:567
  110.6 2.4 %prepare.1.m_hbm = bf16[2,512,512]{2,1,0:T(8,128)(2,1)} custom-call(s32[1]{0:T(128)} %bitcast.5.me_ref, f32[2,16,8,512]{3,2,1,0:T(8,128)} %constant.26.clone.both_ref, f32[256,512]{1,0:T(8,128)} %constant.27.clone.one_ref), custom_call_target="tpu_custom_call" | custom-call | tf_op jit(solution)/shard_map/prepare/pallas_call | solution.py:463
  113.0 1.2 collective-permute-start.10
  114.2 1.5 collective-permute-start.11
  115.7 1.1 collective-permute-start.12
  116.8 2.4 %collective-permute-start.13 = (f32[2,2,8,8,128]{4,3,2,1,0:T(8,128)S(1)}, f32[2,2,8,8,128]{4,3,2,1,0:T(8,128)S(1)}, u32[]{:S(2)}, u32[]{:S(2)}) collective-permute-start(f32[2,2,8,8,128]{4,3,2,1,0:T(8,128)S(1)} %copy-done.22), channel_id=1, source_target_pairs={{0,14},{1,15},{2,12},{3,13},{4,10},{5,11},{6,8},{7,9},{8,6},{9,7},... | collective-permute-start | bytes 393224 | tf_op jit(solution)/shard_map/ppermute | solution.py:573
  119.2 1.2 collective-permute-start.14
  120.4 13.6 %collective-permute-done.10.refs_11_ = f32[2,2,8,8,128]{4,3,2,1,0:T(8,128)S(1)} collective-permute-done((f32[2,2,8,8,128]{4,3,2,1,0:T(8,128)}, f32[2,2,8,8,128]{4,3,2,1,0:T(8,128)S(1)}, u32[]{:S(2)}, u32[]{:S(2)}) %collective-permute-start.10) | collective-permute-done | bytes 131104 | tf_op jit(solution)/shard_map/ppermute | solution.py:573
  134.0 10.1 %collective-permute-done.12.refs_13_ = f32[2,2,8,8,128]{4,3,2,1,0:T(8,128)S(1)} collective-permute-done((f32[2,2,8,8,128]{4,3,2,1,0:T(8,128)}, f32[2,2,8,8,128]{4,3,2,1,0:T(8,128)S(1)}, u32[]{:S(2)}, u32[]{:S(2)}) %collective-permute-start.12) | collective-permute-done | bytes 131104 | tf_op jit(solution)/shard_map/ppermute | solution.py:573
  144.1 4.8 %collective-permute-done.13.refs_14_ = f32[2,2,8,8,128]{4,3,2,1,0:T(8,128)S(1)} collective-permute-done((f32[2,2,8,8,128]{4,3,2,1,0:T(8,128)S(1)}, f32[2,2,8,8,128]{4,3,2,1,0:T(8,128)S(1)}, u32[]{:S(2)}, u32[]{:S(2)}) %collective-permute-start.13) | collective-permute-done | bytes 131104 | tf_op jit(solution)/shard_map/ppermute | solution.py:573
  148.9 3.2 %collective-permute-done.14.refs_15_ = f32[2,2,8,8,128]{4,3,2,1,0:T(8,128)S(1)} collective-permute-done((f32[2,2,8,8,128]{4,3,2,1,0:T(8,128)S(1)}, f32[2,2,8,8,128]{4,3,2,1,0:T(8,128)S(1)}, u32[]{:S(2)}, u32[]{:S(2)}) %collective-permute-start.14) | collective-permute-done | bytes 131104 | tf_op jit(solution)/shard_map/ppermute | solution.py:573
  152.1 7.7 %all-to-all-done.2 = f32[32,128,128]{2,1,0:T(8,128)} async-done(((f32[32,128,128]{2,1,0:T(8,128)}), f32[32,128,128]{2,1,0:T(8,128)}, u32[]{:S(2)}, u32[]{:S(2)}) %all-to-all-start.2) | async-done | bytes 2097184 | tf_op jit(solution)/shard_map/all_to_all | solution.py:567
  159.8 8.3 %to_frequencies.1 = f32[2,8,128,512]{3,2,1,0:T(8,128)} custom-call(f32[32,2,8,8,128]{4,3,2,1,0:T(8,128)} %bitcast.10.y_hbm, bf16[2,512,512]{2,1,0:T(8,128)(2,1)} %prepare.1.m_hbm, f32[2,2,8,8,128]{4,3,2,1,0:T(8,128)} %get-tuple-element.69.refs_0_, f32[2,2,8,8,128]{4,3,2,1,0:T(8,128)} %copy-done.6, f32[2,2,8,8,128]{4,3,2,1,0:T(8,128)} %copy-done.7, ...), custom_call_target="tpu_custom_call" | custom-call | tf_op jit(solution)/shard_map/to_frequencies/pallas_call | solution.py:545
  (56 shorter events, 0.8 us)
Async XLA Ops:
  4.9 56.3 %all-to-all-start = ((f32[32,128,128]{2,1,0:T(8,128)}), f32[32,128,128]{2,1,0:T(8,128)}, u32[]{:S(2)}, u32[]{:S(2)}) async-start(f32[32,128,128]{2,1,0:T(8,128)} %bitcast.14), calls=%async_computation | async-start | bytes 4194304 | tf_op jit(solution)/shard_map/all_to_all | solution.py:567
  61.2 35.7 %copy-start = (bf16[256,256]{1,0:T(8,128)(2,1)S(1)}, bf16[256,256]{1,0:T(8,128)(2,1)}, u32[]{:S(2)}) copy-start(bf16[256,256]{1,0:T(8,128)(2,1)} %constant.25.clone.sl_ref) | copy-start | bytes 393220
  61.2 35.7 %copy-start.1 = (bf16[256,256]{1,0:T(8,128)(2,1)S(1)}, bf16[256,256]{1,0:T(8,128)(2,1)}, u32[]{:S(2)}) copy-start(bf16[256,256]{1,0:T(8,128)(2,1)} %constant.24.clone.sh_ref) | copy-start | bytes 393220
  61.2 35.7 %copy-start.2 = (bf16[256,256]{1,0:T(8,128)(2,1)S(1)}, bf16[256,256]{1,0:T(8,128)(2,1)}, u32[]{:S(2)}) copy-start(bf16[256,256]{1,0:T(8,128)(2,1)} %constant.23.clone.cl_ref) | copy-start | bytes 393220
  61.2 35.7 %copy-start.3 = (bf16[256,256]{1,0:T(8,128)(2,1)S(1)}, bf16[256,256]{1,0:T(8,128)(2,1)}, u32[]{:S(2)}) copy-start(bf16[256,256]{1,0:T(8,128)(2,1)} %constant.22.clone.ch_ref) | copy-start | bytes 393220
  61.2 35.7 %copy-start.4 = (s32[3,16]{1,0:T(4,128)S(1)}, s32[3,16]{1,0:T(4,128)}, u32[]{:S(2)}) copy-start(s32[3,16]{1,0:T(4,128)} %mirror_ref.3) | copy-start | bytes 580
  61.2 35.7 %copy-start.5 = (s32[8,2]{0,1:T(2,128)S(1)}, s32[8,2]{0,1:T(2,128)}, u32[]{:S(2)}) copy-start(s32[8,2]{0,1:T(2,128)} %param.16) | copy-start | bytes 196
  61.3 35.7 %all-to-all-start.1 = ((f32[32,64,128]{2,1,0:T(8,128)}), f32[32,64,128]{2,1,0:T(8,128)S(1)}, u32[]{:S(2)}, u32[]{:S(2)}) async-start(f32[32,64,128]{2,1,0:T(8,128)} %bitcast.15), calls=%async_computation.1 | async-start | bytes 2097152 | tf_op jit(solution)/shard_map/all_to_all | solution.py:567
  74.4 11.8 %collective-permute-start = (f32[2,2,8,8,128]{4,3,2,1,0:T(8,128)}, f32[2,2,8,8,128]{4,3,2,1,0:T(8,128)S(1)}, u32[]{:S(2)}, u32[]{:S(2)}) collective-permute-start(f32[2,2,8,8,128]{4,3,2,1,0:T(8,128)} %get-tuple-element.49), channel_id=1, source_target_pairs={{0,8},{1,9},{2,10},{3,11},{4,12},{5,13},{6,14},{7,15},{8,0},{9,1},... | collective-permute-start | bytes 393224 | tf_op jit(solution)/shard_map/ppermute | solution.py:573
  76.0 13.0 %collective-permute-start.1 = (f32[2,2,8,8,128]{4,3,2,1,0:T(8,128)}, f32[2,2,8,8,128]{4,3,2,1,0:T(8,128)S(1)}, u32[]{:S(2)}, u32[]{:S(2)}) collective-permute-start(f32[2,2,8,8,128]{4,3,2,1,0:T(8,128)} %get-tuple-element.50), channel_id=1, source_target_pairs={{0,9},{1,8},{2,11},{3,10},{4,13},{5,12},{6,15},{7,14},{8,1},{9,0},... | collective-permute-start | bytes 393224 | tf_op jit(solution)/shard_map/ppermute | solution.py:573
  76.0 18.8 %collective-permute-start.2 = (f32[2,2,8,8,128]{4,3,2,1,0:T(8,128)}, f32[2,2,8,8,128]{4,3,2,1,0:T(8,128)S(1)}, u32[]{:S(2)}, u32[]{:S(2)}) collective-permute-start(f32[2,2,8,8,128]{4,3,2,1,0:T(8,128)} %get-tuple-element.51), channel_id=1, source_target_pairs={{0,10},{1,11},{2,8},{3,9},{4,14},{5,15},{6,12},{7,13},{8,2},{9,3},... | collective-permute-start | bytes 393224 | tf_op jit(solution)/shard_map/ppermute | solution.py:573
  78.4 16.6 %collective-permute-start.3 = (f32[2,2,8,8,128]{4,3,2,1,0:T(8,128)}, f32[2,2,8,8,128]{4,3,2,1,0:T(8,128)S(1)}, u32[]{:S(2)}, u32[]{:S(2)}) collective-permute-start(f32[2,2,8,8,128]{4,3,2,1,0:T(8,128)} %get-tuple-element.52), channel_id=1, source_target_pairs={{0,1},{1,0},{2,3},{3,2},{4,5},{5,4},{6,7},{7,6},{8,9},{9,8},{10,11... | collective-permute-start | bytes 393224 | tf_op jit(solution)/shard_map/ppermute | solution.py:573
  78.8 17.7 %collective-permute-start.4 = (f32[2,2,8,8,128]{4,3,2,1,0:T(8,128)}, f32[2,2,8,8,128]{4,3,2,1,0:T(8,128)S(1)}, u32[]{:S(2)}, u32[]{:S(2)}) collective-permute-start(f32[2,2,8,8,128]{4,3,2,1,0:T(8,128)} %get-tuple-element.53), channel_id=1, source_target_pairs={{0,2},{1,3},{2,0},{3,1},{4,6},{5,7},{6,4},{7,5},{8,10},{9,11},{10,... | collective-permute-start | bytes 393224 | tf_op jit(solution)/shard_map/ppermute | solution.py:573
  86.3 17.3 %copy-start.6 = (f32[2,2,8,8,128]{4,3,2,1,0:T(8,128)}, f32[2,2,8,8,128]{4,3,2,1,0:T(8,128)S(1)}, u32[]{:S(2)}) copy-start(f32[2,2,8,8,128]{4,3,2,1,0:T(8,128)S(1)} %collective-permute-done.refs_1_) | copy-start | bytes 393220
  86.3 17.4 %collective-permute-start.5 = (f32[2,2,8,8,128]{4,3,2,1,0:T(8,128)}, f32[2,2,8,8,128]{4,3,2,1,0:T(8,128)S(1)}, u32[]{:S(2)}, u32[]{:S(2)}) collective-permute-start(f32[2,2,8,8,128]{4,3,2,1,0:T(8,128)} %get-tuple-element.55), channel_id=1, source_target_pairs={{0,11},{1,10},{2,9},{3,8},{4,15},{5,14},{6,13},{7,12},{8,3},{9,2},... | collective-permute-start | bytes 393224 | tf_op jit(solution)/shard_map/ppermute | solution.py:573
  89.1 14.5 %copy-start.7 = (f32[2,2,8,8,128]{4,3,2,1,0:T(8,128)}, f32[2,2,8,8,128]{4,3,2,1,0:T(8,128)S(1)}, u32[]{:S(2)}) copy-start(f32[2,2,8,8,128]{4,3,2,1,0:T(8,128)S(1)} %collective-permute-done.1.refs_2_) | copy-start | bytes 393220
  89.1 14.6 %collective-permute-start.6 = (f32[2,2,8,8,128]{4,3,2,1,0:T(8,128)}, f32[2,2,8,8,128]{4,3,2,1,0:T(8,128)S(1)}, u32[]{:S(2)}, u32[]{:S(2)}) collective-permute-start(f32[2,2,8,8,128]{4,3,2,1,0:T(8,128)} %get-tuple-element.56), channel_id=1, source_target_pairs={{0,12},{1,13},{2,14},{3,15},{4,8},{5,9},{6,10},{7,11},{8,4},{9,5},... | collective-permute-start | bytes 393224 | tf_op jit(solution)/shard_map/ppermute | solution.py:573
  94.8 8.8 %copy-start.8 = (f32[2,2,8,8,128]{4,3,2,1,0:T(8,128)}, f32[2,2,8,8,128]{4,3,2,1,0:T(8,128)S(1)}, u32[]{:S(2)}) copy-start(f32[2,2,8,8,128]{4,3,2,1,0:T(8,128)S(1)} %collective-permute-done.2.refs_3_) | copy-start | bytes 393220
  94.8 8.9 %collective-permute-start.7 = (f32[2,2,8,8,128]{4,3,2,1,0:T(8,128)}, f32[2,2,8,8,128]{4,3,2,1,0:T(8,128)S(1)}, u32[]{:S(2)}, u32[]{:S(2)}) collective-permute-start(f32[2,2,8,8,128]{4,3,2,1,0:T(8,128)} %get-tuple-element.57), channel_id=1, source_target_pairs={{0,13},{1,12},{2,15},{3,14},{4,9},{5,8},{6,11},{7,10},{8,5},{9,4},... | collective-permute-start | bytes 393224 | tf_op jit(solution)/shard_map/ppermute | solution.py:573
  95.1 8.6 %collective-permute-start.8 = (f32[2,2,8,8,128]{4,3,2,1,0:T(8,128)}, f32[2,2,8,8,128]{4,3,2,1,0:T(8,128)S(1)}, u32[]{:S(2)}, u32[]{:S(2)}) collective-permute-start(f32[2,2,8,8,128]{4,3,2,1,0:T(8,128)} %get-tuple-element.58), channel_id=1, source_target_pairs={{0,3},{1,2},{2,1},{3,0},{4,7},{5,6},{6,5},{7,4},{8,11},{9,10},{10,... | collective-permute-start | bytes 393224 | tf_op jit(solution)/shard_map/ppermute | solution.py:573
  96.6 9.1 %collective-permute-start.9 = (f32[2,2,8,8,128]{4,3,2,1,0:T(8,128)}, f32[2,2,8,8,128]{4,3,2,1,0:T(8,128)S(1)}, u32[]{:S(2)}, u32[]{:S(2)}) collective-permute-start(f32[2,2,8,8,128]{4,3,2,1,0:T(8,128)} %get-tuple-element.59), channel_id=1, source_target_pairs={{0,4},{1,5},{2,6},{3,7},{4,0},{5,1},{6,2},{7,3},{8,12},{9,13},{10,... | collective-permute-start | bytes 393224 | tf_op jit(solution)/shard_map/ppermute | solution.py:573
  106.3 53.5 %all-to-all-start.2 = ((f32[32,128,128]{2,1,0:T(8,128)}), f32[32,128,128]{2,1,0:T(8,128)}, u32[]{:S(2)}, u32[]{:S(2)}) async-start(f32[32,128,128]{2,1,0:T(8,128)} %bitcast.9), calls=%async_computation.2 | async-start | bytes 4194304 | tf_op jit(solution)/shard_map/all_to_all | solution.py:567
  110.6 8.6 %copy-start.21 = (f32[2,2,8,8,128]{4,3,2,1,0:T(8,128)S(1)}, f32[2,2,8,8,128]{4,3,2,1,0:T(8,128)}, u32[]{:S(2)}) copy-start(f32[2,2,8,8,128]{4,3,2,1,0:T(8,128)} %get-tuple-element.84) | copy-start | bytes 393220
  113.0 21.1 %collective-permute-start.10 = (f32[2,2,8,8,128]{4,3,2,1,0:T(8,128)}, f32[2,2,8,8,128]{4,3,2,1,0:T(8,128)S(1)}, u32[]{:S(2)}, u32[]{:S(2)}) collective-permute-start(f32[2,2,8,8,128]{4,3,2,1,0:T(8,128)} %get-tuple-element.80), channel_id=1, source_target_pairs={{0,5},{1,4},{2,7},{3,6},{4,1},{5,0},{6,3},{7,2},{8,13},{9,12},{10,... | collective-permute-start | bytes 393224 | tf_op jit(solution)/shard_map/ppermute | solution.py:573
  114.2 19.8 %collective-permute-start.11 = (f32[2,2,8,8,128]{4,3,2,1,0:T(8,128)}, f32[2,2,8,8,128]{4,3,2,1,0:T(8,128)S(1)}, u32[]{:S(2)}, u32[]{:S(2)}) collective-permute-start(f32[2,2,8,8,128]{4,3,2,1,0:T(8,128)} %get-tuple-element.81), channel_id=1, source_target_pairs={{0,6},{1,7},{2,4},{3,5},{4,2},{5,3},{6,0},{7,1},{8,14},{9,15},{10,... | collective-permute-start | bytes 393224 | tf_op jit(solution)/shard_map/ppermute | solution.py:573
  115.7 28.4 %collective-permute-start.12 = (f32[2,2,8,8,128]{4,3,2,1,0:T(8,128)}, f32[2,2,8,8,128]{4,3,2,1,0:T(8,128)S(1)}, u32[]{:S(2)}, u32[]{:S(2)}) collective-permute-start(f32[2,2,8,8,128]{4,3,2,1,0:T(8,128)} %get-tuple-element.82), channel_id=1, source_target_pairs={{0,7},{1,6},{2,5},{3,4},{4,3},{5,2},{6,1},{7,0},{8,15},{9,14},{10,... | collective-permute-start | bytes 393224 | tf_op jit(solution)/shard_map/ppermute | solution.py:573
  116.8 32.0 %collective-permute-start.13 = (f32[2,2,8,8,128]{4,3,2,1,0:T(8,128)S(1)}, f32[2,2,8,8,128]{4,3,2,1,0:T(8,128)S(1)}, u32[]{:S(2)}, u32[]{:S(2)}) collective-permute-start(f32[2,2,8,8,128]{4,3,2,1,0:T(8,128)S(1)} %copy-done.22), channel_id=1, source_target_pairs={{0,14},{1,15},{2,12},{3,13},{4,10},{5,11},{6,8},{7,9},{8,6},{9,7},... | collective-permute-start | bytes 393224 | tf_op jit(solution)/shard_map/ppermute | solution.py:573
  119.2 32.9 %collective-permute-start.14 = (f32[2,2,8,8,128]{4,3,2,1,0:T(8,128)S(1)}, f32[2,2,8,8,128]{4,3,2,1,0:T(8,128)S(1)}, u32[]{:S(2)}, u32[]{:S(2)}) collective-permute-start(f32[2,2,8,8,128]{4,3,2,1,0:T(8,128)S(1)} %copy-done.21), channel_id=1, source_target_pairs={{0,15},{1,14},{2,13},{3,12},{4,11},{5,10},{6,9},{7,8},{8,7},{9,6},... | collective-permute-start | bytes 393224 | tf_op jit(solution)/shard_map/ppermute | solution.py:573
  134.0 25.7 %copy-start.16 = (f32[2,2,8,8,128]{4,3,2,1,0:T(8,128)}, f32[2,2,8,8,128]{4,3,2,1,0:T(8,128)S(1)}, u32[]{:S(2)}) copy-start(f32[2,2,8,8,128]{4,3,2,1,0:T(8,128)S(1)} %collective-permute-done.10.refs_11_) | copy-start | bytes 393220
  134.0 25.7 %copy-start.17 = (f32[2,2,8,8,128]{4,3,2,1,0:T(8,128)}, f32[2,2,8,8,128]{4,3,2,1,0:T(8,128)S(1)}, u32[]{:S(2)}) copy-start(f32[2,2,8,8,128]{4,3,2,1,0:T(8,128)S(1)} %collective-permute-done.11.refs_12_) | copy-start | bytes 393220
  144.1 15.6 %copy-start.18 = (f32[2,2,8,8,128]{4,3,2,1,0:T(8,128)}, f32[2,2,8,8,128]{4,3,2,1,0:T(8,128)S(1)}, u32[]{:S(2)}) copy-start(f32[2,2,8,8,128]{4,3,2,1,0:T(8,128)S(1)} %collective-permute-done.12.refs_13_) | copy-start | bytes 393220
  148.9 10.9 %copy-start.19 = (f32[2,2,8,8,128]{4,3,2,1,0:T(8,128)}, f32[2,2,8,8,128]{4,3,2,1,0:T(8,128)S(1)}, u32[]{:S(2)}) copy-start(f32[2,2,8,8,128]{4,3,2,1,0:T(8,128)S(1)} %collective-permute-done.13.refs_14_) | copy-start | bytes 393220
  (9 other events, 38.0 us)

commit v11 on v9

--- a/solution.py
+++ b/solution.py
@@ -465,44 +465,67 @@
         in_specs=[smem, vmem, vmem],
         out_specs=vmem,
         out_shape=jax.ShapeDtypeStruct((2, depth, one.shape[1]), jnp.bfloat16),
-        compiler_params=pltpu.CompilerParams(vmem_limit_bytes=63 << 20),
+        compiler_params=pltpu.CompilerParams(vmem_limit_bytes=32 << 20),
         name="prepare",
     )(me, both, one)
 
 
-def frequency_kernel(order, y_hbm, m_hbm, *refs):
-    pieces, (out_ref, y_ref, m_ref, held, stage, y_sems, m_sems, in_sems, sems) = refs[:-9], refs[-9:]
-    near = len(pieces)
+def fold_kernel(order, *refs):
+    pieces, (out_ref, held, stage, in_sems, sems) = refs[:-5], refs[-5:]
+    near, _, _, components, rows, lanes = held.shape
+    loads = [pltpu.make_async_copy(piece, held.at[slot], in_sems.at[slot]) for slot, piece in zip(order, pieces)]
+    for copy in loads:
+        copy.start()
+    for copy in loads:
+        copy.wait()
+    copies = []
+    for c in range(components):
+        part = [[held[:, half, ri, c].reshape(near * rows, lanes) for ri in range(2)] for half in range(2)]
+        sums = [part[0][ri] + part[1][ri] for ri in range(2)]
+        differences = [part[0][ri] - part[1][ri] for ri in range(2)]
+        first = jnp.concatenate([sums[0], -differences[1]], axis=0).T
+        second = jnp.concatenate([sums[1], differences[0]], axis=0).T
+        for place, value in enumerate(split_value(jnp.concatenate([first, second], axis=0))):
+            stage[c, place] = value
+        copies.append(pltpu.make_async_copy(stage.at[c], out_ref.at[c], sems.at[c]))
+        copies[-1].start()
+    for copy in copies:
+        copy.wait()
+
+
+def fold(pieces, order):
+    _, _, components, rows, lanes = pieces[0].shape
+    shape = (components, 2, 2 * lanes, 2 * len(pieces) * rows)
+    hbm = pl.BlockSpec(memory_space=pltpu.HBM)
+    return pl.pallas_call(
+        functools.partial(fold_kernel, order),
+        in_specs=[hbm] * len(pieces),
+        out_specs=hbm,
+        out_shape=jax.ShapeDtypeStruct(shape, jnp.bfloat16),
+        scratch_shapes=[
+            pltpu.VMEM((len(pieces),) + pieces[0].shape, jnp.float32),
+            pltpu.VMEM(shape, jnp.bfloat16),
+            pltpu.SemaphoreType.DMA((len(pieces),)),
+            pltpu.SemaphoreType.DMA((components,)),
+        ],
+        compiler_params=pltpu.CompilerParams(vmem_limit_bytes=32 << 20),
+        name="fold",
+    )(*pieces)
+
+
+def frequency_kernel(y_ref, m_hbm, f_hbm, out_ref, m_ref, f_ref, stage, m_sem, f_sems, sems):
     devices, _, components, rows, lanes = y_ref.shape
     groups = sems.shape[0]
     members = components // groups
     depth = devices * rows
-    cuts = [pl.ds(group * members, members) for group in range(groups)]
-    matrices = [
-        pltpu.make_async_copy(m_hbm.at[:, pl.ds(start, depth)], m_ref.at[:, pl.ds(start, depth)], m_sems.at[part])
-        for part, start in enumerate((0, depth))
-    ]
-    blocks = [
-        pltpu.make_async_copy(y_hbm.at[:, :, cut], y_ref.at[:, :, cut], y_sems.at[group])
-        for group, cut in enumerate(cuts)
-    ]
-    spans = [pl.ds(part * components // 2, components // 2) for part in range(2)]
-    loads = [
-        [
-            pltpu.make_async_copy(piece.at[:, :, span], held.at[slot, :, :, span], in_sems.at[part, slot])
-            for slot, piece in zip(order, pieces)
-        ]
-        for part, span in enumerate(spans)
-    ]
-    for copy in [matrices[0], blocks[0], matrices[1]] + loads[0] + blocks[1:] + loads[1]:
+    load = pltpu.make_async_copy(m_hbm, m_ref, m_sem)
+    spans = [pl.ds(group * members, members) for group in range(groups)]
+    loads = [pltpu.make_async_copy(f_hbm.at[span], f_ref.at[span], f_sems.at[k]) for k, span in enumerate(spans)]
+    for copy in [load] + loads:
         copy.start()
     upper_rows = lax.broadcasted_iota(jnp.int32, (devices, rows, lanes), 1) < rows // 2
 
-    def part_of(values, start):
-        matrix = [m_ref[part, start : start + depth] for part in range(2)]
-        return dot3(split_value(jnp.concatenate(values, axis=0)), matrix, ((1,), (0,)))
-
-    def one_part(group):
+    def one_values(group):
         values = []
         for c in range(group * members, (group + 1) * members):
             folded = []
@@ -512,62 +535,52 @@
                 folded.append((tile + turned, turned - tile))
             first = jnp.where(upper_rows, folded[0][0], -folded[1][1])
             second = jnp.where(upper_rows, folded[1][0], folded[0][1])
-            values.append(first.reshape(devices * rows, lanes).T)
-            values.append(second.reshape(devices * rows, lanes).T)
-        return part_of(values, 0)
-
-    def both_part(group):
-        values = []
-        for c in range(group * members, (group + 1) * members):
-            part = [[held[:, half, ri, c].reshape(near * rows, lanes) for ri in range(2)] for half in range(2)]
-            sums = [part[0][ri] + part[1][ri] for ri in range(2)]
-            differences = [part[0][ri] - part[1][ri] for ri in range(2)]
-            values.append(jnp.concatenate([sums[0], -differences[1]], axis=0).T)
-            values.append(jnp.concatenate([sums[1], differences[0]], axis=0).T)
-        return part_of(values, depth)
+            values.append(first.reshape(depth, lanes).T)
+            values.append(second.reshape(depth, lanes).T)
+        return split_value(jnp.concatenate(values, axis=0))
 
     copies = []
-    matrices[0].wait()
-    for group in range(groups):
-        blocks[group].wait()
-        d = one_part(group)
+    for group, span in enumerate(spans):
+        parts = one_values(group)
         if group == 0:
-            matrices[1].wait()
-        if group % (groups // 2) == 0:
-            for copy in loads[group // (groups // 2)]:
-                copy.wait()
-        d = (d + both_part(group)).reshape(members, 2, lanes, d.shape[1])
+            load.wait()
+            matrix = (m_ref[0], m_ref[1])
+        loads[group].wait()
+        own = range(group * members, (group + 1) * members)
+        value = [
+            jnp.concatenate([parts[place], jnp.concatenate([f_ref[c, place] for c in own], axis=0)], axis=1)
+            for place in range(2)
+        ]
+        d = dot3(value, matrix, ((1,), (0,))).reshape(members, 2, lanes, stage.shape[3])
         for ri in range(2):
             stage[ri, group * members : (group + 1) * members] = d[:, ri]
-        copies.append(pltpu.make_async_copy(stage.at[:, cuts[group]], out_ref.at[:, cuts[group]], sems.at[group]))
+        copies.append(pltpu.make_async_copy(stage.at[:, span], out_ref.at[:, span], sems.at[group]))
         copies[-1].start()
     for copy in copies:
         copy.wait()
 
 
-def to_frequencies(y, pieces, order, matrix):
+def to_frequencies(y, matrix, folded):
     _, _, components, _, lanes = y.shape
     shape = (2, components, lanes, matrix.shape[2])
     hbm = pl.BlockSpec(memory_space=pltpu.HBM)
     groups = components // 2
     return pl.pallas_call(
-        functools.partial(frequency_kernel, order),
-        in_specs=[hbm] * (2 + len(pieces)),
+        frequency_kernel,
+        in_specs=[pl.BlockSpec(memory_space=pltpu.VMEM), hbm, hbm],
         out_specs=hbm,
         out_shape=jax.ShapeDtypeStruct(shape, jnp.float32),
         scratch_shapes=[
-            pltpu.VMEM(y.shape, jnp.float32),
             pltpu.VMEM(matrix.shape, jnp.bfloat16),
-            pltpu.VMEM((len(pieces),) + pieces[0].shape, jnp.float32),
+            pltpu.VMEM(folded.shape, jnp.bfloat16),
             pltpu.VMEM(shape, jnp.float32),
+            pltpu.SemaphoreType.DMA,
             pltpu.SemaphoreType.DMA((groups,)),
-            pltpu.SemaphoreType.DMA((2,)),
-            pltpu.SemaphoreType.DMA((2, len(pieces))),
             pltpu.SemaphoreType.DMA((groups,)),
         ],
-        compiler_params=pltpu.CompilerParams(vmem_limit_bytes=63 << 20),
+        compiler_params=pltpu.CompilerParams(vmem_limit_bytes=44 << 20),
         name="to_frequencies",
-    )(y, matrix, *pieces)
+    )(y, matrix, folded)
 
 
 def exchange(x):
@@ -725,9 +738,9 @@
     one = to_times(one_times_kernel, green, jnp.asarray(one_fermion), shape, devices, "one_times")
     both, one = lax.optimization_barrier((exchange(both), one))
     pieces = both_middle(both, pair_table, mirror_map, me, near)
-    first = near // 2
-    early = list(range(first, first + near // 4)) + [1]
-    beside = [first + near // 4, first + near // 4 + 1, 2, 3]
+    first, count = near // 2, near // 4
+    early = list(range(first, first + count)) + [1]
+    beside = [first + count, first + count + 1, 2, 3]
     late = [slot for slot in range(1, near) if slot not in early + beside]
     moved = {0: pieces[0]}
 
@@ -741,7 +754,7 @@
     matrix, sent = lax.optimization_barrier((prepare(me, both_boson, one_boson), [pieces[slot] for slot in late]))
     moved |= zip(late, [swap(piece, slot, devices) for slot, piece in zip(late, sent)])
     order = [0] + early + beside + late
-    return to_frequencies(exchange(one), [moved[slot] for slot in order], order, matrix)
+    return to_frequencies(exchange(one), matrix, fold([moved[slot] for slot in order], order))
 
 
 def solution(mesh):

time: 169 us -> 170 us (level)
  local copies, waits for them, and re-layouts: 0.86 us -> 9.04 us
  waiting for transfers between devices: 92.3 us -> 85.9 us
    unnamed x46 -> x60, local copies, waits for them, and re-layouts: 0.86 us -> 9.04 us
    all_to_all x3, waiting for transfers between devices: 48.2 us -> 42.3 us  [exchange(): lax.all_to_all(flat, 'kb', split_axis=0, concat_axis=0, tiled=True)]
    pallas_call x1, Pallas kernels: 2.37 us -> 0.14 us  [prepare(): pl.pallas_call(prepare_kernel, in_specs=[smem, vmem, vmem], out_specs=vme...]
    pallas_call x1 -> x2, Pallas kernels: 8.47 us -> 9.9 us  [the longest x1 5.48 us: to_frequencies(): pl.pallas_call(frequency_kernel, in_specs=[pl.BlockSpec(memory_space=pltp...]
  transfers between devices with their start and end apart: 18 -> 18, of which waited for: 9 -> 9; matrix products, arithmetic and copies ran while one was open for 0% -> 0% of each run, Pallas kernels for 15% -> 16%
where the time goes in v11:
time: 170 us; the launch traced here: 169 us
  waiting for transfers between devices  85.9 us (51%)
  Pallas kernels  36.7 us (22%)
  starting transfers between devices  36.6 us (22%)
  local copies, waits for them, and re-layouts  9.04 us (5%)
    ppermute x15, waiting for transfers between devices, swap(): lax.ppermute(piece, 'kb', [(device, device ^ slot) for device in range(de...  43.6 us
    all_to_all x3, waiting for transfers between devices, exchange(): lax.all_to_all(flat, 'kb', split_axis=0, concat_axis=0, tiled=True)  42.3 us
    ppermute x15, starting transfers between devices, swap(): lax.ppermute(piece, 'kb', [(device, device ^ slot) for device in range(de...  19.7 us
    all_to_all x3, starting transfers between devices, exchange(): lax.all_to_all(flat, 'kb', split_axis=0, concat_axis=0, tiled=True)  16.9 us
    pallas_call x2, Pallas kernels, to_times(): pl.pallas_call(kernel, in_specs=[hbm, hbm], out_specs=hbm, out_shape=jax....  11.6 us
    unnamed x60, local copies, waits for them, and re-layouts  9.04 us
    pallas_call x1, Pallas kernels, both_middle(): pl.pallas_call(both_middle_kernel, in_specs=[pl.BlockSpec(memory_space=pl...  8.96 us
    pallas_call x1, Pallas kernels, one_middle(): pl.pallas_call(one_middle_kernel, in_specs=specs, out_specs=pl.BlockSpec(...  6.11 us
  transfers between devices with their start and end apart: 18, of which 9 were waited for; matrix products, arithmetic and copies ran while one was open for 0% of the time, Pallas kernels for 16%

profile of v11, /device:TPU:0, one launch (start us, length us, event | category | flops | bytes accessed | tf_op | source)
XLA Modules:
  0.0 168.7 jit_solution(16477886193224045176)
XLA Ops:
  0.0 4.9 %both_times.1 = f32[32,2,2,4,8,128]{5,4,3,2,1,0:T(8,128)} custom-call(f32[2,4,128,512]{3,2,1,0:T(8,128)} %g_hbm.2, f32[256,512]{1,0:T(8,128)} %constant.20.clone.m_hbm), custom_call_target="tpu_custom_call" | custom-call | tf_op jit(solution)/shard_map/both_times/pallas_call | solution.py:186
  4.9 7.4 %all-to-all-start = ((f32[32,128,128]{2,1,0:T(8,128)}), f32[32,128,128]{2,1,0:T(8,128)}, u32[]{:S(2)}, u32[]{:S(2)}) async-start(f32[32,128,128]{2,1,0:T(8,128)} %bitcast.16), calls=%async_computation | async-start | bytes 4194304 | tf_op jit(solution)/shard_map/all_to_all | solution.py:588
  12.3 6.7 %one_times.1 = f32[32,2,4,8,128]{4,3,2,1,0:T(8,128)} custom-call(f32[2,4,128,512]{3,2,1,0:T(8,128)} %g_hbm.2, f32[512,512]{1,0:T(8,128)} %constant.21.clone.m_hbm), custom_call_target="tpu_custom_call" | custom-call | tf_op jit(solution)/shard_map/one_times/pallas_call | solution.py:186
  19.1 42.2 %all-to-all-done = f32[32,128,128]{2,1,0:T(8,128)} async-done(((f32[32,128,128]{2,1,0:T(8,128)}), f32[32,128,128]{2,1,0:T(8,128)}, u32[]{:S(2)}, u32[]{:S(2)}) %all-to-all-start) | async-done | bytes 2097184 | tf_op jit(solution)/shard_map/all_to_all | solution.py:588
  61.3 4.2 %all-to-all-start.1 = ((f32[32,64,128]{2,1,0:T(8,128)}), f32[32,64,128]{2,1,0:T(8,128)S(1)}, u32[]{:S(2)}, u32[]{:S(2)}) async-start(f32[32,64,128]{2,1,0:T(8,128)} %bitcast.17), calls=%async_computation.1 | async-start | bytes 2097152 | tf_op jit(solution)/shard_map/all_to_all | solution.py:588
  65.5 9.0 %both_middle.1 = (f32[2,2,8,8,128]{4,3,2,1,0:T(8,128)}, f32[2,2,8,8,128]{4,3,2,1,0:T(8,128)}, f32[2,2,8,8,128]{4,3,2,1,0:T(8,128)}, f32[2,2,8,8,128]{4,3,2,1,0:T...) custom-call(s32[1]{0:T(128)} %bitcast.5.me_ref, ...), custom_call_target="tpu_custom_call" | custom-call | tf_op jit(solution)/shard_map/both_middle/pallas_call | solution.py:434
  74.4 1.6 collective-permute-start
  76.1 2.4 %collective-permute-start.2 = (f32[2,2,8,8,128]{4,3,2,1,0:T(8,128)}, f32[2,2,8,8,128]{4,3,2,1,0:T(8,128)S(1)}, u32[]{:S(2)}, u32[]{:S(2)}) collective-permute-start(f32[2,2,8,8,128]{4,3,2,1,0:T(8,128)} %get-tuple-element.51), channel_id=1, source_target_pairs={{0,10},{1,11},{2,8},{3,9},{4,14},{5,15},{6,12},{7,13},{8,2},{9,3},... | collective-permute-start | bytes 393224 | tf_op jit(solution)/shard_map/ppermute | solution.py:594
  79.1 7.2 %collective-permute-done.refs_1_ = f32[2,2,8,8,128]{4,3,2,1,0:T(8,128)S(1)} collective-permute-done((f32[2,2,8,8,128]{4,3,2,1,0:T(8,128)}, f32[2,2,8,8,128]{4,3,2,1,0:T(8,128)S(1)}, u32[]{:S(2)}, u32[]{:S(2)}) %collective-permute-start) | collective-permute-done | bytes 131104 | tf_op jit(solution)/shard_map/ppermute | solution.py:594
  86.3 3.5 %collective-permute-start.5 = (f32[2,2,8,8,128]{4,3,2,1,0:T(8,128)}, f32[2,2,8,8,128]{4,3,2,1,0:T(8,128)S(1)}, u32[]{:S(2)}, u32[]{:S(2)}) collective-permute-start(f32[2,2,8,8,128]{4,3,2,1,0:T(8,128)} %get-tuple-element.55), channel_id=1, source_target_pairs={{0,12},{1,13},{2,14},{3,15},{4,8},{5,9},{6,10},{7,11},{8,4},{9,5},... | collective-permute-start | bytes 393224 | tf_op jit(solution)/shard_map/ppermute | solution.py:594
  89.7 2.5 %collective-permute-start.6 = (f32[2,2,8,8,128]{4,3,2,1,0:T(8,128)}, f32[2,2,8,8,128]{4,3,2,1,0:T(8,128)S(1)}, u32[]{:S(2)}, u32[]{:S(2)}) collective-permute-start(f32[2,2,8,8,128]{4,3,2,1,0:T(8,128)} %get-tuple-element.56), channel_id=1, source_target_pairs={{0,13},{1,12},{2,15},{3,14},{4,9},{5,8},{6,11},{7,10},{8,5},{9,4},... | collective-permute-start | bytes 393224 | tf_op jit(solution)/shard_map/ppermute | solution.py:594
  92.3 2.5 %collective-permute-done.2.refs_3_ = f32[2,2,8,8,128]{4,3,2,1,0:T(8,128)S(1)} collective-permute-done((f32[2,2,8,8,128]{4,3,2,1,0:T(8,128)}, f32[2,2,8,8,128]{4,3,2,1,0:T(8,128)S(1)}, u32[]{:S(2)}, u32[]{:S(2)}) %collective-permute-start.2) | collective-permute-done | bytes 131104 | tf_op jit(solution)/shard_map/ppermute | solution.py:594
  95.2 1.4 collective-permute-done.3.refs_4_
  96.7 0.8 collective-permute-start.8
  97.5 6.1 %one_middle.1 = f32[16,2,2,8,8,128]{5,4,3,2,1,0:T(8,128)S(1)} custom-call(s32[2,8]{1,0:T(2,128)S(1)} %bitcast.15, s32[3,16]{1,0:T(4,128)S(1)} %copy-done.22, bf16[256,256]{1,0:T(8,128)(2,1)S(1)} %copy-done.17, bf16[256,256]{1,0:T(8,128)(2,1)S(1)} %copy-done.16, bf16[256,256]{1,0:T(8,128)(2,1)S(1)} %copy-done.15, bf16[256,256]{1,0:T(8,128)(2,1)S(1)} %copy-done.14, ...), custom_call_target="tpu_custom_call" | custom-call | flops 6000000000 | bytes 12000000 | tf_op jit(solution)/shard_map/one_middle/pallas_call | solution.py:407
  103.7 1.3 copy-done.2
  105.0 0.6 copy-done.10
  107.0 5.3 %all-to-all-start.2 = ((f32[32,128,128]{2,1,0:T(8,128)}), f32[32,128,128]{2,1,0:T(8,128)S(1)}, u32[]{:S(2)}, u32[]{:S(2)}) async-start(f32[32,128,128]{2,1,0:T(8,128)} %bitcast.12), calls=%async_computation.2 | async-start | bytes 4194304 | tf_op jit(solution)/shard_map/all_to_all | solution.py:588
  112.3 1.0 copy-done.3
  113.3 1.0 copy-done.4
  114.6 0.7 copy-done.29
  115.3 1.6 collective-permute-start.9
  116.8 2.4 %collective-permute-start.11 = (f32[2,2,8,8,128]{4,3,2,1,0:T(8,128)S(1)}, f32[2,2,8,8,128]{4,3,2,1,0:T(8,128)S(1)}, u32[]{:S(2)}, u32[]{:S(2)}) collective-permute-start(f32[2,2,8,8,128]{4,3,2,1,0:T(8,128)S(1)} %copy-done.27), channel_id=1, source_target_pairs={{0,6},{1,7},{2,4},{3,5},{4,2},{5,3},{6,0},{7,1},{8,14},{9,15},{10,... | collective-permute-start | bytes 393224 | tf_op jit(solution)/shard_map/ppermute | solution.py:594
  119.7 3.4 %collective-permute-start.13 = (f32[2,2,8,8,128]{4,3,2,1,0:T(8,128)S(1)}, f32[2,2,8,8,128]{4,3,2,1,0:T(8,128)S(1)}, u32[]{:S(2)}, u32[]{:S(2)}) collective-permute-start(f32[2,2,8,8,128]{4,3,2,1,0:T(8,128)S(1)} %copy-done.25), channel_id=1, source_target_pairs={{0,14},{1,15},{2,12},{3,13},{4,10},{5,11},{6,8},{7,9},{8,6},{9,7},... | collective-permute-start | bytes 393224 | tf_op jit(solution)/shard_map/ppermute | solution.py:594
  123.0 24.0 %collective-permute-done.9.refs_10_ = f32[2,2,8,8,128]{4,3,2,1,0:T(8,128)S(1)} collective-permute-done((f32[2,2,8,8,128]{4,3,2,1,0:T(8,128)S(1)}, f32[2,2,8,8,128]{4,3,2,1,0:T(8,128)S(1)}, u32[]{:S(2)}, u32[]{:S(2)}) %collective-permute-start.9) | collective-permute-done | bytes 131104 | tf_op jit(solution)/shard_map/ppermute | solution.py:594
  147.0 2.2 %collective-permute-done.10.refs_11_ = f32[2,2,8,8,128]{4,3,2,1,0:T(8,128)S(1)} collective-permute-done((f32[2,2,8,8,128]{4,3,2,1,0:T(8,128)S(1)}, f32[2,2,8,8,128]{4,3,2,1,0:T(8,128)S(1)}, u32[]{:S(2)}, u32[]{:S(2)}) %collective-permute-start.10) | collective-permute-done | bytes 131104 | tf_op jit(solution)/shard_map/ppermute | solution.py:594
  149.2 1.5 collective-permute-done.13.refs_14_
  150.7 4.8 %collective-permute-done.14.refs_15_ = f32[2,2,8,8,128]{4,3,2,1,0:T(8,128)S(1)} collective-permute-done((f32[2,2,8,8,128]{4,3,2,1,0:T(8,128)S(1)}, f32[2,2,8,8,128]{4,3,2,1,0:T(8,128)S(1)}, u32[]{:S(2)}, u32[]{:S(2)}) %collective-permute-start.14) | collective-permute-done | bytes 131104 | tf_op jit(solution)/shard_map/ppermute | solution.py:594
  155.5 4.4 %fold.1.f_hbm = bf16[8,2,256,256]{3,2,1,0:T(8,128)(2,1)S(1)} custom-call(f32[2,2,8,8,128]{4,3,2,1,0:T(8,128)S(1)} %copy-done.5, f32[2,2,8,8,128]{4,3,2,1,0:T(8,128)S(1)} %collective-permute-done.refs_1_, f32[2,2,8,8,128]{4,3,2,1,0:T(8,128)S(1)} %collective-permute-done.1.refs_2_, f32[2,2,8,8,128]{4,3,2,1,0:T(8,128)S(1)} %collective-permute-done.2.refs_3_, ...), custom_call_target="tpu_custom_call" | custom-call | tf_op jit(solution)/shard_map/fold/pallas_call | solution.py:500
  160.0 1.3 copy-done
  161.5 1.6 copy-done.1
  163.0 5.5 %to_frequencies.1 = f32[2,8,128,512]{3,2,1,0:T(8,128)} custom-call(f32[32,2,8,8,128]{4,3,2,1,0:T(8,128)S(1)} %bitcast.11, bf16[2,512,512]{2,1,0:T(8,128)(2,1)S(1)} %prepare.1.m_hbm, bf16[8,2,256,256]{3,2,1,0:T(8,128)(2,1)S(1)} %copy-done.1), custom_call_target="tpu_custom_call" | custom-call | tf_op jit(solution)/shard_map/to_frequencies/pallas_call | solution.py:568
  (71 shorter events, 3.3 us)
Async XLA Ops:
  4.9 56.3 %all-to-all-start = ((f32[32,128,128]{2,1,0:T(8,128)}), f32[32,128,128]{2,1,0:T(8,128)}, u32[]{:S(2)}, u32[]{:S(2)}) async-start(f32[32,128,128]{2,1,0:T(8,128)} %bitcast.16), calls=%async_computation | async-start | bytes 4194304 | tf_op jit(solution)/shard_map/all_to_all | solution.py:588
  61.2 36.2 %copy-start.14 = (bf16[256,256]{1,0:T(8,128)(2,1)S(1)}, bf16[256,256]{1,0:T(8,128)(2,1)}, u32[]{:S(2)}) copy-start(bf16[256,256]{1,0:T(8,128)(2,1)} %constant.25.clone.sl_ref) | copy-start | bytes 393220
  61.2 36.3 %copy-start.15 = (bf16[256,256]{1,0:T(8,128)(2,1)S(1)}, bf16[256,256]{1,0:T(8,128)(2,1)}, u32[]{:S(2)}) copy-start(bf16[256,256]{1,0:T(8,128)(2,1)} %constant.24.clone.sh_ref) | copy-start | bytes 393220
  61.2 36.3 %copy-start.16 = (bf16[256,256]{1,0:T(8,128)(2,1)S(1)}, bf16[256,256]{1,0:T(8,128)(2,1)}, u32[]{:S(2)}) copy-start(bf16[256,256]{1,0:T(8,128)(2,1)} %constant.23.clone.cl_ref) | copy-start | bytes 393220
  61.2 36.3 %copy-start.17 = (bf16[256,256]{1,0:T(8,128)(2,1)S(1)}, bf16[256,256]{1,0:T(8,128)(2,1)}, u32[]{:S(2)}) copy-start(bf16[256,256]{1,0:T(8,128)(2,1)} %constant.22.clone.ch_ref) | copy-start | bytes 393220
  61.2 36.3 %copy-start.22 = (s32[3,16]{1,0:T(4,128)S(1)}, s32[3,16]{1,0:T(4,128)}, u32[]{:S(2)}) copy-start(s32[3,16]{1,0:T(4,128)} %mirror_ref.3) | copy-start | bytes 580
  61.2 36.3 %copy-start.23 = (s32[8,2]{0,1:T(2,128)S(1)}, s32[8,2]{0,1:T(2,128)}, u32[]{:S(2)}) copy-start(s32[8,2]{0,1:T(2,128)} %param.16) | copy-start | bytes 196
  61.3 36.2 %all-to-all-start.1 = ((f32[32,64,128]{2,1,0:T(8,128)}), f32[32,64,128]{2,1,0:T(8,128)S(1)}, u32[]{:S(2)}, u32[]{:S(2)}) async-start(f32[32,64,128]{2,1,0:T(8,128)} %bitcast.17), calls=%async_computation.1 | async-start | bytes 2097152 | tf_op jit(solution)/shard_map/all_to_all | solution.py:588
  74.4 11.8 %collective-permute-start = (f32[2,2,8,8,128]{4,3,2,1,0:T(8,128)}, f32[2,2,8,8,128]{4,3,2,1,0:T(8,128)S(1)}, u32[]{:S(2)}, u32[]{:S(2)}) collective-permute-start(f32[2,2,8,8,128]{4,3,2,1,0:T(8,128)} %get-tuple-element.49), channel_id=1, source_target_pairs={{0,8},{1,9},{2,10},{3,11},{4,12},{5,13},{6,14},{7,15},{8,0},{9,1},... | collective-permute-start | bytes 393224 | tf_op jit(solution)/shard_map/ppermute | solution.py:594
  76.1 13.7 %collective-permute-start.1 = (f32[2,2,8,8,128]{4,3,2,1,0:T(8,128)}, f32[2,2,8,8,128]{4,3,2,1,0:T(8,128)S(1)}, u32[]{:S(2)}, u32[]{:S(2)}) collective-permute-start(f32[2,2,8,8,128]{4,3,2,1,0:T(8,128)} %get-tuple-element.50), channel_id=1, source_target_pairs={{0,9},{1,8},{2,11},{3,10},{4,13},{5,12},{6,15},{7,14},{8,1},{9,0},... | collective-permute-start | bytes 393224 | tf_op jit(solution)/shard_map/ppermute | solution.py:594
  76.1 18.7 %collective-permute-start.2 = (f32[2,2,8,8,128]{4,3,2,1,0:T(8,128)}, f32[2,2,8,8,128]{4,3,2,1,0:T(8,128)S(1)}, u32[]{:S(2)}, u32[]{:S(2)}) collective-permute-start(f32[2,2,8,8,128]{4,3,2,1,0:T(8,128)} %get-tuple-element.51), channel_id=1, source_target_pairs={{0,10},{1,11},{2,8},{3,9},{4,14},{5,15},{6,12},{7,13},{8,2},{9,3},... | collective-permute-start | bytes 393224 | tf_op jit(solution)/shard_map/ppermute | solution.py:594
  78.5 18.2 %collective-permute-start.3 = (f32[2,2,8,8,128]{4,3,2,1,0:T(8,128)}, f32[2,2,8,8,128]{4,3,2,1,0:T(8,128)S(1)}, u32[]{:S(2)}, u32[]{:S(2)}) collective-permute-start(f32[2,2,8,8,128]{4,3,2,1,0:T(8,128)} %get-tuple-element.52), channel_id=1, source_target_pairs={{0,11},{1,10},{2,9},{3,8},{4,15},{5,14},{6,13},{7,12},{8,3},{9,2},... | collective-permute-start | bytes 393224 | tf_op jit(solution)/shard_map/ppermute | solution.py:594
  78.9 18.6 %collective-permute-start.4 = (f32[2,2,8,8,128]{4,3,2,1,0:T(8,128)}, f32[2,2,8,8,128]{4,3,2,1,0:T(8,128)S(1)}, u32[]{:S(2)}, u32[]{:S(2)}) collective-permute-start(f32[2,2,8,8,128]{4,3,2,1,0:T(8,128)} %get-tuple-element.53), channel_id=1, source_target_pairs={{0,1},{1,0},{2,3},{3,2},{4,5},{5,4},{6,7},{7,6},{8,9},{9,8},{10,11... | collective-permute-start | bytes 393224 | tf_op jit(solution)/shard_map/ppermute | solution.py:594
  86.3 18.7 %collective-permute-start.5 = (f32[2,2,8,8,128]{4,3,2,1,0:T(8,128)}, f32[2,2,8,8,128]{4,3,2,1,0:T(8,128)S(1)}, u32[]{:S(2)}, u32[]{:S(2)}) collective-permute-start(f32[2,2,8,8,128]{4,3,2,1,0:T(8,128)} %get-tuple-element.55), channel_id=1, source_target_pairs={{0,12},{1,13},{2,14},{3,15},{4,8},{5,9},{6,10},{7,11},{8,4},{9,5},... | collective-permute-start | bytes 393224 | tf_op jit(solution)/shard_map/ppermute | solution.py:594
  89.7 15.9 %collective-permute-start.6 = (f32[2,2,8,8,128]{4,3,2,1,0:T(8,128)}, f32[2,2,8,8,128]{4,3,2,1,0:T(8,128)S(1)}, u32[]{:S(2)}, u32[]{:S(2)}) collective-permute-start(f32[2,2,8,8,128]{4,3,2,1,0:T(8,128)} %get-tuple-element.56), channel_id=1, source_target_pairs={{0,13},{1,12},{2,15},{3,14},{4,9},{5,8},{6,11},{7,10},{8,5},{9,4},... | collective-permute-start | bytes 393224 | tf_op jit(solution)/shard_map/ppermute | solution.py:594
  94.8 11.5 %collective-permute-start.7 = (f32[2,2,8,8,128]{4,3,2,1,0:T(8,128)}, f32[2,2,8,8,128]{4,3,2,1,0:T(8,128)S(1)}, u32[]{:S(2)}, u32[]{:S(2)}) collective-permute-start(f32[2,2,8,8,128]{4,3,2,1,0:T(8,128)} %get-tuple-element.57), channel_id=1, source_target_pairs={{0,2},{1,3},{2,0},{3,1},{4,6},{5,7},{6,4},{7,5},{8,10},{9,11},{10,... | collective-permute-start | bytes 393224 | tf_op jit(solution)/shard_map/ppermute | solution.py:594
  96.7 9.6 %collective-permute-start.8 = (f32[2,2,8,8,128]{4,3,2,1,0:T(8,128)}, f32[2,2,8,8,128]{4,3,2,1,0:T(8,128)S(1)}, u32[]{:S(2)}, u32[]{:S(2)}) collective-permute-start(f32[2,2,8,8,128]{4,3,2,1,0:T(8,128)} %get-tuple-element.58), channel_id=1, source_target_pairs={{0,3},{1,2},{2,1},{3,0},{4,7},{5,6},{6,5},{7,4},{8,11},{9,10},{10,... | collective-permute-start | bytes 393224 | tf_op jit(solution)/shard_map/ppermute | solution.py:594
  107.0 54.5 %all-to-all-start.2 = ((f32[32,128,128]{2,1,0:T(8,128)}), f32[32,128,128]{2,1,0:T(8,128)S(1)}, u32[]{:S(2)}, u32[]{:S(2)}) async-start(f32[32,128,128]{2,1,0:T(8,128)} %bitcast.12), calls=%async_computation.2 | async-start | bytes 4194304 | tf_op jit(solution)/shard_map/all_to_all | solution.py:588
  114.4 32.6 %copy-start.24 = (f32[2,2,8,8,128]{4,3,2,1,0:T(8,128)S(1)}, f32[2,2,8,8,128]{4,3,2,1,0:T(8,128)}, u32[]{:S(2)}) copy-start(f32[2,2,8,8,128]{4,3,2,1,0:T(8,128)} %get-tuple-element.84) | copy-start | bytes 393220
  114.4 41.1 %copy-start.5 = (f32[2,2,8,8,128]{4,3,2,1,0:T(8,128)S(1)}, f32[2,2,8,8,128]{4,3,2,1,0:T(8,128)}, u32[]{:S(2)}) copy-start(f32[2,2,8,8,128]{4,3,2,1,0:T(8,128)} %get-tuple-element.69.refs_0_) | copy-start | bytes 393220
  114.4 41.1 %copy-start.7 = (f32[2,2,8,8,128]{4,3,2,1,0:T(8,128)S(1)}, f32[2,2,8,8,128]{4,3,2,1,0:T(8,128)}, u32[]{:S(2)}) copy-start(f32[2,2,8,8,128]{4,3,2,1,0:T(8,128)} %copy-done.6) | copy-start | bytes 393220
  114.4 41.1 %copy-start.9 = (f32[2,2,8,8,128]{4,3,2,1,0:T(8,128)S(1)}, f32[2,2,8,8,128]{4,3,2,1,0:T(8,128)}, u32[]{:S(2)}) copy-start(f32[2,2,8,8,128]{4,3,2,1,0:T(8,128)} %copy-done.8) | copy-start | bytes 393220
  114.4 41.1 %copy-start.11 = (f32[2,2,8,8,128]{4,3,2,1,0:T(8,128)S(1)}, f32[2,2,8,8,128]{4,3,2,1,0:T(8,128)}, u32[]{:S(2)}) copy-start(f32[2,2,8,8,128]{4,3,2,1,0:T(8,128)} %copy-done.10) | copy-start | bytes 393220
  114.4 41.1 %copy-start.13 = (f32[2,2,8,8,128]{4,3,2,1,0:T(8,128)S(1)}, f32[2,2,8,8,128]{4,3,2,1,0:T(8,128)}, u32[]{:S(2)}) copy-start(f32[2,2,8,8,128]{4,3,2,1,0:T(8,128)} %copy-done.12) | copy-start | bytes 393220
  114.5 41.1 %copy-start.19 = (f32[2,2,8,8,128]{4,3,2,1,0:T(8,128)S(1)}, f32[2,2,8,8,128]{4,3,2,1,0:T(8,128)}, u32[]{:S(2)}) copy-start(f32[2,2,8,8,128]{4,3,2,1,0:T(8,128)} %copy-done.18) | copy-start | bytes 393220
  114.5 41.1 %copy-start.21 = (f32[2,2,8,8,128]{4,3,2,1,0:T(8,128)S(1)}, f32[2,2,8,8,128]{4,3,2,1,0:T(8,128)}, u32[]{:S(2)}) copy-start(f32[2,2,8,8,128]{4,3,2,1,0:T(8,128)} %copy-done.20) | copy-start | bytes 393220
  115.3 31.7 %collective-permute-start.9 = (f32[2,2,8,8,128]{4,3,2,1,0:T(8,128)S(1)}, f32[2,2,8,8,128]{4,3,2,1,0:T(8,128)S(1)}, u32[]{:S(2)}, u32[]{:S(2)}) collective-permute-start(f32[2,2,8,8,128]{4,3,2,1,0:T(8,128)S(1)} %copy-done.29), channel_id=1, source_target_pairs={{0,4},{1,5},{2,6},{3,7},{4,0},{5,1},{6,2},{7,3},{8,12},{9,13},{10,... | collective-permute-start | bytes 393224 | tf_op jit(solution)/shard_map/ppermute | solution.py:594
  116.8 32.3 %collective-permute-start.10 = (f32[2,2,8,8,128]{4,3,2,1,0:T(8,128)S(1)}, f32[2,2,8,8,128]{4,3,2,1,0:T(8,128)S(1)}, u32[]{:S(2)}, u32[]{:S(2)}) collective-permute-start(f32[2,2,8,8,128]{4,3,2,1,0:T(8,128)S(1)} %copy-done.28), channel_id=1, source_target_pairs={{0,5},{1,4},{2,7},{3,6},{4,1},{5,0},{6,3},{7,2},{8,13},{9,12},{10,... | collective-permute-start | bytes 393224 | tf_op jit(solution)/shard_map/ppermute | solution.py:594
  116.8 32.3 %collective-permute-start.11 = (f32[2,2,8,8,128]{4,3,2,1,0:T(8,128)S(1)}, f32[2,2,8,8,128]{4,3,2,1,0:T(8,128)S(1)}, u32[]{:S(2)}, u32[]{:S(2)}) collective-permute-start(f32[2,2,8,8,128]{4,3,2,1,0:T(8,128)S(1)} %copy-done.27), channel_id=1, source_target_pairs={{0,6},{1,7},{2,4},{3,5},{4,2},{5,3},{6,0},{7,1},{8,14},{9,15},{10,... | collective-permute-start | bytes 393224 | tf_op jit(solution)/shard_map/ppermute | solution.py:594
  119.2 29.9 %collective-permute-start.12 = (f32[2,2,8,8,128]{4,3,2,1,0:T(8,128)S(1)}, f32[2,2,8,8,128]{4,3,2,1,0:T(8,128)S(1)}, u32[]{:S(2)}, u32[]{:S(2)}) collective-permute-start(f32[2,2,8,8,128]{4,3,2,1,0:T(8,128)S(1)} %copy-done.26), channel_id=1, source_target_pairs={{0,7},{1,6},{2,5},{3,4},{4,3},{5,2},{6,1},{7,0},{8,15},{9,14},{10,... | collective-permute-start | bytes 393224 | tf_op jit(solution)/shard_map/ppermute | solution.py:594
  119.7 31.0 %collective-permute-start.13 = (f32[2,2,8,8,128]{4,3,2,1,0:T(8,128)S(1)}, f32[2,2,8,8,128]{4,3,2,1,0:T(8,128)S(1)}, u32[]{:S(2)}, u32[]{:S(2)}) collective-permute-start(f32[2,2,8,8,128]{4,3,2,1,0:T(8,128)S(1)} %copy-done.25), channel_id=1, source_target_pairs={{0,14},{1,15},{2,12},{3,13},{4,10},{5,11},{6,8},{7,9},{8,6},{9,7},... | collective-permute-start | bytes 393224 | tf_op jit(solution)/shard_map/ppermute | solution.py:594
  147.0 8.5 %collective-permute-start.14 = (f32[2,2,8,8,128]{4,3,2,1,0:T(8,128)S(1)}, f32[2,2,8,8,128]{4,3,2,1,0:T(8,128)S(1)}, u32[]{:S(2)}, u32[]{:S(2)}) collective-permute-start(f32[2,2,8,8,128]{4,3,2,1,0:T(8,128)S(1)} %copy-done.24), channel_id=1, source_target_pairs={{0,15},{1,14},{2,13},{3,12},{4,11},{5,10},{6,9},{7,8},{8,7},{9,6},... | collective-permute-start | bytes 393224 | tf_op jit(solution)/shard_map/ppermute | solution.py:594
  (16 other events, 38.2 us)

commit v12 on v11

--- a/solution.py
+++ b/solution.py
@@ -419,7 +419,7 @@
             pltpu.VMEM((GROUPS, side, 2, 2, components // GROUPS, rows, lanes), jnp.float32),
             pltpu.SemaphoreType.DMA((GROUPS,)),
         ],
-        compiler_params=pltpu.CompilerParams(vmem_limit_bytes=44 << 20),
+        compiler_params=pltpu.CompilerParams(vmem_limit_bytes=60416 << 10),
         cost_estimate=pl.CostEstimate(flops=6_000_000_000, bytes_accessed=12_000_000, transcendentals=0),
         name="one_middle",
     )(*args)
@@ -465,7 +465,7 @@
         in_specs=[smem, vmem, vmem],
         out_specs=vmem,
         out_shape=jax.ShapeDtypeStruct((2, depth, one.shape[1]), jnp.bfloat16),
-        compiler_params=pltpu.CompilerParams(vmem_limit_bytes=32 << 20),
+        compiler_params=pltpu.CompilerParams(vmem_limit_bytes=60620 << 10),
         name="prepare",
     )(me, both, one)
 
@@ -508,7 +508,7 @@
             pltpu.SemaphoreType.DMA((len(pieces),)),
             pltpu.SemaphoreType.DMA((components,)),
         ],
-        compiler_params=pltpu.CompilerParams(vmem_limit_bytes=32 << 20),
+        compiler_params=pltpu.CompilerParams(vmem_limit_bytes=59699 << 10),
         name="fold",
     )(*pieces)
 
@@ -578,7 +578,7 @@
             pltpu.SemaphoreType.DMA((groups,)),
             pltpu.SemaphoreType.DMA((groups,)),
         ],
-        compiler_params=pltpu.CompilerParams(vmem_limit_bytes=44 << 20),
+        compiler_params=pltpu.CompilerParams(vmem_limit_bytes=59904 << 10),
         name="to_frequencies",
     )(y, matrix, folded)
 

time: 170 us -> 172 us (1.012)
  Pallas kernels: 36.7 us -> 42.1 us
  local copies, waits for them, and re-layouts: 9.04 us -> 3.76 us
  waiting for transfers between devices: 85.9 us -> 88.2 us
    unnamed x60 -> x46, local copies, waits for them, and re-layouts: 9.04 us -> 3.76 us
    pallas_call x1, Pallas kernels: 5.48 us -> 8.32 us  [to_frequencies(): pl.pallas_call(frequency_kernel, in_specs=[pl.BlockSpec(memory_space=pltp...]
    pallas_call x1, Pallas kernels: 0.14 us -> 2.43 us  [prepare(): pl.pallas_call(prepare_kernel, in_specs=[smem, vmem, vmem], out_specs=vme...]
    all_to_all x3, waiting for transfers between devices: 42.3 us -> 44.1 us  [exchange(): lax.all_to_all(flat, 'kb', split_axis=0, concat_axis=0, tiled=True)]
  transfers between devices with their start and end apart: 18 -> 18, of which waited for: 9 -> 9; matrix products, arithmetic and copies ran while one was open for 0% -> 0% of each run, Pallas kernels for 16% -> 17%
where the time goes in v12:
time: 172 us; the launch traced here: 171 us
  waiting for transfers between devices  88.2 us (51%)
  Pallas kernels  42.1 us (24%)
  starting transfers between devices  36.6 us (21%)
  local copies, waits for them, and re-layouts  3.76 us (2%)
    all_to_all x3, waiting for transfers between devices, exchange(): lax.all_to_all(flat, 'kb', split_axis=0, concat_axis=0, tiled=True)  44.1 us
    ppermute x15, waiting for transfers between devices, swap(): lax.ppermute(piece, 'kb', [(device, device ^ slot) for device in range(de...  44 us
    ppermute x15, starting transfers between devices, swap(): lax.ppermute(piece, 'kb', [(device, device ^ slot) for device in range(de...  19.7 us
    all_to_all x3, starting transfers between devices, exchange(): lax.all_to_all(flat, 'kb', split_axis=0, concat_axis=0, tiled=True)  16.9 us
    pallas_call x2, Pallas kernels, to_times(): pl.pallas_call(kernel, in_specs=[hbm, hbm], out_specs=hbm, out_shape=jax....  11.6 us
    pallas_call x1, Pallas kernels, both_middle(): pl.pallas_call(both_middle_kernel, in_specs=[pl.BlockSpec(memory_space=pl...  8.96 us
    pallas_call x1, Pallas kernels, to_frequencies(): pl.pallas_call(frequency_kernel, in_specs=[pl.BlockSpec(memory_space=pltp...  8.32 us
    pallas_call x1, Pallas kernels, one_middle(): pl.pallas_call(one_middle_kernel, in_specs=specs, out_specs=pl.BlockSpec(...  7.51 us
  transfers between devices with their start and end apart: 18, of which 9 were waited for; matrix products, arithmetic and copies ran while one was open for 0% of the time, Pallas kernels for 17%

profile of v12, /device:TPU:0, one launch (start us, length us, event | category | flops | bytes accessed | tf_op | source)
XLA Modules:
  0.0 171.1 jit_solution(12369667018496679534)
XLA Ops:
  0.0 4.9 %both_times.1 = f32[32,2,2,4,8,128]{5,4,3,2,1,0:T(8,128)} custom-call(f32[2,4,128,512]{3,2,1,0:T(8,128)} %g_hbm.2, f32[256,512]{1,0:T(8,128)} %constant.20.clone.m_hbm), custom_call_target="tpu_custom_call" | custom-call | tf_op jit(solution)/shard_map/both_times/pallas_call | solution.py:186
  4.9 7.4 %all-to-all-start = ((f32[32,128,128]{2,1,0:T(8,128)}), f32[32,128,128]{2,1,0:T(8,128)}, u32[]{:S(2)}, u32[]{:S(2)}) async-start(f32[32,128,128]{2,1,0:T(8,128)} %bitcast.11), calls=%async_computation | async-start | bytes 4194304 | tf_op jit(solution)/shard_map/all_to_all | solution.py:588
  12.3 6.7 %one_times.1 = f32[32,2,4,8,128]{4,3,2,1,0:T(8,128)} custom-call(f32[2,4,128,512]{3,2,1,0:T(8,128)} %g_hbm.2, f32[512,512]{1,0:T(8,128)} %constant.21.clone.m_hbm), custom_call_target="tpu_custom_call" | custom-call | tf_op jit(solution)/shard_map/one_times/pallas_call | solution.py:186
  19.1 42.2 %all-to-all-done = f32[32,128,128]{2,1,0:T(8,128)} async-done(((f32[32,128,128]{2,1,0:T(8,128)}), f32[32,128,128]{2,1,0:T(8,128)}, u32[]{:S(2)}, u32[]{:S(2)}) %all-to-all-start) | async-done | bytes 2097184 | tf_op jit(solution)/shard_map/all_to_all | solution.py:588
  61.2 4.2 %all-to-all-start.1 = ((f32[32,64,128]{2,1,0:T(8,128)}), f32[32,64,128]{2,1,0:T(8,128)S(1)}, u32[]{:S(2)}, u32[]{:S(2)}) async-start(f32[32,64,128]{2,1,0:T(8,128)} %bitcast.13), calls=%async_computation.1 | async-start | bytes 2097152 | tf_op jit(solution)/shard_map/all_to_all | solution.py:588
  65.4 9.0 %both_middle.1 = (f32[2,2,8,8,128]{4,3,2,1,0:T(8,128)}, f32[2,2,8,8,128]{4,3,2,1,0:T(8,128)}, f32[2,2,8,8,128]{4,3,2,1,0:T(8,128)}, f32[2,2,8,8,128]{4,3,2,1,0:T...) custom-call(s32[1]{0:T(128)} %bitcast.5.me_ref, ...), custom_call_target="tpu_custom_call" | custom-call | tf_op jit(solution)/shard_map/both_middle/pallas_call | solution.py:434
  74.4 1.6 collective-permute-start
  76.0 2.4 %collective-permute-start.2 = (f32[2,2,8,8,128]{4,3,2,1,0:T(8,128)}, f32[2,2,8,8,128]{4,3,2,1,0:T(8,128)S(1)}, u32[]{:S(2)}, u32[]{:S(2)}) collective-permute-start(f32[2,2,8,8,128]{4,3,2,1,0:T(8,128)} %get-tuple-element.51), channel_id=1, source_target_pairs={{0,10},{1,11},{2,8},{3,9},{4,14},{5,15},{6,12},{7,13},{8,2},{9,3},... | collective-permute-start | bytes 393224 | tf_op jit(solution)/shard_map/ppermute | solution.py:594
  79.1 7.1 %collective-permute-done.refs_1_ = f32[2,2,8,8,128]{4,3,2,1,0:T(8,128)S(1)} collective-permute-done((f32[2,2,8,8,128]{4,3,2,1,0:T(8,128)}, f32[2,2,8,8,128]{4,3,2,1,0:T(8,128)S(1)}, u32[]{:S(2)}, u32[]{:S(2)}) %collective-permute-start) | collective-permute-done | bytes 131104 | tf_op jit(solution)/shard_map/ppermute | solution.py:594
  86.2 3.5 %collective-permute-start.5 = (f32[2,2,8,8,128]{4,3,2,1,0:T(8,128)}, f32[2,2,8,8,128]{4,3,2,1,0:T(8,128)S(1)}, u32[]{:S(2)}, u32[]{:S(2)}) collective-permute-start(f32[2,2,8,8,128]{4,3,2,1,0:T(8,128)} %get-tuple-element.55), channel_id=1, source_target_pairs={{0,12},{1,13},{2,14},{3,15},{4,8},{5,9},{6,10},{7,11},{8,4},{9,5},... | collective-permute-start | bytes 393224 | tf_op jit(solution)/shard_map/ppermute | solution.py:594
  89.7 2.5 %collective-permute-start.6 = (f32[2,2,8,8,128]{4,3,2,1,0:T(8,128)}, f32[2,2,8,8,128]{4,3,2,1,0:T(8,128)S(1)}, u32[]{:S(2)}, u32[]{:S(2)}) collective-permute-start(f32[2,2,8,8,128]{4,3,2,1,0:T(8,128)} %get-tuple-element.56), channel_id=1, source_target_pairs={{0,13},{1,12},{2,15},{3,14},{4,9},{5,8},{6,11},{7,10},{8,5},{9,4},... | collective-permute-start | bytes 393224 | tf_op jit(solution)/shard_map/ppermute | solution.py:594
  92.2 2.5 %collective-permute-done.2.refs_3_ = f32[2,2,8,8,128]{4,3,2,1,0:T(8,128)S(1)} collective-permute-done((f32[2,2,8,8,128]{4,3,2,1,0:T(8,128)}, f32[2,2,8,8,128]{4,3,2,1,0:T(8,128)S(1)}, u32[]{:S(2)}, u32[]{:S(2)}) %collective-permute-start.2) | collective-permute-done | bytes 131104 | tf_op jit(solution)/shard_map/ppermute | solution.py:594
  95.2 1.4 collective-permute-done.3.refs_4_
  96.6 0.8 collective-permute-start.8
  97.4 1.0 copy-done.1
  98.4 7.5 %one_middle.1 = f32[16,2,2,8,8,128]{5,4,3,2,1,0:T(8,128)} custom-call(s32[2,8]{1,0:T(2,128)} %bitcast.17, s32[3,16]{1,0:T(4,128)} %mirror_ref.3, bf16[256,256]{1,0:T(8,128)(2,1)} %constant.22.clone.ch_ref, bf16[256,256]{1,0:T(8,128)(2,1)} %constant.23.clone.cl_ref, bf16[256,256]{1,0:T(8,128)(2,1)} %constant.24.clone.sh_ref, ...), custom_call_target="tpu_custom_call" | custom-call | flops 6000000000 | bytes 12000000 | tf_op jit(solution)/shard_map/one_middle/pallas_call | solution.py:407
  106.1 0.6 copy-done.7
  106.8 5.3 %all-to-all-start.2 = ((f32[32,128,128]{2,1,0:T(8,128)}), f32[32,128,128]{2,1,0:T(8,128)S(1)}, u32[]{:S(2)}, u32[]{:S(2)}) async-start(f32[32,128,128]{2,1,0:T(8,128)} %bitcast.14), calls=%async_computation.2 | async-start | bytes 4194304 | tf_op jit(solution)/shard_map/all_to_all | solution.py:588
  112.2 2.4 %prepare.1.m_hbm = bf16[2,512,512]{2,1,0:T(8,128)(2,1)} custom-call(s32[1]{0:T(128)} %bitcast.5.me_ref, f32[2,16,8,512]{3,2,1,0:T(8,128)} %constant.26.clone.both_ref, f32[256,512]{1,0:T(8,128)} %constant.27.clone.one_ref), custom_call_target="tpu_custom_call" | custom-call | tf_op jit(solution)/shard_map/prepare/pallas_call | solution.py:463
  114.6 1.6 collective-permute-start.9
  116.2 2.4 %collective-permute-start.11 = (f32[2,2,8,8,128]{4,3,2,1,0:T(8,128)S(1)}, f32[2,2,8,8,128]{4,3,2,1,0:T(8,128)S(1)}, u32[]{:S(2)}, u32[]{:S(2)}) collective-permute-start(f32[2,2,8,8,128]{4,3,2,1,0:T(8,128)S(1)} %copy-done.20), channel_id=1, source_target_pairs={{0,6},{1,7},{2,4},{3,5},{4,2},{5,3},{6,0},{7,1},{8,14},{9,15},{10,... | collective-permute-start | bytes 393224 | tf_op jit(solution)/shard_map/ppermute | solution.py:594
  118.6 0.4 collective-permute-start.12
  119.0 3.4 %collective-permute-start.13 = (f32[2,2,8,8,128]{4,3,2,1,0:T(8,128)S(1)}, f32[2,2,8,8,128]{4,3,2,1,0:T(8,128)S(1)}, u32[]{:S(2)}, u32[]{:S(2)}) collective-permute-start(f32[2,2,8,8,128]{4,3,2,1,0:T(8,128)S(1)} %copy-done.18), channel_id=1, source_target_pairs={{0,14},{1,15},{2,12},{3,13},{4,10},{5,11},{6,8},{7,9},{8,6},{9,7},... | collective-permute-start | bytes 393224 | tf_op jit(solution)/shard_map/ppermute | solution.py:594
  122.4 24.5 %collective-permute-done.9.refs_10_ = f32[2,2,8,8,128]{4,3,2,1,0:T(8,128)S(1)} collective-permute-done((f32[2,2,8,8,128]{4,3,2,1,0:T(8,128)S(1)}, f32[2,2,8,8,128]{4,3,2,1,0:T(8,128)S(1)}, u32[]{:S(2)}, u32[]{:S(2)}) %collective-permute-start.9) | collective-permute-done | bytes 131104 | tf_op jit(solution)/shard_map/ppermute | solution.py:594
  146.8 2.2 %collective-permute-done.10.refs_11_ = f32[2,2,8,8,128]{4,3,2,1,0:T(8,128)S(1)} collective-permute-done((f32[2,2,8,8,128]{4,3,2,1,0:T(8,128)S(1)}, f32[2,2,8,8,128]{4,3,2,1,0:T(8,128)S(1)}, u32[]{:S(2)}, u32[]{:S(2)}) %collective-permute-start.10) | collective-permute-done | bytes 131104 | tf_op jit(solution)/shard_map/ppermute | solution.py:594
  149.0 1.5 collective-permute-done.13.refs_14_
  150.5 4.8 %collective-permute-done.14.refs_15_ = f32[2,2,8,8,128]{4,3,2,1,0:T(8,128)S(1)} collective-permute-done((f32[2,2,8,8,128]{4,3,2,1,0:T(8,128)S(1)}, f32[2,2,8,8,128]{4,3,2,1,0:T(8,128)S(1)}, u32[]{:S(2)}, u32[]{:S(2)}) %collective-permute-start.14) | collective-permute-done | bytes 131104 | tf_op jit(solution)/shard_map/ppermute | solution.py:594
  155.4 0.6 copy-done.16
  156.0 3.3 %fold.1.f_hbm = bf16[8,2,256,256]{3,2,1,0:T(8,128)(2,1)} custom-call(f32[2,2,8,8,128]{4,3,2,1,0:T(8,128)} %get-tuple-element.69.refs_0_, f32[2,2,8,8,128]{4,3,2,1,0:T(8,128)} %copy-done.2, f32[2,2,8,8,128]{4,3,2,1,0:T(8,128)} %copy-done.3, f32[2,2,8,8,128]{4,3,2,1,0:T(8,128)} %copy-done.4, f32[2,2,8,8,128]{4,3,2,1,0:T(8,128)} %copy-done.5, ...), custom_call_target="tpu_custom_call" | custom-call | tf_op jit(solution)/shard_map/fold/pallas_call | solution.py:500
  159.3 2.0 %all-to-all-done.2 = f32[32,128,128]{2,1,0:T(8,128)S(1)} async-done(((f32[32,128,128]{2,1,0:T(8,128)}), f32[32,128,128]{2,1,0:T(8,128)S(1)}, u32[]{:S(2)}, u32[]{:S(2)}) %all-to-all-start.2) | async-done | bytes 2097184 | tf_op jit(solution)/shard_map/all_to_all | solution.py:588
  161.3 1.3 copy-done
  162.6 8.3 %to_frequencies.1 = f32[2,8,128,512]{3,2,1,0:T(8,128)} custom-call(f32[32,2,8,8,128]{4,3,2,1,0:T(8,128)} %bitcast.12, bf16[2,512,512]{2,1,0:T(8,128)(2,1)} %prepare.1.m_hbm, bf16[8,2,256,256]{3,2,1,0:T(8,128)(2,1)} %fold.1.f_hbm), custom_call_target="tpu_custom_call" | custom-call | tf_op jit(solution)/shard_map/to_frequencies/pallas_call | solution.py:568
  (57 shorter events, 1.3 us)
Async XLA Ops:
  4.9 56.3 %all-to-all-start = ((f32[32,128,128]{2,1,0:T(8,128)}), f32[32,128,128]{2,1,0:T(8,128)}, u32[]{:S(2)}, u32[]{:S(2)}) async-start(f32[32,128,128]{2,1,0:T(8,128)} %bitcast.11), calls=%async_computation | async-start | bytes 4194304 | tf_op jit(solution)/shard_map/all_to_all | solution.py:588
  61.2 36.2 %all-to-all-start.1 = ((f32[32,64,128]{2,1,0:T(8,128)}), f32[32,64,128]{2,1,0:T(8,128)S(1)}, u32[]{:S(2)}, u32[]{:S(2)}) async-start(f32[32,64,128]{2,1,0:T(8,128)} %bitcast.13), calls=%async_computation.1 | async-start | bytes 2097152 | tf_op jit(solution)/shard_map/all_to_all | solution.py:588
  74.4 11.8 %collective-permute-start = (f32[2,2,8,8,128]{4,3,2,1,0:T(8,128)}, f32[2,2,8,8,128]{4,3,2,1,0:T(8,128)S(1)}, u32[]{:S(2)}, u32[]{:S(2)}) collective-permute-start(f32[2,2,8,8,128]{4,3,2,1,0:T(8,128)} %get-tuple-element.49), channel_id=1, source_target_pairs={{0,8},{1,9},{2,10},{3,11},{4,12},{5,13},{6,14},{7,15},{8,0},{9,1},... | collective-permute-start | bytes 393224 | tf_op jit(solution)/shard_map/ppermute | solution.py:594
  76.0 13.7 %collective-permute-start.1 = (f32[2,2,8,8,128]{4,3,2,1,0:T(8,128)}, f32[2,2,8,8,128]{4,3,2,1,0:T(8,128)S(1)}, u32[]{:S(2)}, u32[]{:S(2)}) collective-permute-start(f32[2,2,8,8,128]{4,3,2,1,0:T(8,128)} %get-tuple-element.50), channel_id=1, source_target_pairs={{0,9},{1,8},{2,11},{3,10},{4,13},{5,12},{6,15},{7,14},{8,1},{9,0},... | collective-permute-start | bytes 393224 | tf_op jit(solution)/shard_map/ppermute | solution.py:594
  76.0 18.7 %collective-permute-start.2 = (f32[2,2,8,8,128]{4,3,2,1,0:T(8,128)}, f32[2,2,8,8,128]{4,3,2,1,0:T(8,128)S(1)}, u32[]{:S(2)}, u32[]{:S(2)}) collective-permute-start(f32[2,2,8,8,128]{4,3,2,1,0:T(8,128)} %get-tuple-element.51), channel_id=1, source_target_pairs={{0,10},{1,11},{2,8},{3,9},{4,14},{5,15},{6,12},{7,13},{8,2},{9,3},... | collective-permute-start | bytes 393224 | tf_op jit(solution)/shard_map/ppermute | solution.py:594
  78.4 18.2 %collective-permute-start.3 = (f32[2,2,8,8,128]{4,3,2,1,0:T(8,128)}, f32[2,2,8,8,128]{4,3,2,1,0:T(8,128)S(1)}, u32[]{:S(2)}, u32[]{:S(2)}) collective-permute-start(f32[2,2,8,8,128]{4,3,2,1,0:T(8,128)} %get-tuple-element.52), channel_id=1, source_target_pairs={{0,11},{1,10},{2,9},{3,8},{4,15},{5,14},{6,13},{7,12},{8,3},{9,2},... | collective-permute-start | bytes 393224 | tf_op jit(solution)/shard_map/ppermute | solution.py:594
  78.8 18.6 %collective-permute-start.4 = (f32[2,2,8,8,128]{4,3,2,1,0:T(8,128)}, f32[2,2,8,8,128]{4,3,2,1,0:T(8,128)S(1)}, u32[]{:S(2)}, u32[]{:S(2)}) collective-permute-start(f32[2,2,8,8,128]{4,3,2,1,0:T(8,128)} %get-tuple-element.53), channel_id=1, source_target_pairs={{0,1},{1,0},{2,3},{3,2},{4,5},{5,4},{6,7},{7,6},{8,9},{9,8},{10,11... | collective-permute-start | bytes 393224 | tf_op jit(solution)/shard_map/ppermute | solution.py:594
  86.2 19.7 %copy-start.2 = (f32[2,2,8,8,128]{4,3,2,1,0:T(8,128)}, f32[2,2,8,8,128]{4,3,2,1,0:T(8,128)S(1)}, u32[]{:S(2)}) copy-start(f32[2,2,8,8,128]{4,3,2,1,0:T(8,128)S(1)} %collective-permute-done.refs_1_) | copy-start | bytes 393220
  86.2 19.8 %collective-permute-start.5 = (f32[2,2,8,8,128]{4,3,2,1,0:T(8,128)}, f32[2,2,8,8,128]{4,3,2,1,0:T(8,128)S(1)}, u32[]{:S(2)}, u32[]{:S(2)}) collective-permute-start(f32[2,2,8,8,128]{4,3,2,1,0:T(8,128)} %get-tuple-element.55), channel_id=1, source_target_pairs={{0,12},{1,13},{2,14},{3,15},{4,8},{5,9},{6,10},{7,11},{8,4},{9,5},... | collective-permute-start | bytes 393224 | tf_op jit(solution)/shard_map/ppermute | solution.py:594
  89.7 16.3 %copy-start.3 = (f32[2,2,8,8,128]{4,3,2,1,0:T(8,128)}, f32[2,2,8,8,128]{4,3,2,1,0:T(8,128)S(1)}, u32[]{:S(2)}) copy-start(f32[2,2,8,8,128]{4,3,2,1,0:T(8,128)S(1)} %collective-permute-done.1.refs_2_) | copy-start | bytes 393220
  89.7 16.3 %collective-permute-start.6 = (f32[2,2,8,8,128]{4,3,2,1,0:T(8,128)}, f32[2,2,8,8,128]{4,3,2,1,0:T(8,128)S(1)}, u32[]{:S(2)}, u32[]{:S(2)}) collective-permute-start(f32[2,2,8,8,128]{4,3,2,1,0:T(8,128)} %get-tuple-element.56), channel_id=1, source_target_pairs={{0,13},{1,12},{2,15},{3,14},{4,9},{5,8},{6,11},{7,10},{8,5},{9,4},... | collective-permute-start | bytes 393224 | tf_op jit(solution)/shard_map/ppermute | solution.py:594
  94.8 11.2 %copy-start.4 = (f32[2,2,8,8,128]{4,3,2,1,0:T(8,128)}, f32[2,2,8,8,128]{4,3,2,1,0:T(8,128)S(1)}, u32[]{:S(2)}) copy-start(f32[2,2,8,8,128]{4,3,2,1,0:T(8,128)S(1)} %collective-permute-done.2.refs_3_) | copy-start | bytes 393220
  94.8 11.3 %collective-permute-start.7 = (f32[2,2,8,8,128]{4,3,2,1,0:T(8,128)}, f32[2,2,8,8,128]{4,3,2,1,0:T(8,128)S(1)}, u32[]{:S(2)}, u32[]{:S(2)}) collective-permute-start(f32[2,2,8,8,128]{4,3,2,1,0:T(8,128)} %get-tuple-element.57), channel_id=1, source_target_pairs={{0,2},{1,3},{2,0},{3,1},{4,6},{5,7},{6,4},{7,5},{8,10},{9,11},{10,... | collective-permute-start | bytes 393224 | tf_op jit(solution)/shard_map/ppermute | solution.py:594
  96.6 9.4 %copy-start.5 = (f32[2,2,8,8,128]{4,3,2,1,0:T(8,128)}, f32[2,2,8,8,128]{4,3,2,1,0:T(8,128)S(1)}, u32[]{:S(2)}) copy-start(f32[2,2,8,8,128]{4,3,2,1,0:T(8,128)S(1)} %collective-permute-done.3.refs_4_) | copy-start | bytes 393220
  96.6 9.5 %collective-permute-start.8 = (f32[2,2,8,8,128]{4,3,2,1,0:T(8,128)}, f32[2,2,8,8,128]{4,3,2,1,0:T(8,128)S(1)}, u32[]{:S(2)}, u32[]{:S(2)}) collective-permute-start(f32[2,2,8,8,128]{4,3,2,1,0:T(8,128)} %get-tuple-element.58), channel_id=1, source_target_pairs={{0,3},{1,2},{2,1},{3,0},{4,7},{5,6},{6,5},{7,4},{8,11},{9,10},{10,... | collective-permute-start | bytes 393224 | tf_op jit(solution)/shard_map/ppermute | solution.py:594
  97.4 8.6 %copy-start.6 = (f32[2,2,8,8,128]{4,3,2,1,0:T(8,128)}, f32[2,2,8,8,128]{4,3,2,1,0:T(8,128)S(1)}, u32[]{:S(2)}) copy-start(f32[2,2,8,8,128]{4,3,2,1,0:T(8,128)S(1)} %collective-permute-done.4.refs_5_) | copy-start | bytes 393220
  106.8 54.5 %all-to-all-start.2 = ((f32[32,128,128]{2,1,0:T(8,128)}), f32[32,128,128]{2,1,0:T(8,128)S(1)}, u32[]{:S(2)}, u32[]{:S(2)}) async-start(f32[32,128,128]{2,1,0:T(8,128)} %bitcast.14), calls=%async_computation.2 | async-start | bytes 4194304 | tf_op jit(solution)/shard_map/all_to_all | solution.py:588
  112.1 4.0 %copy-start.21 = (f32[2,2,8,8,128]{4,3,2,1,0:T(8,128)S(1)}, f32[2,2,8,8,128]{4,3,2,1,0:T(8,128)}, u32[]{:S(2)}) copy-start(f32[2,2,8,8,128]{4,3,2,1,0:T(8,128)} %get-tuple-element.80) | copy-start | bytes 393220
  112.1 6.4 %copy-start.19 = (f32[2,2,8,8,128]{4,3,2,1,0:T(8,128)S(1)}, f32[2,2,8,8,128]{4,3,2,1,0:T(8,128)}, u32[]{:S(2)}) copy-start(f32[2,2,8,8,128]{4,3,2,1,0:T(8,128)} %get-tuple-element.82) | copy-start | bytes 393220
  112.2 6.9 %copy-start.18 = (f32[2,2,8,8,128]{4,3,2,1,0:T(8,128)S(1)}, f32[2,2,8,8,128]{4,3,2,1,0:T(8,128)}, u32[]{:S(2)}) copy-start(f32[2,2,8,8,128]{4,3,2,1,0:T(8,128)} %get-tuple-element.83) | copy-start | bytes 393220
  112.2 34.7 %copy-start.17 = (f32[2,2,8,8,128]{4,3,2,1,0:T(8,128)S(1)}, f32[2,2,8,8,128]{4,3,2,1,0:T(8,128)}, u32[]{:S(2)}) copy-start(f32[2,2,8,8,128]{4,3,2,1,0:T(8,128)} %get-tuple-element.84) | copy-start | bytes 393220
  114.6 32.2 %collective-permute-start.9 = (f32[2,2,8,8,128]{4,3,2,1,0:T(8,128)S(1)}, f32[2,2,8,8,128]{4,3,2,1,0:T(8,128)S(1)}, u32[]{:S(2)}, u32[]{:S(2)}) collective-permute-start(f32[2,2,8,8,128]{4,3,2,1,0:T(8,128)S(1)} %copy-done.22), channel_id=1, source_target_pairs={{0,4},{1,5},{2,6},{3,7},{4,0},{5,1},{6,2},{7,3},{8,12},{9,13},{10,... | collective-permute-start | bytes 393224 | tf_op jit(solution)/shard_map/ppermute | solution.py:594
  116.2 32.8 %collective-permute-start.10 = (f32[2,2,8,8,128]{4,3,2,1,0:T(8,128)S(1)}, f32[2,2,8,8,128]{4,3,2,1,0:T(8,128)S(1)}, u32[]{:S(2)}, u32[]{:S(2)}) collective-permute-start(f32[2,2,8,8,128]{4,3,2,1,0:T(8,128)S(1)} %copy-done.21), channel_id=1, source_target_pairs={{0,5},{1,4},{2,7},{3,6},{4,1},{5,0},{6,3},{7,2},{8,13},{9,12},{10,... | collective-permute-start | bytes 393224 | tf_op jit(solution)/shard_map/ppermute | solution.py:594
  116.2 32.8 %collective-permute-start.11 = (f32[2,2,8,8,128]{4,3,2,1,0:T(8,128)S(1)}, f32[2,2,8,8,128]{4,3,2,1,0:T(8,128)S(1)}, u32[]{:S(2)}, u32[]{:S(2)}) collective-permute-start(f32[2,2,8,8,128]{4,3,2,1,0:T(8,128)S(1)} %copy-done.20), channel_id=1, source_target_pairs={{0,6},{1,7},{2,4},{3,5},{4,2},{5,3},{6,0},{7,1},{8,14},{9,15},{10,... | collective-permute-start | bytes 393224 | tf_op jit(solution)/shard_map/ppermute | solution.py:594
  118.6 30.4 %collective-permute-start.12 = (f32[2,2,8,8,128]{4,3,2,1,0:T(8,128)S(1)}, f32[2,2,8,8,128]{4,3,2,1,0:T(8,128)S(1)}, u32[]{:S(2)}, u32[]{:S(2)}) collective-permute-start(f32[2,2,8,8,128]{4,3,2,1,0:T(8,128)S(1)} %copy-done.19), channel_id=1, source_target_pairs={{0,7},{1,6},{2,5},{3,4},{4,3},{5,2},{6,1},{7,0},{8,15},{9,14},{10,... | collective-permute-start | bytes 393224 | tf_op jit(solution)/shard_map/ppermute | solution.py:594
  119.0 31.5 %collective-permute-start.13 = (f32[2,2,8,8,128]{4,3,2,1,0:T(8,128)S(1)}, f32[2,2,8,8,128]{4,3,2,1,0:T(8,128)S(1)}, u32[]{:S(2)}, u32[]{:S(2)}) collective-permute-start(f32[2,2,8,8,128]{4,3,2,1,0:T(8,128)S(1)} %copy-done.18), channel_id=1, source_target_pairs={{0,14},{1,15},{2,12},{3,13},{4,10},{5,11},{6,8},{7,9},{8,6},{9,7},... | collective-permute-start | bytes 393224 | tf_op jit(solution)/shard_map/ppermute | solution.py:594
  146.8 8.5 %copy-start.11 = (f32[2,2,8,8,128]{4,3,2,1,0:T(8,128)}, f32[2,2,8,8,128]{4,3,2,1,0:T(8,128)S(1)}, u32[]{:S(2)}) copy-start(f32[2,2,8,8,128]{4,3,2,1,0:T(8,128)S(1)} %collective-permute-done.9.refs_10_) | copy-start | bytes 393220
  146.8 8.5 %collective-permute-start.14 = (f32[2,2,8,8,128]{4,3,2,1,0:T(8,128)S(1)}, f32[2,2,8,8,128]{4,3,2,1,0:T(8,128)S(1)}, u32[]{:S(2)}, u32[]{:S(2)}) collective-permute-start(f32[2,2,8,8,128]{4,3,2,1,0:T(8,128)S(1)} %copy-done.17), channel_id=1, source_target_pairs={{0,15},{1,14},{2,13},{3,12},{4,11},{5,10},{6,9},{7,8},{8,7},{9,6},... | collective-permute-start | bytes 393224 | tf_op jit(solution)/shard_map/ppermute | solution.py:594
  149.0 6.3 %copy-start.12 = (f32[2,2,8,8,128]{4,3,2,1,0:T(8,128)}, f32[2,2,8,8,128]{4,3,2,1,0:T(8,128)S(1)}, u32[]{:S(2)}) copy-start(f32[2,2,8,8,128]{4,3,2,1,0:T(8,128)S(1)} %collective-permute-done.10.refs_11_) | copy-start | bytes 393220
  149.0 6.3 %copy-start.13 = (f32[2,2,8,8,128]{4,3,2,1,0:T(8,128)}, f32[2,2,8,8,128]{4,3,2,1,0:T(8,128)S(1)}, u32[]{:S(2)}) copy-start(f32[2,2,8,8,128]{4,3,2,1,0:T(8,128)S(1)} %collective-permute-done.11.refs_12_) | copy-start | bytes 393220
  149.0 6.3 %copy-start.14 = (f32[2,2,8,8,128]{4,3,2,1,0:T(8,128)}, f32[2,2,8,8,128]{4,3,2,1,0:T(8,128)S(1)}, u32[]{:S(2)}) copy-start(f32[2,2,8,8,128]{4,3,2,1,0:T(8,128)S(1)} %collective-permute-done.12.refs_13_) | copy-start | bytes 393220
  150.5 4.8 %copy-start.15 = (f32[2,2,8,8,128]{4,3,2,1,0:T(8,128)}, f32[2,2,8,8,128]{4,3,2,1,0:T(8,128)S(1)}, u32[]{:S(2)}) copy-start(f32[2,2,8,8,128]{4,3,2,1,0:T(8,128)S(1)} %collective-permute-done.13.refs_14_) | copy-start | bytes 393220
  (9 other events, 12.3 us)

commit v13 on v12

--- a/solution.py
+++ b/solution.py
@@ -419,7 +419,7 @@
             pltpu.VMEM((GROUPS, side, 2, 2, components // GROUPS, rows, lanes), jnp.float32),
             pltpu.SemaphoreType.DMA((GROUPS,)),
         ],
-        compiler_params=pltpu.CompilerParams(vmem_limit_bytes=60416 << 10),
+        compiler_params=pltpu.CompilerParams(vmem_limit_bytes=59500 << 10),
         cost_estimate=pl.CostEstimate(flops=6_000_000_000, bytes_accessed=12_000_000, transcendentals=0),
         name="one_middle",
     )(*args)
@@ -465,7 +465,7 @@
         in_specs=[smem, vmem, vmem],
         out_specs=vmem,
         out_shape=jax.ShapeDtypeStruct((2, depth, one.shape[1]), jnp.bfloat16),
-        compiler_params=pltpu.CompilerParams(vmem_limit_bytes=60620 << 10),
+        compiler_params=pltpu.CompilerParams(vmem_limit_bytes=59500 << 10),
         name="prepare",
     )(me, both, one)
 
@@ -508,7 +508,7 @@
             pltpu.SemaphoreType.DMA((len(pieces),)),
             pltpu.SemaphoreType.DMA((components,)),
         ],
-        compiler_params=pltpu.CompilerParams(vmem_limit_bytes=59699 << 10),
+        compiler_params=pltpu.CompilerParams(vmem_limit_bytes=59400 << 10),
         name="fold",
     )(*pieces)
 
@@ -578,7 +578,7 @@
             pltpu.SemaphoreType.DMA((groups,)),
             pltpu.SemaphoreType.DMA((groups,)),
         ],
-        compiler_params=pltpu.CompilerParams(vmem_limit_bytes=59904 << 10),
+        compiler_params=pltpu.CompilerParams(vmem_limit_bytes=59400 << 10),
         name="to_frequencies",
     )(y, matrix, folded)
 

time: 172 us -> 172 us (level)
  no operation moved by 1% of the time
where the time goes in v13:
time: 172 us; the launch traced here: 171 us
  waiting for transfers between devices  88.2 us (51%)
  Pallas kernels  42.1 us (24%)
  starting transfers between devices  36.6 us (21%)
  local copies, waits for them, and re-layouts  3.76 us (2%)
    all_to_all x3, waiting for transfers between devices, exchange(): lax.all_to_all(flat, 'kb', split_axis=0, concat_axis=0, tiled=True)  44.1 us
    ppermute x15, waiting for transfers between devices, swap(): lax.ppermute(piece, 'kb', [(device, device ^ slot) for device in range(de...  44.1 us
    ppermute x15, starting transfers between devices, swap(): lax.ppermute(piece, 'kb', [(device, device ^ slot) for device in range(de...  19.7 us
    all_to_all x3, starting transfers between devices, exchange(): lax.all_to_all(flat, 'kb', split_axis=0, concat_axis=0, tiled=True)  16.9 us
    pallas_call x2, Pallas kernels, to_times(): pl.pallas_call(kernel, in_specs=[hbm, hbm], out_specs=hbm, out_shape=jax....  11.6 us
    pallas_call x1, Pallas kernels, both_middle(): pl.pallas_call(both_middle_kernel, in_specs=[pl.BlockSpec(memory_space=pl...  8.95 us
    pallas_call x1, Pallas kernels, to_frequencies(): pl.pallas_call(frequency_kernel, in_specs=[pl.BlockSpec(memory_space=pltp...  8.32 us
    pallas_call x1, Pallas kernels, one_middle(): pl.pallas_call(one_middle_kernel, in_specs=specs, out_specs=pl.BlockSpec(...  7.51 us
  transfers between devices with their start and end apart: 18, of which 9 were waited for; matrix products, arithmetic and copies ran while one was open for 0% of the time, Pallas kernels for 17%

profile of v13, /device:TPU:0, one launch (start us, length us, event | category | flops | bytes accessed | tf_op | source)
XLA Modules:
  0.0 171.1 jit_solution(1797413914877500461)
XLA Ops:
  0.0 4.9 %both_times.1 = f32[32,2,2,4,8,128]{5,4,3,2,1,0:T(8,128)} custom-call(f32[2,4,128,512]{3,2,1,0:T(8,128)} %g_hbm.2, f32[256,512]{1,0:T(8,128)} %constant.20.clone.m_hbm), custom_call_target="tpu_custom_call" | custom-call | tf_op jit(solution)/shard_map/both_times/pallas_call | solution.py:186
  4.9 7.4 %all-to-all-start = ((f32[32,128,128]{2,1,0:T(8,128)}), f32[32,128,128]{2,1,0:T(8,128)}, u32[]{:S(2)}, u32[]{:S(2)}) async-start(f32[32,128,128]{2,1,0:T(8,128)} %bitcast.11), calls=%async_computation | async-start | bytes 4194304 | tf_op jit(solution)/shard_map/all_to_all | solution.py:588
  12.3 6.7 %one_times.1 = f32[32,2,4,8,128]{4,3,2,1,0:T(8,128)} custom-call(f32[2,4,128,512]{3,2,1,0:T(8,128)} %g_hbm.2, f32[512,512]{1,0:T(8,128)} %constant.21.clone.m_hbm), custom_call_target="tpu_custom_call" | custom-call | tf_op jit(solution)/shard_map/one_times/pallas_call | solution.py:186
  19.1 42.2 %all-to-all-done = f32[32,128,128]{2,1,0:T(8,128)} async-done(((f32[32,128,128]{2,1,0:T(8,128)}), f32[32,128,128]{2,1,0:T(8,128)}, u32[]{:S(2)}, u32[]{:S(2)}) %all-to-all-start) | async-done | bytes 2097184 | tf_op jit(solution)/shard_map/all_to_all | solution.py:588
  61.2 4.2 %all-to-all-start.1 = ((f32[32,64,128]{2,1,0:T(8,128)}), f32[32,64,128]{2,1,0:T(8,128)S(1)}, u32[]{:S(2)}, u32[]{:S(2)}) async-start(f32[32,64,128]{2,1,0:T(8,128)} %bitcast.13), calls=%async_computation.1 | async-start | bytes 2097152 | tf_op jit(solution)/shard_map/all_to_all | solution.py:588
  65.4 8.9 %both_middle.1 = (f32[2,2,8,8,128]{4,3,2,1,0:T(8,128)}, f32[2,2,8,8,128]{4,3,2,1,0:T(8,128)}, f32[2,2,8,8,128]{4,3,2,1,0:T(8,128)}, f32[2,2,8,8,128]{4,3,2,1,0:T...) custom-call(s32[1]{0:T(128)} %bitcast.5.me_ref, ...), custom_call_target="tpu_custom_call" | custom-call | tf_op jit(solution)/shard_map/both_middle/pallas_call | solution.py:434
  74.4 1.6 collective-permute-start
  76.0 2.4 %collective-permute-start.2 = (f32[2,2,8,8,128]{4,3,2,1,0:T(8,128)}, f32[2,2,8,8,128]{4,3,2,1,0:T(8,128)S(1)}, u32[]{:S(2)}, u32[]{:S(2)}) collective-permute-start(f32[2,2,8,8,128]{4,3,2,1,0:T(8,128)} %get-tuple-element.51), channel_id=1, source_target_pairs={{0,10},{1,11},{2,8},{3,9},{4,14},{5,15},{6,12},{7,13},{8,2},{9,3},... | collective-permute-start | bytes 393224 | tf_op jit(solution)/shard_map/ppermute | solution.py:594
  79.0 7.2 %collective-permute-done.refs_1_ = f32[2,2,8,8,128]{4,3,2,1,0:T(8,128)S(1)} collective-permute-done((f32[2,2,8,8,128]{4,3,2,1,0:T(8,128)}, f32[2,2,8,8,128]{4,3,2,1,0:T(8,128)S(1)}, u32[]{:S(2)}, u32[]{:S(2)}) %collective-permute-start) | collective-permute-done | bytes 131104 | tf_op jit(solution)/shard_map/ppermute | solution.py:594
  86.2 3.5 %collective-permute-start.5 = (f32[2,2,8,8,128]{4,3,2,1,0:T(8,128)}, f32[2,2,8,8,128]{4,3,2,1,0:T(8,128)S(1)}, u32[]{:S(2)}, u32[]{:S(2)}) collective-permute-start(f32[2,2,8,8,128]{4,3,2,1,0:T(8,128)} %get-tuple-element.55), channel_id=1, source_target_pairs={{0,12},{1,13},{2,14},{3,15},{4,8},{5,9},{6,10},{7,11},{8,4},{9,5},... | collective-permute-start | bytes 393224 | tf_op jit(solution)/shard_map/ppermute | solution.py:594
  89.7 2.5 %collective-permute-start.6 = (f32[2,2,8,8,128]{4,3,2,1,0:T(8,128)}, f32[2,2,8,8,128]{4,3,2,1,0:T(8,128)S(1)}, u32[]{:S(2)}, u32[]{:S(2)}) collective-permute-start(f32[2,2,8,8,128]{4,3,2,1,0:T(8,128)} %get-tuple-element.56), channel_id=1, source_target_pairs={{0,13},{1,12},{2,15},{3,14},{4,9},{5,8},{6,11},{7,10},{8,5},{9,4},... | collective-permute-start | bytes 393224 | tf_op jit(solution)/shard_map/ppermute | solution.py:594
  92.2 2.5 %collective-permute-done.2.refs_3_ = f32[2,2,8,8,128]{4,3,2,1,0:T(8,128)S(1)} collective-permute-done((f32[2,2,8,8,128]{4,3,2,1,0:T(8,128)}, f32[2,2,8,8,128]{4,3,2,1,0:T(8,128)S(1)}, u32[]{:S(2)}, u32[]{:S(2)}) %collective-permute-start.2) | collective-permute-done | bytes 131104 | tf_op jit(solution)/shard_map/ppermute | solution.py:594
  95.2 1.4 collective-permute-done.3.refs_4_
  96.6 0.8 collective-permute-start.8
  97.4 1.0 copy-done.1
  98.4 7.5 %one_middle.1 = f32[16,2,2,8,8,128]{5,4,3,2,1,0:T(8,128)} custom-call(s32[2,8]{1,0:T(2,128)} %bitcast.17, s32[3,16]{1,0:T(4,128)} %mirror_ref.3, bf16[256,256]{1,0:T(8,128)(2,1)} %constant.22.clone.ch_ref, bf16[256,256]{1,0:T(8,128)(2,1)} %constant.23.clone.cl_ref, bf16[256,256]{1,0:T(8,128)(2,1)} %constant.24.clone.sh_ref, ...), custom_call_target="tpu_custom_call" | custom-call | flops 6000000000 | bytes 12000000 | tf_op jit(solution)/shard_map/one_middle/pallas_call | solution.py:407
  106.1 0.6 copy-done.7
  106.8 5.3 %all-to-all-start.2 = ((f32[32,128,128]{2,1,0:T(8,128)}), f32[32,128,128]{2,1,0:T(8,128)S(1)}, u32[]{:S(2)}, u32[]{:S(2)}) async-start(f32[32,128,128]{2,1,0:T(8,128)} %bitcast.14), calls=%async_computation.2 | async-start | bytes 4194304 | tf_op jit(solution)/shard_map/all_to_all | solution.py:588
  112.2 2.4 %prepare.1.m_hbm = bf16[2,512,512]{2,1,0:T(8,128)(2,1)} custom-call(s32[1]{0:T(128)} %bitcast.5.me_ref, f32[2,16,8,512]{3,2,1,0:T(8,128)} %constant.26.clone.both_ref, f32[256,512]{1,0:T(8,128)} %constant.27.clone.one_ref), custom_call_target="tpu_custom_call" | custom-call | tf_op jit(solution)/shard_map/prepare/pallas_call | solution.py:463
  114.6 1.6 collective-permute-start.9
  116.2 2.4 %collective-permute-start.11 = (f32[2,2,8,8,128]{4,3,2,1,0:T(8,128)S(1)}, f32[2,2,8,8,128]{4,3,2,1,0:T(8,128)S(1)}, u32[]{:S(2)}, u32[]{:S(2)}) collective-permute-start(f32[2,2,8,8,128]{4,3,2,1,0:T(8,128)S(1)} %copy-done.20), channel_id=1, source_target_pairs={{0,6},{1,7},{2,4},{3,5},{4,2},{5,3},{6,0},{7,1},{8,14},{9,15},{10,... | collective-permute-start | bytes 393224 | tf_op jit(solution)/shard_map/ppermute | solution.py:594
  118.6 0.4 collective-permute-start.12
  119.0 3.4 %collective-permute-start.13 = (f32[2,2,8,8,128]{4,3,2,1,0:T(8,128)S(1)}, f32[2,2,8,8,128]{4,3,2,1,0:T(8,128)S(1)}, u32[]{:S(2)}, u32[]{:S(2)}) collective-permute-start(f32[2,2,8,8,128]{4,3,2,1,0:T(8,128)S(1)} %copy-done.18), channel_id=1, source_target_pairs={{0,14},{1,15},{2,12},{3,13},{4,10},{5,11},{6,8},{7,9},{8,6},{9,7},... | collective-permute-start | bytes 393224 | tf_op jit(solution)/shard_map/ppermute | solution.py:594
  122.4 24.5 %collective-permute-done.9.refs_10_ = f32[2,2,8,8,128]{4,3,2,1,0:T(8,128)S(1)} collective-permute-done((f32[2,2,8,8,128]{4,3,2,1,0:T(8,128)S(1)}, f32[2,2,8,8,128]{4,3,2,1,0:T(8,128)S(1)}, u32[]{:S(2)}, u32[]{:S(2)}) %collective-permute-start.9) | collective-permute-done | bytes 131104 | tf_op jit(solution)/shard_map/ppermute | solution.py:594
  146.8 2.2 %collective-permute-done.10.refs_11_ = f32[2,2,8,8,128]{4,3,2,1,0:T(8,128)S(1)} collective-permute-done((f32[2,2,8,8,128]{4,3,2,1,0:T(8,128)S(1)}, f32[2,2,8,8,128]{4,3,2,1,0:T(8,128)S(1)}, u32[]{:S(2)}, u32[]{:S(2)}) %collective-permute-start.10) | collective-permute-done | bytes 131104 | tf_op jit(solution)/shard_map/ppermute | solution.py:594
  149.0 1.5 collective-permute-done.13.refs_14_
  150.5 4.8 %collective-permute-done.14.refs_15_ = f32[2,2,8,8,128]{4,3,2,1,0:T(8,128)S(1)} collective-permute-done((f32[2,2,8,8,128]{4,3,2,1,0:T(8,128)S(1)}, f32[2,2,8,8,128]{4,3,2,1,0:T(8,128)S(1)}, u32[]{:S(2)}, u32[]{:S(2)}) %collective-permute-start.14) | collective-permute-done | bytes 131104 | tf_op jit(solution)/shard_map/ppermute | solution.py:594
  155.4 0.6 copy-done.16
  156.0 3.3 %fold.1.f_hbm = bf16[8,2,256,256]{3,2,1,0:T(8,128)(2,1)} custom-call(f32[2,2,8,8,128]{4,3,2,1,0:T(8,128)} %get-tuple-element.69.refs_0_, f32[2,2,8,8,128]{4,3,2,1,0:T(8,128)} %copy-done.2, f32[2,2,8,8,128]{4,3,2,1,0:T(8,128)} %copy-done.3, f32[2,2,8,8,128]{4,3,2,1,0:T(8,128)} %copy-done.4, f32[2,2,8,8,128]{4,3,2,1,0:T(8,128)} %copy-done.5, ...), custom_call_target="tpu_custom_call" | custom-call | tf_op jit(solution)/shard_map/fold/pallas_call | solution.py:500
  159.3 2.0 %all-to-all-done.2 = f32[32,128,128]{2,1,0:T(8,128)S(1)} async-done(((f32[32,128,128]{2,1,0:T(8,128)}), f32[32,128,128]{2,1,0:T(8,128)S(1)}, u32[]{:S(2)}, u32[]{:S(2)}) %all-to-all-start.2) | async-done | bytes 2097184 | tf_op jit(solution)/shard_map/all_to_all | solution.py:588
  161.3 1.3 copy-done
  162.6 8.3 %to_frequencies.1 = f32[2,8,128,512]{3,2,1,0:T(8,128)} custom-call(f32[32,2,8,8,128]{4,3,2,1,0:T(8,128)} %bitcast.12, bf16[2,512,512]{2,1,0:T(8,128)(2,1)} %prepare.1.m_hbm, bf16[8,2,256,256]{3,2,1,0:T(8,128)(2,1)} %fold.1.f_hbm), custom_call_target="tpu_custom_call" | custom-call | tf_op jit(solution)/shard_map/to_frequencies/pallas_call | solution.py:568
  (57 shorter events, 1.3 us)
Async XLA Ops:
  4.9 56.3 %all-to-all-start = ((f32[32,128,128]{2,1,0:T(8,128)}), f32[32,128,128]{2,1,0:T(8,128)}, u32[]{:S(2)}, u32[]{:S(2)}) async-start(f32[32,128,128]{2,1,0:T(8,128)} %bitcast.11), calls=%async_computation | async-start | bytes 4194304 | tf_op jit(solution)/shard_map/all_to_all | solution.py:588
  61.2 36.2 %all-to-all-start.1 = ((f32[32,64,128]{2,1,0:T(8,128)}), f32[32,64,128]{2,1,0:T(8,128)S(1)}, u32[]{:S(2)}, u32[]{:S(2)}) async-start(f32[32,64,128]{2,1,0:T(8,128)} %bitcast.13), calls=%async_computation.1 | async-start | bytes 2097152 | tf_op jit(solution)/shard_map/all_to_all | solution.py:588
  74.4 11.8 %collective-permute-start = (f32[2,2,8,8,128]{4,3,2,1,0:T(8,128)}, f32[2,2,8,8,128]{4,3,2,1,0:T(8,128)S(1)}, u32[]{:S(2)}, u32[]{:S(2)}) collective-permute-start(f32[2,2,8,8,128]{4,3,2,1,0:T(8,128)} %get-tuple-element.49), channel_id=1, source_target_pairs={{0,8},{1,9},{2,10},{3,11},{4,12},{5,13},{6,14},{7,15},{8,0},{9,1},... | collective-permute-start | bytes 393224 | tf_op jit(solution)/shard_map/ppermute | solution.py:594
  76.0 13.7 %collective-permute-start.1 = (f32[2,2,8,8,128]{4,3,2,1,0:T(8,128)}, f32[2,2,8,8,128]{4,3,2,1,0:T(8,128)S(1)}, u32[]{:S(2)}, u32[]{:S(2)}) collective-permute-start(f32[2,2,8,8,128]{4,3,2,1,0:T(8,128)} %get-tuple-element.50), channel_id=1, source_target_pairs={{0,9},{1,8},{2,11},{3,10},{4,13},{5,12},{6,15},{7,14},{8,1},{9,0},... | collective-permute-start | bytes 393224 | tf_op jit(solution)/shard_map/ppermute | solution.py:594
  76.0 18.7 %collective-permute-start.2 = (f32[2,2,8,8,128]{4,3,2,1,0:T(8,128)}, f32[2,2,8,8,128]{4,3,2,1,0:T(8,128)S(1)}, u32[]{:S(2)}, u32[]{:S(2)}) collective-permute-start(f32[2,2,8,8,128]{4,3,2,1,0:T(8,128)} %get-tuple-element.51), channel_id=1, source_target_pairs={{0,10},{1,11},{2,8},{3,9},{4,14},{5,15},{6,12},{7,13},{8,2},{9,3},... | collective-permute-start | bytes 393224 | tf_op jit(solution)/shard_map/ppermute | solution.py:594
  78.4 18.2 %collective-permute-start.3 = (f32[2,2,8,8,128]{4,3,2,1,0:T(8,128)}, f32[2,2,8,8,128]{4,3,2,1,0:T(8,128)S(1)}, u32[]{:S(2)}, u32[]{:S(2)}) collective-permute-start(f32[2,2,8,8,128]{4,3,2,1,0:T(8,128)} %get-tuple-element.52), channel_id=1, source_target_pairs={{0,11},{1,10},{2,9},{3,8},{4,15},{5,14},{6,13},{7,12},{8,3},{9,2},... | collective-permute-start | bytes 393224 | tf_op jit(solution)/shard_map/ppermute | solution.py:594
  78.8 18.6 %collective-permute-start.4 = (f32[2,2,8,8,128]{4,3,2,1,0:T(8,128)}, f32[2,2,8,8,128]{4,3,2,1,0:T(8,128)S(1)}, u32[]{:S(2)}, u32[]{:S(2)}) collective-permute-start(f32[2,2,8,8,128]{4,3,2,1,0:T(8,128)} %get-tuple-element.53), channel_id=1, source_target_pairs={{0,1},{1,0},{2,3},{3,2},{4,5},{5,4},{6,7},{7,6},{8,9},{9,8},{10,11... | collective-permute-start | bytes 393224 | tf_op jit(solution)/shard_map/ppermute | solution.py:594
  86.2 19.8 %copy-start.2 = (f32[2,2,8,8,128]{4,3,2,1,0:T(8,128)}, f32[2,2,8,8,128]{4,3,2,1,0:T(8,128)S(1)}, u32[]{:S(2)}) copy-start(f32[2,2,8,8,128]{4,3,2,1,0:T(8,128)S(1)} %collective-permute-done.refs_1_) | copy-start | bytes 393220
  86.2 19.8 %collective-permute-start.5 = (f32[2,2,8,8,128]{4,3,2,1,0:T(8,128)}, f32[2,2,8,8,128]{4,3,2,1,0:T(8,128)S(1)}, u32[]{:S(2)}, u32[]{:S(2)}) collective-permute-start(f32[2,2,8,8,128]{4,3,2,1,0:T(8,128)} %get-tuple-element.55), channel_id=1, source_target_pairs={{0,12},{1,13},{2,14},{3,15},{4,8},{5,9},{6,10},{7,11},{8,4},{9,5},... | collective-permute-start | bytes 393224 | tf_op jit(solution)/shard_map/ppermute | solution.py:594
  89.7 16.3 %copy-start.3 = (f32[2,2,8,8,128]{4,3,2,1,0:T(8,128)}, f32[2,2,8,8,128]{4,3,2,1,0:T(8,128)S(1)}, u32[]{:S(2)}) copy-start(f32[2,2,8,8,128]{4,3,2,1,0:T(8,128)S(1)} %collective-permute-done.1.refs_2_) | copy-start | bytes 393220
  89.7 16.3 %collective-permute-start.6 = (f32[2,2,8,8,128]{4,3,2,1,0:T(8,128)}, f32[2,2,8,8,128]{4,3,2,1,0:T(8,128)S(1)}, u32[]{:S(2)}, u32[]{:S(2)}) collective-permute-start(f32[2,2,8,8,128]{4,3,2,1,0:T(8,128)} %get-tuple-element.56), channel_id=1, source_target_pairs={{0,13},{1,12},{2,15},{3,14},{4,9},{5,8},{6,11},{7,10},{8,5},{9,4},... | collective-permute-start | bytes 393224 | tf_op jit(solution)/shard_map/ppermute | solution.py:594
  94.8 11.2 %copy-start.4 = (f32[2,2,8,8,128]{4,3,2,1,0:T(8,128)}, f32[2,2,8,8,128]{4,3,2,1,0:T(8,128)S(1)}, u32[]{:S(2)}) copy-start(f32[2,2,8,8,128]{4,3,2,1,0:T(8,128)S(1)} %collective-permute-done.2.refs_3_) | copy-start | bytes 393220
  94.8 11.3 %collective-permute-start.7 = (f32[2,2,8,8,128]{4,3,2,1,0:T(8,128)}, f32[2,2,8,8,128]{4,3,2,1,0:T(8,128)S(1)}, u32[]{:S(2)}, u32[]{:S(2)}) collective-permute-start(f32[2,2,8,8,128]{4,3,2,1,0:T(8,128)} %get-tuple-element.57), channel_id=1, source_target_pairs={{0,2},{1,3},{2,0},{3,1},{4,6},{5,7},{6,4},{7,5},{8,10},{9,11},{10,... | collective-permute-start | bytes 393224 | tf_op jit(solution)/shard_map/ppermute | solution.py:594
  96.6 9.4 %copy-start.5 = (f32[2,2,8,8,128]{4,3,2,1,0:T(8,128)}, f32[2,2,8,8,128]{4,3,2,1,0:T(8,128)S(1)}, u32[]{:S(2)}) copy-start(f32[2,2,8,8,128]{4,3,2,1,0:T(8,128)S(1)} %collective-permute-done.3.refs_4_) | copy-start | bytes 393220
  96.6 9.5 %collective-permute-start.8 = (f32[2,2,8,8,128]{4,3,2,1,0:T(8,128)}, f32[2,2,8,8,128]{4,3,2,1,0:T(8,128)S(1)}, u32[]{:S(2)}, u32[]{:S(2)}) collective-permute-start(f32[2,2,8,8,128]{4,3,2,1,0:T(8,128)} %get-tuple-element.58), channel_id=1, source_target_pairs={{0,3},{1,2},{2,1},{3,0},{4,7},{5,6},{6,5},{7,4},{8,11},{9,10},{10,... | collective-permute-start | bytes 393224 | tf_op jit(solution)/shard_map/ppermute | solution.py:594
  97.4 8.6 %copy-start.6 = (f32[2,2,8,8,128]{4,3,2,1,0:T(8,128)}, f32[2,2,8,8,128]{4,3,2,1,0:T(8,128)S(1)}, u32[]{:S(2)}) copy-start(f32[2,2,8,8,128]{4,3,2,1,0:T(8,128)S(1)} %collective-permute-done.4.refs_5_) | copy-start | bytes 393220
  106.8 54.5 %all-to-all-start.2 = ((f32[32,128,128]{2,1,0:T(8,128)}), f32[32,128,128]{2,1,0:T(8,128)S(1)}, u32[]{:S(2)}, u32[]{:S(2)}) async-start(f32[32,128,128]{2,1,0:T(8,128)} %bitcast.14), calls=%async_computation.2 | async-start | bytes 4194304 | tf_op jit(solution)/shard_map/all_to_all | solution.py:588
  112.1 4.0 %copy-start.21 = (f32[2,2,8,8,128]{4,3,2,1,0:T(8,128)S(1)}, f32[2,2,8,8,128]{4,3,2,1,0:T(8,128)}, u32[]{:S(2)}) copy-start(f32[2,2,8,8,128]{4,3,2,1,0:T(8,128)} %get-tuple-element.80) | copy-start | bytes 393220
  112.1 6.4 %copy-start.19 = (f32[2,2,8,8,128]{4,3,2,1,0:T(8,128)S(1)}, f32[2,2,8,8,128]{4,3,2,1,0:T(8,128)}, u32[]{:S(2)}) copy-start(f32[2,2,8,8,128]{4,3,2,1,0:T(8,128)} %get-tuple-element.82) | copy-start | bytes 393220
  112.2 6.9 %copy-start.18 = (f32[2,2,8,8,128]{4,3,2,1,0:T(8,128)S(1)}, f32[2,2,8,8,128]{4,3,2,1,0:T(8,128)}, u32[]{:S(2)}) copy-start(f32[2,2,8,8,128]{4,3,2,1,0:T(8,128)} %get-tuple-element.83) | copy-start | bytes 393220
  112.2 34.7 %copy-start.17 = (f32[2,2,8,8,128]{4,3,2,1,0:T(8,128)S(1)}, f32[2,2,8,8,128]{4,3,2,1,0:T(8,128)}, u32[]{:S(2)}) copy-start(f32[2,2,8,8,128]{4,3,2,1,0:T(8,128)} %get-tuple-element.84) | copy-start | bytes 393220
  114.6 32.2 %collective-permute-start.9 = (f32[2,2,8,8,128]{4,3,2,1,0:T(8,128)S(1)}, f32[2,2,8,8,128]{4,3,2,1,0:T(8,128)S(1)}, u32[]{:S(2)}, u32[]{:S(2)}) collective-permute-start(f32[2,2,8,8,128]{4,3,2,1,0:T(8,128)S(1)} %copy-done.22), channel_id=1, source_target_pairs={{0,4},{1,5},{2,6},{3,7},{4,0},{5,1},{6,2},{7,3},{8,12},{9,13},{10,... | collective-permute-start | bytes 393224 | tf_op jit(solution)/shard_map/ppermute | solution.py:594
  116.2 32.8 %collective-permute-start.10 = (f32[2,2,8,8,128]{4,3,2,1,0:T(8,128)S(1)}, f32[2,2,8,8,128]{4,3,2,1,0:T(8,128)S(1)}, u32[]{:S(2)}, u32[]{:S(2)}) collective-permute-start(f32[2,2,8,8,128]{4,3,2,1,0:T(8,128)S(1)} %copy-done.21), channel_id=1, source_target_pairs={{0,5},{1,4},{2,7},{3,6},{4,1},{5,0},{6,3},{7,2},{8,13},{9,12},{10,... | collective-permute-start | bytes 393224 | tf_op jit(solution)/shard_map/ppermute | solution.py:594
  116.2 32.8 %collective-permute-start.11 = (f32[2,2,8,8,128]{4,3,2,1,0:T(8,128)S(1)}, f32[2,2,8,8,128]{4,3,2,1,0:T(8,128)S(1)}, u32[]{:S(2)}, u32[]{:S(2)}) collective-permute-start(f32[2,2,8,8,128]{4,3,2,1,0:T(8,128)S(1)} %copy-done.20), channel_id=1, source_target_pairs={{0,6},{1,7},{2,4},{3,5},{4,2},{5,3},{6,0},{7,1},{8,14},{9,15},{10,... | collective-permute-start | bytes 393224 | tf_op jit(solution)/shard_map/ppermute | solution.py:594
  118.6 30.4 %collective-permute-start.12 = (f32[2,2,8,8,128]{4,3,2,1,0:T(8,128)S(1)}, f32[2,2,8,8,128]{4,3,2,1,0:T(8,128)S(1)}, u32[]{:S(2)}, u32[]{:S(2)}) collective-permute-start(f32[2,2,8,8,128]{4,3,2,1,0:T(8,128)S(1)} %copy-done.19), channel_id=1, source_target_pairs={{0,7},{1,6},{2,5},{3,4},{4,3},{5,2},{6,1},{7,0},{8,15},{9,14},{10,... | collective-permute-start | bytes 393224 | tf_op jit(solution)/shard_map/ppermute | solution.py:594
  119.0 31.5 %collective-permute-start.13 = (f32[2,2,8,8,128]{4,3,2,1,0:T(8,128)S(1)}, f32[2,2,8,8,128]{4,3,2,1,0:T(8,128)S(1)}, u32[]{:S(2)}, u32[]{:S(2)}) collective-permute-start(f32[2,2,8,8,128]{4,3,2,1,0:T(8,128)S(1)} %copy-done.18), channel_id=1, source_target_pairs={{0,14},{1,15},{2,12},{3,13},{4,10},{5,11},{6,8},{7,9},{8,6},{9,7},... | collective-permute-start | bytes 393224 | tf_op jit(solution)/shard_map/ppermute | solution.py:594
  146.8 8.5 %copy-start.11 = (f32[2,2,8,8,128]{4,3,2,1,0:T(8,128)}, f32[2,2,8,8,128]{4,3,2,1,0:T(8,128)S(1)}, u32[]{:S(2)}) copy-start(f32[2,2,8,8,128]{4,3,2,1,0:T(8,128)S(1)} %collective-permute-done.9.refs_10_) | copy-start | bytes 393220
  146.8 8.5 %collective-permute-start.14 = (f32[2,2,8,8,128]{4,3,2,1,0:T(8,128)S(1)}, f32[2,2,8,8,128]{4,3,2,1,0:T(8,128)S(1)}, u32[]{:S(2)}, u32[]{:S(2)}) collective-permute-start(f32[2,2,8,8,128]{4,3,2,1,0:T(8,128)S(1)} %copy-done.17), channel_id=1, source_target_pairs={{0,15},{1,14},{2,13},{3,12},{4,11},{5,10},{6,9},{7,8},{8,7},{9,6},... | collective-permute-start | bytes 393224 | tf_op jit(solution)/shard_map/ppermute | solution.py:594
  149.0 6.3 %copy-start.12 = (f32[2,2,8,8,128]{4,3,2,1,0:T(8,128)}, f32[2,2,8,8,128]{4,3,2,1,0:T(8,128)S(1)}, u32[]{:S(2)}) copy-start(f32[2,2,8,8,128]{4,3,2,1,0:T(8,128)S(1)} %collective-permute-done.10.refs_11_) | copy-start | bytes 393220
  149.0 6.3 %copy-start.13 = (f32[2,2,8,8,128]{4,3,2,1,0:T(8,128)}, f32[2,2,8,8,128]{4,3,2,1,0:T(8,128)S(1)}, u32[]{:S(2)}) copy-start(f32[2,2,8,8,128]{4,3,2,1,0:T(8,128)S(1)} %collective-permute-done.11.refs_12_) | copy-start | bytes 393220
  149.0 6.3 %copy-start.14 = (f32[2,2,8,8,128]{4,3,2,1,0:T(8,128)}, f32[2,2,8,8,128]{4,3,2,1,0:T(8,128)S(1)}, u32[]{:S(2)}) copy-start(f32[2,2,8,8,128]{4,3,2,1,0:T(8,128)S(1)} %collective-permute-done.12.refs_13_) | copy-start | bytes 393220
  150.5 4.8 %copy-start.15 = (f32[2,2,8,8,128]{4,3,2,1,0:T(8,128)}, f32[2,2,8,8,128]{4,3,2,1,0:T(8,128)S(1)}, u32[]{:S(2)}) copy-start(f32[2,2,8,8,128]{4,3,2,1,0:T(8,128)S(1)} %collective-permute-done.13.refs_14_) | copy-start | bytes 393220
  (9 other events, 12.3 us)

commit v14 on v13

--- a/solution.py
+++ b/solution.py
@@ -419,7 +419,7 @@
             pltpu.VMEM((GROUPS, side, 2, 2, components // GROUPS, rows, lanes), jnp.float32),
             pltpu.SemaphoreType.DMA((GROUPS,)),
         ],
-        compiler_params=pltpu.CompilerParams(vmem_limit_bytes=59500 << 10),
+        compiler_params=pltpu.CompilerParams(vmem_limit_bytes=45056 << 10),
         cost_estimate=pl.CostEstimate(flops=6_000_000_000, bytes_accessed=12_000_000, transcendentals=0),
         name="one_middle",
     )(*args)
@@ -578,7 +578,7 @@
             pltpu.SemaphoreType.DMA((groups,)),
             pltpu.SemaphoreType.DMA((groups,)),
         ],
-        compiler_params=pltpu.CompilerParams(vmem_limit_bytes=59400 << 10),
+        compiler_params=pltpu.CompilerParams(vmem_limit_bytes=56320 << 10),
         name="to_frequencies",
     )(y, matrix, folded)
 

time: 172 us -> 170 us (0.988)
    unnamed x46 -> x56, local copies, waits for them, and re-layouts: 3.76 us -> 2.78 us
  transfers between devices with their start and end apart: 18 -> 18, of which waited for: 9 -> 9; matrix products, arithmetic and copies ran while one was open for 0% -> 0% of each run, Pallas kernels for 17% -> 16%
where the time goes in v14:
time: 170 us; the launch traced here: 169 us
  waiting for transfers between devices  88.3 us (52%)
  Pallas kernels  41.2 us (24%)
  starting transfers between devices  36.6 us (22%)
  local copies, waits for them, and re-layouts  2.78 us (2%)
    all_to_all x3, waiting for transfers between devices, exchange(): lax.all_to_all(flat, 'kb', split_axis=0, concat_axis=0, tiled=True)  44.2 us
    ppermute x15, waiting for transfers between devices, swap(): lax.ppermute(piece, 'kb', [(device, device ^ slot) for device in range(de...  44.1 us
    ppermute x15, starting transfers between devices, swap(): lax.ppermute(piece, 'kb', [(device, device ^ slot) for device in range(de...  19.7 us
    all_to_all x3, starting transfers between devices, exchange(): lax.all_to_all(flat, 'kb', split_axis=0, concat_axis=0, tiled=True)  16.9 us
    pallas_call x2, Pallas kernels, to_times(): pl.pallas_call(kernel, in_specs=[hbm, hbm], out_specs=hbm, out_shape=jax....  11.6 us
    pallas_call x1, Pallas kernels, both_middle(): pl.pallas_call(both_middle_kernel, in_specs=[pl.BlockSpec(memory_space=pl...  8.93 us
    pallas_call x1, Pallas kernels, to_frequencies(): pl.pallas_call(frequency_kernel, in_specs=[pl.BlockSpec(memory_space=pltp...  8.32 us
    pallas_call x1, Pallas kernels, one_middle(): pl.pallas_call(one_middle_kernel, in_specs=specs, out_specs=pl.BlockSpec(...  6.58 us
  transfers between devices with their start and end apart: 18, of which 9 were waited for; matrix products, arithmetic and copies ran while one was open for 0% of the time, Pallas kernels for 16%

profile of v14, /device:TPU:0, one launch (start us, length us, event | category | flops | bytes accessed | tf_op | source)
XLA Modules:
  0.0 169.3 jit_solution(897459927147617922)
XLA Ops:
  0.0 4.9 %both_times.1 = f32[32,2,2,4,8,128]{5,4,3,2,1,0:T(8,128)} custom-call(f32[2,4,128,512]{3,2,1,0:T(8,128)} %g_hbm.2, f32[256,512]{1,0:T(8,128)} %constant.20.clone.m_hbm), custom_call_target="tpu_custom_call" | custom-call | tf_op jit(solution)/shard_map/both_times/pallas_call | solution.py:186
  4.9 7.4 %all-to-all-start = ((f32[32,128,128]{2,1,0:T(8,128)}), f32[32,128,128]{2,1,0:T(8,128)}, u32[]{:S(2)}, u32[]{:S(2)}) async-start(f32[32,128,128]{2,1,0:T(8,128)} %bitcast.14), calls=%async_computation | async-start | bytes 4194304 | tf_op jit(solution)/shard_map/all_to_all | solution.py:588
  12.3 6.7 %one_times.1 = f32[32,2,4,8,128]{4,3,2,1,0:T(8,128)} custom-call(f32[2,4,128,512]{3,2,1,0:T(8,128)} %g_hbm.2, f32[512,512]{1,0:T(8,128)} %constant.21.clone.m_hbm), custom_call_target="tpu_custom_call" | custom-call | tf_op jit(solution)/shard_map/one_times/pallas_call | solution.py:186
  19.1 42.2 %all-to-all-done = f32[32,128,128]{2,1,0:T(8,128)} async-done(((f32[32,128,128]{2,1,0:T(8,128)}), f32[32,128,128]{2,1,0:T(8,128)}, u32[]{:S(2)}, u32[]{:S(2)}) %all-to-all-start) | async-done | bytes 2097184 | tf_op jit(solution)/shard_map/all_to_all | solution.py:588
  61.3 4.2 %all-to-all-start.1 = ((f32[32,64,128]{2,1,0:T(8,128)}), f32[32,64,128]{2,1,0:T(8,128)S(1)}, u32[]{:S(2)}, u32[]{:S(2)}) async-start(f32[32,64,128]{2,1,0:T(8,128)} %bitcast.16), calls=%async_computation.1 | async-start | bytes 2097152 | tf_op jit(solution)/shard_map/all_to_all | solution.py:588
  65.5 8.9 %both_middle.1 = (f32[2,2,8,8,128]{4,3,2,1,0:T(8,128)}, f32[2,2,8,8,128]{4,3,2,1,0:T(8,128)}, f32[2,2,8,8,128]{4,3,2,1,0:T(8,128)}, f32[2,2,8,8,128]{4,3,2,1,0:T...) custom-call(s32[1]{0:T(128)} %bitcast.5.me_ref, ...), custom_call_target="tpu_custom_call" | custom-call | tf_op jit(solution)/shard_map/both_middle/pallas_call | solution.py:434
  74.4 1.6 collective-permute-start
  76.0 2.4 %collective-permute-start.2 = (f32[2,2,8,8,128]{4,3,2,1,0:T(8,128)}, f32[2,2,8,8,128]{4,3,2,1,0:T(8,128)S(1)}, u32[]{:S(2)}, u32[]{:S(2)}) collective-permute-start(f32[2,2,8,8,128]{4,3,2,1,0:T(8,128)} %get-tuple-element.51), channel_id=1, source_target_pairs={{0,10},{1,11},{2,8},{3,9},{4,14},{5,15},{6,12},{7,13},{8,2},{9,3},... | collective-permute-start | bytes 393224 | tf_op jit(solution)/shard_map/ppermute | solution.py:594
  79.1 7.2 %collective-permute-done.refs_1_ = f32[2,2,8,8,128]{4,3,2,1,0:T(8,128)S(1)} collective-permute-done((f32[2,2,8,8,128]{4,3,2,1,0:T(8,128)}, f32[2,2,8,8,128]{4,3,2,1,0:T(8,128)S(1)}, u32[]{:S(2)}, u32[]{:S(2)}) %collective-permute-start) | collective-permute-done | bytes 131104 | tf_op jit(solution)/shard_map/ppermute | solution.py:594
  86.3 3.5 %collective-permute-start.5 = (f32[2,2,8,8,128]{4,3,2,1,0:T(8,128)}, f32[2,2,8,8,128]{4,3,2,1,0:T(8,128)S(1)}, u32[]{:S(2)}, u32[]{:S(2)}) collective-permute-start(f32[2,2,8,8,128]{4,3,2,1,0:T(8,128)} %get-tuple-element.55), channel_id=1, source_target_pairs={{0,12},{1,13},{2,14},{3,15},{4,8},{5,9},{6,10},{7,11},{8,4},{9,5},... | collective-permute-start | bytes 393224 | tf_op jit(solution)/shard_map/ppermute | solution.py:594
  89.7 2.5 %collective-permute-start.6 = (f32[2,2,8,8,128]{4,3,2,1,0:T(8,128)}, f32[2,2,8,8,128]{4,3,2,1,0:T(8,128)S(1)}, u32[]{:S(2)}, u32[]{:S(2)}) collective-permute-start(f32[2,2,8,8,128]{4,3,2,1,0:T(8,128)} %get-tuple-element.56), channel_id=1, source_target_pairs={{0,13},{1,12},{2,15},{3,14},{4,9},{5,8},{6,11},{7,10},{8,5},{9,4},... | collective-permute-start | bytes 393224 | tf_op jit(solution)/shard_map/ppermute | solution.py:594
  92.3 2.5 %collective-permute-done.2.refs_3_ = f32[2,2,8,8,128]{4,3,2,1,0:T(8,128)S(1)} collective-permute-done((f32[2,2,8,8,128]{4,3,2,1,0:T(8,128)}, f32[2,2,8,8,128]{4,3,2,1,0:T(8,128)S(1)}, u32[]{:S(2)}, u32[]{:S(2)}) %collective-permute-start.2) | collective-permute-done | bytes 131104 | tf_op jit(solution)/shard_map/ppermute | solution.py:594
  94.8 0.4 collective-permute-start.7
  95.2 1.4 collective-permute-done.3.refs_4_
  96.7 0.8 collective-permute-start.8
  97.5 6.6 %one_middle.1 = f32[16,2,2,8,8,128]{5,4,3,2,1,0:T(8,128)} custom-call(s32[2,8]{1,0:T(2,128)S(1)} %bitcast.13, s32[3,16]{1,0:T(4,128)S(1)} %copy-done.4, bf16[256,256]{1,0:T(8,128)(2,1)S(1)} %copy-done.3, bf16[256,256]{1,0:T(8,128)(2,1)S(1)} %copy-done.2, bf16[256,256]{1,0:T(8,128)(2,1)S(1)} %copy-done.1, bf16[256,256]{1,0:T(8,128)(2,1)S(1)} %copy-done, ...), custom_call_target="tpu_custom_call" | custom-call | flops 6000000000 | bytes 12000000 | tf_op jit(solution)/shard_map/one_middle/pallas_call | solution.py:407
  104.2 0.6 copy-done.12
  105.0 5.3 %all-to-all-start.2 = ((f32[32,128,128]{2,1,0:T(8,128)}), f32[32,128,128]{2,1,0:T(8,128)S(1)}, u32[]{:S(2)}, u32[]{:S(2)}) async-start(f32[32,128,128]{2,1,0:T(8,128)} %bitcast.9), calls=%async_computation.2 | async-start | bytes 4194304 | tf_op jit(solution)/shard_map/all_to_all | solution.py:588
  110.3 2.4 %prepare.1.m_hbm = bf16[2,512,512]{2,1,0:T(8,128)(2,1)} custom-call(s32[1]{0:T(128)} %bitcast.5.me_ref, f32[2,16,8,512]{3,2,1,0:T(8,128)} %constant.26.clone.both_ref, f32[256,512]{1,0:T(8,128)} %constant.27.clone.one_ref), custom_call_target="tpu_custom_call" | custom-call | tf_op jit(solution)/shard_map/prepare/pallas_call | solution.py:463
  112.8 1.6 collective-permute-start.9
  114.3 2.4 %collective-permute-start.11 = (f32[2,2,8,8,128]{4,3,2,1,0:T(8,128)S(1)}, f32[2,2,8,8,128]{4,3,2,1,0:T(8,128)S(1)}, u32[]{:S(2)}, u32[]{:S(2)}) collective-permute-start(f32[2,2,8,8,128]{4,3,2,1,0:T(8,128)S(1)} %copy-done.25), channel_id=1, source_target_pairs={{0,6},{1,7},{2,4},{3,5},{4,2},{5,3},{6,0},{7,1},{8,14},{9,15},{10,... | collective-permute-start | bytes 393224 | tf_op jit(solution)/shard_map/ppermute | solution.py:594
  116.7 0.4 collective-permute-start.12
  117.2 3.4 %collective-permute-start.13 = (f32[2,2,8,8,128]{4,3,2,1,0:T(8,128)S(1)}, f32[2,2,8,8,128]{4,3,2,1,0:T(8,128)S(1)}, u32[]{:S(2)}, u32[]{:S(2)}) collective-permute-start(f32[2,2,8,8,128]{4,3,2,1,0:T(8,128)S(1)} %copy-done.23), channel_id=1, source_target_pairs={{0,14},{1,15},{2,12},{3,13},{4,10},{5,11},{6,8},{7,9},{8,6},{9,7},... | collective-permute-start | bytes 393224 | tf_op jit(solution)/shard_map/ppermute | solution.py:594
  120.5 24.5 %collective-permute-done.9.refs_10_ = f32[2,2,8,8,128]{4,3,2,1,0:T(8,128)S(1)} collective-permute-done((f32[2,2,8,8,128]{4,3,2,1,0:T(8,128)S(1)}, f32[2,2,8,8,128]{4,3,2,1,0:T(8,128)S(1)}, u32[]{:S(2)}, u32[]{:S(2)}) %collective-permute-start.9) | collective-permute-done | bytes 131104 | tf_op jit(solution)/shard_map/ppermute | solution.py:594
  145.0 2.2 %collective-permute-done.10.refs_11_ = f32[2,2,8,8,128]{4,3,2,1,0:T(8,128)S(1)} collective-permute-done((f32[2,2,8,8,128]{4,3,2,1,0:T(8,128)S(1)}, f32[2,2,8,8,128]{4,3,2,1,0:T(8,128)S(1)}, u32[]{:S(2)}, u32[]{:S(2)}) %collective-permute-start.10) | collective-permute-done | bytes 131104 | tf_op jit(solution)/shard_map/ppermute | solution.py:594
  147.2 1.5 collective-permute-done.13.refs_14_
  148.7 4.8 %collective-permute-done.14.refs_15_ = f32[2,2,8,8,128]{4,3,2,1,0:T(8,128)S(1)} collective-permute-done((f32[2,2,8,8,128]{4,3,2,1,0:T(8,128)S(1)}, f32[2,2,8,8,128]{4,3,2,1,0:T(8,128)S(1)}, u32[]{:S(2)}, u32[]{:S(2)}) %collective-permute-start.14) | collective-permute-done | bytes 131104 | tf_op jit(solution)/shard_map/ppermute | solution.py:594
  153.5 0.6 copy-done.21
  154.1 3.3 %fold.1.f_hbm = bf16[8,2,256,256]{3,2,1,0:T(8,128)(2,1)} custom-call(f32[2,2,8,8,128]{4,3,2,1,0:T(8,128)} %get-tuple-element.69.refs_0_, f32[2,2,8,8,128]{4,3,2,1,0:T(8,128)} %copy-done.7, f32[2,2,8,8,128]{4,3,2,1,0:T(8,128)} %copy-done.8, f32[2,2,8,8,128]{4,3,2,1,0:T(8,128)} %copy-done.9, f32[2,2,8,8,128]{4,3,2,1,0:T(8,128)} %copy-done.10, ...), custom_call_target="tpu_custom_call" | custom-call | tf_op jit(solution)/shard_map/fold/pallas_call | solution.py:500
  157.4 2.0 %all-to-all-done.2 = f32[32,128,128]{2,1,0:T(8,128)S(1)} async-done(((f32[32,128,128]{2,1,0:T(8,128)}), f32[32,128,128]{2,1,0:T(8,128)S(1)}, u32[]{:S(2)}, u32[]{:S(2)}) %all-to-all-start.2) | async-done | bytes 2097184 | tf_op jit(solution)/shard_map/all_to_all | solution.py:588
  159.4 1.3 copy-done.6
  160.8 8.3 %to_frequencies.1 = f32[2,8,128,512]{3,2,1,0:T(8,128)} custom-call(f32[32,2,8,8,128]{4,3,2,1,0:T(8,128)} %bitcast.15, bf16[2,512,512]{2,1,0:T(8,128)(2,1)} %prepare.1.m_hbm, bf16[8,2,256,256]{3,2,1,0:T(8,128)(2,1)} %fold.1.f_hbm), custom_call_target="tpu_custom_call" | custom-call | tf_op jit(solution)/shard_map/to_frequencies/pallas_call | solution.py:568
  (67 shorter events, 0.9 us)
Async XLA Ops:
  4.9 56.3 %all-to-all-start = ((f32[32,128,128]{2,1,0:T(8,128)}), f32[32,128,128]{2,1,0:T(8,128)}, u32[]{:S(2)}, u32[]{:S(2)}) async-start(f32[32,128,128]{2,1,0:T(8,128)} %bitcast.14), calls=%async_computation | async-start | bytes 4194304 | tf_op jit(solution)/shard_map/all_to_all | solution.py:588
  61.2 36.2 %copy-start = (bf16[256,256]{1,0:T(8,128)(2,1)S(1)}, bf16[256,256]{1,0:T(8,128)(2,1)}, u32[]{:S(2)}) copy-start(bf16[256,256]{1,0:T(8,128)(2,1)} %constant.25.clone.sl_ref) | copy-start | bytes 393220
  61.2 36.3 %copy-start.1 = (bf16[256,256]{1,0:T(8,128)(2,1)S(1)}, bf16[256,256]{1,0:T(8,128)(2,1)}, u32[]{:S(2)}) copy-start(bf16[256,256]{1,0:T(8,128)(2,1)} %constant.24.clone.sh_ref) | copy-start | bytes 393220
  61.2 36.3 %copy-start.2 = (bf16[256,256]{1,0:T(8,128)(2,1)S(1)}, bf16[256,256]{1,0:T(8,128)(2,1)}, u32[]{:S(2)}) copy-start(bf16[256,256]{1,0:T(8,128)(2,1)} %constant.23.clone.cl_ref) | copy-start | bytes 393220
  61.2 36.3 %copy-start.3 = (bf16[256,256]{1,0:T(8,128)(2,1)S(1)}, bf16[256,256]{1,0:T(8,128)(2,1)}, u32[]{:S(2)}) copy-start(bf16[256,256]{1,0:T(8,128)(2,1)} %constant.22.clone.ch_ref) | copy-start | bytes 393220
  61.2 36.3 %copy-start.4 = (s32[3,16]{1,0:T(4,128)S(1)}, s32[3,16]{1,0:T(4,128)}, u32[]{:S(2)}) copy-start(s32[3,16]{1,0:T(4,128)} %mirror_ref.3) | copy-start | bytes 580
  61.2 36.3 %copy-start.5 = (s32[8,2]{0,1:T(2,128)S(1)}, s32[8,2]{0,1:T(2,128)}, u32[]{:S(2)}) copy-start(s32[8,2]{0,1:T(2,128)} %param.16) | copy-start | bytes 196
  61.3 36.2 %all-to-all-start.1 = ((f32[32,64,128]{2,1,0:T(8,128)}), f32[32,64,128]{2,1,0:T(8,128)S(1)}, u32[]{:S(2)}, u32[]{:S(2)}) async-start(f32[32,64,128]{2,1,0:T(8,128)} %bitcast.16), calls=%async_computation.1 | async-start | bytes 2097152 | tf_op jit(solution)/shard_map/all_to_all | solution.py:588
  74.4 11.9 %collective-permute-start = (f32[2,2,8,8,128]{4,3,2,1,0:T(8,128)}, f32[2,2,8,8,128]{4,3,2,1,0:T(8,128)S(1)}, u32[]{:S(2)}, u32[]{:S(2)}) collective-permute-start(f32[2,2,8,8,128]{4,3,2,1,0:T(8,128)} %get-tuple-element.49), channel_id=1, source_target_pairs={{0,8},{1,9},{2,10},{3,11},{4,12},{5,13},{6,14},{7,15},{8,0},{9,1},... | collective-permute-start | bytes 393224 | tf_op jit(solution)/shard_map/ppermute | solution.py:594
  76.0 13.7 %collective-permute-start.1 = (f32[2,2,8,8,128]{4,3,2,1,0:T(8,128)}, f32[2,2,8,8,128]{4,3,2,1,0:T(8,128)S(1)}, u32[]{:S(2)}, u32[]{:S(2)}) collective-permute-start(f32[2,2,8,8,128]{4,3,2,1,0:T(8,128)} %get-tuple-element.50), channel_id=1, source_target_pairs={{0,9},{1,8},{2,11},{3,10},{4,13},{5,12},{6,15},{7,14},{8,1},{9,0},... | collective-permute-start | bytes 393224 | tf_op jit(solution)/shard_map/ppermute | solution.py:594
  76.0 18.8 %collective-permute-start.2 = (f32[2,2,8,8,128]{4,3,2,1,0:T(8,128)}, f32[2,2,8,8,128]{4,3,2,1,0:T(8,128)S(1)}, u32[]{:S(2)}, u32[]{:S(2)}) collective-permute-start(f32[2,2,8,8,128]{4,3,2,1,0:T(8,128)} %get-tuple-element.51), channel_id=1, source_target_pairs={{0,10},{1,11},{2,8},{3,9},{4,14},{5,15},{6,12},{7,13},{8,2},{9,3},... | collective-permute-start | bytes 393224 | tf_op jit(solution)/shard_map/ppermute | solution.py:594
  78.4 18.2 %collective-permute-start.3 = (f32[2,2,8,8,128]{4,3,2,1,0:T(8,128)}, f32[2,2,8,8,128]{4,3,2,1,0:T(8,128)S(1)}, u32[]{:S(2)}, u32[]{:S(2)}) collective-permute-start(f32[2,2,8,8,128]{4,3,2,1,0:T(8,128)} %get-tuple-element.52), channel_id=1, source_target_pairs={{0,11},{1,10},{2,9},{3,8},{4,15},{5,14},{6,13},{7,12},{8,3},{9,2},... | collective-permute-start | bytes 393224 | tf_op jit(solution)/shard_map/ppermute | solution.py:594
  78.8 18.6 %collective-permute-start.4 = (f32[2,2,8,8,128]{4,3,2,1,0:T(8,128)}, f32[2,2,8,8,128]{4,3,2,1,0:T(8,128)S(1)}, u32[]{:S(2)}, u32[]{:S(2)}) collective-permute-start(f32[2,2,8,8,128]{4,3,2,1,0:T(8,128)} %get-tuple-element.53), channel_id=1, source_target_pairs={{0,1},{1,0},{2,3},{3,2},{4,5},{5,4},{6,7},{7,6},{8,9},{9,8},{10,11... | collective-permute-start | bytes 393224 | tf_op jit(solution)/shard_map/ppermute | solution.py:594
  86.3 17.9 %copy-start.7 = (f32[2,2,8,8,128]{4,3,2,1,0:T(8,128)}, f32[2,2,8,8,128]{4,3,2,1,0:T(8,128)S(1)}, u32[]{:S(2)}) copy-start(f32[2,2,8,8,128]{4,3,2,1,0:T(8,128)S(1)} %collective-permute-done.refs_1_) | copy-start | bytes 393220
  86.3 17.9 %collective-permute-start.5 = (f32[2,2,8,8,128]{4,3,2,1,0:T(8,128)}, f32[2,2,8,8,128]{4,3,2,1,0:T(8,128)S(1)}, u32[]{:S(2)}, u32[]{:S(2)}) collective-permute-start(f32[2,2,8,8,128]{4,3,2,1,0:T(8,128)} %get-tuple-element.55), channel_id=1, source_target_pairs={{0,12},{1,13},{2,14},{3,15},{4,8},{5,9},{6,10},{7,11},{8,4},{9,5},... | collective-permute-start | bytes 393224 | tf_op jit(solution)/shard_map/ppermute | solution.py:594
  89.7 14.4 %copy-start.8 = (f32[2,2,8,8,128]{4,3,2,1,0:T(8,128)}, f32[2,2,8,8,128]{4,3,2,1,0:T(8,128)S(1)}, u32[]{:S(2)}) copy-start(f32[2,2,8,8,128]{4,3,2,1,0:T(8,128)S(1)} %collective-permute-done.1.refs_2_) | copy-start | bytes 393220
  89.7 14.4 %collective-permute-start.6 = (f32[2,2,8,8,128]{4,3,2,1,0:T(8,128)}, f32[2,2,8,8,128]{4,3,2,1,0:T(8,128)S(1)}, u32[]{:S(2)}, u32[]{:S(2)}) collective-permute-start(f32[2,2,8,8,128]{4,3,2,1,0:T(8,128)} %get-tuple-element.56), channel_id=1, source_target_pairs={{0,13},{1,12},{2,15},{3,14},{4,9},{5,8},{6,11},{7,10},{8,5},{9,4},... | collective-permute-start | bytes 393224 | tf_op jit(solution)/shard_map/ppermute | solution.py:594
  94.8 9.3 %copy-start.9 = (f32[2,2,8,8,128]{4,3,2,1,0:T(8,128)}, f32[2,2,8,8,128]{4,3,2,1,0:T(8,128)S(1)}, u32[]{:S(2)}) copy-start(f32[2,2,8,8,128]{4,3,2,1,0:T(8,128)S(1)} %collective-permute-done.2.refs_3_) | copy-start | bytes 393220
  94.8 9.4 %collective-permute-start.7 = (f32[2,2,8,8,128]{4,3,2,1,0:T(8,128)}, f32[2,2,8,8,128]{4,3,2,1,0:T(8,128)S(1)}, u32[]{:S(2)}, u32[]{:S(2)}) collective-permute-start(f32[2,2,8,8,128]{4,3,2,1,0:T(8,128)} %get-tuple-element.57), channel_id=1, source_target_pairs={{0,2},{1,3},{2,0},{3,1},{4,6},{5,7},{6,4},{7,5},{8,10},{9,11},{10,... | collective-permute-start | bytes 393224 | tf_op jit(solution)/shard_map/ppermute | solution.py:594
  96.7 7.5 %copy-start.10 = (f32[2,2,8,8,128]{4,3,2,1,0:T(8,128)}, f32[2,2,8,8,128]{4,3,2,1,0:T(8,128)S(1)}, u32[]{:S(2)}) copy-start(f32[2,2,8,8,128]{4,3,2,1,0:T(8,128)S(1)} %collective-permute-done.3.refs_4_) | copy-start | bytes 393220
  96.7 7.6 %collective-permute-start.8 = (f32[2,2,8,8,128]{4,3,2,1,0:T(8,128)}, f32[2,2,8,8,128]{4,3,2,1,0:T(8,128)S(1)}, u32[]{:S(2)}, u32[]{:S(2)}) collective-permute-start(f32[2,2,8,8,128]{4,3,2,1,0:T(8,128)} %get-tuple-element.58), channel_id=1, source_target_pairs={{0,3},{1,2},{2,1},{3,0},{4,7},{5,6},{6,5},{7,4},{8,11},{9,10},{10,... | collective-permute-start | bytes 393224 | tf_op jit(solution)/shard_map/ppermute | solution.py:594
  97.5 6.7 %copy-start.11 = (f32[2,2,8,8,128]{4,3,2,1,0:T(8,128)}, f32[2,2,8,8,128]{4,3,2,1,0:T(8,128)S(1)}, u32[]{:S(2)}) copy-start(f32[2,2,8,8,128]{4,3,2,1,0:T(8,128)S(1)} %collective-permute-done.4.refs_5_) | copy-start | bytes 393220
  105.0 54.4 %all-to-all-start.2 = ((f32[32,128,128]{2,1,0:T(8,128)}), f32[32,128,128]{2,1,0:T(8,128)S(1)}, u32[]{:S(2)}, u32[]{:S(2)}) async-start(f32[32,128,128]{2,1,0:T(8,128)} %bitcast.9), calls=%async_computation.2 | async-start | bytes 4194304 | tf_op jit(solution)/shard_map/all_to_all | solution.py:588
  110.3 6.9 %copy-start.23 = (f32[2,2,8,8,128]{4,3,2,1,0:T(8,128)S(1)}, f32[2,2,8,8,128]{4,3,2,1,0:T(8,128)}, u32[]{:S(2)}) copy-start(f32[2,2,8,8,128]{4,3,2,1,0:T(8,128)} %get-tuple-element.83) | copy-start | bytes 393220
  110.3 34.7 %copy-start.22 = (f32[2,2,8,8,128]{4,3,2,1,0:T(8,128)S(1)}, f32[2,2,8,8,128]{4,3,2,1,0:T(8,128)}, u32[]{:S(2)}) copy-start(f32[2,2,8,8,128]{4,3,2,1,0:T(8,128)} %get-tuple-element.84) | copy-start | bytes 393220
  112.8 32.2 %collective-permute-start.9 = (f32[2,2,8,8,128]{4,3,2,1,0:T(8,128)S(1)}, f32[2,2,8,8,128]{4,3,2,1,0:T(8,128)S(1)}, u32[]{:S(2)}, u32[]{:S(2)}) collective-permute-start(f32[2,2,8,8,128]{4,3,2,1,0:T(8,128)S(1)} %copy-done.27), channel_id=1, source_target_pairs={{0,4},{1,5},{2,6},{3,7},{4,0},{5,1},{6,2},{7,3},{8,12},{9,13},{10,... | collective-permute-start | bytes 393224 | tf_op jit(solution)/shard_map/ppermute | solution.py:594
  114.3 32.8 %collective-permute-start.10 = (f32[2,2,8,8,128]{4,3,2,1,0:T(8,128)S(1)}, f32[2,2,8,8,128]{4,3,2,1,0:T(8,128)S(1)}, u32[]{:S(2)}, u32[]{:S(2)}) collective-permute-start(f32[2,2,8,8,128]{4,3,2,1,0:T(8,128)S(1)} %copy-done.26), channel_id=1, source_target_pairs={{0,5},{1,4},{2,7},{3,6},{4,1},{5,0},{6,3},{7,2},{8,13},{9,12},{10,... | collective-permute-start | bytes 393224 | tf_op jit(solution)/shard_map/ppermute | solution.py:594
  114.3 32.8 %collective-permute-start.11 = (f32[2,2,8,8,128]{4,3,2,1,0:T(8,128)S(1)}, f32[2,2,8,8,128]{4,3,2,1,0:T(8,128)S(1)}, u32[]{:S(2)}, u32[]{:S(2)}) collective-permute-start(f32[2,2,8,8,128]{4,3,2,1,0:T(8,128)S(1)} %copy-done.25), channel_id=1, source_target_pairs={{0,6},{1,7},{2,4},{3,5},{4,2},{5,3},{6,0},{7,1},{8,14},{9,15},{10,... | collective-permute-start | bytes 393224 | tf_op jit(solution)/shard_map/ppermute | solution.py:594
  116.7 30.4 %collective-permute-start.12 = (f32[2,2,8,8,128]{4,3,2,1,0:T(8,128)S(1)}, f32[2,2,8,8,128]{4,3,2,1,0:T(8,128)S(1)}, u32[]{:S(2)}, u32[]{:S(2)}) collective-permute-start(f32[2,2,8,8,128]{4,3,2,1,0:T(8,128)S(1)} %copy-done.24), channel_id=1, source_target_pairs={{0,7},{1,6},{2,5},{3,4},{4,3},{5,2},{6,1},{7,0},{8,15},{9,14},{10,... | collective-permute-start | bytes 393224 | tf_op jit(solution)/shard_map/ppermute | solution.py:594
  117.2 31.5 %collective-permute-start.13 = (f32[2,2,8,8,128]{4,3,2,1,0:T(8,128)S(1)}, f32[2,2,8,8,128]{4,3,2,1,0:T(8,128)S(1)}, u32[]{:S(2)}, u32[]{:S(2)}) collective-permute-start(f32[2,2,8,8,128]{4,3,2,1,0:T(8,128)S(1)} %copy-done.23), channel_id=1, source_target_pairs={{0,14},{1,15},{2,12},{3,13},{4,10},{5,11},{6,8},{7,9},{8,6},{9,7},... | collective-permute-start | bytes 393224 | tf_op jit(solution)/shard_map/ppermute | solution.py:594
  145.0 8.5 %copy-start.16 = (f32[2,2,8,8,128]{4,3,2,1,0:T(8,128)}, f32[2,2,8,8,128]{4,3,2,1,0:T(8,128)S(1)}, u32[]{:S(2)}) copy-start(f32[2,2,8,8,128]{4,3,2,1,0:T(8,128)S(1)} %collective-permute-done.9.refs_10_) | copy-start | bytes 393220
  145.0 8.5 %collective-permute-start.14 = (f32[2,2,8,8,128]{4,3,2,1,0:T(8,128)S(1)}, f32[2,2,8,8,128]{4,3,2,1,0:T(8,128)S(1)}, u32[]{:S(2)}, u32[]{:S(2)}) collective-permute-start(f32[2,2,8,8,128]{4,3,2,1,0:T(8,128)S(1)} %copy-done.22), channel_id=1, source_target_pairs={{0,15},{1,14},{2,13},{3,12},{4,11},{5,10},{6,9},{7,8},{8,7},{9,6},... | collective-permute-start | bytes 393224 | tf_op jit(solution)/shard_map/ppermute | solution.py:594
  (14 other events, 45.6 us)

commit v15 on v11

--- a/solution.py
+++ b/solution.py
@@ -465,7 +465,7 @@
         in_specs=[smem, vmem, vmem],
         out_specs=vmem,
         out_shape=jax.ShapeDtypeStruct((2, depth, one.shape[1]), jnp.bfloat16),
-        compiler_params=pltpu.CompilerParams(vmem_limit_bytes=32 << 20),
+        compiler_params=pltpu.CompilerParams(vmem_limit_bytes=63 << 20),
         name="prepare",
     )(me, both, one)
 
@@ -508,12 +508,12 @@
             pltpu.SemaphoreType.DMA((len(pieces),)),
             pltpu.SemaphoreType.DMA((components,)),
         ],
-        compiler_params=pltpu.CompilerParams(vmem_limit_bytes=32 << 20),
+        compiler_params=pltpu.CompilerParams(vmem_limit_bytes=63 << 20),
         name="fold",
     )(*pieces)
 
 
-def frequency_kernel(y_ref, m_hbm, f_hbm, out_ref, m_ref, f_ref, stage, m_sem, f_sems, sems):
+def frequency_kernel(y_hbm, m_hbm, f_hbm, out_ref, y_ref, m_ref, f_ref, stage, y_sems, m_sem, f_sems, sems):
     devices, _, components, rows, lanes = y_ref.shape
     groups = sems.shape[0]
     members = components // groups
@@ -521,8 +521,13 @@
     load = pltpu.make_async_copy(m_hbm, m_ref, m_sem)
     spans = [pl.ds(group * members, members) for group in range(groups)]
     loads = [pltpu.make_async_copy(f_hbm.at[span], f_ref.at[span], f_sems.at[k]) for k, span in enumerate(spans)]
-    for copy in [load] + loads:
-        copy.start()
+    blocks = [
+        pltpu.make_async_copy(y_hbm.at[:, :, span], y_ref.at[:, :, span], y_sems.at[k]) for k, span in enumerate(spans)
+    ]
+    load.start()
+    for pair in zip(blocks, loads):
+        for copy in pair:
+            copy.start()
     upper_rows = lax.broadcasted_iota(jnp.int32, (devices, rows, lanes), 1) < rows // 2
 
     def one_values(group):
@@ -541,6 +546,7 @@
 
     copies = []
     for group, span in enumerate(spans):
+        blocks[group].wait()
         parts = one_values(group)
         if group == 0:
             load.wait()
@@ -567,18 +573,20 @@
     groups = components // 2
     return pl.pallas_call(
         frequency_kernel,
-        in_specs=[pl.BlockSpec(memory_space=pltpu.VMEM), hbm, hbm],
+        in_specs=[hbm, hbm, hbm],
         out_specs=hbm,
         out_shape=jax.ShapeDtypeStruct(shape, jnp.float32),
         scratch_shapes=[
+            pltpu.VMEM(y.shape, jnp.float32),
             pltpu.VMEM(matrix.shape, jnp.bfloat16),
             pltpu.VMEM(folded.shape, jnp.bfloat16),
             pltpu.VMEM(shape, jnp.float32),
+            pltpu.SemaphoreType.DMA((groups,)),
             pltpu.SemaphoreType.DMA,
             pltpu.SemaphoreType.DMA((groups,)),
             pltpu.SemaphoreType.DMA((groups,)),
         ],
-        compiler_params=pltpu.CompilerParams(vmem_limit_bytes=44 << 20),
+        compiler_params=pltpu.CompilerParams(vmem_limit_bytes=63 << 20),
         name="to_frequencies",
     )(y, matrix, folded)
 

time: 170 us -> 168 us (0.988)
  local copies, waits for them, and re-layouts: 9.04 us -> 1.45 us
  Pallas kernels: 36.7 us -> 40.9 us
  waiting for transfers between devices: 85.9 us -> 88.4 us
    unnamed x60 -> x46, local copies, waits for them, and re-layouts: 9.04 us -> 1.45 us
    pallas_call x1, Pallas kernels: 5.48 us -> 8.1 us  [to_frequencies(): pl.pallas_call(frequency_kernel, in_specs=[hbm, hbm, hbm], out_specs=hbm,...]
    pallas_call x1, Pallas kernels: 0.14 us -> 2.38 us  [prepare(): pl.pallas_call(prepare_kernel, in_specs=[smem, vmem, vmem], out_specs=vme...]
    all_to_all x3, waiting for transfers between devices: 42.3 us -> 44.3 us  [exchange(): lax.all_to_all(flat, 'kb', split_axis=0, concat_axis=0, tiled=True)]
  transfers between devices with their start and end apart: 18 -> 18, of which waited for: 9 -> 9; matrix products, arithmetic and copies ran while one was open for 0% -> 0% of each run, Pallas kernels for 16% -> 17%
where the time goes in v15:
time: 168 us
  waiting for transfers between devices  88.4 us (53%)
  Pallas kernels  40.9 us (24%)
  starting transfers between devices  36.6 us (22%)
    all_to_all x3, waiting for transfers between devices, exchange(): lax.all_to_all(flat, 'kb', split_axis=0, concat_axis=0, tiled=True)  44.3 us
    ppermute x15, waiting for transfers between devices, swap(): lax.ppermute(piece, 'kb', [(device, device ^ slot) for device in range(de...  44.1 us
    ppermute x15, starting transfers between devices, swap(): lax.ppermute(piece, 'kb', [(device, device ^ slot) for device in range(de...  19.6 us
    all_to_all x3, starting transfers between devices, exchange(): lax.all_to_all(flat, 'kb', split_axis=0, concat_axis=0, tiled=True)  17 us
    pallas_call x2, Pallas kernels, to_times(): pl.pallas_call(kernel, in_specs=[hbm, hbm], out_specs=hbm, out_shape=jax....  11.6 us
    pallas_call x1, Pallas kernels, both_middle(): pl.pallas_call(both_middle_kernel, in_specs=[pl.BlockSpec(memory_space=pl...  8.97 us
    pallas_call x1, Pallas kernels, to_frequencies(): pl.pallas_call(frequency_kernel, in_specs=[hbm, hbm, hbm], out_specs=hbm,...  8.1 us
    pallas_call x1, Pallas kernels, one_middle(): pl.pallas_call(one_middle_kernel, in_specs=specs, out_specs=pl.BlockSpec(...  6.59 us
  transfers between devices with their start and end apart: 18, of which 9 were waited for; matrix products, arithmetic and copies ran while one was open for 0% of the time, Pallas kernels for 17%

profile of v15, /device:TPU:0, one launch (start us, length us, event | category | flops | bytes accessed | tf_op | source)
XLA Modules:
  0.0 167.8 jit_solution(9638047301260563725)
XLA Ops:
  0.0 4.9 %both_times.1 = f32[32,2,2,4,8,128]{5,4,3,2,1,0:T(8,128)} custom-call(f32[2,4,128,512]{3,2,1,0:T(8,128)} %g_hbm.2, f32[256,512]{1,0:T(8,128)} %constant.20.clone.m_hbm), custom_call_target="tpu_custom_call" | custom-call | tf_op jit(solution)/shard_map/both_times/pallas_call | solution.py:186
  4.9 7.4 %all-to-all-start = ((f32[32,128,128]{2,1,0:T(8,128)}), f32[32,128,128]{2,1,0:T(8,128)}, u32[]{:S(2)}, u32[]{:S(2)}) async-start(f32[32,128,128]{2,1,0:T(8,128)} %bitcast.14), calls=%async_computation | async-start | bytes 4194304 | tf_op jit(solution)/shard_map/all_to_all | solution.py:596
  12.3 6.7 %one_times.1 = f32[32,2,4,8,128]{4,3,2,1,0:T(8,128)} custom-call(f32[2,4,128,512]{3,2,1,0:T(8,128)} %g_hbm.2, f32[512,512]{1,0:T(8,128)} %constant.21.clone.m_hbm), custom_call_target="tpu_custom_call" | custom-call | tf_op jit(solution)/shard_map/one_times/pallas_call | solution.py:186
  19.1 42.2 %all-to-all-done = f32[32,128,128]{2,1,0:T(8,128)} async-done(((f32[32,128,128]{2,1,0:T(8,128)}), f32[32,128,128]{2,1,0:T(8,128)}, u32[]{:S(2)}, u32[]{:S(2)}) %all-to-all-start) | async-done | bytes 2097184 | tf_op jit(solution)/shard_map/all_to_all | solution.py:596
  61.3 4.2 %all-to-all-start.1 = ((f32[32,64,128]{2,1,0:T(8,128)}), f32[32,64,128]{2,1,0:T(8,128)S(1)}, u32[]{:S(2)}, u32[]{:S(2)}) async-start(f32[32,64,128]{2,1,0:T(8,128)} %bitcast.15), calls=%async_computation.1 | async-start | bytes 2097152 | tf_op jit(solution)/shard_map/all_to_all | solution.py:596
  65.5 9.0 %both_middle.1 = (f32[2,2,8,8,128]{4,3,2,1,0:T(8,128)}, f32[2,2,8,8,128]{4,3,2,1,0:T(8,128)}, f32[2,2,8,8,128]{4,3,2,1,0:T(8,128)}, f32[2,2,8,8,128]{4,3,2,1,0:T...) custom-call(s32[1]{0:T(128)} %bitcast.5.me_ref, ...), custom_call_target="tpu_custom_call" | custom-call | tf_op jit(solution)/shard_map/both_middle/pallas_call | solution.py:434
  74.4 1.6 collective-permute-start
  76.1 2.4 %collective-permute-start.2 = (f32[2,2,8,8,128]{4,3,2,1,0:T(8,128)}, f32[2,2,8,8,128]{4,3,2,1,0:T(8,128)S(1)}, u32[]{:S(2)}, u32[]{:S(2)}) collective-permute-start(f32[2,2,8,8,128]{4,3,2,1,0:T(8,128)} %get-tuple-element.51), channel_id=1, source_target_pairs={{0,10},{1,11},{2,8},{3,9},{4,14},{5,15},{6,12},{7,13},{8,2},{9,3},... | collective-permute-start | bytes 393224 | tf_op jit(solution)/shard_map/ppermute | solution.py:602
  78.5 0.4 collective-permute-start.3
  79.1 7.1 %collective-permute-done.refs_1_ = f32[2,2,8,8,128]{4,3,2,1,0:T(8,128)S(1)} collective-permute-done((f32[2,2,8,8,128]{4,3,2,1,0:T(8,128)}, f32[2,2,8,8,128]{4,3,2,1,0:T(8,128)S(1)}, u32[]{:S(2)}, u32[]{:S(2)}) %collective-permute-start) | collective-permute-done | bytes 131104 | tf_op jit(solution)/shard_map/ppermute | solution.py:602
  86.3 3.5 %collective-permute-start.5 = (f32[2,2,8,8,128]{4,3,2,1,0:T(8,128)}, f32[2,2,8,8,128]{4,3,2,1,0:T(8,128)S(1)}, u32[]{:S(2)}, u32[]{:S(2)}) collective-permute-start(f32[2,2,8,8,128]{4,3,2,1,0:T(8,128)} %get-tuple-element.55), channel_id=1, source_target_pairs={{0,12},{1,13},{2,14},{3,15},{4,8},{5,9},{6,10},{7,11},{8,4},{9,5},... | collective-permute-start | bytes 393224 | tf_op jit(solution)/shard_map/ppermute | solution.py:602
  89.7 2.5 %collective-permute-start.6 = (f32[2,2,8,8,128]{4,3,2,1,0:T(8,128)}, f32[2,2,8,8,128]{4,3,2,1,0:T(8,128)S(1)}, u32[]{:S(2)}, u32[]{:S(2)}) collective-permute-start(f32[2,2,8,8,128]{4,3,2,1,0:T(8,128)} %get-tuple-element.56), channel_id=1, source_target_pairs={{0,13},{1,12},{2,15},{3,14},{4,9},{5,8},{6,11},{7,10},{8,5},{9,4},... | collective-permute-start | bytes 393224 | tf_op jit(solution)/shard_map/ppermute | solution.py:602
  92.3 2.5 %collective-permute-done.2.refs_3_ = f32[2,2,8,8,128]{4,3,2,1,0:T(8,128)S(1)} collective-permute-done((f32[2,2,8,8,128]{4,3,2,1,0:T(8,128)}, f32[2,2,8,8,128]{4,3,2,1,0:T(8,128)S(1)}, u32[]{:S(2)}, u32[]{:S(2)}) %collective-permute-start.2) | collective-permute-done | bytes 131104 | tf_op jit(solution)/shard_map/ppermute | solution.py:602
  94.8 0.4 collective-permute-start.7
  95.2 1.4 collective-permute-done.3.refs_4_
  96.7 0.8 collective-permute-start.8
  97.5 6.6 %one_middle.1 = f32[16,2,2,8,8,128]{5,4,3,2,1,0:T(8,128)} custom-call(s32[2,8]{1,0:T(2,128)S(1)} %bitcast.13, s32[3,16]{1,0:T(4,128)S(1)} %copy-done.4, bf16[256,256]{1,0:T(8,128)(2,1)S(1)} %copy-done.3, bf16[256,256]{1,0:T(8,128)(2,1)S(1)} %copy-done.2, bf16[256,256]{1,0:T(8,128)(2,1)S(1)} %copy-done.1, bf16[256,256]{1,0:T(8,128)(2,1)S(1)} %copy-done, ...), custom_call_target="tpu_custom_call" | custom-call | flops 6000000000 | bytes 12000000 | tf_op jit(solution)/shard_map/one_middle/pallas_call | solution.py:407
  104.3 0.6 copy-done.11
  105.0 5.4 %all-to-all-start.2 = ((f32[32,128,128]{2,1,0:T(8,128)}), f32[32,128,128]{2,1,0:T(8,128)}, u32[]{:S(2)}, u32[]{:S(2)}) async-start(f32[32,128,128]{2,1,0:T(8,128)} %bitcast.9), calls=%async_computation.2 | async-start | bytes 4194304 | tf_op jit(solution)/shard_map/all_to_all | solution.py:596
  110.4 2.4 %prepare.1.m_hbm = bf16[2,512,512]{2,1,0:T(8,128)(2,1)} custom-call(s32[1]{0:T(128)} %bitcast.5.me_ref, f32[2,16,8,512]{3,2,1,0:T(8,128)} %constant.26.clone.both_ref, f32[256,512]{1,0:T(8,128)} %constant.27.clone.one_ref), custom_call_target="tpu_custom_call" | custom-call | tf_op jit(solution)/shard_map/prepare/pallas_call | solution.py:463
  112.8 1.5 collective-permute-start.9
  114.3 2.4 %collective-permute-start.11 = (f32[2,2,8,8,128]{4,3,2,1,0:T(8,128)}, f32[2,2,8,8,128]{4,3,2,1,0:T(8,128)S(1)}, u32[]{:S(2)}, u32[]{:S(2)}) collective-permute-start(f32[2,2,8,8,128]{4,3,2,1,0:T(8,128)} %get-tuple-element.81), channel_id=1, source_target_pairs={{0,6},{1,7},{2,4},{3,5},{4,2},{5,3},{6,0},{7,1},{8,14},{9,15},{10,... | collective-permute-start | bytes 393224 | tf_op jit(solution)/shard_map/ppermute | solution.py:602
  116.7 0.5 collective-permute-start.12
  117.2 3.3 %collective-permute-start.13 = (f32[2,2,8,8,128]{4,3,2,1,0:T(8,128)}, f32[2,2,8,8,128]{4,3,2,1,0:T(8,128)S(1)}, u32[]{:S(2)}, u32[]{:S(2)}) collective-permute-start(f32[2,2,8,8,128]{4,3,2,1,0:T(8,128)} %get-tuple-element.83), channel_id=1, source_target_pairs={{0,14},{1,15},{2,12},{3,13},{4,10},{5,11},{6,8},{7,9},{8,6},{9,7},... | collective-permute-start | bytes 393224 | tf_op jit(solution)/shard_map/ppermute | solution.py:602
  120.5 24.5 %collective-permute-done.9.refs_10_ = f32[2,2,8,8,128]{4,3,2,1,0:T(8,128)S(1)} collective-permute-done((f32[2,2,8,8,128]{4,3,2,1,0:T(8,128)S(1)}, f32[2,2,8,8,128]{4,3,2,1,0:T(8,128)S(1)}, u32[]{:S(2)}, u32[]{:S(2)}) %collective-permute-start.9) | collective-permute-done | bytes 131104 | tf_op jit(solution)/shard_map/ppermute | solution.py:602
  145.0 2.2 %collective-permute-done.10.refs_11_ = f32[2,2,8,8,128]{4,3,2,1,0:T(8,128)S(1)} collective-permute-done((f32[2,2,8,8,128]{4,3,2,1,0:T(8,128)}, f32[2,2,8,8,128]{4,3,2,1,0:T(8,128)S(1)}, u32[]{:S(2)}, u32[]{:S(2)}) %collective-permute-start.10) | collective-permute-done | bytes 131104 | tf_op jit(solution)/shard_map/ppermute | solution.py:602
  147.2 1.6 collective-permute-done.13.refs_14_
  148.8 4.7 %collective-permute-done.14.refs_15_ = f32[2,2,8,8,128]{4,3,2,1,0:T(8,128)S(1)} collective-permute-done((f32[2,2,8,8,128]{4,3,2,1,0:T(8,128)S(1)}, f32[2,2,8,8,128]{4,3,2,1,0:T(8,128)S(1)}, u32[]{:S(2)}, u32[]{:S(2)}) %collective-permute-start.14) | collective-permute-done | bytes 131104 | tf_op jit(solution)/shard_map/ppermute | solution.py:602
  153.5 0.6 copy-done.20
  154.1 3.3 %fold.1.f_hbm = bf16[8,2,256,256]{3,2,1,0:T(8,128)(2,1)} custom-call(f32[2,2,8,8,128]{4,3,2,1,0:T(8,128)} %get-tuple-element.69.refs_0_, f32[2,2,8,8,128]{4,3,2,1,0:T(8,128)} %copy-done.6, f32[2,2,8,8,128]{4,3,2,1,0:T(8,128)} %copy-done.7, f32[2,2,8,8,128]{4,3,2,1,0:T(8,128)} %copy-done.8, f32[2,2,8,8,128]{4,3,2,1,0:T(8,128)} %copy-done.9, ...), custom_call_target="tpu_custom_call" | custom-call | tf_op jit(solution)/shard_map/fold/pallas_call | solution.py:500
  157.4 2.1 %all-to-all-done.2 = f32[32,128,128]{2,1,0:T(8,128)} async-done(((f32[32,128,128]{2,1,0:T(8,128)}), f32[32,128,128]{2,1,0:T(8,128)}, u32[]{:S(2)}, u32[]{:S(2)}) %all-to-all-start.2) | async-done | bytes 2097184 | tf_op jit(solution)/shard_map/all_to_all | solution.py:596
  159.6 8.1 %to_frequencies.1 = f32[2,8,128,512]{3,2,1,0:T(8,128)} custom-call(f32[32,2,8,8,128]{4,3,2,1,0:T(8,128)} %bitcast.10.y_hbm, bf16[2,512,512]{2,1,0:T(8,128)(2,1)} %prepare.1.m_hbm, bf16[8,2,256,256]{3,2,1,0:T(8,128)(2,1)} %fold.1.f_hbm), custom_call_target="tpu_custom_call" | custom-call | tf_op jit(solution)/shard_map/to_frequencies/pallas_call | solution.py:574
  (57 shorter events, 0.5 us)
Async XLA Ops:
  4.9 56.3 %all-to-all-start = ((f32[32,128,128]{2,1,0:T(8,128)}), f32[32,128,128]{2,1,0:T(8,128)}, u32[]{:S(2)}, u32[]{:S(2)}) async-start(f32[32,128,128]{2,1,0:T(8,128)} %bitcast.14), calls=%async_computation | async-start | bytes 4194304 | tf_op jit(solution)/shard_map/all_to_all | solution.py:596
  61.2 36.2 %copy-start = (bf16[256,256]{1,0:T(8,128)(2,1)S(1)}, bf16[256,256]{1,0:T(8,128)(2,1)}, u32[]{:S(2)}) copy-start(bf16[256,256]{1,0:T(8,128)(2,1)} %constant.25.clone.sl_ref) | copy-start | bytes 393220
  61.2 36.3 %copy-start.1 = (bf16[256,256]{1,0:T(8,128)(2,1)S(1)}, bf16[256,256]{1,0:T(8,128)(2,1)}, u32[]{:S(2)}) copy-start(bf16[256,256]{1,0:T(8,128)(2,1)} %constant.24.clone.sh_ref) | copy-start | bytes 393220
  61.2 36.3 %copy-start.2 = (bf16[256,256]{1,0:T(8,128)(2,1)S(1)}, bf16[256,256]{1,0:T(8,128)(2,1)}, u32[]{:S(2)}) copy-start(bf16[256,256]{1,0:T(8,128)(2,1)} %constant.23.clone.cl_ref) | copy-start | bytes 393220
  61.2 36.3 %copy-start.3 = (bf16[256,256]{1,0:T(8,128)(2,1)S(1)}, bf16[256,256]{1,0:T(8,128)(2,1)}, u32[]{:S(2)}) copy-start(bf16[256,256]{1,0:T(8,128)(2,1)} %constant.22.clone.ch_ref) | copy-start | bytes 393220
  61.2 36.3 %copy-start.4 = (s32[3,16]{1,0:T(4,128)S(1)}, s32[3,16]{1,0:T(4,128)}, u32[]{:S(2)}) copy-start(s32[3,16]{1,0:T(4,128)} %mirror_ref.3) | copy-start | bytes 580
  61.2 36.3 %copy-start.5 = (s32[8,2]{0,1:T(2,128)S(1)}, s32[8,2]{0,1:T(2,128)}, u32[]{:S(2)}) copy-start(s32[8,2]{0,1:T(2,128)} %param.16) | copy-start | bytes 196
  61.3 36.2 %all-to-all-start.1 = ((f32[32,64,128]{2,1,0:T(8,128)}), f32[32,64,128]{2,1,0:T(8,128)S(1)}, u32[]{:S(2)}, u32[]{:S(2)}) async-start(f32[32,64,128]{2,1,0:T(8,128)} %bitcast.15), calls=%async_computation.1 | async-start | bytes 2097152 | tf_op jit(solution)/shard_map/all_to_all | solution.py:596
  74.4 11.8 %collective-permute-start = (f32[2,2,8,8,128]{4,3,2,1,0:T(8,128)}, f32[2,2,8,8,128]{4,3,2,1,0:T(8,128)S(1)}, u32[]{:S(2)}, u32[]{:S(2)}) collective-permute-start(f32[2,2,8,8,128]{4,3,2,1,0:T(8,128)} %get-tuple-element.49), channel_id=1, source_target_pairs={{0,8},{1,9},{2,10},{3,11},{4,12},{5,13},{6,14},{7,15},{8,0},{9,1},... | collective-permute-start | bytes 393224 | tf_op jit(solution)/shard_map/ppermute | solution.py:602
  76.1 13.7 %collective-permute-start.1 = (f32[2,2,8,8,128]{4,3,2,1,0:T(8,128)}, f32[2,2,8,8,128]{4,3,2,1,0:T(8,128)S(1)}, u32[]{:S(2)}, u32[]{:S(2)}) collective-permute-start(f32[2,2,8,8,128]{4,3,2,1,0:T(8,128)} %get-tuple-element.50), channel_id=1, source_target_pairs={{0,9},{1,8},{2,11},{3,10},{4,13},{5,12},{6,15},{7,14},{8,1},{9,0},... | collective-permute-start | bytes 393224 | tf_op jit(solution)/shard_map/ppermute | solution.py:602
  76.1 18.7 %collective-permute-start.2 = (f32[2,2,8,8,128]{4,3,2,1,0:T(8,128)}, f32[2,2,8,8,128]{4,3,2,1,0:T(8,128)S(1)}, u32[]{:S(2)}, u32[]{:S(2)}) collective-permute-start(f32[2,2,8,8,128]{4,3,2,1,0:T(8,128)} %get-tuple-element.51), channel_id=1, source_target_pairs={{0,10},{1,11},{2,8},{3,9},{4,14},{5,15},{6,12},{7,13},{8,2},{9,3},... | collective-permute-start | bytes 393224 | tf_op jit(solution)/shard_map/ppermute | solution.py:602
  78.5 18.2 %collective-permute-start.3 = (f32[2,2,8,8,128]{4,3,2,1,0:T(8,128)}, f32[2,2,8,8,128]{4,3,2,1,0:T(8,128)S(1)}, u32[]{:S(2)}, u32[]{:S(2)}) collective-permute-start(f32[2,2,8,8,128]{4,3,2,1,0:T(8,128)} %get-tuple-element.52), channel_id=1, source_target_pairs={{0,11},{1,10},{2,9},{3,8},{4,15},{5,14},{6,13},{7,12},{8,3},{9,2},... | collective-permute-start | bytes 393224 | tf_op jit(solution)/shard_map/ppermute | solution.py:602
  78.9 18.6 %collective-permute-start.4 = (f32[2,2,8,8,128]{4,3,2,1,0:T(8,128)}, f32[2,2,8,8,128]{4,3,2,1,0:T(8,128)S(1)}, u32[]{:S(2)}, u32[]{:S(2)}) collective-permute-start(f32[2,2,8,8,128]{4,3,2,1,0:T(8,128)} %get-tuple-element.53), channel_id=1, source_target_pairs={{0,1},{1,0},{2,3},{3,2},{4,5},{5,4},{6,7},{7,6},{8,9},{9,8},{10,11... | collective-permute-start | bytes 393224 | tf_op jit(solution)/shard_map/ppermute | solution.py:602
  86.3 17.9 %copy-start.6 = (f32[2,2,8,8,128]{4,3,2,1,0:T(8,128)}, f32[2,2,8,8,128]{4,3,2,1,0:T(8,128)S(1)}, u32[]{:S(2)}) copy-start(f32[2,2,8,8,128]{4,3,2,1,0:T(8,128)S(1)} %collective-permute-done.refs_1_) | copy-start | bytes 393220
  86.3 17.9 %collective-permute-start.5 = (f32[2,2,8,8,128]{4,3,2,1,0:T(8,128)}, f32[2,2,8,8,128]{4,3,2,1,0:T(8,128)S(1)}, u32[]{:S(2)}, u32[]{:S(2)}) collective-permute-start(f32[2,2,8,8,128]{4,3,2,1,0:T(8,128)} %get-tuple-element.55), channel_id=1, source_target_pairs={{0,12},{1,13},{2,14},{3,15},{4,8},{5,9},{6,10},{7,11},{8,4},{9,5},... | collective-permute-start | bytes 393224 | tf_op jit(solution)/shard_map/ppermute | solution.py:602
  89.7 14.4 %copy-start.7 = (f32[2,2,8,8,128]{4,3,2,1,0:T(8,128)}, f32[2,2,8,8,128]{4,3,2,1,0:T(8,128)S(1)}, u32[]{:S(2)}) copy-start(f32[2,2,8,8,128]{4,3,2,1,0:T(8,128)S(1)} %collective-permute-done.1.refs_2_) | copy-start | bytes 393220
  89.7 14.4 %collective-permute-start.6 = (f32[2,2,8,8,128]{4,3,2,1,0:T(8,128)}, f32[2,2,8,8,128]{4,3,2,1,0:T(8,128)S(1)}, u32[]{:S(2)}, u32[]{:S(2)}) collective-permute-start(f32[2,2,8,8,128]{4,3,2,1,0:T(8,128)} %get-tuple-element.56), channel_id=1, source_target_pairs={{0,13},{1,12},{2,15},{3,14},{4,9},{5,8},{6,11},{7,10},{8,5},{9,4},... | collective-permute-start | bytes 393224 | tf_op jit(solution)/shard_map/ppermute | solution.py:602
  94.8 9.3 %copy-start.8 = (f32[2,2,8,8,128]{4,3,2,1,0:T(8,128)}, f32[2,2,8,8,128]{4,3,2,1,0:T(8,128)S(1)}, u32[]{:S(2)}) copy-start(f32[2,2,8,8,128]{4,3,2,1,0:T(8,128)S(1)} %collective-permute-done.2.refs_3_) | copy-start | bytes 393220
  94.8 9.4 %collective-permute-start.7 = (f32[2,2,8,8,128]{4,3,2,1,0:T(8,128)}, f32[2,2,8,8,128]{4,3,2,1,0:T(8,128)S(1)}, u32[]{:S(2)}, u32[]{:S(2)}) collective-permute-start(f32[2,2,8,8,128]{4,3,2,1,0:T(8,128)} %get-tuple-element.57), channel_id=1, source_target_pairs={{0,2},{1,3},{2,0},{3,1},{4,6},{5,7},{6,4},{7,5},{8,10},{9,11},{10,... | collective-permute-start | bytes 393224 | tf_op jit(solution)/shard_map/ppermute | solution.py:602
  96.7 7.5 %copy-start.9 = (f32[2,2,8,8,128]{4,3,2,1,0:T(8,128)}, f32[2,2,8,8,128]{4,3,2,1,0:T(8,128)S(1)}, u32[]{:S(2)}) copy-start(f32[2,2,8,8,128]{4,3,2,1,0:T(8,128)S(1)} %collective-permute-done.3.refs_4_) | copy-start | bytes 393220
  96.7 7.6 %collective-permute-start.8 = (f32[2,2,8,8,128]{4,3,2,1,0:T(8,128)}, f32[2,2,8,8,128]{4,3,2,1,0:T(8,128)S(1)}, u32[]{:S(2)}, u32[]{:S(2)}) collective-permute-start(f32[2,2,8,8,128]{4,3,2,1,0:T(8,128)} %get-tuple-element.58), channel_id=1, source_target_pairs={{0,3},{1,2},{2,1},{3,0},{4,7},{5,6},{6,5},{7,4},{8,11},{9,10},{10,... | collective-permute-start | bytes 393224 | tf_op jit(solution)/shard_map/ppermute | solution.py:602
  97.5 6.7 %copy-start.10 = (f32[2,2,8,8,128]{4,3,2,1,0:T(8,128)}, f32[2,2,8,8,128]{4,3,2,1,0:T(8,128)S(1)}, u32[]{:S(2)}) copy-start(f32[2,2,8,8,128]{4,3,2,1,0:T(8,128)S(1)} %collective-permute-done.4.refs_5_) | copy-start | bytes 393220
  105.0 54.6 %all-to-all-start.2 = ((f32[32,128,128]{2,1,0:T(8,128)}), f32[32,128,128]{2,1,0:T(8,128)}, u32[]{:S(2)}, u32[]{:S(2)}) async-start(f32[32,128,128]{2,1,0:T(8,128)} %bitcast.9), calls=%async_computation.2 | async-start | bytes 4194304 | tf_op jit(solution)/shard_map/all_to_all | solution.py:596
  110.4 34.6 %copy-start.21 = (f32[2,2,8,8,128]{4,3,2,1,0:T(8,128)S(1)}, f32[2,2,8,8,128]{4,3,2,1,0:T(8,128)}, u32[]{:S(2)}) copy-start(f32[2,2,8,8,128]{4,3,2,1,0:T(8,128)} %get-tuple-element.84) | copy-start | bytes 393220
  112.8 32.2 %collective-permute-start.9 = (f32[2,2,8,8,128]{4,3,2,1,0:T(8,128)S(1)}, f32[2,2,8,8,128]{4,3,2,1,0:T(8,128)S(1)}, u32[]{:S(2)}, u32[]{:S(2)}) collective-permute-start(f32[2,2,8,8,128]{4,3,2,1,0:T(8,128)S(1)} %copy-done.22), channel_id=1, source_target_pairs={{0,4},{1,5},{2,6},{3,7},{4,0},{5,1},{6,2},{7,3},{8,12},{9,13},{10,... | collective-permute-start | bytes 393224 | tf_op jit(solution)/shard_map/ppermute | solution.py:602
  114.3 32.9 %collective-permute-start.10 = (f32[2,2,8,8,128]{4,3,2,1,0:T(8,128)}, f32[2,2,8,8,128]{4,3,2,1,0:T(8,128)S(1)}, u32[]{:S(2)}, u32[]{:S(2)}) collective-permute-start(f32[2,2,8,8,128]{4,3,2,1,0:T(8,128)} %get-tuple-element.80), channel_id=1, source_target_pairs={{0,5},{1,4},{2,7},{3,6},{4,1},{5,0},{6,3},{7,2},{8,13},{9,12},{10,... | collective-permute-start | bytes 393224 | tf_op jit(solution)/shard_map/ppermute | solution.py:602
  114.3 32.9 %collective-permute-start.11 = (f32[2,2,8,8,128]{4,3,2,1,0:T(8,128)}, f32[2,2,8,8,128]{4,3,2,1,0:T(8,128)S(1)}, u32[]{:S(2)}, u32[]{:S(2)}) collective-permute-start(f32[2,2,8,8,128]{4,3,2,1,0:T(8,128)} %get-tuple-element.81), channel_id=1, source_target_pairs={{0,6},{1,7},{2,4},{3,5},{4,2},{5,3},{6,0},{7,1},{8,14},{9,15},{10,... | collective-permute-start | bytes 393224 | tf_op jit(solution)/shard_map/ppermute | solution.py:602
  116.7 30.5 %collective-permute-start.12 = (f32[2,2,8,8,128]{4,3,2,1,0:T(8,128)}, f32[2,2,8,8,128]{4,3,2,1,0:T(8,128)S(1)}, u32[]{:S(2)}, u32[]{:S(2)}) collective-permute-start(f32[2,2,8,8,128]{4,3,2,1,0:T(8,128)} %get-tuple-element.82), channel_id=1, source_target_pairs={{0,7},{1,6},{2,5},{3,4},{4,3},{5,2},{6,1},{7,0},{8,15},{9,14},{10,... | collective-permute-start | bytes 393224 | tf_op jit(solution)/shard_map/ppermute | solution.py:602
  117.2 31.6 %collective-permute-start.13 = (f32[2,2,8,8,128]{4,3,2,1,0:T(8,128)}, f32[2,2,8,8,128]{4,3,2,1,0:T(8,128)S(1)}, u32[]{:S(2)}, u32[]{:S(2)}) collective-permute-start(f32[2,2,8,8,128]{4,3,2,1,0:T(8,128)} %get-tuple-element.83), channel_id=1, source_target_pairs={{0,14},{1,15},{2,12},{3,13},{4,10},{5,11},{6,8},{7,9},{8,6},{9,7},... | collective-permute-start | bytes 393224 | tf_op jit(solution)/shard_map/ppermute | solution.py:602
  145.0 8.5 %copy-start.15 = (f32[2,2,8,8,128]{4,3,2,1,0:T(8,128)}, f32[2,2,8,8,128]{4,3,2,1,0:T(8,128)S(1)}, u32[]{:S(2)}) copy-start(f32[2,2,8,8,128]{4,3,2,1,0:T(8,128)S(1)} %collective-permute-done.9.refs_10_) | copy-start | bytes 393220
  145.0 8.5 %collective-permute-start.14 = (f32[2,2,8,8,128]{4,3,2,1,0:T(8,128)S(1)}, f32[2,2,8,8,128]{4,3,2,1,0:T(8,128)S(1)}, u32[]{:S(2)}, u32[]{:S(2)}) collective-permute-start(f32[2,2,8,8,128]{4,3,2,1,0:T(8,128)S(1)} %copy-done.21), channel_id=1, source_target_pairs={{0,15},{1,14},{2,13},{3,12},{4,11},{5,10},{6,9},{7,8},{8,7},{9,6},... | collective-permute-start | bytes 393224 | tf_op jit(solution)/shard_map/ppermute | solution.py:602
  147.2 6.3 %copy-start.16 = (f32[2,2,8,8,128]{4,3,2,1,0:T(8,128)}, f32[2,2,8,8,128]{4,3,2,1,0:T(8,128)S(1)}, u32[]{:S(2)}) copy-start(f32[2,2,8,8,128]{4,3,2,1,0:T(8,128)S(1)} %collective-permute-done.10.refs_11_) | copy-start | bytes 393220
  (9 other events, 23.2 us)
